TPU v7x, 256 devices: a whole 4x4x8 slice. The times are simulated.
256 devices in a mesh: rows: 64 (over z_lo, y, x, core), heads: 4 (over z_hi).
Axes of the slice: x: 4, y: 4, z: 8 (z_hi: 4, z_lo: 2; z = z_hi * 2 + z_lo), core: 2. Of those that a mesh axis runs over, the one named last changes fastest.
Arguments:
- signal: bfloat16 [131072, 1024], P('rows'), may hold values from -40 to 40
- w_qkv: bfloat16 [1024, 3072], P(None, 'heads'), may hold values from -1 to 1
- w_out: bfloat16 [1024, 1024], P('heads'), may hold values from -0.1875 to 0.1875
Outputs:
- mixed: bfloat16 [131072, 1024], P('rows', 'heads')
All inputs are finite; a program needn't handle non-finite values.
Results may differ from a plain program's by a relative error of at most 0.0082.
Values may be sent and summed in bfloat16 or wider, within the bound.
No kernel may reach another device: no remote copies, remote signals or barrier semaphores. Data moves between devices by JAX's collectives and lax.ppermute only.
A program may use at most 64 MiB of HBM per device.

v0:
```python
import jax
import jax.numpy as jnp
from jax import lax
from jax.sharding import PartitionSpec as P

D = 1024
HEADS = 16
C = 512


def softmax_bf(scores, causal_mask):
    scores = jnp.where(causal_mask, scores, jnp.float32(-1e30))
    top_score = jnp.max(scores, axis=-1, keepdims=True)
    expo = jnp.exp(scores - top_score)
    return (expo / jnp.sum(expo, axis=-1, keepdims=True)).astype(jnp.bfloat16)


def lower_mask(length):
    position = jnp.arange(length, dtype=jnp.int32)
    return position[None, :] <= position[:, None]


def row_attend(queries, keys_in, values_in):
    scale_factor = 1.0 / jnp.sqrt(jnp.float32(queries.shape[-1]))
    scores = (
        jnp.einsum("rqhe,rkhe->rhqk", queries, keys_in, preferred_element_type=jnp.float32)
        * scale_factor
    )
    weights_bf = softmax_bf(scores, lower_mask(queries.shape[1])[None, None])
    result = jnp.einsum(
        "rhqk,rkhe->rqhe", weights_bf, values_in, preferred_element_type=jnp.float32
    )
    return result.astype(jnp.bfloat16)


def column_attend(arrived, half_heads, head_dim):
    total_rows = arrived.shape[0]
    columns = arrived.shape[2]
    blocks = arrived.reshape(total_rows, columns, 3, half_heads, head_dim)
    scale_factor = 1.0 / jnp.sqrt(jnp.float32(head_dim))
    scores = (
        jnp.einsum(
            "qche,kche->chqk", blocks[:, :, 0], blocks[:, :, 1], preferred_element_type=jnp.float32
        )
        * scale_factor
    )
    weights_bf = softmax_bf(scores, lower_mask(total_rows)[None, None])
    result = jnp.einsum(
        "chqk,kche->qche", weights_bf, blocks[:, :, 2], preferred_element_type=jnp.float32
    )
    return result.astype(jnp.bfloat16).reshape(total_rows, 1, columns, half_heads * head_dim)


def local(signal, w_qkv, w_out):
    n_rows = lax.axis_size("rows")
    n_groups = lax.axis_size("heads")
    head_dim = D // HEADS
    local_heads = HEADS // n_groups
    half_heads = local_heads // 2
    tok_local = signal.shape[0]
    row_count = tok_local // C
    col_block = C // n_rows
    projected = jnp.dot(signal, w_qkv, preferred_element_type=jnp.float32).astype(jnp.bfloat16)
    projected = projected.reshape(row_count, C, 3, local_heads, head_dim)
    col_send = projected[:, :, :, half_heads:].reshape(
        row_count, n_rows, col_block, 3 * half_heads * head_dim
    )
    arrived = lax.all_to_all(col_send, "rows", split_axis=1, concat_axis=0, tiled=True)
    outcome = column_attend(arrived, half_heads, head_dim)
    col_back = lax.all_to_all(outcome, "rows", split_axis=0, concat_axis=1, tiled=True)
    row_out = row_attend(
        projected[:, :, 0, :half_heads],
        projected[:, :, 1, :half_heads],
        projected[:, :, 2, :half_heads],
    )
    col_out = col_back.reshape(row_count, C, half_heads, head_dim)
    attended = jnp.concatenate([row_out, col_out], axis=2).reshape(
        tok_local, local_heads * head_dim
    )
    partial_terms = jnp.dot(attended, w_out, preferred_element_type=jnp.float32)
    summed = lax.psum_scatter(partial_terms, "heads", scatter_dimension=1, tiled=True)
    return summed.astype(jnp.bfloat16)


def solution(mesh):
    return jax.shard_map(
        local,
        mesh=mesh,
        in_specs=(P("rows", None), P(None, "heads"), P("heads", None)),
        out_specs=P("rows", "heads"),
        check_vma=False,
    )
```

profile of v0, /device:TPU:1, one launch (start us, length us, event | category | flops | bytes accessed | tf_op | source)
XLA Modules:
  0.0 282.2 jit_solution(9697694999210610771)
XLA Ops:
  6.5 0.0 copy-start
  6.5 1.4 copy-done
  7.9 7.3 %convolution_convert_fusion = bf16[2048,768]{1,0:T(8,128)(2,1)} fusion(bf16[2048,1024]{1,0:T(8,128)(2,1)} %param.3, bf16[1024,768]{1,0:T(8,128)(2,1)S(1)} %copy-done), kind=kOutput, calls=%fused_computation.13 | convolution fusion | flops 3222798336 | bytes 8912896 | tf_op jit(solution)/shard_map/dot_general | solution.py:63
  15.2 4.7 %copy.24 = bf16[2048,768]{0,1:T(8,128)(2,1)} copy(bf16[2048,768]{1,0:T(8,128)(2,1)} %convolution_convert_fusion) | data formatting | bytes 6291456 | tf_op jit(solution)/shard_map/convert_element_type | solution.py:63
  20.0 4.8 %reshape.48 = bf16[4,512,3,4,64]{1,0,4,3,2:T(4,128)(2,1)S(1)} reshape(bf16[2048,768]{0,1:T(8,128)(2,1)} %copy.24) | data formatting | bytes 6291456 | tf_op jit(solution)/shard_map/reshape | solution.py:64
  24.7 1.7 slice.31
  26.4 9.1 %copy.29 = bf16[4,512,3,2,64]{4,3,2,1,0:T(2,128)(2,1)} copy(bf16[4,512,3,2,64]{1,0,4,3,2:T(4,128)(2,1)} %slice.31) | data formatting | bytes 3145728 | tf_op jit(solution)/shard_map/slice | solution.py:65
  35.5 6.6 %reshape.49 = bf16[4,64,8,384]{3,2,1,0:T(8,128)(2,1)} reshape(bf16[4,512,3,2,64]{4,3,2,1,0:T(2,128)(2,1)} %copy.29) | data formatting | bytes 3145728 | tf_op jit(solution)/shard_map/reshape | solution.py:65
  42.1 2.8 copy.30
  44.9 10.5 %all-to-all-start = ((bf16[4,64,8,384]{3,2,0,1:T(8,128)(2,1)}), bf16[4,64,8,384]{3,2,0,1:T(8,128)(2,1)}, u32[]{:S(2)}, u32[]{:S(2)}) async-start(bf16[4,64,8,384]{3,2,0,1:T(8,128)(2,1)} %copy.30), calls=%async_computation | async-start | bytes 3145728 | tf_op jit(solution)/shard_map/all_to_all | solution.py:68
  55.4 0.1 iota_compare_fusion
  55.5 1.5 fusion.26
  57.1 7.6 %fusion.29 = (f32[4,2,512]{2,1,0:T(2,128)S(1)}, f32[4,2,512,512]{2,3,1,0:T(8,128)}) fusion(pred[512,512]{0,1:T(8,128)(4,1)S(1)} %iota_compare_fusion, bf16[4,512,1,2,64]{1,0,4,3,2:T(4,128)(2,1)} %get-tuple-element.6, bf16[4,512,1,2,64]{1,0,4,3,2:T(4,128)(2,1)} %get-tuple-element.7), kind=kOutput, calls=%fused_computation.41 | convolution fusion | flops 276824576 | bytes 9715712 | tf_op jit(solution)/shard_map/sub | solution.py:14
  64.7 12.7 %all-to-all-done = bf16[4,64,8,384]{3,2,0,1:T(8,128)(2,1)} async-done(((bf16[4,64,8,384]{3,2,0,1:T(8,128)(2,1)}), bf16[4,64,8,384]{3,2,0,1:T(8,128)(2,1)}, u32[]{:S(2)}, u32[]{:S(2)}) %all-to-all-start) | async-done | bytes 1572896 | tf_op jit(solution)/shard_map/all_to_all | solution.py:68
  77.4 5.5 %reshape.50 = bf16[256,8,3,2,64]{4,3,2,1,0:T(2,128)(2,1)S(1)} reshape(bf16[64,4,1,8,384]{4,3,1,0,2:T(8,128)(2,1)} %bitcast.5) | data formatting | bytes 3145728 | tf_op jit(solution)/shard_map/reshape | solution.py:39
  82.9 3.2 %fusion.27 = (bf16[256,8,1,2,64]{4,3,2,1,0:T(2,128)(2,1)}, bf16[256,8,1,2,64]{4,3,2,1,0:T(2,128)(2,1)}, bf16[256,8,1,2,64]{4,3,2,1,0:T(2,128)(2,1)}) fusion(bf16[256,8,3,2,64]{4,3,2,1,0:T(2,128)(2,1)S(1)} %reshape.50), kind=kLoop, calls=%fused_computation.39 | loop fusion | bytes 3145728 | tf_op jit(solution)/shard_map/slice | solution.py:49
  86.1 2.4 copy.44
  88.5 2.4 copy.45
  90.9 2.4 copy.46
  93.3 0.8 fusion.17
  94.0 1.2 fusion.28
  95.2 0.0 copy-start.3
  95.2 0.5 fusion.13
  95.7 1.1 copy.35
  96.8 6.4 %all-to-all-start.1 = ((bf16[256,1,8,128]{3,2,1,0:T(8,128)(2,1)}), bf16[256,1,8,128]{3,2,1,0:T(8,128)(2,1)S(1)}, u32[]{:S(2)}, u32[]{:S(2)}) async-start(bf16[256,1,8,128]{3,2,1,0:T(8,128)(2,1)} %copy.35), calls=%async_computation.1 | async-start | bytes 1048576 | tf_op jit(solution)/shard_map/all_to_all | solution.py:70
  103.2 0.3 reduce-scatter.2.cloned.1.call-start
  103.5 0.0 copy-done.3
  103.5 4.2 %fusion.14 = bf16[4,512,2,64]{1,3,2,0:T(8,128)(2,1)S(1)} fusion(f32[4,2,512,512]{2,3,1,0:T(8,128)} %get-tuple-element.14, f32[4,2,512]{2,1,0:T(2,128)S(1)} %get-tuple-element.13, bf16[4,512,1,2,64]{1,0,4,3,2:T(4,128)(2,1)S(1)} %copy-done.3), kind=kOutput, calls=%fused_computation.21 | convolution fusion | flops 272891904 | bytes 9453568 | tf_op jit(solution)/shard_map/rhqk,rkhe->rqhe/dot_general | solution.py:30
  107.7 7.7 %all-to-all-done.1 = bf16[256,1,8,128]{3,2,1,0:T(8,128)(2,1)S(1)} async-done(((bf16[256,1,8,128]{3,2,1,0:T(8,128)(2,1)}), bf16[256,1,8,128]{3,2,1,0:T(8,128)(2,1)S(1)}, u32[]{:S(2)}, u32[]{:S(2)}) %all-to-all-start.1) | async-done | bytes 524320 | tf_op jit(solution)/shard_map/all_to_all | solution.py:70
  115.4 0.1 copy.36
  115.5 0.4 reshape.52
  115.9 0.0 copy-start.2
  115.9 0.7 copy.37
  116.7 0.1 pad_maximum_fusion
  116.8 0.8 copy.38
  117.6 0.3 copy.47
  117.9 0.0 copy-done.2
  117.9 4.5 %fusion.30 = f32[2048,1024]{1,0:T(8,128)} fusion(bf16[2048,256]{0,1:T(8,128)(2,1)S(1)} %bitcast.64, bf16[256,1024]{1,0:T(8,128)(2,1)S(1)} %copy-done.2), kind=kOutput, calls=%fused_computation.42 | convolution fusion | flops 1073741824 | bytes 9961472 | tf_op jit(solution)/shard_map/dot_general | solution.py:80
  122.4 0.0 copy-start.1
  122.4 0.0 reduce-scatter.2.cloned.1.call-update
  122.4 150.3 %reduce-scatter.2.cloned.1.call-done = f32[2048,256]{1,0:T(8,128)} async-done(((f32[2048,1024]{1,0:T(8,128)}), f32[2048,256]{1,0:T(8,128)}) %reduce-scatter.2.cloned.1.call-update) | async-done | bytes 2097168 | tf_op jit(solution)/shard_map/reduce_scatter | solution.py:81
  272.7 2.7 convert_element_type.31
  275.3 0.0 copy-done.1
  (1 shorter events, 0.0 us)
Async XLA Ops:
  6.5 1.4 copy-start
  44.9 32.5 %all-to-all-start = ((bf16[4,64,8,384]{3,2,0,1:T(8,128)(2,1)}), bf16[4,64,8,384]{3,2,0,1:T(8,128)(2,1)}, u32[]{:S(2)}, u32[]{:S(2)}) async-start(bf16[4,64,8,384]{3,2,0,1:T(8,128)(2,1)} %copy.30), calls=%async_computation | async-start | bytes 3145728 | tf_op jit(solution)/shard_map/all_to_all | solution.py:68
  95.2 8.3 %copy-start.3 = (bf16[4,512,1,2,64]{1,0,4,3,2:T(4,128)(2,1)S(1)}, bf16[4,512,1,2,64]{1,0,4,3,2:T(4,128)(2,1)}, u32[]{:S(2)}) copy-start(bf16[4,512,1,2,64]{1,0,4,3,2:T(4,128)(2,1)} %get-tuple-element.5) | copy-start | bytes 1572868
  96.8 18.6 %all-to-all-start.1 = ((bf16[256,1,8,128]{3,2,1,0:T(8,128)(2,1)}), bf16[256,1,8,128]{3,2,1,0:T(8,128)(2,1)S(1)}, u32[]{:S(2)}, u32[]{:S(2)}) async-start(bf16[256,1,8,128]{3,2,1,0:T(8,128)(2,1)} %copy.35), calls=%async_computation.1 | async-start | bytes 1048576 | tf_op jit(solution)/shard_map/all_to_all | solution.py:70
  103.2 169.5 %reduce-scatter.2.cloned.1.call-start = ((), (), s32[]{:S(2)}) async-start(), calls=%async_computation.3 | async-start | bytes 10485760 | tf_op jit(solution)/shard_map/reduce_scatter | solution.py:81
  115.9 2.0 copy-start.2
  122.4 153.0 %copy-start.1 = (bf16[1024,768]{1,0:T(8,128)(2,1)S(1)}, bf16[1024,768]{1,0:T(8,128)(2,1)}, u32[]{:S(2)}) copy-start(bf16[1024,768]{1,0:T(8,128)(2,1)} %param.4) | copy-start | bytes 4718596
Sparse Core Ops, SparseCore 0:
  122.5 150.1 reduce-scatter.1
where the time goes:
time: 286 us; the launch traced here: 282 us
  waiting for transfers between devices  171 us (60%)
  local copies, waits for them, and re-layouts  51.8 us (18%)
  matrix products  24.8 us (9%)
  starting transfers between devices  17.2 us (6%)
  between operations  13.6 us (5%)
  other arithmetic  4.07 us (1%)
    reduce_scatter x1, waiting for transfers between devices, local(): lax.psum_scatter(partial_terms, 'heads', scatter_dimension=1, tiled=True)  150 us
    all_to_all x1, waiting for transfers between devices, local(): lax.all_to_all(col_send, 'rows', split_axis=1, concat_axis=0, tiled=True)  12.7 us
    slice x2, local copies, waits for them, and re-layouts, local(): projected[:, :, :, half_heads:]  10.8 us
    all_to_all x1, starting transfers between devices, local(): lax.all_to_all(col_send, 'rows', split_axis=1, concat_axis=0, tiled=True)  10.5 us
    reshape x2, local copies, waits for them, and re-layouts, local(): projected[:, :, :, half_heads:]  9.36 us
    unnamed x12, local copies, waits for them, and re-layouts  8.84 us
    all_to_all x1, waiting for transfers between devices, local(): lax.all_to_all(outcome, 'rows', split_axis=0, concat_axis=1, tiled=True)  7.73 us
    sub x1, matrix products, softmax_bf(): expo = jnp.exp(scores - top_score)  7.64 us
  transfers between devices with their start and end apart: 3, of which 3 were waited for; matrix products, arithmetic and copies ran while one was open for 5% of the time, Pallas kernels for 0%

commit v1 on v0

v1 whole, which is shorter than its diff:
```python
import jax
import jax.numpy as jnp
from jax import lax
from jax.experimental import pallas as pl
from jax.experimental.pallas import tpu as pltpu
from jax.sharding import PartitionSpec as P

D = 1024
HEADS = 16
C = 512
GROUPS = 4
DIM = 64
HALF = 128
ROWS_LOCAL = 4
BLOCK = 128
BF = jnp.bfloat16
F32 = jnp.float32
VMEM = pltpu.VMEM
MIB = 1 << 20


def whole():
    return pl.BlockSpec(memory_space=VMEM)


def anywhere():
    return pl.BlockSpec(memory_space=pl.ANY)


def smem():
    return pl.BlockSpec(memory_space=pltpu.SMEM)


def one_hot(source_of):
    out_at = lax.broadcasted_iota(jnp.int32, (BLOCK, BLOCK), 0)
    in_at = lax.broadcasted_iota(jnp.int32, (BLOCK, BLOCK), 1)
    return (in_at == source_of(out_at)).astype(F32).astype(BF)


def move(pick, data):
    return jnp.dot(pick, data, preferred_element_type=F32).astype(BF)


def attend(qkv, length, store):
    lane = lax.broadcasted_iota(jnp.int32, (1, HALF), 1)
    first = lane < DIM
    query = qkv[:, :HALF]
    query_a = jnp.where(first, query, 0.0).astype(BF)
    query_b = jnp.where(first, 0.0, query).astype(BF)
    key = qkv[:, HALF : 2 * HALF].astype(BF)
    value = qkv[:, 2 * HALF :].astype(BF)
    for block in range(length // BLOCK):
        lo = block * BLOCK
        hi = lo + BLOCK
        both = jnp.concatenate([query_a[lo:hi], query_b[lo:hi]], axis=0)
        scores = lax.dot_general(
            both, key[:hi], (((1,), (1,)), ((), ())), preferred_element_type=F32
        )
        at_query = lax.broadcasted_iota(jnp.int32, scores.shape, 0) % BLOCK + lo
        at_key = lax.broadcasted_iota(jnp.int32, scores.shape, 1)
        scores = jnp.where(at_key <= at_query, scores, F32(-1e30))
        top = jnp.max(scores, axis=-1, keepdims=True)
        expo = jnp.exp((scores - top) * F32(0.125))
        total = jnp.sum(expo, axis=-1, keepdims=True)
        out = jnp.dot(expo.astype(BF), value[:hi], preferred_element_type=F32) / total
        store(block, jnp.where(first, out[:BLOCK], out[BLOCK:]).astype(BF))


def prep_kernel(meta, sig_ref, out_ref):
    pick = one_hot(lambda o: ((o // 2) % 4) * 32 + (o // 8) * 2 + o % 2)
    out_ref[...] = move(pick, sig_ref[...].reshape(BLOCK, D))


def prep(meta, sig):
    return pl.pallas_call(
        prep_kernel,
        grid_spec=pltpu.PrefetchScalarGridSpec(
            num_scalar_prefetch=1,
            grid=(4,),
            in_specs=[pl.BlockSpec((4, 32, D), lambda b, meta: (0, meta[0] * 4 + b, 0))],
            out_specs=pl.BlockSpec((BLOCK, D), lambda b, meta: (b, 0)),
        ),
        out_shape=jax.ShapeDtypeStruct((C, D), BF),
        cost_estimate=pl.CostEstimate(flops=2 * C * D * BLOCK, bytes_accessed=2 * MIB, transcendentals=0),
        name="prep",
    )(meta, sig)


def row_kernel(meta, sig_ref, w_ref, out0, out1, out2, out3, held):
    g = meta[0]
    weight = jnp.concatenate(
        [w_ref[:, 0:HALF], w_ref[:, 256 : 256 + HALF], w_ref[:, 512 : 512 + HALF]], axis=1
    )
    qkv = jnp.dot(sig_ref[0], weight, preferred_element_type=F32)

    def store(block, out):
        held[block * BLOCK : (block + 1) * BLOCK, :] = out

    attend(qkv, C, store)
    for k, out in enumerate((out0, out1, out2, out3)):
        at = pl.multiple_of(lax.rem(g + k, GROUPS) * BLOCK, BLOCK)
        out[0] = held[pl.ds(at, BLOCK), :]


def row_part(meta, sig, w_qkv):
    return pl.pallas_call(
        row_kernel,
        grid_spec=pltpu.PrefetchScalarGridSpec(
            num_scalar_prefetch=1,
            grid=(ROWS_LOCAL,),
            in_specs=[
                pl.BlockSpec((1, C, D), lambda r, meta: (r, 0, 0)),
                pl.BlockSpec((D, 768), lambda r, meta: (0, 0)),
            ],
            out_specs=[pl.BlockSpec((1, BLOCK, HALF), lambda r, meta: (r, 0, 0))] * GROUPS,
            scratch_shapes=[VMEM((C, HALF), BF)],
        ),
        out_shape=[jax.ShapeDtypeStruct((ROWS_LOCAL, BLOCK, HALF), BF)] * GROUPS,
        compiler_params=pltpu.CompilerParams(vmem_limit_bytes=24 * MIB),
        cost_estimate=pl.CostEstimate(
            flops=6 * 10**9, bytes_accessed=6 * MIB, transcendentals=2 * 10**6
        ),
        name="row_part",
    )(meta, sig, w_qkv)


def column_kernel(meta, got_ref, w_ref, *refs):
    near = refs[0:4]
    far = refs[4:8]
    out_ref, held, weights, outs, sems = refs[8:]
    x = meta[1]
    core = meta[2]
    copies = []
    for d in range(4):
        from_x = lax.rem(x + 4 - d, 4) * 2
        for n, (ref, at) in enumerate(((near[d], from_x + core), (far[d], from_x + 1 - core))):
            rows = pl.ds(pl.multiple_of(at * BLOCK, BLOCK), BLOCK)
            copy = pltpu.make_async_copy(ref, weights.at[:, rows, :], sems.at[2 * d + n])
            copy.start()
            copies.append(copy)
    pick = one_hot(lambda o: (o % 64) * 2 + o // 64)
    for b in range(4):
        moved = move(pick, got_ref[b * BLOCK : (b + 1) * BLOCK, :])
        held[b * 64 : b * 64 + 64, :] = moved[:64]
        held[256 + b * 64 : 256 + b * 64 + 64, :] = moved[64:]

    def group(k, weight):
        qkv = jnp.dot(held[...], weight, preferred_element_type=F32)
        for c in range(2):

            def store(block, out):
                lo = c * 256 + block * BLOCK
                outs[lo : lo + BLOCK, k * HALF : (k + 1) * HALF] = out

            attend(qkv[c * 256 : (c + 1) * 256], 256, store)

    group(
        0,
        jnp.concatenate(
            [w_ref[:, HALF:256], w_ref[:, 256 + HALF : 512], w_ref[:, 512 + HALF :]], axis=1
        ),
    )
    for copy in copies:
        copy.wait()
    for k in range(1, GROUPS):
        group(k, weights[k - 1])
    back = one_hot(lambda o: (o % 2) * 64 + o // 2)
    for b in range(4):
        both = jnp.concatenate(
            [outs[b * 64 : b * 64 + 64, :], outs[256 + b * 64 : 256 + b * 64 + 64, :]], axis=0
        )
        out_ref[b * BLOCK : (b + 1) * BLOCK, :] = move(back, both)


def column_part(meta, got, w_qkv, near, far):
    return pl.pallas_call(
        column_kernel,
        in_specs=[smem(), whole(), whole()] + [anywhere()] * 8,
        out_specs=whole(),
        out_shape=jax.ShapeDtypeStruct((C, C), BF),
        scratch_shapes=[
            VMEM((C, D), BF),
            VMEM((3, D, 3 * HALF), BF),
            VMEM((C, C), BF),
            pltpu.SemaphoreType.DMA((8,)),
        ],
        compiler_params=pltpu.CompilerParams(vmem_limit_bytes=24 * MIB),
        cost_estimate=pl.CostEstimate(
            flops=4 * 10**9, bytes_accessed=6 * MIB, transcendentals=10**6
        ),
        name="column_part",
    )(meta, got, w_qkv, *near, *far)


def out_kernel(meta, got_ref, row0, row1, row2, row3, *refs):
    own = refs[0]
    near = refs[1:4]
    far = refs[4:7]
    outs = refs[7:11]
    weights, attended, sems = refs[11:]
    g = meta[0]
    core = meta[2]
    copies = [pltpu.make_async_copy(own, weights.at[pl.ds(0, 256), :], sems.at[0])]
    for k in range(1, GROUPS):
        for n, (ref, at) in enumerate(((near[k - 1], core), (far[k - 1], 1 - core))):
            rows = pl.ds(pl.multiple_of(k * 256 + at * BLOCK, BLOCK), BLOCK)
            copies.append(
                pltpu.make_async_copy(ref, weights.at[rows, :], sems.at[2 * k - 1 + n])
            )
    for copy in copies:
        copy.start()
    for k, row in enumerate((row0, row1, row2, row3)):
        attended[:, k * 256 : k * 256 + HALF] = row[...].reshape(C, HALF)
    pick = one_hot(lambda o: ((o // 2) % 16) * 8 + (o // 32) * 2 + o % 2)
    for b in range(4):
        moved = move(pick, got_ref[b * BLOCK : (b + 1) * BLOCK, :])
        for r in range(ROWS_LOCAL):
            lo = r * BLOCK + b * 32
            for k in range(GROUPS):
                attended[lo : lo + 32, k * 256 + HALF : (k + 1) * 256] = moved[
                    r * 32 : (r + 1) * 32, k * HALF : (k + 1) * HALF
                ]
    for copy in copies:
        copy.wait()
    left = attended[...]
    for k in range(GROUPS):
        at = pl.multiple_of(lax.rem(g + k, GROUPS) * 256, 256)
        outs[k][...] = jnp.dot(
            left, weights[:, pl.ds(at, 256)], preferred_element_type=F32
        ).astype(BF)


def out_part(meta, got, rows, own, near, far):
    return pl.pallas_call(
        out_kernel,
        in_specs=[smem()] + [whole()] * 5 + [anywhere()] * 7,
        out_specs=[whole()] * GROUPS,
        out_shape=[jax.ShapeDtypeStruct((C, 256), BF)] * GROUPS,
        scratch_shapes=[
            VMEM((D, D), BF),
            VMEM((C, D), BF),
            pltpu.SemaphoreType.DMA((7,)),
        ],
        compiler_params=pltpu.CompilerParams(vmem_limit_bytes=24 * MIB),
        cost_estimate=pl.CostEstimate(
            flops=10**9, bytes_accessed=5 * MIB, transcendentals=0
        ),
        name="out_part",
    )(meta, got, *rows, own, *near, *far)


def place_kernel(meta, in0, in1, in2, in3, out_ref, sems):
    g = meta[0]
    copies = []
    for k, ref in enumerate((in0, in1, in2, in3)):
        at = lax.rem(g + GROUPS - k, GROUPS)
        copies.append(pltpu.make_async_copy(ref, out_ref.at[:, at], sems.at[k]))
    for copy in copies:
        copy.start()
    for copy in copies:
        copy.wait()


def place(meta, parts):
    return pl.pallas_call(
        place_kernel,
        in_specs=[smem()] + [anywhere()] * GROUPS,
        out_specs=anywhere(),
        out_shape=jax.ShapeDtypeStruct((ROWS_LOCAL, GROUPS, BLOCK, 256), BF),
        scratch_shapes=[pltpu.SemaphoreType.DMA((GROUPS,))],
        cost_estimate=pl.CostEstimate(flops=0, bytes_accessed=2 * MIB, transcendentals=0),
        name="place",
    )(meta, *[part.reshape(ROWS_LOCAL, BLOCK, 256) for part in parts])


def to_group(data, k):
    return lax.ppermute(data, "heads", [(j, (j + k) % GROUPS) for j in range(GROUPS)])


def along_x(data, d):
    return lax.ppermute(
        data, "rows", [(i, i // 8 * 8 + (i // 2 % 4 + d) % 4 * 2 + i % 2) for i in range(64)]
    )


def other_core(data):
    return lax.ppermute(data, "rows", [(i, i ^ 1) for i in range(64)])


def local(signal, w_qkv, w_out):
    i = lax.axis_index("rows")
    g = lax.axis_index("heads")
    core = i % 2
    x = i // 2 % 4
    meta = jnp.stack([g, x, core]).astype(jnp.int32)
    sig = signal.reshape(ROWS_LOCAL, C, D)

    mine = lax.dynamic_slice_in_dim(w_qkv, (i % 8) * BLOCK, BLOCK, axis=0)
    mine = jnp.concatenate([mine[:, HALF:256], mine[:, 256 + HALF : 512], mine[:, 512 + HALF :]], axis=1)
    others = jnp.stack([to_group(mine, k) for k in (1, 2, 3)])
    near = [others] + [along_x(others, d) for d in (1, 2, 3)]
    far = [other_core(part) for part in near]

    send = prep(meta, sig).reshape(64, 8, D)
    got = lax.all_to_all(send, "rows", split_axis=0, concat_axis=0, tiled=True).reshape(C, D)

    rows = row_part(meta, sig, w_qkv)
    rows = [rows[0]] + [to_group(rows[k], k) for k in (1, 2, 3)]

    half = lax.dynamic_slice_in_dim(w_out, core * BLOCK, BLOCK, axis=0)
    out_near = [to_group(half, k) for k in (1, 2, 3)]
    out_far = [other_core(part) for part in out_near]

    columns = column_part(meta, got, w_qkv, near, far).reshape(64, 8, C)
    back = lax.all_to_all(columns, "rows", split_axis=0, concat_axis=0, tiled=True).reshape(C, C)

    parts = out_part(meta, back, rows, w_out, out_near, out_far)
    parts = [parts[0]] + [to_group(parts[k], k) for k in (1, 2, 3)]
    return place(meta, parts).reshape(ROWS_LOCAL * C, 256)


def solution(mesh):
    return jax.shard_map(
        local,
        mesh=mesh,
        in_specs=(P("rows", None), P(None, "heads"), P("heads", None)),
        out_specs=P("rows", "heads"),
        check_vma=False,
    )
```

time: 286 us -> 198 us (0.69)
  waiting for transfers between devices: 171 us -> 57.6 us
  Pallas kernels: 0 us -> 53.6 us
  starting transfers between devices: 17.2 us -> 66.8 us
  local copies, waits for them, and re-layouts: 51.8 us -> 17 us
  matrix products: 24.8 us -> 0 us
  between operations: 13.6 us -> 0.35 us
  other arithmetic: 4.07 us -> 0.67 us
    reduce_scatter x1 -> x0, waiting for transfers between devices: 150 us -> none  [local(): lax.psum_scatter(partial_terms, 'heads', scatter_dimension=1, tiled=True)]
    ppermute x0 -> x22, waiting for transfers between devices: none -> 57.6 us  [the longest x12 50.7 us: to_group(): lax.ppermute(data, 'heads', [(j, (j + k) % GROUPS) for j in range(GROUPS)])]
    pallas_call x0 -> x5, Pallas kernels: none -> 53.6 us  [the longest x1 33.6 us: place(): pl.pallas_call(place_kernel, in_specs=[smem()] + [anywhere()] * GROUPS, o...]
    ppermute x0 -> x22, starting transfers between devices: none -> 50 us  [the longest x12 32 us: to_group(): lax.ppermute(data, 'heads', [(j, (j + k) % GROUPS) for j in range(GROUPS)])]
    reshape x7 -> x0, local copies, waits for them, and re-layouts: 21.9 us -> none  [the longest x2 9.36 us: local(): projected[:, :, :, half_heads:]]
    all_to_all x2, waiting for transfers between devices: 20.4 us -> 0.01 us  [the longest x1 0.01 us: local(): lax.all_to_all(columns, 'rows', split_axis=0, concat_axis=0, tiled=True)]
    dot_general x5 -> x0, matrix products: 17.2 us -> none  [the longest x1 7.28 us: local(): jnp.dot(signal, w_qkv, preferred_element_type=jnp.float32)]
    slice x4 -> x1, local copies, waits for them, and re-layouts: 15.4 us -> 0.03 us  [local(): mine[:, HALF:256]]
  transfers between devices with their start and end apart: 3 -> 24, of which waited for: 3 -> 11; matrix products, arithmetic and copies ran while one was open for 5% -> 0% of each run, Pallas kernels for 0% -> 4%
where the time goes in v1:
time: 198 us; the launch traced here: 196 us
  starting transfers between devices  66.8 us (34%)
  waiting for transfers between devices  57.6 us (29%)
  Pallas kernels  53.6 us (27%)
  local copies, waits for them, and re-layouts  17 us (9%)
    ppermute x12, waiting for transfers between devices, to_group(): lax.ppermute(data, 'heads', [(j, (j + k) % GROUPS) for j in range(GROUPS)])  50.7 us
    pallas_call x1, Pallas kernels, place(): pl.pallas_call(place_kernel, in_specs=[smem()] + [anywhere()] * GROUPS, o...  33.6 us
    ppermute x12, starting transfers between devices, to_group(): lax.ppermute(data, 'heads', [(j, (j + k) % GROUPS) for j in range(GROUPS)])  32 us
    unnamed x48, local copies, waits for them, and re-layouts  16.9 us
    ppermute x7, starting transfers between devices, other_core(): return lax.ppermute(data, 'rows', [(i, i ^ 1) for i in range(64)])  13 us
    all_to_all x1, starting transfers between devices, local(): lax.all_to_all(send, 'rows', split_axis=0, concat_axis=0, tiled=True)  10.5 us
    pallas_call x1, Pallas kernels, row_part(): pl.pallas_call(row_kernel, grid_spec=pltpu.PrefetchScalarGridSpec(num_sca...  7.21 us
    ppermute x3, waiting for transfers between devices, along_x(): lax.ppermute(data, 'rows', [(i, i // 8 * 8 + (i // 2 % 4 + d) % 4 * 2 + i...  6.87 us
  transfers between devices with their start and end apart: 24, of which 11 were waited for; matrix products, arithmetic and copies ran while one was open for 0% of the time, Pallas kernels for 4%

profile of v1, /device:TPU:1, one launch (start us, length us, event | category | flops | bytes accessed | tf_op | source)
XLA Modules:
  0.0 196.0 jit_solution(11584064659098863246)
XLA Ops:
  0.6 4.4 %prep.1 = bf16[512,1024]{1,0:T(8,128)(2,1)} custom-call(s32[3]{0:T(128)} %pad_add_fusion.meta, bf16[4,512,1024]{2,1,0:T(8,128)(2,1)} %bitcast.16), custom_call_target="tpu_custom_call" | custom-call | flops 134217728 | bytes 2097152 | tf_op jit(solution)/shard_map/prep/pallas_call | solution.py:75
  5.0 10.5 %all-to-all-start = ((bf16[64,8,1024]{2,1,0:T(8,128)(2,1)}), bf16[64,8,1024]{2,1,0:T(8,128)(2,1)S(1)}, u32[]{:S(2)}, u32[]{:S(2)}) async-start(bf16[64,8,1024]{2,1,0:T(8,128)(2,1)} %bitcast.21), calls=%async_computation | async-start | bytes 2097152 | tf_op jit(solution)/shard_map/all_to_all | solution.py:305
  15.6 5.2 %collective-permute-start.2 = (bf16[128,384]{1,0:T(8,128)(2,1)S(1)}, bf16[128,384]{1,0:T(8,128)(2,1)S(1)}, u32[]{:S(2)}, u32[]{:S(2)}) collective-permute-start(bf16[128,384]{1,0:T(8,128)(2,1)S(1)} %pad_maximum_fusion.1), channel_id=1, source_target_pairs={{0,3},{1,0},{2,1},{3,2},{4,7},{5,4},{6,5},{7,6},{8,11},{9,8},{10,9... | collective-permute-start | bytes 294920 | tf_op jit(solution)/shard_map/ppermute | solution.py:277
  20.8 1.2 collective-permute-start.1
  22.0 2.1 %collective-permute-start = (bf16[128,384]{1,0:T(8,128)(2,1)S(1)}, bf16[128,384]{1,0:T(8,128)(2,1)S(1)}, u32[]{:S(2)}, u32[]{:S(2)}) collective-permute-start(bf16[128,384]{1,0:T(8,128)(2,1)S(1)} %pad_maximum_fusion.1), channel_id=1, source_target_pairs={{0,1},{1,2},{2,3},{3,0},{4,5},{5,6},{6,7},{7,4},{8,9},{9,10},{10,1... | collective-permute-start | bytes 294920 | tf_op jit(solution)/shard_map/ppermute | solution.py:277
  24.1 13.6 %collective-permute-done.1 = bf16[128,384]{1,0:T(8,128)(2,1)S(1)} collective-permute-done((bf16[128,384]{1,0:T(8,128)(2,1)S(1)}, bf16[128,384]{1,0:T(8,128)(2,1)S(1)}, u32[]{:S(2)}, u32[]{:S(2)}) %collective-permute-start.1) | collective-permute-done | bytes 98336 | tf_op jit(solution)/shard_map/ppermute | solution.py:277
  37.6 3.3 %collective-permute-done = bf16[128,384]{1,0:T(8,128)(2,1)S(1)} collective-permute-done((bf16[128,384]{1,0:T(8,128)(2,1)S(1)}, bf16[128,384]{1,0:T(8,128)(2,1)S(1)}, u32[]{:S(2)}, u32[]{:S(2)}) %collective-permute-start) | collective-permute-done | bytes 98336 | tf_op jit(solution)/shard_map/ppermute | solution.py:277
  41.0 1.4 collective-permute-start.3
  42.4 2.4 %collective-permute-start.4 = (bf16[3,128,384]{2,1,0:T(8,128)(2,1)S(1)}, bf16[3,128,384]{2,1,0:T(8,128)(2,1)S(1)}, u32[]{:S(2)}, u32[]{:S(2)}) collective-permute-start(bf16[3,128,384]{2,1,0:T(8,128)(2,1)S(1)} %pad_maximum_fusion.refs_0_), channel_id=1, source_target_pairs={{0,16},{4,20},{8,24},{12,28},{16,0},{20,4},{24,8},{28,12},{32,48},... | collective-permute-start | bytes 884744 | tf_op jit(solution)/shard_map/ppermute | solution.py:281
  44.8 1.2 collective-permute-start.5
  46.0 1.7 collective-permute-start.6
  47.7 2.3 %collective-permute-done.3.refs_1_ = bf16[3,128,384]{2,1,0:T(8,128)(2,1)S(1)} collective-permute-done((bf16[3,128,384]{2,1,0:T(8,128)(2,1)S(1)}, bf16[3,128,384]{2,1,0:T(8,128)(2,1)S(1)}, u32[]{:S(2)}, u32[]{:S(2)}) %collective-permute-start.3) | collective-permute-done | bytes 294944 | tf_op jit(solution)/shard_map/ppermute | solution.py:281
  50.0 2.0 %collective-permute-start.7 = (bf16[3,128,384]{2,1,0:T(8,128)(2,1)S(1)}, bf16[3,128,384]{2,1,0:T(8,128)(2,1)S(1)}, u32[]{:S(2)}, u32[]{:S(2)}) collective-permute-start(bf16[3,128,384]{2,1,0:T(8,128)(2,1)S(1)} %collective-permute-done.3.refs_1_), channel_id=1, source_target_pairs={{0,4},{4,0},{8,12},{12,8},{16,20},{20,16},{24,28},{28,24},{32,36},... | collective-permute-start | bytes 884744 | tf_op jit(solution)/shard_map/ppermute | solution.py:287
  52.7 4.6 %collective-permute-done.4.refs_2_ = bf16[3,128,384]{2,1,0:T(8,128)(2,1)S(1)} collective-permute-done((bf16[3,128,384]{2,1,0:T(8,128)(2,1)S(1)}, bf16[3,128,384]{2,1,0:T(8,128)(2,1)S(1)}, u32[]{:S(2)}, u32[]{:S(2)}) %collective-permute-start.4) | collective-permute-done | bytes 294944 | tf_op jit(solution)/shard_map/ppermute | solution.py:281
  57.3 1.8 collective-permute-start.8
  59.1 0.7 copy-done.7
  60.6 0.7 copy-done.11
  61.3 0.7 copy-done.13
  62.0 0.7 copy-done.15
  63.5 1.0 copy-done.6
  64.4 1.0 copy-done.8
  65.4 1.0 copy-done.10
  66.4 1.0 copy-done.12
  67.3 1.0 copy-done.14
  68.3 1.0 copy-done.16
  69.2 1.0 copy-done.18
  70.2 5.9 %column_part.1 = bf16[512,512]{1,0:T(8,128)(2,1)} custom-call(s32[3]{0:T(128)S(1)} %copy-done.4, bf16[512,1024]{1,0:T(8,128)(2,1)S(1)} %bitcast.18, bf16[1024,768]{1,0:T(8,128)(2,1)S(1)} %copy-done.3, bf16[3,128,384]{2,1,0:T(8,128)(2,1)S(1)} %pad_maximum_fusion.refs_0_, bf16[3,128,384]{2,1,0:T(8,128)(2,1)S(1)} %copy-done.6, ...), custom_call_target="tpu_custom_call" | custom-call | flops 4000000000 | bytes 6291456 | tf_op jit(solution)/shard_map/column_part/pallas_call | solution.py:176
  76.1 6.3 %all-to-all-start.1 = ((bf16[64,8,512]{2,1,0:T(8,128)(2,1)}), bf16[64,8,512]{2,1,0:T(8,128)(2,1)S(1)}, u32[]{:S(2)}, u32[]{:S(2)}) async-start(bf16[64,8,512]{2,1,0:T(8,128)(2,1)} %bitcast.9), calls=%async_computation.1 | async-start | bytes 1048576 | tf_op jit(solution)/shard_map/all_to_all | solution.py:315
  82.5 3.3 %collective-permute-start.13 = (bf16[128,1024]{1,0:T(8,128)(2,1)S(1)}, bf16[128,1024]{1,0:T(8,128)(2,1)S(1)}, u32[]{:S(2)}, u32[]{:S(2)}) collective-permute-start(bf16[128,1024]{1,0:T(8,128)(2,1)S(1)} %constant_dynamic-slice_fusion), channel_id=1, source_target_pairs={{0,1},{1,2},{2,3},{3,0},{4,5},{5,6},{6,7},{7,4},{8,9},{9,10},{10,1... | collective-permute-start | bytes 786440 | tf_op jit(solution)/shard_map/ppermute | solution.py:277
  85.9 3.3 %collective-permute-start.15 = (bf16[128,1024]{1,0:T(8,128)(2,1)S(1)}, bf16[128,1024]{1,0:T(8,128)(2,1)S(1)}, u32[]{:S(2)}, u32[]{:S(2)}) collective-permute-start(bf16[128,1024]{1,0:T(8,128)(2,1)S(1)} %constant_dynamic-slice_fusion), channel_id=1, source_target_pairs={{0,3},{1,0},{2,1},{3,2},{4,7},{5,4},{6,5},{7,6},{8,11},{9,8},{10,9... | collective-permute-start | bytes 786440 | tf_op jit(solution)/shard_map/ppermute | solution.py:277
  89.2 2.2 %copy-done = bf16[2048,1024]{1,0:T(8,128)(2,1)S(1)} copy-done((bf16[2048,1024]{1,0:T(8,128)(2,1)S(1)}, bf16[2048,1024]{1,0:T(8,128)(2,1)}, u32[]{:S(2)}) %copy-start) | copy-done | bytes 4194328
  91.4 7.2 %row_part.1 = (bf16[4,128,128]{2,1,0:T(8,128)(2,1)S(1)}, bf16[4,128,128]{2,1,0:T(8,128)(2,1)S(1)}, bf16[4,128,128]{2,1,0:T(8,128)(2,1)S(1)}, bf16[4,128,128]{2,1,0:T(8,128)(2,1)S(1)}) custom-call(s32[3]{0:T(128)S(1)} %copy-done.4, bf16[4,512,1024]{2,1,0:T(8,128)(2,1)S(1)} %bitcast.17, bf16[1024,768]{1,0:T(8,128)(2,1)S(1)} %copy-done.3), custom_call_target="tpu_custom_call" | custom-call | flops 6000000000 | bytes 6291456 | tf_op jit(solution)/shard_map/row_part/pallas_call | solution.py:106
  99.3 1.9 collective-permute-done.13.refs_1_
  101.2 6.9 %collective-permute-start.16 = (bf16[128,1024]{1,0:T(8,128)(2,1)S(1)}, bf16[128,1024]{1,0:T(8,128)(2,1)S(1)}, u32[]{:S(2)}, u32[]{:S(2)}) collective-permute-start(bf16[128,1024]{1,0:T(8,128)(2,1)S(1)} %collective-permute-done.13.refs_1_), channel_id=1, source_target_pairs={{0,4},{4,0},{8,12},{12,8},{16,20},{20,16},{24,28},{28,24},{32,36},... | collective-permute-start | bytes 786440 | tf_op jit(solution)/shard_map/ppermute | solution.py:287
  108.6 8.0 %collective-permute-start.11 = (bf16[4,128,128]{2,1,0:T(8,128)(2,1)S(1)}, bf16[4,128,128]{2,1,0:T(8,128)(2,1)S(1)}, u32[]{:S(2)}, u32[]{:S(2)}) collective-permute-start(bf16[4,128,128]{2,1,0:T(8,128)(2,1)S(1)} %get-tuple-element.15), channel_id=1, source_target_pairs={{0,2},{1,3},{2,0},{3,1},{4,6},{5,7},{6,4},{7,5},{8,10},{9,11},{10,... | collective-permute-start | bytes 393224 | tf_op jit(solution)/shard_map/ppermute | solution.py:277
  116.6 1.4 collective-permute-done.10.row1
  118.0 3.9 %collective-permute-start.12 = (bf16[4,128,128]{2,1,0:T(8,128)(2,1)S(1)}, bf16[4,128,128]{2,1,0:T(8,128)(2,1)S(1)}, u32[]{:S(2)}, u32[]{:S(2)}) collective-permute-start(bf16[4,128,128]{2,1,0:T(8,128)(2,1)S(1)} %get-tuple-element.16), channel_id=1, source_target_pairs={{0,3},{1,0},{2,1},{3,2},{4,7},{5,4},{6,5},{7,6},{8,11},{9,8},{10,9... | collective-permute-start | bytes 393224 | tf_op jit(solution)/shard_map/ppermute | solution.py:277
  121.9 1.6 collective-permute-done.11.row2
  123.5 7.9 %collective-permute-done.12.row3 = bf16[4,128,128]{2,1,0:T(8,128)(2,1)S(1)} collective-permute-done((bf16[4,128,128]{2,1,0:T(8,128)(2,1)S(1)}, bf16[4,128,128]{2,1,0:T(8,128)(2,1)S(1)}, u32[]{:S(2)}, u32[]{:S(2)}) %collective-permute-start.12) | collective-permute-done | bytes 131104 | tf_op jit(solution)/shard_map/ppermute | solution.py:277
  131.5 0.9 copy-done.20
  132.4 2.5 %out_part.1 = (bf16[512,256]{1,0:T(8,128)(2,1)S(1)}, bf16[512,256]{1,0:T(8,128)(2,1)S(1)}, bf16[512,256]{1,0:T(8,128)(2,1)S(1)}, bf16[512,256]{1,0:T(8,128)(2,1)S(1)}) custom-call(s32[3]{0:T(128)S(1)} %copy-done.4, bf16[512,512]{1,0:T(8,128)(2,1)S(1)} %bitcast.19, bf16[4,128,128]{2,1,0:T(8,128)(2,1)S(1)} %copy-done.20, ...), custom_call_target="tpu_custom_call" | custom-call | flops 1000000000 | bytes 5242880 | tf_op jit(solution)/shard_map/out_part/pallas_call | solution.py:234
  135.6 1.7 collective-permute-start.19
  137.3 1.5 collective-permute-start.20
  138.8 1.8 collective-permute-start.21
  140.6 7.6 %collective-permute-done.19 = bf16[512,256]{1,0:T(8,128)(2,1)S(1)} collective-permute-done((bf16[512,256]{1,0:T(8,128)(2,1)S(1)}, bf16[512,256]{1,0:T(8,128)(2,1)S(1)}, u32[]{:S(2)}, u32[]{:S(2)}) %collective-permute-start.19) | collective-permute-done | bytes 262176 | tf_op jit(solution)/shard_map/ppermute | solution.py:277
  148.2 10.1 %collective-permute-done.20 = bf16[512,256]{1,0:T(8,128)(2,1)S(1)} collective-permute-done((bf16[512,256]{1,0:T(8,128)(2,1)S(1)}, bf16[512,256]{1,0:T(8,128)(2,1)S(1)}, u32[]{:S(2)}, u32[]{:S(2)}) %collective-permute-start.20) | collective-permute-done | bytes 262176 | tf_op jit(solution)/shard_map/ppermute | solution.py:277
  158.4 3.2 %collective-permute-done.21 = bf16[512,256]{1,0:T(8,128)(2,1)S(1)} collective-permute-done((bf16[512,256]{1,0:T(8,128)(2,1)S(1)}, bf16[512,256]{1,0:T(8,128)(2,1)S(1)}, u32[]{:S(2)}, u32[]{:S(2)}) %collective-permute-start.21) | collective-permute-done | bytes 262176 | tf_op jit(solution)/shard_map/ppermute | solution.py:277
  162.3 33.6 %place.1 = bf16[4,4,128,256]{3,2,1,0:T(8,128)(2,1)} custom-call(s32[3]{0:T(128)} %pad_add_fusion.meta, bf16[4,128,256]{2,1,0:T(8,128)(2,1)} %bitcast.20, bf16[4,128,256]{2,1,0:T(8,128)(2,1)} %bitcast.22, bf16[4,128,256]{2,1,0:T(8,128)(2,1)} %bitcast.23, bf16[4,128,256]{2,1,0:T(8,128)(2,1)} %bitcast.24), custom_call_target="tpu_custom_call" | custom-call | bytes 2097152 | tf_op jit(solution)/shard_map/place/pallas_call | solution.py:265
  (58 shorter events, 5.5 us)
Async XLA Ops:
  5.0 10.5 %copy-start.3 = (bf16[1024,768]{1,0:T(8,128)(2,1)S(1)}, bf16[1024,768]{1,0:T(8,128)(2,1)}, u32[]{:S(2)}) copy-start(bf16[1024,768]{1,0:T(8,128)(2,1)} %w_ref.3) | copy-start | bytes 4718596
  5.0 58.4 %copy-start.4 = (s32[3]{0:T(128)S(1)}, s32[3]{0:T(128)}, u32[]{:S(2)}) copy-start(s32[3]{0:T(128)} %pad_add_fusion.meta) | copy-start | bytes 40
  5.0 58.4 %all-to-all-start = ((bf16[64,8,1024]{2,1,0:T(8,128)(2,1)}), bf16[64,8,1024]{2,1,0:T(8,128)(2,1)S(1)}, u32[]{:S(2)}, u32[]{:S(2)}) async-start(bf16[64,8,1024]{2,1,0:T(8,128)(2,1)} %bitcast.21), calls=%async_computation | async-start | bytes 2097152 | tf_op jit(solution)/shard_map/all_to_all | solution.py:305
  15.6 8.5 %collective-permute-start.2 = (bf16[128,384]{1,0:T(8,128)(2,1)S(1)}, bf16[128,384]{1,0:T(8,128)(2,1)S(1)}, u32[]{:S(2)}, u32[]{:S(2)}) collective-permute-start(bf16[128,384]{1,0:T(8,128)(2,1)S(1)} %pad_maximum_fusion.1), channel_id=1, source_target_pairs={{0,3},{1,0},{2,1},{3,2},{4,7},{5,4},{6,5},{7,6},{8,11},{9,8},{10,9... | collective-permute-start | bytes 294920 | tf_op jit(solution)/shard_map/ppermute | solution.py:277
  20.8 16.8 %collective-permute-start.1 = (bf16[128,384]{1,0:T(8,128)(2,1)S(1)}, bf16[128,384]{1,0:T(8,128)(2,1)S(1)}, u32[]{:S(2)}, u32[]{:S(2)}) collective-permute-start(bf16[128,384]{1,0:T(8,128)(2,1)S(1)} %pad_maximum_fusion.1), channel_id=1, source_target_pairs={{0,2},{1,3},{2,0},{3,1},{4,6},{5,7},{6,4},{7,5},{8,10},{9,11},{10,... | collective-permute-start | bytes 294920 | tf_op jit(solution)/shard_map/ppermute | solution.py:277
  22.0 19.0 %collective-permute-start = (bf16[128,384]{1,0:T(8,128)(2,1)S(1)}, bf16[128,384]{1,0:T(8,128)(2,1)S(1)}, u32[]{:S(2)}, u32[]{:S(2)}) collective-permute-start(bf16[128,384]{1,0:T(8,128)(2,1)S(1)} %pad_maximum_fusion.1), channel_id=1, source_target_pairs={{0,1},{1,2},{2,3},{3,0},{4,5},{5,6},{6,7},{7,4},{8,9},{9,10},{10,1... | collective-permute-start | bytes 294920 | tf_op jit(solution)/shard_map/ppermute | solution.py:277
  41.0 9.0 %collective-permute-start.3 = (bf16[3,128,384]{2,1,0:T(8,128)(2,1)S(1)}, bf16[3,128,384]{2,1,0:T(8,128)(2,1)S(1)}, u32[]{:S(2)}, u32[]{:S(2)}) collective-permute-start(bf16[3,128,384]{2,1,0:T(8,128)(2,1)S(1)} %pad_maximum_fusion.refs_0_), channel_id=1, source_target_pairs={{0,8},{4,12},{8,16},{12,20},{16,24},{20,28},{24,0},{28,4},{32,40},... | collective-permute-start | bytes 884744 | tf_op jit(solution)/shard_map/ppermute | solution.py:281
  42.4 14.9 %collective-permute-start.4 = (bf16[3,128,384]{2,1,0:T(8,128)(2,1)S(1)}, bf16[3,128,384]{2,1,0:T(8,128)(2,1)S(1)}, u32[]{:S(2)}, u32[]{:S(2)}) collective-permute-start(bf16[3,128,384]{2,1,0:T(8,128)(2,1)S(1)} %pad_maximum_fusion.refs_0_), channel_id=1, source_target_pairs={{0,16},{4,20},{8,24},{12,28},{16,0},{20,4},{24,8},{28,12},{32,48},... | collective-permute-start | bytes 884744 | tf_op jit(solution)/shard_map/ppermute | solution.py:281
  44.8 15.0 %collective-permute-start.5 = (bf16[3,128,384]{2,1,0:T(8,128)(2,1)S(1)}, bf16[3,128,384]{2,1,0:T(8,128)(2,1)S(1)}, u32[]{:S(2)}, u32[]{:S(2)}) collective-permute-start(bf16[3,128,384]{2,1,0:T(8,128)(2,1)S(1)} %pad_maximum_fusion.refs_0_), channel_id=1, source_target_pairs={{0,24},{4,28},{8,0},{12,4},{16,8},{20,12},{24,16},{28,20},{32,56},... | collective-permute-start | bytes 884744 | tf_op jit(solution)/shard_map/ppermute | solution.py:281
  46.0 14.5 %collective-permute-start.6 = (bf16[3,128,384]{2,1,0:T(8,128)(2,1)S(1)}, bf16[3,128,384]{2,1,0:T(8,128)(2,1)S(1)}, u32[]{:S(2)}, u32[]{:S(2)}) collective-permute-start(bf16[3,128,384]{2,1,0:T(8,128)(2,1)S(1)} %pad_maximum_fusion.refs_0_), channel_id=1, source_target_pairs={{0,4},{4,0},{8,12},{12,8},{16,20},{20,16},{24,28},{28,24},{32,36},... | collective-permute-start | bytes 884744 | tf_op jit(solution)/shard_map/ppermute | solution.py:287
  50.0 11.3 %collective-permute-start.7 = (bf16[3,128,384]{2,1,0:T(8,128)(2,1)S(1)}, bf16[3,128,384]{2,1,0:T(8,128)(2,1)S(1)}, u32[]{:S(2)}, u32[]{:S(2)}) collective-permute-start(bf16[3,128,384]{2,1,0:T(8,128)(2,1)S(1)} %collective-permute-done.3.refs_1_), channel_id=1, source_target_pairs={{0,4},{4,0},{8,12},{12,8},{16,20},{20,16},{24,28},{28,24},{32,36},... | collective-permute-start | bytes 884744 | tf_op jit(solution)/shard_map/ppermute | solution.py:287
  52.0 0.7 copy-start.5
  57.3 4.7 %collective-permute-start.8 = (bf16[3,128,384]{2,1,0:T(8,128)(2,1)S(1)}, bf16[3,128,384]{2,1,0:T(8,128)(2,1)S(1)}, u32[]{:S(2)}, u32[]{:S(2)}) collective-permute-start(bf16[3,128,384]{2,1,0:T(8,128)(2,1)S(1)} %collective-permute-done.4.refs_2_), channel_id=1, source_target_pairs={{0,4},{4,0},{8,12},{12,8},{16,20},{20,16},{24,28},{28,24},{32,36},... | collective-permute-start | bytes 884744 | tf_op jit(solution)/shard_map/ppermute | solution.py:287
  59.1 0.7 copy-start.7
  59.8 2.9 %collective-permute-start.9 = (bf16[3,128,384]{2,1,0:T(8,128)(2,1)S(1)}, bf16[3,128,384]{2,1,0:T(8,128)(2,1)S(1)}, u32[]{:S(2)}, u32[]{:S(2)}) collective-permute-start(bf16[3,128,384]{2,1,0:T(8,128)(2,1)S(1)} %collective-permute-done.5.refs_3_), channel_id=1, source_target_pairs={{0,4},{4,0},{8,12},{12,8},{16,20},{20,16},{24,28},{28,24},{32,36},... | collective-permute-start | bytes 884744 | tf_op jit(solution)/shard_map/ppermute | solution.py:287
  59.8 0.7 copy-start.9
  60.6 0.7 copy-start.11
  61.3 0.7 copy-start.13
  62.0 0.7 copy-start.15
  62.7 0.7 copy-start.17
  63.5 1.0 copy-start.6
  64.4 1.0 copy-start.8
  65.4 1.0 copy-start.10
  66.4 1.0 copy-start.12
  67.3 1.0 copy-start.14
  68.3 1.0 copy-start.16
  69.2 1.0 copy-start.18
  70.2 12.3 %copy-start.2 = (bf16[256,1024]{1,0:T(8,128)(2,1)S(1)}, bf16[256,1024]{1,0:T(8,128)(2,1)}, u32[]{:S(2)}) copy-start(bf16[256,1024]{1,0:T(8,128)(2,1)} %refs_0_.1) | copy-start | bytes 1572868
  76.1 55.3 %all-to-all-start.1 = ((bf16[64,8,512]{2,1,0:T(8,128)(2,1)}), bf16[64,8,512]{2,1,0:T(8,128)(2,1)S(1)}, u32[]{:S(2)}, u32[]{:S(2)}) async-start(bf16[64,8,512]{2,1,0:T(8,128)(2,1)} %bitcast.9), calls=%async_computation.1 | async-start | bytes 1048576 | tf_op jit(solution)/shard_map/all_to_all | solution.py:315
  82.5 18.6 %collective-permute-start.13 = (bf16[128,1024]{1,0:T(8,128)(2,1)S(1)}, bf16[128,1024]{1,0:T(8,128)(2,1)S(1)}, u32[]{:S(2)}, u32[]{:S(2)}) collective-permute-start(bf16[128,1024]{1,0:T(8,128)(2,1)S(1)} %constant_dynamic-slice_fusion), channel_id=1, source_target_pairs={{0,1},{1,2},{2,3},{3,0},{4,5},{5,6},{6,7},{7,4},{8,9},{9,10},{10,1... | collective-permute-start | bytes 786440 | tf_op jit(solution)/shard_map/ppermute | solution.py:277
  85.8 22.3 %collective-permute-start.14 = (bf16[128,1024]{1,0:T(8,128)(2,1)S(1)}, bf16[128,1024]{1,0:T(8,128)(2,1)S(1)}, u32[]{:S(2)}, u32[]{:S(2)}) collective-permute-start(bf16[128,1024]{1,0:T(8,128)(2,1)S(1)} %constant_dynamic-slice_fusion), channel_id=1, source_target_pairs={{0,2},{1,3},{2,0},{3,1},{4,6},{5,7},{6,4},{7,5},{8,10},{9,11},{10,... | collective-permute-start | bytes 786440 | tf_op jit(solution)/shard_map/ppermute | solution.py:277
  85.9 22.3 %collective-permute-start.15 = (bf16[128,1024]{1,0:T(8,128)(2,1)S(1)}, bf16[128,1024]{1,0:T(8,128)(2,1)S(1)}, u32[]{:S(2)}, u32[]{:S(2)}) collective-permute-start(bf16[128,1024]{1,0:T(8,128)(2,1)S(1)} %constant_dynamic-slice_fusion), channel_id=1, source_target_pairs={{0,3},{1,0},{2,1},{3,2},{4,7},{5,4},{6,5},{7,6},{8,11},{9,8},{10,9... | collective-permute-start | bytes 786440 | tf_op jit(solution)/shard_map/ppermute | solution.py:277
  89.2 2.2 %copy-start = (bf16[2048,1024]{1,0:T(8,128)(2,1)S(1)}, bf16[2048,1024]{1,0:T(8,128)(2,1)}, u32[]{:S(2)}) copy-start(bf16[2048,1024]{1,0:T(8,128)(2,1)} %param.3) | copy-start | bytes 12582916
  98.6 0.7 copy-start.19
  99.3 18.8 %collective-permute-start.10 = (bf16[4,128,128]{2,1,0:T(8,128)(2,1)S(1)}, bf16[4,128,128]{2,1,0:T(8,128)(2,1)S(1)}, u32[]{:S(2)}, u32[]{:S(2)}) collective-permute-start(bf16[4,128,128]{2,1,0:T(8,128)(2,1)S(1)} %get-tuple-element.14), channel_id=1, source_target_pairs={{0,1},{1,2},{2,3},{3,0},{4,5},{5,6},{6,7},{7,4},{8,9},{9,10},{10,1... | collective-permute-start | bytes 393224 | tf_op jit(solution)/shard_map/ppermute | solution.py:277
  101.2 30.3 %collective-permute-start.16 = (bf16[128,1024]{1,0:T(8,128)(2,1)S(1)}, bf16[128,1024]{1,0:T(8,128)(2,1)S(1)}, u32[]{:S(2)}, u32[]{:S(2)}) collective-permute-start(bf16[128,1024]{1,0:T(8,128)(2,1)S(1)} %collective-permute-done.13.refs_1_), channel_id=1, source_target_pairs={{0,4},{4,0},{8,12},{12,8},{16,20},{20,16},{24,28},{28,24},{32,36},... | collective-permute-start | bytes 786440 | tf_op jit(solution)/shard_map/ppermute | solution.py:287
  108.1 23.4 %collective-permute-start.17 = (bf16[128,1024]{1,0:T(8,128)(2,1)S(1)}, bf16[128,1024]{1,0:T(8,128)(2,1)S(1)}, u32[]{:S(2)}, u32[]{:S(2)}) collective-permute-start(bf16[128,1024]{1,0:T(8,128)(2,1)S(1)} %collective-permute-done.14.refs_2_), channel_id=1, source_target_pairs={{0,4},{4,0},{8,12},{12,8},{16,20},{20,16},{24,28},{28,24},{32,36},... | collective-permute-start | bytes 786440 | tf_op jit(solution)/shard_map/ppermute | solution.py:287
  108.2 23.3 %collective-permute-start.18 = (bf16[128,1024]{1,0:T(8,128)(2,1)S(1)}, bf16[128,1024]{1,0:T(8,128)(2,1)S(1)}, u32[]{:S(2)}, u32[]{:S(2)}) collective-permute-start(bf16[128,1024]{1,0:T(8,128)(2,1)S(1)} %collective-permute-done.15.refs_3_), channel_id=1, source_target_pairs={{0,4},{4,0},{8,12},{12,8},{16,20},{20,16},{24,28},{28,24},{32,36},... | collective-permute-start | bytes 786440 | tf_op jit(solution)/shard_map/ppermute | solution.py:287
  108.6 14.9 %collective-permute-start.11 = (bf16[4,128,128]{2,1,0:T(8,128)(2,1)S(1)}, bf16[4,128,128]{2,1,0:T(8,128)(2,1)S(1)}, u32[]{:S(2)}, u32[]{:S(2)}) collective-permute-start(bf16[4,128,128]{2,1,0:T(8,128)(2,1)S(1)} %get-tuple-element.15), channel_id=1, source_target_pairs={{0,2},{1,3},{2,0},{3,1},{4,6},{5,7},{6,4},{7,5},{8,10},{9,11},{10,... | collective-permute-start | bytes 393224 | tf_op jit(solution)/shard_map/ppermute | solution.py:277
  118.0 13.4 %collective-permute-start.12 = (bf16[4,128,128]{2,1,0:T(8,128)(2,1)S(1)}, bf16[4,128,128]{2,1,0:T(8,128)(2,1)S(1)}, u32[]{:S(2)}, u32[]{:S(2)}) collective-permute-start(bf16[4,128,128]{2,1,0:T(8,128)(2,1)S(1)} %get-tuple-element.16), channel_id=1, source_target_pairs={{0,3},{1,0},{2,1},{3,2},{4,7},{5,4},{6,5},{7,6},{8,11},{9,8},{10,9... | collective-permute-start | bytes 393224 | tf_op jit(solution)/shard_map/ppermute | solution.py:277
  131.5 0.9 copy-start.20
  134.9 0.7 copy-start.1
  135.6 12.7 %collective-permute-start.19 = (bf16[512,256]{1,0:T(8,128)(2,1)S(1)}, bf16[512,256]{1,0:T(8,128)(2,1)S(1)}, u32[]{:S(2)}, u32[]{:S(2)}) collective-permute-start(bf16[512,256]{1,0:T(8,128)(2,1)S(1)} %get-tuple-element.18), channel_id=1, source_target_pairs={{0,1},{1,2},{2,3},{3,0},{4,5},{5,6},{6,7},{7,4},{8,9},{9,10},{10,1... | collective-permute-start | bytes 786440 | tf_op jit(solution)/shard_map/ppermute | solution.py:277
  137.3 21.1 %collective-permute-start.20 = (bf16[512,256]{1,0:T(8,128)(2,1)S(1)}, bf16[512,256]{1,0:T(8,128)(2,1)S(1)}, u32[]{:S(2)}, u32[]{:S(2)}) collective-permute-start(bf16[512,256]{1,0:T(8,128)(2,1)S(1)} %get-tuple-element.19), channel_id=1, source_target_pairs={{0,2},{1,3},{2,0},{3,1},{4,6},{5,7},{6,4},{7,5},{8,10},{9,11},{10,... | collective-permute-start | bytes 786440 | tf_op jit(solution)/shard_map/ppermute | solution.py:277
  138.8 22.8 %collective-permute-start.21 = (bf16[512,256]{1,0:T(8,128)(2,1)S(1)}, bf16[512,256]{1,0:T(8,128)(2,1)S(1)}, u32[]{:S(2)}, u32[]{:S(2)}) collective-permute-start(bf16[512,256]{1,0:T(8,128)(2,1)S(1)} %get-tuple-element.20), channel_id=1, source_target_pairs={{0,3},{1,0},{2,1},{3,2},{4,7},{5,4},{6,5},{7,6},{8,11},{9,8},{10,9... | collective-permute-start | bytes 786440 | tf_op jit(solution)/shard_map/ppermute | solution.py:277
  148.2 13.4 %copy-start.21 = (bf16[512,256]{1,0:T(8,128)(2,1)}, bf16[512,256]{1,0:T(8,128)(2,1)S(1)}, u32[]{:S(2)}) copy-start(bf16[512,256]{1,0:T(8,128)(2,1)S(1)} %collective-permute-done.19) | copy-start | bytes 786436
  158.4 3.2 %copy-start.22 = (bf16[512,256]{1,0:T(8,128)(2,1)}, bf16[512,256]{1,0:T(8,128)(2,1)S(1)}, u32[]{:S(2)}) copy-start(bf16[512,256]{1,0:T(8,128)(2,1)S(1)} %collective-permute-done.20) | copy-start | bytes 786436
  161.6 0.7 copy-start.23

commit v2 on v0

v2 whole, which is shorter than its diff:
```python
import jax
import jax.numpy as jnp
from jax import lax
from jax.experimental import pallas as pl
from jax.experimental.pallas import tpu as pltpu
from jax.sharding import PartitionSpec as P

D = 1024
HEADS = 16
C = 512
GROUPS = 4
DIM = 64
HALF = 128
ROWS_LOCAL = 4
BLOCK = 128
BF = jnp.bfloat16
F32 = jnp.float32
VMEM = pltpu.VMEM
MIB = 1 << 20
ORDER = (2, 1, 3)
SCALE = 0.125 * 1.4426950408889634


def whole():
    return pl.BlockSpec(memory_space=VMEM)


def anywhere():
    return pl.BlockSpec(memory_space=pl.ANY)


def smem():
    return pl.BlockSpec(memory_space=pltpu.SMEM)


def one_hot(source_of):
    out_at = lax.broadcasted_iota(jnp.int32, (BLOCK, BLOCK), 0)
    in_at = lax.broadcasted_iota(jnp.int32, (BLOCK, BLOCK), 1)
    return (in_at == source_of(out_at)).astype(F32).astype(BF)


def move(pick, data):
    return jnp.dot(pick, data, preferred_element_type=F32).astype(BF)


def causal():
    at_query = lax.broadcasted_iota(jnp.int32, (2 * BLOCK, BLOCK), 0) % BLOCK
    return lax.broadcasted_iota(jnp.int32, (2 * BLOCK, BLOCK), 1) <= at_query


def attend(qkv, allowed, store):
    length = qkv.shape[0]
    first = lax.broadcasted_iota(jnp.int32, (1, HALF), 1) < DIM
    query = qkv[:, :HALF]
    query_a = jnp.where(first, query, 0.0).astype(BF)
    query_b = jnp.where(first, 0.0, query).astype(BF)
    key = qkv[:, HALF : 2 * HALF].astype(BF)
    value = qkv[:, 2 * HALF :].astype(BF)
    value = jnp.concatenate([value, jnp.ones((length, HALF), BF)], axis=1)
    for block in range(length // BLOCK):
        lo = block * BLOCK
        hi = lo + BLOCK
        both = jnp.concatenate([query_a[lo:hi], query_b[lo:hi]], axis=0)
        scores = lax.dot_general(
            both, key[:hi], (((1,), (1,)), ((), ())), preferred_element_type=F32
        )
        pieces = [scores[:, n * BLOCK : (n + 1) * BLOCK] for n in range(block)]
        pieces.append(jnp.where(allowed, scores[:, lo:], F32(-1e30)))
        top = pieces[0]
        for piece in pieces[1:]:
            top = jnp.maximum(top, piece)
        top = jnp.max(top, axis=-1, keepdims=True)
        expo = [jnp.exp2((piece - top) * F32(SCALE)).astype(BF) for piece in pieces]
        out = jnp.dot(jnp.concatenate(expo, axis=1), value[:hi], preferred_element_type=F32)
        out = jnp.where(jnp.concatenate([first, first], axis=1), out[:BLOCK], out[BLOCK:])
        store(lo, (out[:, :HALF] / out[:, HALF:]).astype(BF))


def call(kernel, name, flops=0, moved=MIB, **options):
    return pl.pallas_call(
        kernel,
        compiler_params=pltpu.CompilerParams(vmem_limit_bytes=56 * MIB),
        cost_estimate=pl.CostEstimate(flops=flops, bytes_accessed=moved, transcendentals=0),
        name=name,
        **options,
    )


def like(*shape):
    return jax.ShapeDtypeStruct(shape, BF)


def cut_kernel(meta, query_ref, key_ref, value_ref, col_ref, row_ref, *outs):
    g = meta[0]
    for k, out_ref in zip(ORDER, outs):
        out_ref[:, :HALF] = query_ref[...]
        out_ref[:, HALF : 2 * HALF] = key_ref[...]
        out_ref[:, 2 * HALF : 3 * HALF] = value_ref[...]
        out_ref[:, 3 * HALF : 4 * HALF] = col_ref[...]
        at = pl.multiple_of(lax.rem(g + k, GROUPS) * 256, 256)
        out_ref[:, 4 * HALF :] = row_ref[:, pl.ds(at, 256)]


def cut(meta, w_qkv, w_out):
    def part(n):
        return pl.BlockSpec((BLOCK, HALF), lambda b, meta: (meta[1] * 2 + meta[2], 2 * n + 1))

    return call(
        cut_kernel,
        "cut",
        grid_spec=pltpu.PrefetchScalarGridSpec(
            num_scalar_prefetch=1,
            grid=(1,),
            in_specs=[
                part(0),
                part(1),
                part(2),
                pl.BlockSpec((BLOCK, HALF), lambda b, meta: (1, meta[1] * 2 + meta[2])),
                pl.BlockSpec((BLOCK, D), lambda b, meta: (0, 0)),
            ],
            out_specs=[pl.BlockSpec((BLOCK, 6 * HALF), lambda b, meta: (0, 0))] * 3,
        ),
        out_shape=[like(BLOCK, 6 * HALF)] * 3,
    )(meta, w_qkv, w_qkv, w_qkv, w_out, w_out)


def mid_kernel(in0, in1, in2, out_ref, row_ref):
    for n, ref in enumerate((in0, in1, in2)):
        out_ref[n] = ref[:, : 4 * HALF]
        row_ref[n] = ref[:, 4 * HALF :]


def mid(parts):
    return call(
        mid_kernel,
        "mid",
        flops=10**12,
        in_specs=[whole()] * 3,
        out_specs=[whole()] * 2,
        out_shape=[like(3, BLOCK, 4 * HALF), like(3, BLOCK, 256)],
    )(*parts)


def stack_kernel(in0, in1, in2, in3, after, out_ref):
    for n, ref in enumerate((in0, in1, in2, in3)):
        out_ref[n] = ref[...]


def stack(parts, after):
    return call(
        stack_kernel,
        "stack",
        flops=10**9,
        in_specs=[whole()] * 4 + [anywhere()],
        out_specs=whole(),
        out_shape=like(4, 3, BLOCK, 4 * HALF),
    )(*parts, after)


def prep_kernel(meta, sig_ref, out_ref):
    pick = one_hot(lambda o: ((o // 2) % 4) * 32 + (o // 8) * 2 + o % 2)
    for b in range(2):
        part = sig_ref[:, b * 32 : (b + 1) * 32, :].reshape(BLOCK, D)
        out_ref[b * BLOCK : (b + 1) * BLOCK, :] = move(pick, part)


def prep(meta, sig):
    return call(
        prep_kernel,
        "prep",
        flops=2 * C * D * BLOCK,
        moved=2 * MIB,
        grid_spec=pltpu.PrefetchScalarGridSpec(
            num_scalar_prefetch=1,
            grid=(2,),
            in_specs=[pl.BlockSpec((4, 64, D), lambda b, meta: (0, meta[0] * 2 + b, 0))],
            out_specs=pl.BlockSpec((256, D), lambda b, meta: (b, 0)),
        ),
        out_shape=like(C, D),
    )(meta, sig)


def row_kernel(sig_ref, query_ref, key_ref, value_ref, out_ref):
    weight = jnp.concatenate([query_ref[...], key_ref[...], value_ref[...]], axis=1)
    qkv = jnp.dot(sig_ref[0], weight, preferred_element_type=F32)

    def store(lo, out):
        out_ref[0, lo : lo + BLOCK, :] = out

    attend(qkv, causal(), store)


def row_part(sig, w_qkv):
    def part(n):
        return pl.BlockSpec((D, HALF), lambda r: (0, 2 * n))

    return call(
        row_kernel,
        "row_part",
        flops=6 * 10**9,
        moved=6 * MIB,
        grid=(ROWS_LOCAL,),
        in_specs=[pl.BlockSpec((1, C, D), lambda r: (r, 0, 0)), part(0), part(1), part(2)],
        out_specs=pl.BlockSpec((1, C, HALF), lambda r: (r, 0, 0)),
        out_shape=like(ROWS_LOCAL, C, HALF),
    )(sig, w_qkv, w_qkv, w_qkv)


def column_kernel(
    meta, got_ref, w_ref, w_out_ref, near, far, out_ref, held, weights, mixers, outs, sems
):
    x = meta[1]
    core = meta[2]
    copies = []
    for d in range(4):
        from_x = lax.rem(x + 4 - d, 4) * 2
        for n, (ref, at) in enumerate(((near, from_x + core), (far, from_x + 1 - core))):
            rows = pl.ds(pl.multiple_of(at * BLOCK, BLOCK), BLOCK)
            sem = 4 * d + 2 * n
            copies.append(
                pltpu.make_async_copy(
                    ref.at[d, :, :, : 3 * HALF], weights.at[:, rows, :], sems.at[sem]
                )
            )
            copies.append(
                pltpu.make_async_copy(
                    ref.at[d, :, :, 3 * HALF :], mixers.at[:, at], sems.at[sem + 1]
                )
            )
    for copy in copies:
        copy.start()
    pick = one_hot(lambda o: (o % 64) * 2 + o // 64)
    for b in range(4):
        moved = move(pick, got_ref[b * BLOCK : (b + 1) * BLOCK, :])
        held[b * 64 : b * 64 + 64, :] = moved[:64]
        held[256 + b * 64 : 256 + b * 64 + 64, :] = moved[64:]
    allowed = causal()

    def group(k, weight):
        qkv = jnp.dot(held[...], weight, preferred_element_type=F32)
        for c in range(2):

            def store(lo, out):
                at = c * 256 + lo
                outs[at : at + BLOCK, k * HALF : (k + 1) * HALF] = out

            attend(qkv[c * 256 : (c + 1) * 256], allowed, store)

    group(
        0,
        jnp.concatenate(
            [w_ref[:, HALF:256], w_ref[:, 256 + HALF : 512], w_ref[:, 512 + HALF :]], axis=1
        ),
    )
    for copy in copies:
        copy.wait()
    for n in range(3):
        group(n + 1, weights[n])
    mixer = jnp.concatenate(
        [w_out_ref[HALF:, :]]
        + [jnp.concatenate([mixers[n, s] for s in range(8)], axis=1) for n in range(3)],
        axis=0,
    )
    back = one_hot(lambda o: (o % 2) * 64 + o // 2)
    for b in range(4):
        both = jnp.concatenate(
            [outs[b * 64 : b * 64 + 64, :], outs[256 + b * 64 : 256 + b * 64 + 64, :]], axis=0
        )
        mixed = jnp.dot(move(back, both), mixer, preferred_element_type=F32).astype(BF)
        for j in range(GROUPS):
            out_ref[b * 16 : (b + 1) * 16, j] = mixed[:, j * 256 : (j + 1) * 256].reshape(16, 8, 256)


def column_part(meta, got, w_qkv, w_out, near, far):
    return call(
        column_kernel,
        "column_part",
        flops=4 * 10**9,
        moved=6 * MIB,
        in_specs=[smem(), whole(), whole(), whole(), anywhere(), anywhere()],
        out_specs=whole(),
        out_shape=like(64, GROUPS, 8, 256),
        scratch_shapes=[
            VMEM((C, D), BF),
            VMEM((3, D, 3 * HALF), BF),
            VMEM((3, 8, BLOCK, HALF), BF),
            VMEM((C, C), BF),
            pltpu.SemaphoreType.DMA((16,)),
        ],
    )(meta, got, w_qkv, w_out, near, far)


def join_kernel(meta, got_ref, rows_ref, own_ref, w_ref, out_ref):
    g = meta[0]
    weight = jnp.concatenate([own_ref[...]] + [w_ref[n] for n in range(3)], axis=0)
    pick = one_hot(lambda o: ((o // 2) % 16) * 8 + (o // 32) * 2 + o % 2)
    columns = [
        jnp.dot(
            pick,
            got_ref[b * 16 : (b + 1) * 16, 0].reshape(BLOCK, 256),
            preferred_element_type=F32,
        )
        for b in range(4)
    ]
    for r in range(ROWS_LOCAL):
        left = jnp.concatenate(
            [rows_ref[lax.rem(g + GROUPS - k, GROUPS), r, 0] for k in (0,) + ORDER], axis=1
        )
        right = jnp.concatenate([column[r * 32 : (r + 1) * 32] for column in columns], axis=0)
        mixed = jnp.dot(left, weight, preferred_element_type=F32) + right
        out_ref[r, 0] = mixed.astype(BF)


def join(meta, got, rows, w_out, w_rows):
    return call(
        join_kernel,
        "join",
        flops=2 * 10**9,
        moved=4 * MIB,
        grid_spec=pltpu.PrefetchScalarGridSpec(
            num_scalar_prefetch=1,
            grid=(GROUPS,),
            in_specs=[
                pl.BlockSpec((64, 1, 8, 256), lambda j, meta: (0, j, 0, 0)),
                pl.BlockSpec(
                    (GROUPS, ROWS_LOCAL, 1, BLOCK, HALF), lambda j, meta: (0, 0, j, 0, 0)
                ),
                pl.BlockSpec((BLOCK, 256), lambda j, meta: (0, meta[0])),
                pl.BlockSpec((3, BLOCK, 256), lambda j, meta: (0, 0, 0)),
            ],
            out_specs=pl.BlockSpec((ROWS_LOCAL, 1, BLOCK, 256), lambda j, meta: (0, j, 0, 0)),
        ),
        out_shape=like(ROWS_LOCAL, GROUPS, BLOCK, 256),
    )(meta, got, rows, w_out, w_rows)


def to_group(data, k):
    return lax.ppermute(data, "heads", [(j, (j + k) % GROUPS) for j in range(GROUPS)])


def along_x(data, d):
    return lax.ppermute(
        data, "rows", [(i, i // 8 * 8 + (i // 2 % 4 + d) % 4 * 2 + i % 2) for i in range(64)]
    )


def other_core(data):
    return lax.ppermute(data, "rows", [(i, i ^ 1) for i in range(64)])


def local(signal, w_qkv, w_out):
    i = lax.axis_index("rows")
    g = lax.axis_index("heads")
    meta = jnp.stack([g, i // 2 % 4, i % 2]).astype(jnp.int32)
    sig = signal.reshape(ROWS_LOCAL, C, D)

    cuts = cut(meta, w_qkv, w_out)
    others, w_rows = mid([to_group(part, k) for part, k in zip(cuts, ORDER)])

    send = prep(meta, sig).reshape(64, 8, D)
    got = lax.all_to_all(send, "rows", split_axis=0, concat_axis=0, tiled=True).reshape(C, D)

    own_rows = row_part(sig, w_qkv)
    rows = lax.all_gather(own_rows.reshape(ROWS_LOCAL * C, HALF), "heads", axis=0)

    near = stack([others] + [along_x(others, d) for d in (1, 2, 3)], own_rows)
    far = other_core(near)

    columns = column_part(meta, got, w_qkv, w_out, near, far).reshape(64 * GROUPS, 8, 256)
    back = lax.all_to_all(columns, ("rows", "heads"), split_axis=0, concat_axis=0, tiled=True)
    return join(
        meta,
        back.reshape(64, GROUPS, 8, 256),
        rows.reshape(GROUPS, ROWS_LOCAL, GROUPS, BLOCK, HALF),
        w_out,
        w_rows,
    ).reshape(ROWS_LOCAL * C, 256)


def solution(mesh):
    return jax.shard_map(
        local,
        mesh=mesh,
        in_specs=(P("rows", None), P(None, "heads"), P("heads", None)),
        out_specs=P("rows", "heads"),
        check_vma=False,
    )
```

time: 286 us -> 157 us (0.55); the launches traced: 282 us -> 157 us
  waiting for transfers between devices: 171 us -> 70.9 us
  local copies, waits for them, and re-layouts: 51.8 us -> 4.34 us
  Pallas kernels: 0 us -> 33.2 us
  matrix products: 24.8 us -> 0 us
  starting transfers between devices: 17.2 us -> 34.1 us
  other arithmetic: 4.07 us -> 0.65 us
    reduce_scatter x1 -> x0, waiting for transfers between devices: 150 us -> none  [local(): lax.psum_scatter(partial_terms, 'heads', scatter_dimension=1, tiled=True)]
    all_gather x0 -> x1, waiting for transfers between devices: none -> 47.1 us  [local(): lax.all_gather(own_rows.reshape(ROWS_LOCAL * C, HALF), 'heads', axis=0)]
    pallas_call x0 -> x7, Pallas kernels: none -> 33.2 us  [the longest x1 9.62 us: column_part(): call(column_kernel, 'column_part', flops=4 * 10 ** 9, moved=6 * MIB, in_s...]
    reshape x7 -> x0, local copies, waits for them, and re-layouts: 21.9 us -> none  [the longest x2 9.36 us: local(): projected[:, :, :, half_heads:]]
    ppermute x0 -> x7, waiting for transfers between devices: none -> 18.8 us  [the longest x3 13.3 us: along_x(): lax.ppermute(data, 'rows', [(i, i // 8 * 8 + (i // 2 % 4 + d) % 4 * 2 + i...]
    dot_general x5 -> x0, matrix products: 17.2 us -> none  [the longest x1 7.28 us: local(): jnp.dot(signal, w_qkv, preferred_element_type=jnp.float32)]
    ppermute x0 -> x7, starting transfers between devices: none -> 17.1 us  [the longest x3 11.3 us: to_group(): lax.ppermute(data, 'heads', [(j, (j + k) % GROUPS) for j in range(GROUPS)])]
    all_to_all x2, waiting for transfers between devices: 20.4 us -> 4.91 us  [the longest x1 4.91 us: local(): lax.all_to_all(columns, ('rows', 'heads'), split_axis=0, concat_axis=0, t...]
  transfers between devices with their start and end apart: 3 -> 10, of which waited for: 3 -> 6; matrix products, arithmetic and copies ran while one was open for 5% -> 0% of each run, Pallas kernels for 0% -> 16%
where the time goes in v2:
time: 157 us
  waiting for transfers between devices  70.9 us (45%)
  starting transfers between devices  34.1 us (22%)
  Pallas kernels  33.2 us (21%)
  between operations  13.5 us (9%)
  local copies, waits for them, and re-layouts  4.34 us (3%)
    all_gather x1, waiting for transfers between devices, local(): lax.all_gather(own_rows.reshape(ROWS_LOCAL * C, HALF), 'heads', axis=0)  47.1 us
    ppermute x3, waiting for transfers between devices, along_x(): lax.ppermute(data, 'rows', [(i, i // 8 * 8 + (i // 2 % 4 + d) % 4 * 2 + i...  13.3 us
    ppermute x3, starting transfers between devices, to_group(): lax.ppermute(data, 'heads', [(j, (j + k) % GROUPS) for j in range(GROUPS)])  11.3 us
    all_to_all x1, starting transfers between devices, local(): lax.all_to_all(send, 'rows', split_axis=0, concat_axis=0, tiled=True)  9.65 us
    pallas_call x1, Pallas kernels, column_part(): call(column_kernel, 'column_part', flops=4 * 10 ** 9, moved=6 * MIB, in_s...  9.62 us
    pallas_call x1, Pallas kernels, row_part(): call(row_kernel, 'row_part', flops=6 * 10 ** 9, moved=6 * MIB, grid=(ROWS...  8.1 us
    all_to_all x1, starting transfers between devices, local(): lax.all_to_all(columns, ('rows', 'heads'), split_axis=0, concat_axis=0, t...  7.31 us
    pallas_call x1, Pallas kernels, join(): call(join_kernel, 'join', flops=2 * 10 ** 9, moved=4 * MIB, grid_spec=plt...  5.19 us
  transfers between devices with their start and end apart: 10, of which 6 were waited for; matrix products, arithmetic and copies ran while one was open for 0% of the time, Pallas kernels for 16%

profile of v2, /device:TPU:1, one launch (start us, length us, event | category | flops | bytes accessed | tf_op | source)
XLA Modules:
  0.0 156.7 jit_solution(11289918970468613636)
XLA Ops:
  6.5 0.7 pad_add_fusion.meta
  7.2 2.6 %cut.1 = (bf16[128,768]{1,0:T(8,128)(2,1)}, bf16[128,768]{1,0:T(8,128)(2,1)}, bf16[128,768]{1,0:T(8,128)(2,1)}) custom-call(s32[3]{0:T(128)} %pad_add_fusion.meta, bf16[1024,768]{1,0:T(8,128)(2,1)} %w_ref.1, bf16[1024,768]{1,0:T(8,128)(2,1)} %w_ref.1, bf16[1024,768]{1,0:T(8,128)(2,1)} %w_ref.1, bf16[256,1024]{1,0:T(8,128)(2,1)} %own_ref.1, ...), custom_call_target="tpu_custom_call" | custom-call | bytes 1048576 | tf_op jit(solution)/shard_map/cut/pallas_call | solution.py:108
  9.8 7.7 %collective-permute-start = (bf16[128,768]{1,0:T(8,128)(2,1)}, bf16[128,768]{1,0:T(8,128)(2,1)S(1)}, u32[]{:S(2)}, u32[]{:S(2)}) collective-permute-start(bf16[128,768]{1,0:T(8,128)(2,1)} %get-tuple-element.10), channel_id=1, source_target_pairs={{0,2},{1,3},{2,0},{3,1},{4,6},{5,7},{6,4},{7,5},{8,10},{9,11},{10,... | collective-permute-start | bytes 589832 | tf_op jit(solution)/shard_map/ppermute | solution.py:338
  17.5 1.2 collective-permute-start.1
  18.7 2.4 %collective-permute-start.2 = (bf16[128,768]{1,0:T(8,128)(2,1)}, bf16[128,768]{1,0:T(8,128)(2,1)S(1)}, u32[]{:S(2)}, u32[]{:S(2)}) collective-permute-start(bf16[128,768]{1,0:T(8,128)(2,1)} %get-tuple-element.12), channel_id=1, source_target_pairs={{0,3},{1,0},{2,1},{3,2},{4,7},{5,4},{6,5},{7,6},{8,11},{9,8},{10,9... | collective-permute-start | bytes 589832 | tf_op jit(solution)/shard_map/ppermute | solution.py:338
  21.1 3.1 %prep.1 = bf16[512,1024]{1,0:T(8,128)(2,1)} custom-call(s32[3]{0:T(128)} %pad_add_fusion.meta, bf16[4,512,1024]{2,1,0:T(8,128)(2,1)} %bitcast.11), custom_call_target="tpu_custom_call" | custom-call | flops 134217728 | bytes 2097152 | tf_op jit(solution)/shard_map/prep/pallas_call | solution.py:168
  24.2 9.6 %all-to-all-start = ((bf16[64,8,1024]{2,1,0:T(8,128)(2,1)}), bf16[64,8,1024]{2,1,0:T(8,128)(2,1)}, u32[]{:S(2)}, u32[]{:S(2)}) async-start(bf16[64,8,1024]{2,1,0:T(8,128)(2,1)} %bitcast.13), calls=%async_computation | async-start | bytes 2097152 | tf_op jit(solution)/shard_map/all_to_all | solution.py:361
  33.9 0.0 all-gather.2.cloned.1.call-start
  33.9 0.0 collective-permute-done.in0
  33.9 0.0 copy-start.5
  33.9 0.0 collective-permute-done.1.in1
  33.9 0.0 copy-start.6
  33.9 2.3 %collective-permute-done.2.in2 = bf16[128,768]{1,0:T(8,128)(2,1)S(1)} collective-permute-done((bf16[128,768]{1,0:T(8,128)(2,1)}, bf16[128,768]{1,0:T(8,128)(2,1)S(1)}, u32[]{:S(2)}, u32[]{:S(2)}) %collective-permute-start.2) | collective-permute-done | bytes 196640 | tf_op jit(solution)/shard_map/ppermute | solution.py:338
  36.3 0.0 copy-done.5
  36.3 0.0 copy-done.6
  36.3 0.0 copy-start.7
  36.3 0.7 copy-done.7
  37.0 2.0 %mid.1 = (bf16[3,128,512]{2,1,0:T(8,128)(2,1)}, bf16[3,128,256]{2,1,0:T(8,128)(2,1)}) custom-call(bf16[128,768]{1,0:T(8,128)(2,1)} %copy-done.5, bf16[128,768]{1,0:T(8,128)(2,1)} %copy-done.6, bf16[128,768]{1,0:T(8,128)(2,1)} %copy-done.7), custom_call_target="tpu_custom_call" | custom-call | flops 999999995904 | bytes 1048576 | tf_op jit(solution)/shard_map/mid/pallas_call | solution.py:134
  38.9 1.2 collective-permute-start.3
  40.2 2.6 %collective-permute-start.4 = (bf16[3,128,512]{2,1,0:T(8,128)(2,1)}, bf16[3,128,512]{2,1,0:T(8,128)(2,1)S(1)}, u32[]{:S(2)}, u32[]{:S(2)}) collective-permute-start(bf16[3,128,512]{2,1,0:T(8,128)(2,1)} %get-tuple-element.13.in0), channel_id=1, source_target_pairs={{0,16},{4,20},{8,24},{12,28},{16,0},{20,4},{24,8},{28,12},{32,48},... | collective-permute-start | bytes 1179656 | tf_op jit(solution)/shard_map/ppermute | solution.py:342
  42.7 1.2 collective-permute-start.5
  43.9 8.1 %row_part.1.after = bf16[4,512,128]{2,1,0:T(8,128)(2,1)} custom-call(bf16[4,512,1024]{2,1,0:T(8,128)(2,1)} %bitcast.12, bf16[1024,768]{1,0:T(8,128)(2,1)} %w_ref.1, bf16[1024,768]{1,0:T(8,128)(2,1)} %w_ref.1, bf16[1024,768]{1,0:T(8,128)(2,1)} %w_ref.1), custom_call_target="tpu_custom_call" | custom-call | flops 6000000000 | bytes 6291456 | tf_op jit(solution)/shard_map/row_part/pallas_call | solution.py:197
  52.0 4.7 %collective-permute-done.3.in1 = bf16[3,128,512]{2,1,0:T(8,128)(2,1)S(1)} collective-permute-done((bf16[3,128,512]{2,1,0:T(8,128)(2,1)}, bf16[3,128,512]{2,1,0:T(8,128)(2,1)S(1)}, u32[]{:S(2)}, u32[]{:S(2)}) %collective-permute-start.3) | collective-permute-done | bytes 393248 | tf_op jit(solution)/shard_map/ppermute | solution.py:342
  56.7 0.0 copy-start.2
  56.7 8.6 %collective-permute-done.4.in2 = bf16[3,128,512]{2,1,0:T(8,128)(2,1)S(1)} collective-permute-done((bf16[3,128,512]{2,1,0:T(8,128)(2,1)}, bf16[3,128,512]{2,1,0:T(8,128)(2,1)S(1)}, u32[]{:S(2)}, u32[]{:S(2)}) %collective-permute-start.4) | collective-permute-done | bytes 393248 | tf_op jit(solution)/shard_map/ppermute | solution.py:342
  65.3 0.0 copy-start.3
  65.3 0.0 collective-permute-done.5.in3
  65.3 0.0 copy-done.2
  65.3 0.8 copy-done.3
  66.0 0.0 copy-start.4
  66.0 0.7 copy-done.4
  66.8 2.6 %stack.17.near = bf16[4,3,128,512]{3,2,1,0:T(8,128)(2,1)} custom-call(bf16[3,128,512]{2,1,0:T(8,128)(2,1)} %get-tuple-element.13.in0, bf16[3,128,512]{2,1,0:T(8,128)(2,1)} %copy-done.2, bf16[3,128,512]{2,1,0:T(8,128)(2,1)} %copy-done.3, bf16[3,128,512]{2,1,0:T(8,128)(2,1)} %copy-done.4, bf16[4,512,128]{2,1,0:T(8,128)(2,1)} %row_part.1.after), custom_call_target="tpu_custom_call" | custom-call | flops 1000000000 | bytes 1048576 | tf_op jit(solution)/shard_map/stack/pallas_call | solution.py:150
  69.4 0.9 collective-permute-start.6
  70.2 0.0 all-gather.2.cloned.1.call-update
  70.3 0.0 all-to-all-done
  70.3 3.2 %collective-permute-done.6.far = bf16[4,3,128,512]{3,2,1,0:T(8,128)(2,1)S(1)} collective-permute-done((bf16[4,3,128,512]{3,2,1,0:T(8,128)(2,1)}, bf16[4,3,128,512]{3,2,1,0:T(8,128)(2,1)S(1)}, u32[]{:S(2)}, u32[]{:S(2)}) %collective-permute-start.6) | collective-permute-done | bytes 1572896 | tf_op jit(solution)/shard_map/ppermute | solution.py:348
  73.5 0.0 copy-start.1
  73.5 1.2 copy-done.1
  74.7 9.6 %column_part.1 = bf16[64,4,8,256]{3,2,1,0:T(8,128)(2,1)} custom-call(s32[3]{0:T(128)} %pad_add_fusion.meta, bf16[512,1024]{1,0:T(8,128)(2,1)} %bitcast.5.got_ref, bf16[1024,768]{1,0:T(8,128)(2,1)} %w_ref.1, bf16[256,1024]{1,0:T(8,128)(2,1)} %own_ref.1, bf16[4,3,128,512]{3,2,1,0:T(8,128)(2,1)} %stack.17.near, bf16[4,3,128,512]{3,2,1,0:T(8,128)(2,1)} %copy-done.1), custom_call_target="tpu_custom_call" | custom-call | flops 4000000000 | bytes 6291456 | tf_op jit(solution)/shard_map/column_part/pallas_call | solution.py:275
  84.3 7.3 %all-to-all-start.1 = ((bf16[256,8,256]{2,1,0:T(8,128)(2,1)}), bf16[256,8,256]{2,1,0:T(8,128)(2,1)S(1)}, u32[]{:S(2)}, u32[]{:S(2)}) async-start(bf16[256,8,256]{2,1,0:T(8,128)(2,1)} %bitcast.15), calls=%async_computation.1 | async-start | bytes 2097152 | tf_op jit(solution)/shard_map/all_to_all | solution.py:370
  91.6 47.1 %all-gather.2.cloned.1.call-done = bf16[4,2048,128]{2,1,0:T(8,128)(2,1)} async-done(((bf16[1,2048,128]{2,1,0:T(8,128)(2,1)}), bf16[4,2048,128]{2,1,0:T(8,128)(2,1)}) %all-gather.2.cloned.1.call-update) | async-done | bytes 2097168 | tf_op jit(solution)/shard_map/all_gather | solution.py:364
  138.7 4.9 %all-to-all-done.1 = bf16[256,8,256]{2,1,0:T(8,128)(2,1)S(1)} async-done(((bf16[256,8,256]{2,1,0:T(8,128)(2,1)}), bf16[256,8,256]{2,1,0:T(8,128)(2,1)S(1)}, u32[]{:S(2)}, u32[]{:S(2)}) %all-to-all-start.1) | async-done | bytes 1048608 | tf_op jit(solution)/shard_map/all_to_all | solution.py:370
  143.6 0.0 copy-start
  143.6 1.0 copy-done
  144.6 5.2 %join.1 = bf16[4,4,128,256]{3,2,1,0:T(8,128)(2,1)} custom-call(s32[3]{0:T(128)} %pad_add_fusion.meta, bf16[64,4,8,256]{3,2,1,0:T(8,128)(2,1)} %bitcast.14, bf16[4,4,4,128,128]{4,3,2,1,0:T(8,128)(2,1)} %bitcast.17, bf16[256,1024]{1,0:T(8,128)(2,1)} %own_ref.1, bf16[3,128,256]{2,1,0:T(8,128)(2,1)} %get-tuple-element.14.w_ref), custom_call_target="tpu_custom_call" | custom-call | flops 2000000000 | bytes 4194304 | tf_op jit(solution)/shard_map/join/pallas_call | solution.py:315
Async XLA Ops:
  9.8 24.1 %collective-permute-start = (bf16[128,768]{1,0:T(8,128)(2,1)}, bf16[128,768]{1,0:T(8,128)(2,1)S(1)}, u32[]{:S(2)}, u32[]{:S(2)}) collective-permute-start(bf16[128,768]{1,0:T(8,128)(2,1)} %get-tuple-element.10), channel_id=1, source_target_pairs={{0,2},{1,3},{2,0},{3,1},{4,6},{5,7},{6,4},{7,5},{8,10},{9,11},{10,... | collective-permute-start | bytes 589832 | tf_op jit(solution)/shard_map/ppermute | solution.py:338
  17.5 16.4 %collective-permute-start.1 = (bf16[128,768]{1,0:T(8,128)(2,1)}, bf16[128,768]{1,0:T(8,128)(2,1)S(1)}, u32[]{:S(2)}, u32[]{:S(2)}) collective-permute-start(bf16[128,768]{1,0:T(8,128)(2,1)} %get-tuple-element.11), channel_id=1, source_target_pairs={{0,1},{1,2},{2,3},{3,0},{4,5},{5,6},{6,7},{7,4},{8,9},{9,10},{10,1... | collective-permute-start | bytes 589832 | tf_op jit(solution)/shard_map/ppermute | solution.py:338
  18.7 17.6 %collective-permute-start.2 = (bf16[128,768]{1,0:T(8,128)(2,1)}, bf16[128,768]{1,0:T(8,128)(2,1)S(1)}, u32[]{:S(2)}, u32[]{:S(2)}) collective-permute-start(bf16[128,768]{1,0:T(8,128)(2,1)} %get-tuple-element.12), channel_id=1, source_target_pairs={{0,3},{1,0},{2,1},{3,2},{4,7},{5,4},{6,5},{7,6},{8,11},{9,8},{10,9... | collective-permute-start | bytes 589832 | tf_op jit(solution)/shard_map/ppermute | solution.py:338
  24.2 46.1 %all-to-all-start = ((bf16[64,8,1024]{2,1,0:T(8,128)(2,1)}), bf16[64,8,1024]{2,1,0:T(8,128)(2,1)}, u32[]{:S(2)}, u32[]{:S(2)}) async-start(bf16[64,8,1024]{2,1,0:T(8,128)(2,1)} %bitcast.13), calls=%async_computation | async-start | bytes 2097152 | tf_op jit(solution)/shard_map/all_to_all | solution.py:361
  33.9 104.9 %all-gather.2.cloned.1.call-start = ((), (), s32[]{:S(2)}) async-start(), calls=%async_computation.2 | async-start | bytes 2621440 | tf_op jit(solution)/shard_map/all_gather | solution.py:364
  33.9 2.4 %copy-start.5 = (bf16[128,768]{1,0:T(8,128)(2,1)}, bf16[128,768]{1,0:T(8,128)(2,1)S(1)}, u32[]{:S(2)}) copy-start(bf16[128,768]{1,0:T(8,128)(2,1)S(1)} %collective-permute-done.in0) | copy-start | bytes 589828
  33.9 2.3 %copy-start.6 = (bf16[128,768]{1,0:T(8,128)(2,1)}, bf16[128,768]{1,0:T(8,128)(2,1)S(1)}, u32[]{:S(2)}) copy-start(bf16[128,768]{1,0:T(8,128)(2,1)S(1)} %collective-permute-done.1.in1) | copy-start | bytes 589828
  36.3 0.7 copy-start.7
  38.9 17.7 %collective-permute-start.3 = (bf16[3,128,512]{2,1,0:T(8,128)(2,1)}, bf16[3,128,512]{2,1,0:T(8,128)(2,1)S(1)}, u32[]{:S(2)}, u32[]{:S(2)}) collective-permute-start(bf16[3,128,512]{2,1,0:T(8,128)(2,1)} %get-tuple-element.13.in0), channel_id=1, source_target_pairs={{0,8},{4,12},{8,16},{12,20},{16,24},{20,28},{24,0},{28,4},{32,40},... | collective-permute-start | bytes 1179656 | tf_op jit(solution)/shard_map/ppermute | solution.py:342
  40.2 25.1 %collective-permute-start.4 = (bf16[3,128,512]{2,1,0:T(8,128)(2,1)}, bf16[3,128,512]{2,1,0:T(8,128)(2,1)S(1)}, u32[]{:S(2)}, u32[]{:S(2)}) collective-permute-start(bf16[3,128,512]{2,1,0:T(8,128)(2,1)} %get-tuple-element.13.in0), channel_id=1, source_target_pairs={{0,16},{4,20},{8,24},{12,28},{16,0},{20,4},{24,8},{28,12},{32,48},... | collective-permute-start | bytes 1179656 | tf_op jit(solution)/shard_map/ppermute | solution.py:342
  42.7 22.5 %collective-permute-start.5 = (bf16[3,128,512]{2,1,0:T(8,128)(2,1)}, bf16[3,128,512]{2,1,0:T(8,128)(2,1)S(1)}, u32[]{:S(2)}, u32[]{:S(2)}) collective-permute-start(bf16[3,128,512]{2,1,0:T(8,128)(2,1)} %get-tuple-element.13.in0), channel_id=1, source_target_pairs={{0,24},{4,28},{8,0},{12,4},{16,8},{20,12},{24,16},{28,20},{32,56},... | collective-permute-start | bytes 1179656 | tf_op jit(solution)/shard_map/ppermute | solution.py:342
  56.7 8.6 %copy-start.2 = (bf16[3,128,512]{2,1,0:T(8,128)(2,1)}, bf16[3,128,512]{2,1,0:T(8,128)(2,1)S(1)}, u32[]{:S(2)}) copy-start(bf16[3,128,512]{2,1,0:T(8,128)(2,1)S(1)} %collective-permute-done.3.in1) | copy-start | bytes 1179652
  65.3 0.8 copy-start.3
  66.0 0.7 copy-start.4
  69.4 4.1 %collective-permute-start.6 = (bf16[4,3,128,512]{3,2,1,0:T(8,128)(2,1)}, bf16[4,3,128,512]{3,2,1,0:T(8,128)(2,1)S(1)}, u32[]{:S(2)}, u32[]{:S(2)}) collective-permute-start(bf16[4,3,128,512]{3,2,1,0:T(8,128)(2,1)} %stack.17.near), channel_id=1, source_target_pairs={{0,4},{4,0},{8,12},{12,8},{16,20},{20,16},{24,28},{28,24},{32,36},... | collective-permute-start | bytes 4718600 | tf_op jit(solution)/shard_map/ppermute | solution.py:348
  73.5 1.2 copy-start.1
  84.3 59.4 %all-to-all-start.1 = ((bf16[256,8,256]{2,1,0:T(8,128)(2,1)}), bf16[256,8,256]{2,1,0:T(8,128)(2,1)S(1)}, u32[]{:S(2)}, u32[]{:S(2)}) async-start(bf16[256,8,256]{2,1,0:T(8,128)(2,1)} %bitcast.15), calls=%async_computation.1 | async-start | bytes 2097152 | tf_op jit(solution)/shard_map/all_to_all | solution.py:370
  143.6 1.0 copy-start
Sparse Core Ops, SparseCore 0:
  70.4 68.2 all-gather.1

commit v3 on v2

--- a/solution.py
+++ b/solution.py
@@ -90,20 +90,20 @@
     return jax.ShapeDtypeStruct(shape, BF)
 
 
-def cut_kernel(meta, query_ref, key_ref, value_ref, col_ref, row_ref, *outs):
+def cut_kernel(meta, query_ref, key_ref, value_ref, col_ref, row_ref, out_ref, *rows):
     g = meta[0]
-    for k, out_ref in zip(ORDER, outs):
-        out_ref[:, :HALF] = query_ref[...]
-        out_ref[:, HALF : 2 * HALF] = key_ref[...]
-        out_ref[:, 2 * HALF : 3 * HALF] = value_ref[...]
-        out_ref[:, 3 * HALF : 4 * HALF] = col_ref[...]
+    out_ref[:, :HALF] = query_ref[...]
+    out_ref[:, HALF : 2 * HALF] = key_ref[...]
+    out_ref[:, 2 * HALF : 3 * HALF] = value_ref[...]
+    out_ref[:, 3 * HALF :] = col_ref[...]
+    for k, ref in zip(ORDER, rows):
         at = pl.multiple_of(lax.rem(g + k, GROUPS) * 256, 256)
-        out_ref[:, 4 * HALF :] = row_ref[:, pl.ds(at, 256)]
+        ref[...] = row_ref[:, pl.ds(at, 256)]
 
 
 def cut(meta, w_qkv, w_out):
-    def part(n):
-        return pl.BlockSpec((BLOCK, HALF), lambda b, meta: (meta[1] * 2 + meta[2], 2 * n + 1))
+    def part(n, axis):
+        return pl.BlockSpec((BLOCK, HALF), lambda b, meta: (meta[axis] * 2 + meta[2], 2 * n + 1))
 
     return call(
         cut_kernel,
@@ -112,22 +112,23 @@
             num_scalar_prefetch=1,
             grid=(1,),
             in_specs=[
-                part(0),
-                part(1),
-                part(2),
-                pl.BlockSpec((BLOCK, HALF), lambda b, meta: (1, meta[1] * 2 + meta[2])),
+                part(0, 1),
+                part(1, 1),
+                part(2, 3),
+                pl.BlockSpec((BLOCK, HALF), lambda b, meta: (1, meta[3] * 2 + meta[2])),
                 pl.BlockSpec((BLOCK, D), lambda b, meta: (0, 0)),
             ],
-            out_specs=[pl.BlockSpec((BLOCK, 6 * HALF), lambda b, meta: (0, 0))] * 3,
+            out_specs=[pl.BlockSpec((BLOCK, 4 * HALF), lambda b, meta: (0, 0))]
+            + [pl.BlockSpec((BLOCK, 256), lambda b, meta: (0, 0))] * 3,
         ),
-        out_shape=[like(BLOCK, 6 * HALF)] * 3,
+        out_shape=[like(BLOCK, 4 * HALF)] + [like(BLOCK, 256)] * 3,
     )(meta, w_qkv, w_qkv, w_qkv, w_out, w_out)
 
 
-def mid_kernel(in0, in1, in2, out_ref, row_ref):
+def mid_kernel(in0, in1, in2, x_ref, y_ref):
     for n, ref in enumerate((in0, in1, in2)):
-        out_ref[n] = ref[:, : 4 * HALF]
-        row_ref[n] = ref[:, 4 * HALF :]
+        x_ref[n] = ref[:, :256]
+        y_ref[n] = ref[:, 256:]
 
 
 def mid(parts):
@@ -137,13 +138,14 @@
         flops=10**12,
         in_specs=[whole()] * 3,
         out_specs=[whole()] * 2,
-        out_shape=[like(3, BLOCK, 4 * HALF), like(3, BLOCK, 256)],
+        out_shape=[like(3, BLOCK, 256)] * 2,
     )(*parts)
 
 
-def stack_kernel(in0, in1, in2, in3, after, out_ref):
-    for n, ref in enumerate((in0, in1, in2, in3)):
-        out_ref[n] = ref[...]
+def stack_kernel(*refs):
+    out_ref = refs[-1]
+    for n in range(8):
+        out_ref[n // 4, n % 4] = refs[n][...]
 
 
 def stack(parts, after):
@@ -151,10 +153,10 @@
         stack_kernel,
         "stack",
         flops=10**9,
-        in_specs=[whole()] * 4 + [anywhere()],
+        in_specs=[whole()] * 8 + [anywhere()] * len(after),
         out_specs=whole(),
-        out_shape=like(4, 3, BLOCK, 4 * HALF),
-    )(*parts, after)
+        out_shape=like(2, 4, 3, BLOCK, 256),
+    )(*parts, *after)
 
 
 def prep_kernel(meta, sig_ref, out_ref):
@@ -206,56 +208,74 @@
     )(sig, w_qkv, w_qkv, w_qkv)
 
 
-def column_kernel(
-    meta, got_ref, w_ref, w_out_ref, near, far, out_ref, held, weights, mixers, outs, sems
-):
-    x = meta[1]
-    core = meta[2]
-    copies = []
-    for d in range(4):
-        from_x = lax.rem(x + 4 - d, 4) * 2
-        for n, (ref, at) in enumerate(((near, from_x + core), (far, from_x + 1 - core))):
-            rows = pl.ds(pl.multiple_of(at * BLOCK, BLOCK), BLOCK)
-            sem = 4 * d + 2 * n
-            copies.append(
-                pltpu.make_async_copy(
-                    ref.at[d, :, :, : 3 * HALF], weights.at[:, rows, :], sems.at[sem]
-                )
-            )
-            copies.append(
-                pltpu.make_async_copy(
-                    ref.at[d, :, :, 3 * HALF :], mixers.at[:, at], sems.at[sem + 1]
-                )
-            )
-    for copy in copies:
-        copy.start()
+def columns_of(held, weight, allowed, keep):
+    qkv = jnp.dot(held[...], weight, preferred_element_type=F32)
+    for c in range(2):
+
+        def store(lo, out):
+            keep(c * 256 + lo, out)
+
+        attend(qkv[c * 256 : (c + 1) * 256], allowed, store)
+
+
+def own_kernel(got_ref, w_ref, held, out_ref):
     pick = one_hot(lambda o: (o % 64) * 2 + o // 64)
     for b in range(4):
         moved = move(pick, got_ref[b * BLOCK : (b + 1) * BLOCK, :])
         held[b * 64 : b * 64 + 64, :] = moved[:64]
         held[256 + b * 64 : 256 + b * 64 + 64, :] = moved[64:]
+
+    def keep(lo, out):
+        out_ref[lo : lo + BLOCK, :] = out
+
+    weight = jnp.concatenate(
+        [w_ref[:, HALF:256], w_ref[:, 256 + HALF : 512], w_ref[:, 512 + HALF :]], axis=1
+    )
+    columns_of(held, weight, causal(), keep)
+
+
+def own_part(got, w_qkv):
+    return call(
+        own_kernel,
+        "own_part",
+        flops=10**12,
+        moved=4 * MIB,
+        in_specs=[whole(), whole()],
+        out_specs=[whole(), whole()],
+        out_shape=[like(C, D), like(C, HALF)],
+    )(got, w_qkv)
+
+
+def column_kernel(
+    meta, held, own, w_out_ref, near, far, out_ref, weights, values, mixers, outs, sems
+):
+    core = meta[2]
+    copies = []
+
+    def fetch(source, target):
+        copies.append(pltpu.make_async_copy(source, target, sems.at[len(copies)]))
+
+    for n, d in enumerate((0, 2, 1, 3)):
+        for ref, on in ((near, core), (far, 1 - core)):
+            at = lax.rem(meta[1] + 4 - d, 4) * 2 + on
+            rows = pl.ds(pl.multiple_of(at * BLOCK, BLOCK), BLOCK)
+            fetch(ref.at[0, n], weights.at[:, rows, :])
+            at = lax.rem(meta[3] + 4 - d, 4) * 2 + on
+            rows = pl.ds(pl.multiple_of(at * BLOCK, BLOCK), BLOCK)
+            fetch(ref.at[1, n, :, :, :HALF], values.at[:, rows, :])
+            fetch(ref.at[1, n, :, :, HALF:], mixers.at[:, at])
+    for copy in copies:
+        copy.start()
     allowed = causal()
-
-    def group(k, weight):
-        qkv = jnp.dot(held[...], weight, preferred_element_type=F32)
-        for c in range(2):
-
-            def store(lo, out):
-                at = c * 256 + lo
-                outs[at : at + BLOCK, k * HALF : (k + 1) * HALF] = out
-
-            attend(qkv[c * 256 : (c + 1) * 256], allowed, store)
-
-    group(
-        0,
-        jnp.concatenate(
-            [w_ref[:, HALF:256], w_ref[:, 256 + HALF : 512], w_ref[:, 512 + HALF :]], axis=1
-        ),
-    )
+    outs[:, :HALF] = own[...]
     for copy in copies:
         copy.wait()
     for n in range(3):
-        group(n + 1, weights[n])
+
+        def keep(lo, out):
+            outs[lo : lo + BLOCK, (n + 1) * HALF : (n + 2) * HALF] = out
+
+        columns_of(held, jnp.concatenate([weights[n], values[n]], axis=1), allowed, keep)
     mixer = jnp.concatenate(
         [w_out_ref[HALF:, :]]
         + [jnp.concatenate([mixers[n, s] for s in range(8)], axis=1) for n in range(3)],
@@ -271,28 +291,28 @@
             out_ref[b * 16 : (b + 1) * 16, j] = mixed[:, j * 256 : (j + 1) * 256].reshape(16, 8, 256)
 
 
-def column_part(meta, got, w_qkv, w_out, near, far):
+def column_part(meta, held, own, w_out, near, far):
     return call(
         column_kernel,
         "column_part",
-        flops=4 * 10**9,
+        flops=3 * 10**9,
         moved=6 * MIB,
         in_specs=[smem(), whole(), whole(), whole(), anywhere(), anywhere()],
         out_specs=whole(),
         out_shape=like(64, GROUPS, 8, 256),
         scratch_shapes=[
-            VMEM((C, D), BF),
-            VMEM((3, D, 3 * HALF), BF),
+            VMEM((3, D, 256), BF),
+            VMEM((3, D, HALF), BF),
             VMEM((3, 8, BLOCK, HALF), BF),
             VMEM((C, C), BF),
-            pltpu.SemaphoreType.DMA((16,)),
+            pltpu.SemaphoreType.DMA((24,)),
         ],
-    )(meta, got, w_qkv, w_out, near, far)
-
-
-def join_kernel(meta, got_ref, rows_ref, own_ref, w_ref, out_ref):
+    )(meta, held, own, w_out, near, far)
+
+
+def join_kernel(meta, got_ref, rows_ref, w0, w1, w2, w3, out_ref):
     g = meta[0]
-    weight = jnp.concatenate([own_ref[...]] + [w_ref[n] for n in range(3)], axis=0)
+    weight = jnp.concatenate([w0[...], w1[...], w2[...], w3[...]], axis=0)
     pick = one_hot(lambda o: ((o // 2) % 16) * 8 + (o // 32) * 2 + o % 2)
     columns = [
         jnp.dot(
@@ -326,12 +346,12 @@
                     (GROUPS, ROWS_LOCAL, 1, BLOCK, HALF), lambda j, meta: (0, 0, j, 0, 0)
                 ),
                 pl.BlockSpec((BLOCK, 256), lambda j, meta: (0, meta[0])),
-                pl.BlockSpec((3, BLOCK, 256), lambda j, meta: (0, 0, 0)),
-            ],
+            ]
+            + [pl.BlockSpec((BLOCK, 256), lambda j, meta: (0, 0))] * 3,
             out_specs=pl.BlockSpec((ROWS_LOCAL, 1, BLOCK, 256), lambda j, meta: (0, j, 0, 0)),
         ),
         out_shape=like(ROWS_LOCAL, GROUPS, BLOCK, 256),
-    )(meta, got, rows, w_out, w_rows)
+    )(meta, got, rows, w_out, *w_rows)
 
 
 def to_group(data, k):
@@ -344,6 +364,12 @@
     )
 
 
+def along_y(data, d):
+    return lax.ppermute(
+        data, "rows", [(i, i // 32 * 32 + (i // 8 % 4 + d) % 4 * 8 + i % 8) for i in range(64)]
+    )
+
+
 def other_core(data):
     return lax.ppermute(data, "rows", [(i, i ^ 1) for i in range(64)])
 
@@ -351,11 +377,12 @@
 def local(signal, w_qkv, w_out):
     i = lax.axis_index("rows")
     g = lax.axis_index("heads")
-    meta = jnp.stack([g, i // 2 % 4, i % 2]).astype(jnp.int32)
+    meta = jnp.stack([g, i // 2 % 4, i % 2, i // 8 % 4]).astype(jnp.int32)
     sig = signal.reshape(ROWS_LOCAL, C, D)
 
-    cuts = cut(meta, w_qkv, w_out)
-    others, w_rows = mid([to_group(part, k) for part, k in zip(cuts, ORDER)])
+    mine, *w_rows = cut(meta, w_qkv, w_out)
+    others_x, others_y = mid([to_group(mine, k) for k in ORDER])
+    w_rows = [to_group(part, k) for part, k in zip(w_rows, ORDER)]
 
     send = prep(meta, sig).reshape(64, 8, D)
     got = lax.all_to_all(send, "rows", split_axis=0, concat_axis=0, tiled=True).reshape(C, D)
@@ -363,10 +390,17 @@
     own_rows = row_part(sig, w_qkv)
     rows = lax.all_gather(own_rows.reshape(ROWS_LOCAL * C, HALF), "heads", axis=0)
 
-    near = stack([others] + [along_x(others, d) for d in (1, 2, 3)], own_rows)
+    near = stack(
+        [others_x]
+        + [along_x(others_x, d) for d in (2, 1, 3)]
+        + [others_y]
+        + [along_y(others_y, d) for d in (2, 1, 3)],
+        [own_rows],
+    )
     far = other_core(near)
 
-    columns = column_part(meta, got, w_qkv, w_out, near, far).reshape(64 * GROUPS, 8, 256)
+    held, own = own_part(got, w_qkv)
+    columns = column_part(meta, held, own, w_out, near, far).reshape(64 * GROUPS, 8, 256)
     back = lax.all_to_all(columns, ("rows", "heads"), split_axis=0, concat_axis=0, tiled=True)
     return join(
         meta,

time: 157 us -> 150 us (0.955)
  waiting for transfers between devices: 70.9 us -> 46.2 us
  starting transfers between devices: 34.1 us -> 49 us
  Pallas kernels: 33.2 us -> 36.6 us
    all_gather x1, waiting for transfers between devices: 47.1 us -> 0.02 us  [local(): lax.all_gather(own_rows.reshape(ROWS_LOCAL * C, HALF), 'heads', axis=0)]
    ppermute x3 -> x6, waiting for transfers between devices: 2.33 us -> 39.2 us  [to_group(): lax.ppermute(data, 'heads', [(j, (j + k) % GROUPS) for j in range(GROUPS)])]
    ppermute x3 -> x6, starting transfers between devices: 11.3 us -> 21.3 us  [to_group(): lax.ppermute(data, 'heads', [(j, (j + k) % GROUPS) for j in range(GROUPS)])]
    ppermute x3, waiting for transfers between devices: 13.3 us -> 6.9 us  [along_x(): lax.ppermute(data, 'rows', [(i, i // 8 * 8 + (i // 2 % 4 + d) % 4 * 2 + i...]
    ppermute x0 -> x3, starting transfers between devices: none -> 5.51 us  [along_y(): lax.ppermute(data, 'rows', [(i, i // 32 * 32 + (i // 8 % 4 + d) % 4 * 8 +...]
    all_to_all x1, waiting for transfers between devices: 4.91 us -> 0.01 us  [local(): lax.all_to_all(columns, ('rows', 'heads'), split_axis=0, concat_axis=0, t...]
    pallas_call x2 -> x3, Pallas kernels: 12.2 us -> 15.9 us  [the longest x1 9.17 us: column_part(): call(column_kernel, 'column_part', flops=3 * 10 ** 9, moved=6 * MIB, in_s...]
    ppermute x1, waiting for transfers between devices: 3.21 us -> 0.01 us  [other_core(): return lax.ppermute(data, 'rows', [(i, i ^ 1) for i in range(64)])]
  transfers between devices with their start and end apart: 10 -> 16, of which waited for: 6 -> 2; matrix products, arithmetic and copies ran while one was open for 0% -> 0% of each run, Pallas kernels for 16% -> 19%
where the time goes in v3:
time: 150 us
  starting transfers between devices  49 us (33%)
  waiting for transfers between devices  46.2 us (31%)
  Pallas kernels  36.6 us (24%)
  between operations  13.6 us (9%)
  local copies, waits for them, and re-layouts  3.86 us (3%)
    ppermute x6, waiting for transfers between devices, to_group(): lax.ppermute(data, 'heads', [(j, (j + k) % GROUPS) for j in range(GROUPS)])  39.2 us
    ppermute x6, starting transfers between devices, to_group(): lax.ppermute(data, 'heads', [(j, (j + k) % GROUPS) for j in range(GROUPS)])  21.3 us
    all_to_all x1, starting transfers between devices, local(): lax.all_to_all(send, 'rows', split_axis=0, concat_axis=0, tiled=True)  9.65 us
    pallas_call x1, Pallas kernels, column_part(): call(column_kernel, 'column_part', flops=3 * 10 ** 9, moved=6 * MIB, in_s...  9.17 us
    pallas_call x1, Pallas kernels, row_part(): call(row_kernel, 'row_part', flops=6 * 10 ** 9, moved=6 * MIB, grid=(ROWS...  8.11 us
    ppermute x3, waiting for transfers between devices, along_x(): lax.ppermute(data, 'rows', [(i, i // 8 * 8 + (i // 2 % 4 + d) % 4 * 2 + i...  6.9 us
    ppermute x3, starting transfers between devices, along_x(): lax.ppermute(data, 'rows', [(i, i // 8 * 8 + (i // 2 % 4 + d) % 4 * 2 + i...  5.57 us
    ppermute x3, starting transfers between devices, along_y(): lax.ppermute(data, 'rows', [(i, i // 32 * 32 + (i // 8 % 4 + d) % 4 * 8 +...  5.51 us
  transfers between devices with their start and end apart: 16, of which 2 were waited for; matrix products, arithmetic and copies ran while one was open for 0% of the time, Pallas kernels for 19%

profile of v3, /device:TPU:1, one launch (start us, length us, event | category | flops | bytes accessed | tf_op | source)
XLA Modules:
  0.0 149.9 jit_solution(15128488701194028029)
XLA Ops:
  6.5 0.7 pad_add_fusion.meta
  7.2 2.5 %cut.1 = (bf16[128,512]{1,0:T(8,128)(2,1)}, bf16[128,256]{1,0:T(8,128)(2,1)}, bf16[128,256]{1,0:T(8,128)(2,1)}, bf16[128,256]{1,0:T(8,128)(2,1)}) custom-call(s32[4]{0:T(128)} %pad_add_fusion.meta, bf16[1024,768]{1,0:T(8,128)(2,1)} %value_ref.3, bf16[1024,768]{1,0:T(8,128)(2,1)} %value_ref.3, bf16[1024,768]{1,0:T(8,128)(2,1)} %value_ref.3, ...), custom_call_target="tpu_custom_call" | custom-call | bytes 1048576 | tf_op jit(solution)/shard_map/cut/pallas_call | solution.py:108
  9.7 7.7 %collective-permute-start = (bf16[128,512]{1,0:T(8,128)(2,1)}, bf16[128,512]{1,0:T(8,128)(2,1)S(1)}, u32[]{:S(2)}, u32[]{:S(2)}) collective-permute-start(bf16[128,512]{1,0:T(8,128)(2,1)} %get-tuple-element.15), channel_id=1, source_target_pairs={{0,2},{1,3},{2,0},{3,1},{4,6},{5,7},{6,4},{7,5},{8,10},{9,11},{10,... | collective-permute-start | bytes 393224 | tf_op jit(solution)/shard_map/ppermute | solution.py:358
  17.4 1.2 collective-permute-start.1
  18.6 2.4 %collective-permute-start.2 = (bf16[128,512]{1,0:T(8,128)(2,1)}, bf16[128,512]{1,0:T(8,128)(2,1)S(1)}, u32[]{:S(2)}, u32[]{:S(2)}) collective-permute-start(bf16[128,512]{1,0:T(8,128)(2,1)} %get-tuple-element.15), channel_id=1, source_target_pairs={{0,3},{1,0},{2,1},{3,2},{4,7},{5,4},{6,5},{7,6},{8,11},{9,8},{10,9... | collective-permute-start | bytes 393224 | tf_op jit(solution)/shard_map/ppermute | solution.py:358
  21.0 3.1 %prep.1 = bf16[512,1024]{1,0:T(8,128)(2,1)} custom-call(s32[4]{0:T(128)} %pad_add_fusion.meta, bf16[4,512,1024]{2,1,0:T(8,128)(2,1)} %bitcast.12), custom_call_target="tpu_custom_call" | custom-call | flops 134217728 | bytes 2097152 | tf_op jit(solution)/shard_map/prep/pallas_call | solution.py:170
  24.1 9.6 %all-to-all-start = ((bf16[64,8,1024]{2,1,0:T(8,128)(2,1)}), bf16[64,8,1024]{2,1,0:T(8,128)(2,1)}, u32[]{:S(2)}, u32[]{:S(2)}) async-start(bf16[64,8,1024]{2,1,0:T(8,128)(2,1)} %bitcast.14), calls=%async_computation | async-start | bytes 2097152 | tf_op jit(solution)/shard_map/all_to_all | solution.py:388
  33.7 0.0 all-gather.2.cloned.1.call-start
  33.8 0.0 collective-permute-done.1.in1
  33.8 0.0 collective-permute-done.2.in2
  33.8 0.6 copy-done.7
  34.5 0.1 copy-done.8
  34.5 0.7 copy-done.9
  35.2 1.8 %mid.1 = (bf16[3,128,256]{2,1,0:T(8,128)(2,1)}, bf16[3,128,256]{2,1,0:T(8,128)(2,1)}) custom-call(bf16[128,512]{1,0:T(8,128)(2,1)} %copy-done.7, bf16[128,512]{1,0:T(8,128)(2,1)} %copy-done.8, bf16[128,512]{1,0:T(8,128)(2,1)} %copy-done.9), custom_call_target="tpu_custom_call" | custom-call | flops 999999995904 | bytes 1048576 | tf_op jit(solution)/shard_map/mid/pallas_call | solution.py:135
  37.0 2.9 %collective-permute-start.3 = (bf16[3,128,256]{2,1,0:T(8,128)(2,1)}, bf16[3,128,256]{2,1,0:T(8,128)(2,1)S(1)}, u32[]{:S(2)}, u32[]{:S(2)}) collective-permute-start(bf16[3,128,256]{2,1,0:T(8,128)(2,1)} %get-tuple-element.16.refs_0_), channel_id=1, source_target_pairs={{0,16},{4,20},{8,24},{12,28},{16,0},{20,4},{24,8},{28,12},{32,48},... | collective-permute-start | bytes 589832 | tf_op jit(solution)/shard_map/ppermute | solution.py:362
  39.9 0.3 collective-permute-start.4
  40.2 2.4 %collective-permute-start.5 = (bf16[3,128,256]{2,1,0:T(8,128)(2,1)}, bf16[3,128,256]{2,1,0:T(8,128)(2,1)S(1)}, u32[]{:S(2)}, u32[]{:S(2)}) collective-permute-start(bf16[3,128,256]{2,1,0:T(8,128)(2,1)} %get-tuple-element.16.refs_0_), channel_id=1, source_target_pairs={{0,24},{4,28},{8,0},{12,4},{16,8},{20,12},{24,16},{28,20},{32,56},... | collective-permute-start | bytes 589832 | tf_op jit(solution)/shard_map/ppermute | solution.py:362
  42.6 2.7 %collective-permute-start.6 = (bf16[3,128,256]{2,1,0:T(8,128)(2,1)}, bf16[3,128,256]{2,1,0:T(8,128)(2,1)S(1)}, u32[]{:S(2)}, u32[]{:S(2)}) collective-permute-start(bf16[3,128,256]{2,1,0:T(8,128)(2,1)} %get-tuple-element.17.refs_4_), channel_id=1, source_target_pairs={{0,64},{4,68},{8,72},{12,76},{16,80},{20,84},{24,88},{28,92},{32,9... | collective-permute-start | bytes 589832 | tf_op jit(solution)/shard_map/ppermute | solution.py:368
  45.3 0.3 collective-permute-start.7
  45.6 6.9 %collective-permute-done.3.refs_1_ = bf16[3,128,256]{2,1,0:T(8,128)(2,1)S(1)} collective-permute-done((bf16[3,128,256]{2,1,0:T(8,128)(2,1)}, bf16[3,128,256]{2,1,0:T(8,128)(2,1)S(1)}, u32[]{:S(2)}, u32[]{:S(2)}) %collective-permute-start.3) | collective-permute-done | bytes 196640 | tf_op jit(solution)/shard_map/ppermute | solution.py:362
  52.5 2.5 %collective-permute-start.8 = (bf16[3,128,256]{2,1,0:T(8,128)(2,1)}, bf16[3,128,256]{2,1,0:T(8,128)(2,1)S(1)}, u32[]{:S(2)}, u32[]{:S(2)}) collective-permute-start(bf16[3,128,256]{2,1,0:T(8,128)(2,1)} %get-tuple-element.17.refs_4_), channel_id=1, source_target_pairs={{0,96},{4,100},{8,104},{12,108},{16,112},{20,116},{24,120},{28,124... | collective-permute-start | bytes 589832 | tf_op jit(solution)/shard_map/ppermute | solution.py:368
  55.0 8.1 %row_part.1.refs_8_ = bf16[4,512,128]{2,1,0:T(8,128)(2,1)} custom-call(bf16[4,512,1024]{2,1,0:T(8,128)(2,1)} %bitcast.13, bf16[1024,768]{1,0:T(8,128)(2,1)} %value_ref.3, bf16[1024,768]{1,0:T(8,128)(2,1)} %value_ref.3, bf16[1024,768]{1,0:T(8,128)(2,1)} %value_ref.3), custom_call_target="tpu_custom_call" | custom-call | flops 6000000000 | bytes 6291456 | tf_op jit(solution)/shard_map/row_part/pallas_call | solution.py:199
  63.1 0.0 all-gather.2.cloned.1.call-update
  63.1 0.0 collective-permute-done.4.refs_2_
  63.1 0.0 collective-permute-done.5.refs_3_
  63.2 0.0 collective-permute-done.8.refs_7_
  63.2 0.6 copy-done.2
  63.8 0.1 copy-done.3
  63.9 0.1 copy-done.4
  63.9 0.1 copy-done.5
  64.0 0.7 copy-done.6
  64.7 2.7 %stack.21.near = bf16[2,4,3,128,256]{4,3,2,1,0:T(8,128)(2,1)} custom-call(bf16[3,128,256]{2,1,0:T(8,128)(2,1)} %get-tuple-element.16.refs_0_, bf16[3,128,256]{2,1,0:T(8,128)(2,1)} %copy-done.1, bf16[3,128,256]{2,1,0:T(8,128)(2,1)} %copy-done.2, bf16[3,128,256]{2,1,0:T(8,128)(2,1)} %copy-done.3, bf16[3,128,256]{2,1,0:T(8,128)(2,1)} %get-tuple-element.17.refs_4_, ...), custom_call_target="tpu_custom_call" | custom-call | flops 1000000000 | bytes 1048576 | tf_op jit(solution)/shard_map/stack/pallas_call | solution.py:152
  67.4 1.6 %collective-permute-start.9 = (bf16[2,4,3,128,256]{4,3,2,1,0:T(8,128)(2,1)}, bf16[2,4,3,128,256]{4,3,2,1,0:T(8,128)(2,1)}, u32[]{:S(2)}, u32[]{:S(2)}) collective-permute-start(bf16[2,4,3,128,256]{4,3,2,1,0:T(8,128)(2,1)} %stack.21.near), channel_id=1, source_target_pairs={{0,4},{4,0},{8,12},{12,8},{16,20},{20,16},{24,28},{28,24},{32,36},... | collective-permute-start | bytes 4718600 | tf_op jit(solution)/shard_map/ppermute | solution.py:374
  69.0 4.0 %own_part.1 = (bf16[512,1024]{1,0:T(8,128)(2,1)}, bf16[512,128]{1,0:T(8,128)(2,1)}) custom-call(bf16[512,1024]{1,0:T(8,128)(2,1)} %bitcast.6.got_ref, bf16[1024,768]{1,0:T(8,128)(2,1)} %value_ref.3), custom_call_target="tpu_custom_call" | custom-call | flops 999999995904 | bytes 4194304 | tf_op jit(solution)/shard_map/own_part/pallas_call | solution.py:238
  73.1 0.0 collective-permute-done.9.far
  73.1 9.2 %column_part.1 = bf16[64,4,8,256]{3,2,1,0:T(8,128)(2,1)} custom-call(s32[4]{0:T(128)} %pad_add_fusion.meta, bf16[512,1024]{1,0:T(8,128)(2,1)} %get-tuple-element.13.held, bf16[512,128]{1,0:T(8,128)(2,1)} %get-tuple-element.14.own, bf16[256,1024]{1,0:T(8,128)(2,1)} %w0.1, bf16[2,4,3,128,256]{4,3,2,1,0:T(8,128)(2,1)} %stack.21.near, ...), custom_call_target="tpu_custom_call" | custom-call | flops 3000000000 | bytes 6291456 | tf_op jit(solution)/shard_map/column_part/pallas_call | solution.py:295
  82.3 5.3 %all-to-all-start.1 = ((bf16[256,8,256]{2,1,0:T(8,128)(2,1)}), bf16[256,8,256]{2,1,0:T(8,128)(2,1)S(1)}, u32[]{:S(2)}, u32[]{:S(2)}) async-start(bf16[256,8,256]{2,1,0:T(8,128)(2,1)} %bitcast.16), calls=%async_computation.1 | async-start | bytes 2097152 | tf_op jit(solution)/shard_map/all_to_all | solution.py:404
  87.6 6.4 %collective-permute-start.10 = (bf16[128,256]{1,0:T(8,128)(2,1)S(1)}, bf16[128,256]{1,0:T(8,128)(2,1)S(1)}, u32[]{:S(2)}, u32[]{:S(2)}) collective-permute-start(bf16[128,256]{1,0:T(8,128)(2,1)S(1)} %copy-done.12), channel_id=1, source_target_pairs={{0,2},{1,3},{2,0},{3,1},{4,6},{5,7},{6,4},{7,5},{8,10},{9,11},{10,... | collective-permute-start | bytes 196616 | tf_op jit(solution)/shard_map/ppermute | solution.py:358
  94.0 0.8 collective-permute-start.11
  94.9 2.8 %collective-permute-start.12 = (bf16[128,256]{1,0:T(8,128)(2,1)S(1)}, bf16[128,256]{1,0:T(8,128)(2,1)S(1)}, u32[]{:S(2)}, u32[]{:S(2)}) collective-permute-start(bf16[128,256]{1,0:T(8,128)(2,1)S(1)} %copy-done.10), channel_id=1, source_target_pairs={{0,3},{1,0},{2,1},{3,2},{4,7},{5,4},{6,5},{7,6},{8,11},{9,8},{10,9... | collective-permute-start | bytes 196616 | tf_op jit(solution)/shard_map/ppermute | solution.py:358
  97.6 39.2 %collective-permute-done.10.w1 = bf16[128,256]{1,0:T(8,128)(2,1)S(1)} collective-permute-done((bf16[128,256]{1,0:T(8,128)(2,1)S(1)}, bf16[128,256]{1,0:T(8,128)(2,1)S(1)}, u32[]{:S(2)}, u32[]{:S(2)}) %collective-permute-start.10) | collective-permute-done | bytes 65568 | tf_op jit(solution)/shard_map/ppermute | solution.py:358
  136.8 0.0 collective-permute-done.11.w2
  136.9 0.0 all-gather.2.cloned.1.call-done
  136.9 0.6 copy-done.13
  137.5 0.0 copy-done.14
  137.5 0.0 copy-done.15
  137.5 0.4 copy-done
  137.9 5.1 %join.1 = bf16[4,4,128,256]{3,2,1,0:T(8,128)(2,1)} custom-call(s32[4]{0:T(128)} %pad_add_fusion.meta, bf16[64,4,8,256]{3,2,1,0:T(8,128)(2,1)} %bitcast.15, bf16[4,4,4,128,128]{4,3,2,1,0:T(8,128)(2,1)} %bitcast.18, bf16[256,1024]{1,0:T(8,128)(2,1)} %w0.1, bf16[128,256]{1,0:T(8,128)(2,1)} %copy-done.13, bf16[128,256]{1,0:T(8,128)(2,1)} %copy-done.14, ...), custom_call_target="tpu_custom_call" | custom-call | flops 2000000000 | bytes 4194304 | tf_op jit(solution)/shard_map/join/pallas_call | solution.py:335
  (26 shorter events, 0.1 us)
Async XLA Ops:
  9.7 24.1 %collective-permute-start = (bf16[128,512]{1,0:T(8,128)(2,1)}, bf16[128,512]{1,0:T(8,128)(2,1)S(1)}, u32[]{:S(2)}, u32[]{:S(2)}) collective-permute-start(bf16[128,512]{1,0:T(8,128)(2,1)} %get-tuple-element.15), channel_id=1, source_target_pairs={{0,2},{1,3},{2,0},{3,1},{4,6},{5,7},{6,4},{7,5},{8,10},{9,11},{10,... | collective-permute-start | bytes 393224 | tf_op jit(solution)/shard_map/ppermute | solution.py:358
  17.4 16.4 %collective-permute-start.1 = (bf16[128,512]{1,0:T(8,128)(2,1)}, bf16[128,512]{1,0:T(8,128)(2,1)S(1)}, u32[]{:S(2)}, u32[]{:S(2)}) collective-permute-start(bf16[128,512]{1,0:T(8,128)(2,1)} %get-tuple-element.15), channel_id=1, source_target_pairs={{0,1},{1,2},{2,3},{3,0},{4,5},{5,6},{6,7},{7,4},{8,9},{9,10},{10,1... | collective-permute-start | bytes 393224 | tf_op jit(solution)/shard_map/ppermute | solution.py:358
  18.6 15.2 %collective-permute-start.2 = (bf16[128,512]{1,0:T(8,128)(2,1)}, bf16[128,512]{1,0:T(8,128)(2,1)S(1)}, u32[]{:S(2)}, u32[]{:S(2)}) collective-permute-start(bf16[128,512]{1,0:T(8,128)(2,1)} %get-tuple-element.15), channel_id=1, source_target_pairs={{0,3},{1,0},{2,1},{3,2},{4,7},{5,4},{6,5},{7,6},{8,11},{9,8},{10,9... | collective-permute-start | bytes 393224 | tf_op jit(solution)/shard_map/ppermute | solution.py:358
  24.1 45.0 %all-to-all-start = ((bf16[64,8,1024]{2,1,0:T(8,128)(2,1)}), bf16[64,8,1024]{2,1,0:T(8,128)(2,1)}, u32[]{:S(2)}, u32[]{:S(2)}) async-start(bf16[64,8,1024]{2,1,0:T(8,128)(2,1)} %bitcast.14), calls=%async_computation | async-start | bytes 2097152 | tf_op jit(solution)/shard_map/all_to_all | solution.py:388
  33.7 103.2 %all-gather.2.cloned.1.call-start = ((), (), s32[]{:S(2)}) async-start(), calls=%async_computation.2 | async-start | bytes 2621440 | tf_op jit(solution)/shard_map/all_gather | solution.py:391
  33.8 0.7 copy-start.7
  33.8 0.7 copy-start.8
  34.5 0.7 copy-start.9
  37.0 15.5 %collective-permute-start.3 = (bf16[3,128,256]{2,1,0:T(8,128)(2,1)}, bf16[3,128,256]{2,1,0:T(8,128)(2,1)S(1)}, u32[]{:S(2)}, u32[]{:S(2)}) collective-permute-start(bf16[3,128,256]{2,1,0:T(8,128)(2,1)} %get-tuple-element.16.refs_0_), channel_id=1, source_target_pairs={{0,16},{4,20},{8,24},{12,28},{16,0},{20,4},{24,8},{28,12},{32,48},... | collective-permute-start | bytes 589832 | tf_op jit(solution)/shard_map/ppermute | solution.py:362
  39.9 23.2 %collective-permute-start.4 = (bf16[3,128,256]{2,1,0:T(8,128)(2,1)}, bf16[3,128,256]{2,1,0:T(8,128)(2,1)S(1)}, u32[]{:S(2)}, u32[]{:S(2)}) collective-permute-start(bf16[3,128,256]{2,1,0:T(8,128)(2,1)} %get-tuple-element.16.refs_0_), channel_id=1, source_target_pairs={{0,8},{4,12},{8,16},{12,20},{16,24},{20,28},{24,0},{28,4},{32,40},... | collective-permute-start | bytes 589832 | tf_op jit(solution)/shard_map/ppermute | solution.py:362
  40.2 23.0 %collective-permute-start.5 = (bf16[3,128,256]{2,1,0:T(8,128)(2,1)}, bf16[3,128,256]{2,1,0:T(8,128)(2,1)S(1)}, u32[]{:S(2)}, u32[]{:S(2)}) collective-permute-start(bf16[3,128,256]{2,1,0:T(8,128)(2,1)} %get-tuple-element.16.refs_0_), channel_id=1, source_target_pairs={{0,24},{4,28},{8,0},{12,4},{16,8},{20,12},{24,16},{28,20},{32,56},... | collective-permute-start | bytes 589832 | tf_op jit(solution)/shard_map/ppermute | solution.py:362
  42.6 20.6 %collective-permute-start.6 = (bf16[3,128,256]{2,1,0:T(8,128)(2,1)}, bf16[3,128,256]{2,1,0:T(8,128)(2,1)S(1)}, u32[]{:S(2)}, u32[]{:S(2)}) collective-permute-start(bf16[3,128,256]{2,1,0:T(8,128)(2,1)} %get-tuple-element.17.refs_4_), channel_id=1, source_target_pairs={{0,64},{4,68},{8,72},{12,76},{16,80},{20,84},{24,88},{28,92},{32,9... | collective-permute-start | bytes 589832 | tf_op jit(solution)/shard_map/ppermute | solution.py:368
  45.3 17.9 %collective-permute-start.7 = (bf16[3,128,256]{2,1,0:T(8,128)(2,1)}, bf16[3,128,256]{2,1,0:T(8,128)(2,1)S(1)}, u32[]{:S(2)}, u32[]{:S(2)}) collective-permute-start(bf16[3,128,256]{2,1,0:T(8,128)(2,1)} %get-tuple-element.17.refs_4_), channel_id=1, source_target_pairs={{0,32},{4,36},{8,40},{12,44},{16,48},{20,52},{24,56},{28,60},{32,6... | collective-permute-start | bytes 589832 | tf_op jit(solution)/shard_map/ppermute | solution.py:368
  52.5 10.6 %copy-start.1 = (bf16[3,128,256]{2,1,0:T(8,128)(2,1)}, bf16[3,128,256]{2,1,0:T(8,128)(2,1)S(1)}, u32[]{:S(2)}) copy-start(bf16[3,128,256]{2,1,0:T(8,128)(2,1)S(1)} %collective-permute-done.3.refs_1_) | copy-start | bytes 589828
  52.5 10.7 %collective-permute-start.8 = (bf16[3,128,256]{2,1,0:T(8,128)(2,1)}, bf16[3,128,256]{2,1,0:T(8,128)(2,1)S(1)}, u32[]{:S(2)}, u32[]{:S(2)}) collective-permute-start(bf16[3,128,256]{2,1,0:T(8,128)(2,1)} %get-tuple-element.17.refs_4_), channel_id=1, source_target_pairs={{0,96},{4,100},{8,104},{12,108},{16,112},{20,116},{24,120},{28,124... | collective-permute-start | bytes 589832 | tf_op jit(solution)/shard_map/ppermute | solution.py:368
  63.1 0.7 copy-start.2
  63.1 0.8 copy-start.3
  63.1 0.8 copy-start.4
  63.2 0.8 copy-start.5
  64.0 0.7 copy-start.6
  67.4 5.7 %collective-permute-start.9 = (bf16[2,4,3,128,256]{4,3,2,1,0:T(8,128)(2,1)}, bf16[2,4,3,128,256]{4,3,2,1,0:T(8,128)(2,1)}, u32[]{:S(2)}, u32[]{:S(2)}) collective-permute-start(bf16[2,4,3,128,256]{4,3,2,1,0:T(8,128)(2,1)} %stack.21.near), channel_id=1, source_target_pairs={{0,4},{4,0},{8,12},{12,8},{16,20},{20,16},{24,28},{28,24},{32,36},... | collective-permute-start | bytes 4718600 | tf_op jit(solution)/shard_map/ppermute | solution.py:374
  82.3 5.3 %copy-start.12 = (bf16[128,256]{1,0:T(8,128)(2,1)S(1)}, bf16[128,256]{1,0:T(8,128)(2,1)}, u32[]{:S(2)}) copy-start(bf16[128,256]{1,0:T(8,128)(2,1)} %get-tuple-element.18) | copy-start | bytes 196612
  82.3 11.8 %copy-start.11 = (bf16[128,256]{1,0:T(8,128)(2,1)S(1)}, bf16[128,256]{1,0:T(8,128)(2,1)}, u32[]{:S(2)}) copy-start(bf16[128,256]{1,0:T(8,128)(2,1)} %get-tuple-element.19) | copy-start | bytes 196612
  82.3 12.6 %copy-start.10 = (bf16[128,256]{1,0:T(8,128)(2,1)S(1)}, bf16[128,256]{1,0:T(8,128)(2,1)}, u32[]{:S(2)}) copy-start(bf16[128,256]{1,0:T(8,128)(2,1)} %get-tuple-element.20) | copy-start | bytes 196612
  82.3 54.6 %all-to-all-start.1 = ((bf16[256,8,256]{2,1,0:T(8,128)(2,1)}), bf16[256,8,256]{2,1,0:T(8,128)(2,1)S(1)}, u32[]{:S(2)}, u32[]{:S(2)}) async-start(bf16[256,8,256]{2,1,0:T(8,128)(2,1)} %bitcast.16), calls=%async_computation.1 | async-start | bytes 2097152 | tf_op jit(solution)/shard_map/all_to_all | solution.py:404
  87.6 49.2 %collective-permute-start.10 = (bf16[128,256]{1,0:T(8,128)(2,1)S(1)}, bf16[128,256]{1,0:T(8,128)(2,1)S(1)}, u32[]{:S(2)}, u32[]{:S(2)}) collective-permute-start(bf16[128,256]{1,0:T(8,128)(2,1)S(1)} %copy-done.12), channel_id=1, source_target_pairs={{0,2},{1,3},{2,0},{3,1},{4,6},{5,7},{6,4},{7,5},{8,10},{9,11},{10,... | collective-permute-start | bytes 196616 | tf_op jit(solution)/shard_map/ppermute | solution.py:358
  94.0 42.8 %collective-permute-start.11 = (bf16[128,256]{1,0:T(8,128)(2,1)S(1)}, bf16[128,256]{1,0:T(8,128)(2,1)S(1)}, u32[]{:S(2)}, u32[]{:S(2)}) collective-permute-start(bf16[128,256]{1,0:T(8,128)(2,1)S(1)} %copy-done.11), channel_id=1, source_target_pairs={{0,1},{1,2},{2,3},{3,0},{4,5},{5,6},{6,7},{7,4},{8,9},{9,10},{10,1... | collective-permute-start | bytes 196616 | tf_op jit(solution)/shard_map/ppermute | solution.py:358
  94.9 42.0 %collective-permute-start.12 = (bf16[128,256]{1,0:T(8,128)(2,1)S(1)}, bf16[128,256]{1,0:T(8,128)(2,1)S(1)}, u32[]{:S(2)}, u32[]{:S(2)}) collective-permute-start(bf16[128,256]{1,0:T(8,128)(2,1)S(1)} %copy-done.10), channel_id=1, source_target_pairs={{0,3},{1,0},{2,1},{3,2},{4,7},{5,4},{6,5},{7,6},{8,11},{9,8},{10,9... | collective-permute-start | bytes 196616 | tf_op jit(solution)/shard_map/ppermute | solution.py:358
  136.8 0.6 copy-start.13
  136.9 0.6 copy-start.14
  136.9 0.7 copy-start.15
  136.9 1.0 copy-start
Sparse Core Ops, SparseCore 0:
  63.2 66.0 all-gather.1

commit v4 on v3

--- a/solution.py
+++ b/solution.py
@@ -76,10 +76,10 @@
         store(lo, (out[:, :HALF] / out[:, HALF:]).astype(BF))
 
 
-def call(kernel, name, flops=0, moved=MIB, **options):
+def call(kernel, name, flops=0, moved=MIB, vmem=56 * MIB, **options):
     return pl.pallas_call(
         kernel,
-        compiler_params=pltpu.CompilerParams(vmem_limit_bytes=56 * MIB),
+        compiler_params=pltpu.CompilerParams(vmem_limit_bytes=vmem),
         cost_estimate=pl.CostEstimate(flops=flops, bytes_accessed=moved, transcendentals=0),
         name=name,
         **options,
@@ -90,15 +90,11 @@
     return jax.ShapeDtypeStruct(shape, BF)
 
 
-def cut_kernel(meta, query_ref, key_ref, value_ref, col_ref, row_ref, out_ref, *rows):
-    g = meta[0]
+def cut_kernel(meta, query_ref, key_ref, value_ref, col_ref, out_ref):
     out_ref[:, :HALF] = query_ref[...]
     out_ref[:, HALF : 2 * HALF] = key_ref[...]
     out_ref[:, 2 * HALF : 3 * HALF] = value_ref[...]
     out_ref[:, 3 * HALF :] = col_ref[...]
-    for k, ref in zip(ORDER, rows):
-        at = pl.multiple_of(lax.rem(g + k, GROUPS) * 256, 256)
-        ref[...] = row_ref[:, pl.ds(at, 256)]
 
 
 def cut(meta, w_qkv, w_out):
@@ -116,13 +112,32 @@
                 part(1, 1),
                 part(2, 3),
                 pl.BlockSpec((BLOCK, HALF), lambda b, meta: (1, meta[3] * 2 + meta[2])),
-                pl.BlockSpec((BLOCK, D), lambda b, meta: (0, 0)),
             ],
-            out_specs=[pl.BlockSpec((BLOCK, 4 * HALF), lambda b, meta: (0, 0))]
-            + [pl.BlockSpec((BLOCK, 256), lambda b, meta: (0, 0))] * 3,
+            out_specs=pl.BlockSpec((BLOCK, 4 * HALF), lambda b, meta: (0, 0)),
         ),
-        out_shape=[like(BLOCK, 4 * HALF)] + [like(BLOCK, 256)] * 3,
-    )(meta, w_qkv, w_qkv, w_qkv, w_out, w_out)
+        out_shape=like(BLOCK, 4 * HALF),
+    )(meta, w_qkv, w_qkv, w_qkv, w_out)
+
+
+def split_kernel(meta, row_ref, *outs):
+    for k, ref in zip(ORDER, outs):
+        at = pl.multiple_of(lax.rem(meta[0] + k, GROUPS) * 256, 256)
+        ref[...] = row_ref[:, pl.ds(at, 256)]
+
+
+def split(meta, w_out):
+    return call(
+        split_kernel,
+        "split",
+        flops=10 * 10**9,
+        grid_spec=pltpu.PrefetchScalarGridSpec(
+            num_scalar_prefetch=1,
+            grid=(1,),
+            in_specs=[pl.BlockSpec((BLOCK, D), lambda b, meta: (0, 0))],
+            out_specs=[pl.BlockSpec((BLOCK, 256), lambda b, meta: (0, 0))] * 3,
+        ),
+        out_shape=[like(BLOCK, 256)] * 3,
+    )(meta, w_out)
 
 
 def mid_kernel(in0, in1, in2, x_ref, y_ref):
@@ -136,6 +151,7 @@
         mid_kernel,
         "mid",
         flops=10**12,
+        vmem=16 * MIB,
         in_specs=[whole()] * 3,
         out_specs=[whole()] * 2,
         out_shape=[like(3, BLOCK, 256)] * 2,
@@ -153,20 +169,21 @@
         stack_kernel,
         "stack",
         flops=10**9,
+        vmem=16 * MIB,
         in_specs=[whole()] * 8 + [anywhere()] * len(after),
         out_specs=whole(),
         out_shape=like(2, 4, 3, BLOCK, 256),
     )(*parts, *after)
 
 
-def prep_kernel(meta, sig_ref, out_ref):
+def prep_kernel(meta, sig_ref, after, out_ref):
     pick = one_hot(lambda o: ((o // 2) % 4) * 32 + (o // 8) * 2 + o % 2)
     for b in range(2):
         part = sig_ref[:, b * 32 : (b + 1) * 32, :].reshape(BLOCK, D)
         out_ref[b * BLOCK : (b + 1) * BLOCK, :] = move(pick, part)
 
 
-def prep(meta, sig):
+def prep(meta, sig, after):
     return call(
         prep_kernel,
         "prep",
@@ -175,11 +192,14 @@
         grid_spec=pltpu.PrefetchScalarGridSpec(
             num_scalar_prefetch=1,
             grid=(2,),
-            in_specs=[pl.BlockSpec((4, 64, D), lambda b, meta: (0, meta[0] * 2 + b, 0))],
+            in_specs=[
+                pl.BlockSpec((4, 64, D), lambda b, meta: (0, meta[0] * 2 + b, 0)),
+                anywhere(),
+            ],
             out_specs=pl.BlockSpec((256, D), lambda b, meta: (b, 0)),
         ),
         out_shape=like(C, D),
-    )(meta, sig)
+    )(meta, sig, after)
 
 
 def row_kernel(sig_ref, query_ref, key_ref, value_ref, out_ref):
@@ -310,38 +330,26 @@
     )(meta, held, own, w_out, near, far)
 
 
-def join_kernel(meta, got_ref, rows_ref, w0, w1, w2, w3, out_ref):
+def mix_kernel(meta, rows_ref, w0, w1, w2, w3, out_ref):
     g = meta[0]
     weight = jnp.concatenate([w0[...], w1[...], w2[...], w3[...]], axis=0)
-    pick = one_hot(lambda o: ((o // 2) % 16) * 8 + (o // 32) * 2 + o % 2)
-    columns = [
-        jnp.dot(
-            pick,
-            got_ref[b * 16 : (b + 1) * 16, 0].reshape(BLOCK, 256),
-            preferred_element_type=F32,
-        )
-        for b in range(4)
-    ]
     for r in range(ROWS_LOCAL):
         left = jnp.concatenate(
             [rows_ref[lax.rem(g + GROUPS - k, GROUPS), r, 0] for k in (0,) + ORDER], axis=1
         )
-        right = jnp.concatenate([column[r * 32 : (r + 1) * 32] for column in columns], axis=0)
-        mixed = jnp.dot(left, weight, preferred_element_type=F32) + right
-        out_ref[r, 0] = mixed.astype(BF)
-
-
-def join(meta, got, rows, w_out, w_rows):
-    return call(
-        join_kernel,
-        "join",
+        out_ref[r, 0] = jnp.dot(left, weight, preferred_element_type=F32)
+
+
+def mix(meta, rows, w_out, w_rows):
+    return call(
+        mix_kernel,
+        "mix",
         flops=2 * 10**9,
-        moved=4 * MIB,
+        moved=5 * MIB,
         grid_spec=pltpu.PrefetchScalarGridSpec(
             num_scalar_prefetch=1,
             grid=(GROUPS,),
             in_specs=[
-                pl.BlockSpec((64, 1, 8, 256), lambda j, meta: (0, j, 0, 0)),
                 pl.BlockSpec(
                     (GROUPS, ROWS_LOCAL, 1, BLOCK, HALF), lambda j, meta: (0, 0, j, 0, 0)
                 ),
@@ -350,8 +358,37 @@
             + [pl.BlockSpec((BLOCK, 256), lambda j, meta: (0, 0))] * 3,
             out_specs=pl.BlockSpec((ROWS_LOCAL, 1, BLOCK, 256), lambda j, meta: (0, j, 0, 0)),
         ),
+        out_shape=jax.ShapeDtypeStruct((ROWS_LOCAL, GROUPS, BLOCK, 256), F32),
+    )(meta, rows, w_out, *w_rows)
+
+
+def join_kernel(got_ref, rows_ref, out_ref):
+    pick = one_hot(lambda o: ((o // 2) % 16) * 8 + (o // 32) * 2 + o % 2)
+    for b in range(4):
+        moved = jnp.dot(
+            pick,
+            got_ref[b * 16 : (b + 1) * 16, 0].reshape(BLOCK, 256),
+            preferred_element_type=F32,
+        )
+        for r in range(ROWS_LOCAL):
+            lo = b * 32
+            out_ref[r, 0, lo : lo + 32] = (
+                moved[r * 32 : (r + 1) * 32] + rows_ref[r, 0, lo : lo + 32]
+            ).astype(BF)
+
+
+def join(got, rows):
+    block = pl.BlockSpec((ROWS_LOCAL, 1, BLOCK, 256), lambda j: (0, j, 0, 0))
+    return call(
+        join_kernel,
+        "join",
+        flops=10**8,
+        moved=4 * MIB,
+        grid=(GROUPS,),
+        in_specs=[pl.BlockSpec((64, 1, 8, 256), lambda j: (0, j, 0, 0)), block],
+        out_specs=block,
         out_shape=like(ROWS_LOCAL, GROUPS, BLOCK, 256),
-    )(meta, got, rows, w_out, *w_rows)
+    )(got, rows)
 
 
 def to_group(data, k):
@@ -380,35 +417,31 @@
     meta = jnp.stack([g, i // 2 % 4, i % 2, i // 8 % 4]).astype(jnp.int32)
     sig = signal.reshape(ROWS_LOCAL, C, D)
 
-    mine, *w_rows = cut(meta, w_qkv, w_out)
+    mine = cut(meta, w_qkv, w_out)
+    pieces = split(meta, w_out)
     others_x, others_y = mid([to_group(mine, k) for k in ORDER])
-    w_rows = [to_group(part, k) for part, k in zip(w_rows, ORDER)]
-
-    send = prep(meta, sig).reshape(64, 8, D)
-    got = lax.all_to_all(send, "rows", split_axis=0, concat_axis=0, tiled=True).reshape(C, D)
+    w_rows = [to_group(part, k) for part, k in zip(pieces, ORDER)]
 
     own_rows = row_part(sig, w_qkv)
     rows = lax.all_gather(own_rows.reshape(ROWS_LOCAL * C, HALF), "heads", axis=0)
+
+    send = prep(meta, sig, own_rows).reshape(64, 8, D)
+    got = lax.all_to_all(send, "rows", split_axis=0, concat_axis=0, tiled=True).reshape(C, D)
 
     near = stack(
         [others_x]
         + [along_x(others_x, d) for d in (2, 1, 3)]
         + [others_y]
         + [along_y(others_y, d) for d in (2, 1, 3)],
-        [own_rows],
+        pieces,
     )
     far = other_core(near)
 
     held, own = own_part(got, w_qkv)
     columns = column_part(meta, held, own, w_out, near, far).reshape(64 * GROUPS, 8, 256)
     back = lax.all_to_all(columns, ("rows", "heads"), split_axis=0, concat_axis=0, tiled=True)
-    return join(
-        meta,
-        back.reshape(64, GROUPS, 8, 256),
-        rows.reshape(GROUPS, ROWS_LOCAL, GROUPS, BLOCK, HALF),
-        w_out,
-        w_rows,
-    ).reshape(ROWS_LOCAL * C, 256)
+    mixed = mix(meta, rows.reshape(GROUPS, ROWS_LOCAL, GROUPS, BLOCK, HALF), w_out, w_rows)
+    return join(back.reshape(64, GROUPS, 8, 256), mixed).reshape(ROWS_LOCAL * C, 256)
 
 
 def solution(mesh):

time: 150 us -> 143 us (0.953)
  waiting for transfers between devices: 46.2 us -> 33.1 us
  Pallas kernels: 36.6 us -> 39.4 us
  starting transfers between devices: 49 us -> 51.4 us
    ppermute x6, waiting for transfers between devices: 39.2 us -> 22.1 us  [to_group(): lax.ppermute(data, 'heads', [(j, (j + k) % GROUPS) for j in range(GROUPS)])]
    pallas_call x3 -> x5, Pallas kernels: 9.65 us -> 12.8 us  [the longest x1 5.05 us: mix(): call(mix_kernel, 'mix', flops=2 * 10 ** 9, moved=5 * MIB, grid_spec=pltpu...]
    ppermute x3, waiting for transfers between devices: 6.9 us -> 9.95 us  [along_x(): lax.ppermute(data, 'rows', [(i, i // 8 * 8 + (i // 2 % 4 + d) % 4 * 2 + i...]
    all_to_all x1, starting transfers between devices: 5.31 us -> 7.59 us  [local(): lax.all_to_all(columns, ('rows', 'heads'), split_axis=0, concat_axis=0, t...]
    unnamed x32 -> x20, local copies, waits for them, and re-layouts: 3.86 us -> 4.14 us
  transfers between devices with their start and end apart: 16 -> 16, of which waited for: 2 -> 4; matrix products, arithmetic and copies ran while one was open for 0% -> 0% of each run, Pallas kernels for 19% -> 23%
where the time goes in v4:
time: 143 us; the launch traced here: 142 us
  starting transfers between devices  51.4 us (36%)
  Pallas kernels  39.4 us (28%)
  waiting for transfers between devices  33.1 us (23%)
  between operations  13.5 us (9%)
  local copies, waits for them, and re-layouts  4.14 us (3%)
    ppermute x6, waiting for transfers between devices, to_group(): lax.ppermute(data, 'heads', [(j, (j + k) % GROUPS) for j in range(GROUPS)])  22.1 us
    ppermute x6, starting transfers between devices, to_group(): lax.ppermute(data, 'heads', [(j, (j + k) % GROUPS) for j in range(GROUPS)])  21.2 us
    ppermute x3, waiting for transfers between devices, along_x(): lax.ppermute(data, 'rows', [(i, i // 8 * 8 + (i // 2 % 4 + d) % 4 * 2 + i...  9.95 us
    all_to_all x1, starting transfers between devices, local(): lax.all_to_all(send, 'rows', split_axis=0, concat_axis=0, tiled=True)  9.64 us
    pallas_call x1, Pallas kernels, column_part(): call(column_kernel, 'column_part', flops=3 * 10 ** 9, moved=6 * MIB, in_s...  9.2 us
    pallas_call x1, Pallas kernels, row_part(): call(row_kernel, 'row_part', flops=6 * 10 ** 9, moved=6 * MIB, grid=(ROWS...  8.12 us
    all_to_all x1, starting transfers between devices, local(): lax.all_to_all(columns, ('rows', 'heads'), split_axis=0, concat_axis=0, t...  7.59 us
    ppermute x3, starting transfers between devices, along_x(): lax.ppermute(data, 'rows', [(i, i // 8 * 8 + (i // 2 % 4 + d) % 4 * 2 + i...  5.75 us
  transfers between devices with their start and end apart: 16, of which 4 were waited for; matrix products, arithmetic and copies ran while one was open for 0% of the time, Pallas kernels for 23%

profile of v4, /device:TPU:1, one launch (start us, length us, event | category | flops | bytes accessed | tf_op | source)
XLA Modules:
  0.0 142.2 jit_solution(14758395586842484286)
XLA Ops:
  6.5 0.6 pad_add_fusion.meta
  7.1 2.2 %cut.1 = bf16[128,512]{1,0:T(8,128)(2,1)} custom-call(s32[4]{0:T(128)} %pad_add_fusion.meta, bf16[1024,768]{1,0:T(8,128)(2,1)} %value_ref.3, bf16[1024,768]{1,0:T(8,128)(2,1)} %value_ref.3, bf16[1024,768]{1,0:T(8,128)(2,1)} %value_ref.3, bf16[256,1024]{1,0:T(8,128)(2,1)} %w0.1), custom_call_target="tpu_custom_call" | custom-call | bytes 1048576 | tf_op jit(solution)/shard_map/cut/pallas_call | solution.py:104
  9.3 7.7 %collective-permute-start = (bf16[128,512]{1,0:T(8,128)(2,1)}, bf16[128,512]{1,0:T(8,128)(2,1)S(1)}, u32[]{:S(2)}, u32[]{:S(2)}) collective-permute-start(bf16[128,512]{1,0:T(8,128)(2,1)} %cut.1), channel_id=1, source_target_pairs={{0,2},{1,3},{2,0},{3,1},{4,6},{5,7},{6,4},{7,5},{8,10},{9,11},{10,... | collective-permute-start | bytes 393224 | tf_op jit(solution)/shard_map/ppermute | solution.py:395
  17.0 1.2 collective-permute-start.1
  18.2 2.4 %collective-permute-start.2 = (bf16[128,512]{1,0:T(8,128)(2,1)}, bf16[128,512]{1,0:T(8,128)(2,1)S(1)}, u32[]{:S(2)}, u32[]{:S(2)}) collective-permute-start(bf16[128,512]{1,0:T(8,128)(2,1)} %cut.1), channel_id=1, source_target_pairs={{0,3},{1,0},{2,1},{3,2},{4,7},{5,4},{6,5},{7,6},{8,11},{9,8},{10,9... | collective-permute-start | bytes 393224 | tf_op jit(solution)/shard_map/ppermute | solution.py:395
  20.6 8.1 %row_part.1.after = bf16[4,512,128]{2,1,0:T(8,128)(2,1)} custom-call(bf16[4,512,1024]{2,1,0:T(8,128)(2,1)} %bitcast.12, bf16[1024,768]{1,0:T(8,128)(2,1)} %value_ref.3, bf16[1024,768]{1,0:T(8,128)(2,1)} %value_ref.3, bf16[1024,768]{1,0:T(8,128)(2,1)} %value_ref.3), custom_call_target="tpu_custom_call" | custom-call | flops 6000000000 | bytes 6291456 | tf_op jit(solution)/shard_map/row_part/pallas_call | solution.py:219
  28.7 3.1 %prep.1 = bf16[512,1024]{1,0:T(8,128)(2,1)} custom-call(s32[4]{0:T(128)} %pad_add_fusion.meta, bf16[4,512,1024]{2,1,0:T(8,128)(2,1)} %bitcast.13, bf16[4,512,128]{2,1,0:T(8,128)(2,1)} %row_part.1.after), custom_call_target="tpu_custom_call" | custom-call | flops 134217728 | bytes 2097152 | tf_op jit(solution)/shard_map/prep/pallas_call | solution.py:187
  31.8 9.6 %all-to-all-start = ((bf16[64,8,1024]{2,1,0:T(8,128)(2,1)}), bf16[64,8,1024]{2,1,0:T(8,128)(2,1)}, u32[]{:S(2)}, u32[]{:S(2)}) async-start(bf16[64,8,1024]{2,1,0:T(8,128)(2,1)} %bitcast.14), calls=%async_computation | async-start | bytes 2097152 | tf_op jit(solution)/shard_map/all_to_all | solution.py:429
  41.5 0.0 all-gather.2.cloned.1.call-start
  41.5 0.0 collective-permute-done.in0
  41.5 0.0 collective-permute-done.1.in1
  41.6 0.0 collective-permute-done.2.in2
  41.6 3.0 %collective-permute-start.3 = (bf16[3,128,256]{2,1,0:T(8,128)(2,1)S(1)}, bf16[3,128,256]{2,1,0:T(8,128)(2,1)S(1)}, u32[]{:S(2)}, u32[]{:S(2)}) collective-permute-start(bf16[3,128,256]{2,1,0:T(8,128)(2,1)S(1)} %get-tuple-element.14.refs_0_), channel_id=1, source_target_pairs={{0,16},{4,20},{8,24},{12,28},{16,0},{20,4},{24,8},{28,12},{32,48},... | collective-permute-start | bytes 589832 | tf_op jit(solution)/shard_map/ppermute | solution.py:399
  44.6 0.0 all-gather.2.cloned.1.call-update
  44.6 0.4 collective-permute-start.4
  45.0 2.4 %collective-permute-start.5 = (bf16[3,128,256]{2,1,0:T(8,128)(2,1)S(1)}, bf16[3,128,256]{2,1,0:T(8,128)(2,1)S(1)}, u32[]{:S(2)}, u32[]{:S(2)}) collective-permute-start(bf16[3,128,256]{2,1,0:T(8,128)(2,1)S(1)} %get-tuple-element.14.refs_0_), channel_id=1, source_target_pairs={{0,24},{4,28},{8,0},{12,4},{16,8},{20,12},{24,16},{28,20},{32,56},... | collective-permute-start | bytes 589832 | tf_op jit(solution)/shard_map/ppermute | solution.py:399
  47.4 2.7 %collective-permute-start.6 = (bf16[3,128,256]{2,1,0:T(8,128)(2,1)S(1)}, bf16[3,128,256]{2,1,0:T(8,128)(2,1)S(1)}, u32[]{:S(2)}, u32[]{:S(2)}) collective-permute-start(bf16[3,128,256]{2,1,0:T(8,128)(2,1)S(1)} %get-tuple-element.15.refs_4_), channel_id=1, source_target_pairs={{0,64},{4,68},{8,72},{12,76},{16,80},{20,84},{24,88},{28,92},{32,9... | collective-permute-start | bytes 589832 | tf_op jit(solution)/shard_map/ppermute | solution.py:405
  50.1 0.3 collective-permute-start.7
  50.4 9.9 %collective-permute-done.3.refs_1_ = bf16[3,128,256]{2,1,0:T(8,128)(2,1)S(1)} collective-permute-done((bf16[3,128,256]{2,1,0:T(8,128)(2,1)S(1)}, bf16[3,128,256]{2,1,0:T(8,128)(2,1)S(1)}, u32[]{:S(2)}, u32[]{:S(2)}) %collective-permute-start.3) | collective-permute-done | bytes 196640 | tf_op jit(solution)/shard_map/ppermute | solution.py:399
  60.4 2.5 %collective-permute-start.8 = (bf16[3,128,256]{2,1,0:T(8,128)(2,1)S(1)}, bf16[3,128,256]{2,1,0:T(8,128)(2,1)S(1)}, u32[]{:S(2)}, u32[]{:S(2)}) collective-permute-start(bf16[3,128,256]{2,1,0:T(8,128)(2,1)S(1)} %get-tuple-element.15.refs_4_), channel_id=1, source_target_pairs={{0,96},{4,100},{8,104},{12,108},{16,112},{20,116},{24,120},{28,124... | collective-permute-start | bytes 589832 | tf_op jit(solution)/shard_map/ppermute | solution.py:405
  62.8 2.3 %split.1 = (bf16[128,256]{1,0:T(8,128)(2,1)}, bf16[128,256]{1,0:T(8,128)(2,1)}, bf16[128,256]{1,0:T(8,128)(2,1)}) custom-call(s32[4]{0:T(128)} %pad_add_fusion.meta, bf16[256,1024]{1,0:T(8,128)(2,1)} %w0.1), custom_call_target="tpu_custom_call" | custom-call | flops 10000000000 | bytes 1048576 | tf_op jit(solution)/shard_map/split/pallas_call | solution.py:129
  65.1 0.0 collective-permute-done.4.refs_2_
  65.2 0.0 collective-permute-done.5.refs_3_
  65.2 0.0 collective-permute-done.6.refs_5_
  65.2 1.0 collective-permute-done.7.refs_6_
  66.2 0.8 copy-done
  67.0 0.8 copy-done.2
  67.9 0.8 copy-done.4
  68.7 1.2 stack.21.near
  70.0 1.7 %collective-permute-start.9 = (bf16[2,4,3,128,256]{4,3,2,1,0:T(8,128)(2,1)}, bf16[2,4,3,128,256]{4,3,2,1,0:T(8,128)(2,1)}, u32[]{:S(2)}, u32[]{:S(2)}) collective-permute-start(bf16[2,4,3,128,256]{4,3,2,1,0:T(8,128)(2,1)} %stack.21.near), channel_id=1, source_target_pairs={{0,4},{4,0},{8,12},{12,8},{16,20},{20,16},{24,28},{28,24},{32,36},... | collective-permute-start | bytes 4718600 | tf_op jit(solution)/shard_map/ppermute | solution.py:411
  71.7 0.0 all-to-all-done
  71.7 4.0 %own_part.1 = (bf16[512,1024]{1,0:T(8,128)(2,1)}, bf16[512,128]{1,0:T(8,128)(2,1)}) custom-call(bf16[512,1024]{1,0:T(8,128)(2,1)} %bitcast.6.got_ref, bf16[1024,768]{1,0:T(8,128)(2,1)} %value_ref.3), custom_call_target="tpu_custom_call" | custom-call | flops 999999995904 | bytes 4194304 | tf_op jit(solution)/shard_map/own_part/pallas_call | solution.py:258
  75.7 0.0 collective-permute-done.9.far
  75.7 9.2 %column_part.1 = bf16[64,4,8,256]{3,2,1,0:T(8,128)(2,1)} custom-call(s32[4]{0:T(128)} %pad_add_fusion.meta, bf16[512,1024]{1,0:T(8,128)(2,1)} %get-tuple-element.12.held, bf16[512,128]{1,0:T(8,128)(2,1)} %get-tuple-element.13.own, bf16[256,1024]{1,0:T(8,128)(2,1)} %w0.1, bf16[2,4,3,128,256]{4,3,2,1,0:T(8,128)(2,1)} %stack.21.near, ...), custom_call_target="tpu_custom_call" | custom-call | flops 3000000000 | bytes 6291456 | tf_op jit(solution)/shard_map/column_part/pallas_call | solution.py:315
  84.9 7.6 %all-to-all-start.1 = ((bf16[256,8,256]{2,1,0:T(8,128)(2,1)}), bf16[256,8,256]{2,1,0:T(8,128)(2,1)S(1)}, u32[]{:S(2)}, u32[]{:S(2)}) async-start(bf16[256,8,256]{2,1,0:T(8,128)(2,1)} %bitcast.17), calls=%async_computation.1 | async-start | bytes 2097152 | tf_op jit(solution)/shard_map/all_to_all | solution.py:442
  92.5 6.3 %collective-permute-start.10 = (bf16[128,256]{1,0:T(8,128)(2,1)S(1)}, bf16[128,256]{1,0:T(8,128)(2,1)S(1)}, u32[]{:S(2)}, u32[]{:S(2)}) collective-permute-start(bf16[128,256]{1,0:T(8,128)(2,1)S(1)} %copy-done.5), channel_id=1, source_target_pairs={{0,2},{1,3},{2,0},{3,1},{4,6},{5,7},{6,4},{7,5},{8,10},{9,11},{10,... | collective-permute-start | bytes 196616 | tf_op jit(solution)/shard_map/ppermute | solution.py:395
  98.9 0.8 collective-permute-start.11
  99.7 2.8 %collective-permute-start.12 = (bf16[128,256]{1,0:T(8,128)(2,1)S(1)}, bf16[128,256]{1,0:T(8,128)(2,1)S(1)}, u32[]{:S(2)}, u32[]{:S(2)}) collective-permute-start(bf16[128,256]{1,0:T(8,128)(2,1)S(1)} %copy-done.1), channel_id=1, source_target_pairs={{0,3},{1,0},{2,1},{3,2},{4,7},{5,4},{6,5},{7,6},{8,11},{9,8},{10,9... | collective-permute-start | bytes 196616 | tf_op jit(solution)/shard_map/ppermute | solution.py:395
  102.4 21.3 %collective-permute-done.10.w1 = bf16[128,256]{1,0:T(8,128)(2,1)S(1)} collective-permute-done((bf16[128,256]{1,0:T(8,128)(2,1)S(1)}, bf16[128,256]{1,0:T(8,128)(2,1)S(1)}, u32[]{:S(2)}, u32[]{:S(2)}) %collective-permute-start.10) | collective-permute-done | bytes 65568 | tf_op jit(solution)/shard_map/ppermute | solution.py:395
  123.7 0.8 collective-permute-done.11.w2
  124.5 0.0 collective-permute-done.12.w3
  124.5 0.0 all-gather.2.cloned.1.call-done
  124.5 0.6 copy-done.8
  125.1 0.0 copy-done.9
  125.2 5.0 %mix.1.rows_ref = f32[4,4,128,256]{3,2,1,0:T(8,128)} custom-call(s32[4]{0:T(128)} %pad_add_fusion.meta, bf16[4,4,4,128,128]{4,3,2,1,0:T(8,128)(2,1)} %bitcast.18, bf16[256,1024]{1,0:T(8,128)(2,1)} %w0.1, bf16[128,256]{1,0:T(8,128)(2,1)} %copy-done.7, bf16[128,256]{1,0:T(8,128)(2,1)} %copy-done.8, bf16[128,256]{1,0:T(8,128)(2,1)} %copy-done.9), custom_call_target="tpu_custom_call" | custom-call | flops 2000000000 | bytes 5242880 | tf_op jit(solution)/shard_map/mix/pallas_call | solution.py:344
  130.2 0.0 all-to-all-done.1
  130.2 1.0 copy-done.6
  131.2 4.1 %join.1 = bf16[4,4,128,256]{3,2,1,0:T(8,128)(2,1)} custom-call(bf16[64,4,8,256]{3,2,1,0:T(8,128)(2,1)} %bitcast.15, f32[4,4,128,256]{3,2,1,0:T(8,128)} %mix.1.rows_ref), custom_call_target="tpu_custom_call" | custom-call | flops 100000000 | bytes 4194304 | tf_op jit(solution)/shard_map/join/pallas_call | solution.py:382
  (16 shorter events, 0.1 us)
Async XLA Ops:
  9.3 32.2 %collective-permute-start = (bf16[128,512]{1,0:T(8,128)(2,1)}, bf16[128,512]{1,0:T(8,128)(2,1)S(1)}, u32[]{:S(2)}, u32[]{:S(2)}) collective-permute-start(bf16[128,512]{1,0:T(8,128)(2,1)} %cut.1), channel_id=1, source_target_pairs={{0,2},{1,3},{2,0},{3,1},{4,6},{5,7},{6,4},{7,5},{8,10},{9,11},{10,... | collective-permute-start | bytes 393224 | tf_op jit(solution)/shard_map/ppermute | solution.py:395
  17.0 24.5 %collective-permute-start.1 = (bf16[128,512]{1,0:T(8,128)(2,1)}, bf16[128,512]{1,0:T(8,128)(2,1)S(1)}, u32[]{:S(2)}, u32[]{:S(2)}) collective-permute-start(bf16[128,512]{1,0:T(8,128)(2,1)} %cut.1), channel_id=1, source_target_pairs={{0,1},{1,2},{2,3},{3,0},{4,5},{5,6},{6,7},{7,4},{8,9},{9,10},{10,1... | collective-permute-start | bytes 393224 | tf_op jit(solution)/shard_map/ppermute | solution.py:395
  18.2 23.3 %collective-permute-start.2 = (bf16[128,512]{1,0:T(8,128)(2,1)}, bf16[128,512]{1,0:T(8,128)(2,1)S(1)}, u32[]{:S(2)}, u32[]{:S(2)}) collective-permute-start(bf16[128,512]{1,0:T(8,128)(2,1)} %cut.1), channel_id=1, source_target_pairs={{0,3},{1,0},{2,1},{3,2},{4,7},{5,4},{6,5},{7,6},{8,11},{9,8},{10,9... | collective-permute-start | bytes 393224 | tf_op jit(solution)/shard_map/ppermute | solution.py:395
  31.8 39.9 %all-to-all-start = ((bf16[64,8,1024]{2,1,0:T(8,128)(2,1)}), bf16[64,8,1024]{2,1,0:T(8,128)(2,1)}, u32[]{:S(2)}, u32[]{:S(2)}) async-start(bf16[64,8,1024]{2,1,0:T(8,128)(2,1)} %bitcast.14), calls=%async_computation | async-start | bytes 2097152 | tf_op jit(solution)/shard_map/all_to_all | solution.py:429
  41.5 83.0 %all-gather.2.cloned.1.call-start = ((), (), s32[]{:S(2)}) async-start(), calls=%async_computation.2 | async-start | bytes 2621440 | tf_op jit(solution)/shard_map/all_gather | solution.py:426
  41.6 18.7 %collective-permute-start.3 = (bf16[3,128,256]{2,1,0:T(8,128)(2,1)S(1)}, bf16[3,128,256]{2,1,0:T(8,128)(2,1)S(1)}, u32[]{:S(2)}, u32[]{:S(2)}) collective-permute-start(bf16[3,128,256]{2,1,0:T(8,128)(2,1)S(1)} %get-tuple-element.14.refs_0_), channel_id=1, source_target_pairs={{0,16},{4,20},{8,24},{12,28},{16,0},{20,4},{24,8},{28,12},{32,48},... | collective-permute-start | bytes 589832 | tf_op jit(solution)/shard_map/ppermute | solution.py:399
  44.6 20.5 %collective-permute-start.4 = (bf16[3,128,256]{2,1,0:T(8,128)(2,1)S(1)}, bf16[3,128,256]{2,1,0:T(8,128)(2,1)S(1)}, u32[]{:S(2)}, u32[]{:S(2)}) collective-permute-start(bf16[3,128,256]{2,1,0:T(8,128)(2,1)S(1)} %get-tuple-element.14.refs_0_), channel_id=1, source_target_pairs={{0,8},{4,12},{8,16},{12,20},{16,24},{20,28},{24,0},{28,4},{32,40},... | collective-permute-start | bytes 589832 | tf_op jit(solution)/shard_map/ppermute | solution.py:399
  45.0 20.2 %collective-permute-start.5 = (bf16[3,128,256]{2,1,0:T(8,128)(2,1)S(1)}, bf16[3,128,256]{2,1,0:T(8,128)(2,1)S(1)}, u32[]{:S(2)}, u32[]{:S(2)}) collective-permute-start(bf16[3,128,256]{2,1,0:T(8,128)(2,1)S(1)} %get-tuple-element.14.refs_0_), channel_id=1, source_target_pairs={{0,24},{4,28},{8,0},{12,4},{16,8},{20,12},{24,16},{28,20},{32,56},... | collective-permute-start | bytes 589832 | tf_op jit(solution)/shard_map/ppermute | solution.py:399
  47.4 17.8 %collective-permute-start.6 = (bf16[3,128,256]{2,1,0:T(8,128)(2,1)S(1)}, bf16[3,128,256]{2,1,0:T(8,128)(2,1)S(1)}, u32[]{:S(2)}, u32[]{:S(2)}) collective-permute-start(bf16[3,128,256]{2,1,0:T(8,128)(2,1)S(1)} %get-tuple-element.15.refs_4_), channel_id=1, source_target_pairs={{0,64},{4,68},{8,72},{12,76},{16,80},{20,84},{24,88},{28,92},{32,9... | collective-permute-start | bytes 589832 | tf_op jit(solution)/shard_map/ppermute | solution.py:405
  50.1 16.1 %collective-permute-start.7 = (bf16[3,128,256]{2,1,0:T(8,128)(2,1)S(1)}, bf16[3,128,256]{2,1,0:T(8,128)(2,1)S(1)}, u32[]{:S(2)}, u32[]{:S(2)}) collective-permute-start(bf16[3,128,256]{2,1,0:T(8,128)(2,1)S(1)} %get-tuple-element.15.refs_4_), channel_id=1, source_target_pairs={{0,32},{4,36},{8,40},{12,44},{16,48},{20,52},{24,56},{28,60},{32,6... | collective-permute-start | bytes 589832 | tf_op jit(solution)/shard_map/ppermute | solution.py:405
  60.4 5.8 %collective-permute-start.8 = (bf16[3,128,256]{2,1,0:T(8,128)(2,1)S(1)}, bf16[3,128,256]{2,1,0:T(8,128)(2,1)S(1)}, u32[]{:S(2)}, u32[]{:S(2)}) collective-permute-start(bf16[3,128,256]{2,1,0:T(8,128)(2,1)S(1)} %get-tuple-element.15.refs_4_), channel_id=1, source_target_pairs={{0,96},{4,100},{8,104},{12,108},{16,112},{20,116},{24,120},{28,124... | collective-permute-start | bytes 589832 | tf_op jit(solution)/shard_map/ppermute | solution.py:405
  66.2 0.8 copy-start
  67.0 0.8 copy-start.2
  67.9 0.8 copy-start.4
  70.0 5.7 %collective-permute-start.9 = (bf16[2,4,3,128,256]{4,3,2,1,0:T(8,128)(2,1)}, bf16[2,4,3,128,256]{4,3,2,1,0:T(8,128)(2,1)}, u32[]{:S(2)}, u32[]{:S(2)}) collective-permute-start(bf16[2,4,3,128,256]{4,3,2,1,0:T(8,128)(2,1)} %stack.21.near), channel_id=1, source_target_pairs={{0,4},{4,0},{8,12},{12,8},{16,20},{20,16},{24,28},{28,24},{32,36},... | collective-permute-start | bytes 4718600 | tf_op jit(solution)/shard_map/ppermute | solution.py:411
  84.9 7.6 %copy-start.5 = (bf16[128,256]{1,0:T(8,128)(2,1)S(1)}, bf16[128,256]{1,0:T(8,128)(2,1)}, u32[]{:S(2)}) copy-start(bf16[128,256]{1,0:T(8,128)(2,1)} %get-tuple-element.16.refs_8_) | copy-start | bytes 196612
  84.9 13.9 %copy-start.3 = (bf16[128,256]{1,0:T(8,128)(2,1)S(1)}, bf16[128,256]{1,0:T(8,128)(2,1)}, u32[]{:S(2)}) copy-start(bf16[128,256]{1,0:T(8,128)(2,1)} %get-tuple-element.17.refs_9_) | copy-start | bytes 196612
  84.9 14.8 %copy-start.1 = (bf16[128,256]{1,0:T(8,128)(2,1)S(1)}, bf16[128,256]{1,0:T(8,128)(2,1)}, u32[]{:S(2)}) copy-start(bf16[128,256]{1,0:T(8,128)(2,1)} %get-tuple-element.18.refs_10_) | copy-start | bytes 196612
  84.9 45.3 %all-to-all-start.1 = ((bf16[256,8,256]{2,1,0:T(8,128)(2,1)}), bf16[256,8,256]{2,1,0:T(8,128)(2,1)S(1)}, u32[]{:S(2)}, u32[]{:S(2)}) async-start(bf16[256,8,256]{2,1,0:T(8,128)(2,1)} %bitcast.17), calls=%async_computation.1 | async-start | bytes 2097152 | tf_op jit(solution)/shard_map/all_to_all | solution.py:442
  92.5 31.2 %collective-permute-start.10 = (bf16[128,256]{1,0:T(8,128)(2,1)S(1)}, bf16[128,256]{1,0:T(8,128)(2,1)S(1)}, u32[]{:S(2)}, u32[]{:S(2)}) collective-permute-start(bf16[128,256]{1,0:T(8,128)(2,1)S(1)} %copy-done.5), channel_id=1, source_target_pairs={{0,2},{1,3},{2,0},{3,1},{4,6},{5,7},{6,4},{7,5},{8,10},{9,11},{10,... | collective-permute-start | bytes 196616 | tf_op jit(solution)/shard_map/ppermute | solution.py:395
  98.9 25.6 %collective-permute-start.11 = (bf16[128,256]{1,0:T(8,128)(2,1)S(1)}, bf16[128,256]{1,0:T(8,128)(2,1)S(1)}, u32[]{:S(2)}, u32[]{:S(2)}) collective-permute-start(bf16[128,256]{1,0:T(8,128)(2,1)S(1)} %copy-done.3), channel_id=1, source_target_pairs={{0,1},{1,2},{2,3},{3,0},{4,5},{5,6},{6,7},{7,4},{8,9},{9,10},{10,1... | collective-permute-start | bytes 196616 | tf_op jit(solution)/shard_map/ppermute | solution.py:395
  99.7 24.8 %collective-permute-start.12 = (bf16[128,256]{1,0:T(8,128)(2,1)S(1)}, bf16[128,256]{1,0:T(8,128)(2,1)S(1)}, u32[]{:S(2)}, u32[]{:S(2)}) collective-permute-start(bf16[128,256]{1,0:T(8,128)(2,1)S(1)} %copy-done.1), channel_id=1, source_target_pairs={{0,3},{1,0},{2,1},{3,2},{4,7},{5,4},{6,5},{7,6},{8,11},{9,8},{10,9... | collective-permute-start | bytes 196616 | tf_op jit(solution)/shard_map/ppermute | solution.py:395
  123.7 0.8 copy-start.7
  124.5 0.6 copy-start.8
  124.5 0.7 copy-start.9
  130.2 1.0 copy-start.6
Sparse Core Ops, SparseCore 0:
  44.7 45.2 all-gather.1

commit v5 on v4

--- a/solution.py
+++ b/solution.py
@@ -18,6 +18,7 @@
 VMEM = pltpu.VMEM
 MIB = 1 << 20
 ORDER = (2, 1, 3)
+STEPS = (1, 3, 2)
 SCALE = 0.125 * 1.4426950408889634
 
 
@@ -90,11 +91,14 @@
     return jax.ShapeDtypeStruct(shape, BF)
 
 
-def cut_kernel(meta, query_ref, key_ref, value_ref, col_ref, out_ref):
-    out_ref[:, :HALF] = query_ref[...]
-    out_ref[:, HALF : 2 * HALF] = key_ref[...]
-    out_ref[:, 2 * HALF : 3 * HALF] = value_ref[...]
-    out_ref[:, 3 * HALF :] = col_ref[...]
+def cut_kernel(meta, query_ref, key_ref, value_ref, col_ref, row_ref, *outs):
+    for k, out_ref in zip(ORDER, outs):
+        out_ref[:, :HALF] = query_ref[...]
+        out_ref[:, HALF : 2 * HALF] = key_ref[...]
+        out_ref[:, 2 * HALF : 3 * HALF] = value_ref[...]
+        out_ref[:, 3 * HALF : 4 * HALF] = col_ref[...]
+        at = pl.multiple_of(lax.rem(meta[0] + k, GROUPS) * 256, 256)
+        out_ref[:, 4 * HALF :] = row_ref[:, pl.ds(at, 256)]
 
 
 def cut(meta, w_qkv, w_out):
@@ -112,50 +116,52 @@
                 part(1, 1),
                 part(2, 3),
                 pl.BlockSpec((BLOCK, HALF), lambda b, meta: (1, meta[3] * 2 + meta[2])),
+                pl.BlockSpec((BLOCK, D), lambda b, meta: (0, 0)),
             ],
-            out_specs=pl.BlockSpec((BLOCK, 4 * HALF), lambda b, meta: (0, 0)),
+            out_specs=[pl.BlockSpec((BLOCK, 6 * HALF), lambda b, meta: (0, 0))] * 3,
         ),
-        out_shape=like(BLOCK, 4 * HALF),
-    )(meta, w_qkv, w_qkv, w_qkv, w_out)
-
-
-def split_kernel(meta, row_ref, *outs):
-    for k, ref in zip(ORDER, outs):
-        at = pl.multiple_of(lax.rem(meta[0] + k, GROUPS) * 256, 256)
-        ref[...] = row_ref[:, pl.ds(at, 256)]
-
-
-def split(meta, w_out):
-    return call(
-        split_kernel,
-        "split",
-        flops=10 * 10**9,
-        grid_spec=pltpu.PrefetchScalarGridSpec(
-            num_scalar_prefetch=1,
-            grid=(1,),
-            in_specs=[pl.BlockSpec((BLOCK, D), lambda b, meta: (0, 0))],
-            out_specs=[pl.BlockSpec((BLOCK, 256), lambda b, meta: (0, 0))] * 3,
-        ),
-        out_shape=[like(BLOCK, 256)] * 3,
-    )(meta, w_out)
-
-
-def mid_kernel(in0, in1, in2, x_ref, y_ref):
+        out_shape=[like(BLOCK, 6 * HALF)] * 3,
+    )(meta, w_qkv, w_qkv, w_qkv, w_out, w_out)
+
+
+def mid_kernel(in0, in1, in2, after, x_ref, y_ref, row_ref):
     for n, ref in enumerate((in0, in1, in2)):
         x_ref[n] = ref[:, :256]
-        y_ref[n] = ref[:, 256:]
-
-
-def mid(parts):
+        y_ref[n] = ref[:, 256:512]
+        row_ref[n * BLOCK : (n + 1) * BLOCK, :] = ref[:, 512:]
+
+
+def mid(parts, after):
     return call(
         mid_kernel,
         "mid",
         flops=10**12,
         vmem=16 * MIB,
-        in_specs=[whole()] * 3,
-        out_specs=[whole()] * 2,
-        out_shape=[like(3, BLOCK, 256)] * 2,
-    )(*parts)
+        in_specs=[whole()] * 3 + [anywhere()],
+        out_specs=[whole()] * 3,
+        out_shape=[like(3, BLOCK, 256)] * 2 + [like(3 * BLOCK, 256)],
+    )(*parts, after)
+
+
+def pick_kernel(query_ref, key_ref, value_ref, out_ref):
+    out_ref[:, :HALF] = query_ref[...]
+    out_ref[:, HALF : 2 * HALF] = key_ref[...]
+    out_ref[:, 2 * HALF :] = value_ref[...]
+
+
+def pick_columns(w_qkv):
+    def part(n):
+        return pl.BlockSpec((D, HALF), lambda b: (0, 2 * n + 1))
+
+    return call(
+        pick_kernel,
+        "pick_columns",
+        flops=10**10,
+        grid=(1,),
+        in_specs=[part(0), part(1), part(2)],
+        out_specs=pl.BlockSpec((D, 3 * HALF), lambda b: (0, 0)),
+        out_shape=like(D, 3 * HALF),
+    )(w_qkv, w_qkv, w_qkv)
 
 
 def stack_kernel(*refs):
@@ -176,14 +182,14 @@
     )(*parts, *after)
 
 
-def prep_kernel(meta, sig_ref, after, out_ref):
+def prep_kernel(meta, sig_ref, out_ref):
     pick = one_hot(lambda o: ((o // 2) % 4) * 32 + (o // 8) * 2 + o % 2)
     for b in range(2):
         part = sig_ref[:, b * 32 : (b + 1) * 32, :].reshape(BLOCK, D)
         out_ref[b * BLOCK : (b + 1) * BLOCK, :] = move(pick, part)
 
 
-def prep(meta, sig, after):
+def prep(meta, sig):
     return call(
         prep_kernel,
         "prep",
@@ -192,17 +198,15 @@
         grid_spec=pltpu.PrefetchScalarGridSpec(
             num_scalar_prefetch=1,
             grid=(2,),
-            in_specs=[
-                pl.BlockSpec((4, 64, D), lambda b, meta: (0, meta[0] * 2 + b, 0)),
-                anywhere(),
-            ],
+            in_specs=[pl.BlockSpec((4, 64, D), lambda b, meta: (0, meta[0] * 2 + b, 0))],
             out_specs=pl.BlockSpec((256, D), lambda b, meta: (b, 0)),
         ),
         out_shape=like(C, D),
-    )(meta, sig, after)
-
-
-def row_kernel(sig_ref, query_ref, key_ref, value_ref, out_ref):
+    )(meta, sig)
+
+
+def row_kernel(sig_ref, query_ref, key_ref, value_ref, after, out_ref, token_ref):
+    token_ref[...] = jnp.zeros_like(token_ref)
     weight = jnp.concatenate([query_ref[...], key_ref[...], value_ref[...]], axis=1)
     qkv = jnp.dot(sig_ref[0], weight, preferred_element_type=F32)
 
@@ -212,20 +216,22 @@
     attend(qkv, causal(), store)
 
 
-def row_part(sig, w_qkv):
+def row_part(sig, w_qkv, after):
     def part(n):
         return pl.BlockSpec((D, HALF), lambda r: (0, 2 * n))
 
     return call(
         row_kernel,
         "row_part",
-        flops=6 * 10**9,
-        moved=6 * MIB,
+        moved=1,
         grid=(ROWS_LOCAL,),
-        in_specs=[pl.BlockSpec((1, C, D), lambda r: (r, 0, 0)), part(0), part(1), part(2)],
-        out_specs=pl.BlockSpec((1, C, HALF), lambda r: (r, 0, 0)),
-        out_shape=like(ROWS_LOCAL, C, HALF),
-    )(sig, w_qkv, w_qkv, w_qkv)
+        in_specs=[pl.BlockSpec((1, C, D), lambda r: (r, 0, 0)), part(0), part(1), part(2), anywhere()],
+        out_specs=[
+            pl.BlockSpec((1, C, HALF), lambda r: (r, 0, 0)),
+            pl.BlockSpec((16, HALF), lambda r: (0, 0)),
+        ],
+        out_shape=[like(ROWS_LOCAL, C, HALF), like(16, HALF)],
+    )(sig, w_qkv, w_qkv, w_qkv, after)
 
 
 def columns_of(held, weight, allowed, keep):
@@ -248,10 +254,7 @@
     def keep(lo, out):
         out_ref[lo : lo + BLOCK, :] = out
 
-    weight = jnp.concatenate(
-        [w_ref[:, HALF:256], w_ref[:, 256 + HALF : 512], w_ref[:, 512 + HALF :]], axis=1
-    )
-    columns_of(held, weight, causal(), keep)
+    columns_of(held, w_ref[...], causal(), keep)
 
 
 def own_part(got, w_qkv):
@@ -275,7 +278,7 @@
     def fetch(source, target):
         copies.append(pltpu.make_async_copy(source, target, sems.at[len(copies)]))
 
-    for n, d in enumerate((0, 2, 1, 3)):
+    for n, d in enumerate((0,) + STEPS):
         for ref, on in ((near, core), (far, 1 - core)):
             at = lax.rem(meta[1] + 4 - d, 4) * 2 + on
             rows = pl.ds(pl.multiple_of(at * BLOCK, BLOCK), BLOCK)
@@ -330,9 +333,9 @@
     )(meta, held, own, w_out, near, far)
 
 
-def mix_kernel(meta, rows_ref, w0, w1, w2, w3, out_ref):
+def mix_kernel(meta, rows_ref, own_ref, w_ref, out_ref):
     g = meta[0]
-    weight = jnp.concatenate([w0[...], w1[...], w2[...], w3[...]], axis=0)
+    weight = jnp.concatenate([own_ref[...], w_ref[...]], axis=0)
     for r in range(ROWS_LOCAL):
         left = jnp.concatenate(
             [rows_ref[lax.rem(g + GROUPS - k, GROUPS), r, 0] for k in (0,) + ORDER], axis=1
@@ -354,12 +357,12 @@
                     (GROUPS, ROWS_LOCAL, 1, BLOCK, HALF), lambda j, meta: (0, 0, j, 0, 0)
                 ),
                 pl.BlockSpec((BLOCK, 256), lambda j, meta: (0, meta[0])),
-            ]
-            + [pl.BlockSpec((BLOCK, 256), lambda j, meta: (0, 0))] * 3,
+                pl.BlockSpec((3 * BLOCK, 256), lambda j, meta: (0, 0)),
+            ],
             out_specs=pl.BlockSpec((ROWS_LOCAL, 1, BLOCK, 256), lambda j, meta: (0, j, 0, 0)),
         ),
         out_shape=jax.ShapeDtypeStruct((ROWS_LOCAL, GROUPS, BLOCK, 256), F32),
-    )(meta, rows, w_out, *w_rows)
+    )(meta, rows, w_out, w_rows)
 
 
 def join_kernel(got_ref, rows_ref, out_ref):
@@ -382,6 +385,7 @@
     return call(
         join_kernel,
         "join",
+        vmem=16 * MIB,
         flops=10**8,
         moved=4 * MIB,
         grid=(GROUPS,),
@@ -417,27 +421,27 @@
     meta = jnp.stack([g, i // 2 % 4, i % 2, i // 8 % 4]).astype(jnp.int32)
     sig = signal.reshape(ROWS_LOCAL, C, D)
 
-    mine = cut(meta, w_qkv, w_out)
-    pieces = split(meta, w_out)
-    others_x, others_y = mid([to_group(mine, k) for k in ORDER])
-    w_rows = [to_group(part, k) for part, k in zip(pieces, ORDER)]
-
-    own_rows = row_part(sig, w_qkv)
+    send = prep(meta, sig)
+    own_rows, rows_done = row_part(sig, w_qkv, send)
+    send = send.reshape(64, 8, D)
+    got = lax.all_to_all(send, "rows", split_axis=0, concat_axis=0, tiled=True).reshape(C, D)
     rows = lax.all_gather(own_rows.reshape(ROWS_LOCAL * C, HALF), "heads", axis=0)
 
-    send = prep(meta, sig, own_rows).reshape(64, 8, D)
-    got = lax.all_to_all(send, "rows", split_axis=0, concat_axis=0, tiled=True).reshape(C, D)
+    cuts = cut(meta, w_qkv, w_out)
+    cuts = [to_group(part, k) for part, k in zip(cuts, ORDER)]
+    others_x, others_y, w_rows = mid(cuts, rows_done)
+    w_own = pick_columns(w_qkv)
 
     near = stack(
         [others_x]
-        + [along_x(others_x, d) for d in (2, 1, 3)]
+        + [along_x(others_x, d) for d in STEPS]
         + [others_y]
-        + [along_y(others_y, d) for d in (2, 1, 3)],
-        pieces,
+        + [along_y(others_y, d) for d in STEPS],
+        [w_own],
     )
     far = other_core(near)
 
-    held, own = own_part(got, w_qkv)
+    held, own = own_part(got, w_own)
     columns = column_part(meta, held, own, w_out, near, far).reshape(64 * GROUPS, 8, 256)
     back = lax.all_to_all(columns, ("rows", "heads"), split_axis=0, concat_axis=0, tiled=True)
     mixed = mix(meta, rows.reshape(GROUPS, ROWS_LOCAL, GROUPS, BLOCK, HALF), w_out, w_rows)

time: 143 us -> 131 us (0.916)
  starting transfers between devices: 51.4 us -> 40.5 us
  Pallas kernels: 39.4 us -> 37.7 us
    all_to_all x1, waiting for transfers between devices: 0.01 us -> 24.1 us  [local(): lax.all_to_all(columns, ('rows', 'heads'), split_axis=0, concat_axis=0, t...]
    ppermute x6 -> x3, waiting for transfers between devices: 22.1 us -> 0.01 us  [to_group(): lax.ppermute(data, 'heads', [(j, (j + k) % GROUPS) for j in range(GROUPS)])]
    ppermute x6 -> x3, starting transfers between devices: 21.2 us -> 11.3 us  [to_group(): lax.ppermute(data, 'heads', [(j, (j + k) % GROUPS) for j in range(GROUPS)])]
    ppermute x3, waiting for transfers between devices: 9.95 us -> 2.06 us  [along_x(): lax.ppermute(data, 'rows', [(i, i // 8 * 8 + (i // 2 % 4 + d) % 4 * 2 + i...]
    all_gather x1, waiting for transfers between devices: 0.02 us -> 4.96 us  [local(): lax.all_gather(own_rows.reshape(ROWS_LOCAL * C, HALF), 'heads', axis=0)]
    ppermute x3, waiting for transfers between devices: 1.03 us -> 3.18 us  [along_y(): lax.ppermute(data, 'rows', [(i, i // 32 * 32 + (i // 8 % 4 + d) % 4 * 8 +...]
    pallas_call x3, Pallas kernels: 14.6 us -> 12.7 us  [the longest x1 8.13 us: row_part(): call(row_kernel, 'row_part', moved=1, grid=(ROWS_LOCAL,), in_specs=[pl.Bl...]
    unnamed x20 -> x8, local copies, waits for them, and re-layouts: 4.14 us -> 4.07 us
  transfers between devices with their start and end apart: 16 -> 13, of which waited for: 4 -> 4; matrix products, arithmetic and copies ran while one was open for 0% -> 0% of each run, Pallas kernels for 23% -> 25%
where the time goes in v5:
time: 131 us
  starting transfers between devices  40.5 us (31%)
  Pallas kernels  37.7 us (29%)
  waiting for transfers between devices  34.4 us (26%)
  between operations  13.5 us (10%)
  local copies, waits for them, and re-layouts  4.07 us (3%)
    all_to_all x1, waiting for transfers between devices, local(): lax.all_to_all(columns, ('rows', 'heads'), split_axis=0, concat_axis=0, t...  24.1 us
    ppermute x3, starting transfers between devices, to_group(): lax.ppermute(data, 'heads', [(j, (j + k) % GROUPS) for j in range(GROUPS)])  11.3 us
    all_to_all x1, starting transfers between devices, local(): lax.all_to_all(send, 'rows', split_axis=0, concat_axis=0, tiled=True)  9.66 us
    pallas_call x1, Pallas kernels, column_part(): call(column_kernel, 'column_part', flops=3 * 10 ** 9, moved=6 * MIB, in_s...  9.21 us
    all_to_all x1, starting transfers between devices, local(): lax.all_to_all(columns, ('rows', 'heads'), split_axis=0, concat_axis=0, t...  8.81 us
    pallas_call x1, Pallas kernels, row_part(): call(row_kernel, 'row_part', moved=1, grid=(ROWS_LOCAL,), in_specs=[pl.Bl...  8.13 us
    pallas_call x1, Pallas kernels, mix(): call(mix_kernel, 'mix', flops=2 * 10 ** 9, moved=5 * MIB, grid_spec=pltpu...  5.12 us
    ppermute x3, starting transfers between devices, along_y(): lax.ppermute(data, 'rows', [(i, i // 32 * 32 + (i // 8 % 4 + d) % 4 * 8 +...  5.07 us
  transfers between devices with their start and end apart: 13, of which 4 were waited for; matrix products, arithmetic and copies ran while one was open for 0% of the time, Pallas kernels for 25%

profile of v5, /device:TPU:1, one launch (start us, length us, event | category | flops | bytes accessed | tf_op | source)
XLA Modules:
  0.0 130.7 jit_solution(16764927788246479849)
XLA Ops:
  6.5 0.6 pad_add_fusion.meta
  7.1 2.6 %cut.1 = (bf16[128,768]{1,0:T(8,128)(2,1)}, bf16[128,768]{1,0:T(8,128)(2,1)}, bf16[128,768]{1,0:T(8,128)(2,1)}) custom-call(s32[4]{0:T(128)} %pad_add_fusion.meta, bf16[1024,768]{1,0:T(8,128)(2,1)} %value_ref.5, bf16[1024,768]{1,0:T(8,128)(2,1)} %value_ref.5, bf16[1024,768]{1,0:T(8,128)(2,1)} %value_ref.5, bf16[256,1024]{1,0:T(8,128)(2,1)} %own_ref.1, ...), custom_call_target="tpu_custom_call" | custom-call | bytes 1048576 | tf_op jit(solution)/shard_map/cut/pallas_call | solution.py:108
  9.8 7.7 %collective-permute-start = (bf16[128,768]{1,0:T(8,128)(2,1)}, bf16[128,768]{1,0:T(8,128)(2,1)S(1)}, u32[]{:S(2)}, u32[]{:S(2)}) collective-permute-start(bf16[128,768]{1,0:T(8,128)(2,1)} %get-tuple-element.17), channel_id=1, source_target_pairs={{0,2},{1,3},{2,0},{3,1},{4,6},{5,7},{6,4},{7,5},{8,10},{9,11},{10,... | collective-permute-start | bytes 589832 | tf_op jit(solution)/shard_map/ppermute | solution.py:399
  17.5 1.2 collective-permute-start.1
  18.7 2.4 %collective-permute-start.2 = (bf16[128,768]{1,0:T(8,128)(2,1)}, bf16[128,768]{1,0:T(8,128)(2,1)S(1)}, u32[]{:S(2)}, u32[]{:S(2)}) collective-permute-start(bf16[128,768]{1,0:T(8,128)(2,1)} %get-tuple-element.19), channel_id=1, source_target_pairs={{0,3},{1,0},{2,1},{3,2},{4,7},{5,4},{6,5},{7,6},{8,11},{9,8},{10,9... | collective-permute-start | bytes 589832 | tf_op jit(solution)/shard_map/ppermute | solution.py:399
  21.1 3.1 %prep.1.after = bf16[512,1024]{1,0:T(8,128)(2,1)} custom-call(s32[4]{0:T(128)} %pad_add_fusion.meta, bf16[4,512,1024]{2,1,0:T(8,128)(2,1)} %bitcast.13), custom_call_target="tpu_custom_call" | custom-call | flops 134217728 | bytes 2097152 | tf_op jit(solution)/shard_map/prep/pallas_call | solution.py:193
  24.2 9.7 %all-to-all-start = ((bf16[64,8,1024]{2,1,0:T(8,128)(2,1)}), bf16[64,8,1024]{2,1,0:T(8,128)(2,1)}, u32[]{:S(2)}, u32[]{:S(2)}) async-start(bf16[64,8,1024]{2,1,0:T(8,128)(2,1)} %bitcast.15), calls=%async_computation | async-start | bytes 2097152 | tf_op jit(solution)/shard_map/all_to_all | solution.py:427
  33.8 0.0 all-gather.2.cloned.1.call-start
  33.9 8.1 %row_part.1 = (bf16[4,512,128]{2,1,0:T(8,128)(2,1)}, bf16[16,128]{1,0:T(8,128)(2,1)}) custom-call(bf16[4,512,1024]{2,1,0:T(8,128)(2,1)} %bitcast.14, bf16[1024,768]{1,0:T(8,128)(2,1)} %value_ref.5, bf16[1024,768]{1,0:T(8,128)(2,1)} %value_ref.5, bf16[1024,768]{1,0:T(8,128)(2,1)} %value_ref.5, bf16[512,1024]{1,0:T(8,128)(2,1)} %prep.1.after), custom_call_target="tpu_custom_call" | custom-call | bytes 1 | tf_op jit(solution)/shard_map/row_part/pallas_call | solution.py:223
  42.0 0.0 collective-permute-done.in0
  42.0 0.0 collective-permute-done.1.in1
  42.0 0.0 collective-permute-done.2.in2
  42.0 0.0 copy-start.2
  42.1 0.7 copy-done.2
  42.8 0.0 copy-start.3
  42.8 0.7 copy-done.3
  43.4 1.4 %collective-permute-start.3 = (bf16[3,128,256]{2,1,0:T(8,128)(2,1)S(1)}, bf16[3,128,256]{2,1,0:T(8,128)(2,1)S(1)}, u32[]{:S(2)}, u32[]{:S(2)}) collective-permute-start(bf16[3,128,256]{2,1,0:T(8,128)(2,1)S(1)} %get-tuple-element.21.refs_0_), channel_id=1, source_target_pairs={{0,8},{4,12},{8,16},{12,20},{16,24},{20,28},{24,0},{28,4},{32,40},... | collective-permute-start | bytes 589832 | tf_op jit(solution)/shard_map/ppermute | solution.py:403
  44.8 0.0 all-gather.2.cloned.1.call-update
  44.9 1.4 %collective-permute-start.4 = (bf16[3,128,256]{2,1,0:T(8,128)(2,1)S(1)}, bf16[3,128,256]{2,1,0:T(8,128)(2,1)S(1)}, u32[]{:S(2)}, u32[]{:S(2)}) collective-permute-start(bf16[3,128,256]{2,1,0:T(8,128)(2,1)S(1)} %get-tuple-element.21.refs_0_), channel_id=1, source_target_pairs={{0,24},{4,28},{8,0},{12,4},{16,8},{20,12},{24,16},{28,20},{32,56},... | collective-permute-start | bytes 589832 | tf_op jit(solution)/shard_map/ppermute | solution.py:403
  46.2 1.7 %collective-permute-start.5 = (bf16[3,128,256]{2,1,0:T(8,128)(2,1)S(1)}, bf16[3,128,256]{2,1,0:T(8,128)(2,1)S(1)}, u32[]{:S(2)}, u32[]{:S(2)}) collective-permute-start(bf16[3,128,256]{2,1,0:T(8,128)(2,1)S(1)} %get-tuple-element.21.refs_0_), channel_id=1, source_target_pairs={{0,16},{4,20},{8,24},{12,28},{16,0},{20,4},{24,8},{28,12},{32,48},... | collective-permute-start | bytes 589832 | tf_op jit(solution)/shard_map/ppermute | solution.py:403
  47.9 1.2 collective-permute-start.6
  49.1 1.5 %collective-permute-start.7 = (bf16[3,128,256]{2,1,0:T(8,128)(2,1)S(1)}, bf16[3,128,256]{2,1,0:T(8,128)(2,1)S(1)}, u32[]{:S(2)}, u32[]{:S(2)}) collective-permute-start(bf16[3,128,256]{2,1,0:T(8,128)(2,1)S(1)} %get-tuple-element.22.refs_4_), channel_id=1, source_target_pairs={{0,96},{4,100},{8,104},{12,108},{16,112},{20,116},{24,120},{28,124... | collective-permute-start | bytes 589832 | tf_op jit(solution)/shard_map/ppermute | solution.py:409
  50.6 2.1 %collective-permute-done.3.refs_1_ = bf16[3,128,256]{2,1,0:T(8,128)(2,1)S(1)} collective-permute-done((bf16[3,128,256]{2,1,0:T(8,128)(2,1)S(1)}, bf16[3,128,256]{2,1,0:T(8,128)(2,1)S(1)}, u32[]{:S(2)}, u32[]{:S(2)}) %collective-permute-start.3) | collective-permute-done | bytes 196640 | tf_op jit(solution)/shard_map/ppermute | solution.py:403
  52.6 2.4 %collective-permute-start.8 = (bf16[3,128,256]{2,1,0:T(8,128)(2,1)S(1)}, bf16[3,128,256]{2,1,0:T(8,128)(2,1)S(1)}, u32[]{:S(2)}, u32[]{:S(2)}) collective-permute-start(bf16[3,128,256]{2,1,0:T(8,128)(2,1)S(1)} %get-tuple-element.22.refs_4_), channel_id=1, source_target_pairs={{0,64},{4,68},{8,72},{12,76},{16,80},{20,84},{24,88},{28,92},{32,9... | collective-permute-start | bytes 589832 | tf_op jit(solution)/shard_map/ppermute | solution.py:409
  55.0 2.2 %pick_columns.1.w_ref.refs_8_ = bf16[1024,384]{1,0:T(8,128)(2,1)} custom-call(bf16[1024,768]{1,0:T(8,128)(2,1)} %value_ref.5, bf16[1024,768]{1,0:T(8,128)(2,1)} %value_ref.5, bf16[1024,768]{1,0:T(8,128)(2,1)} %value_ref.5), custom_call_target="tpu_custom_call" | custom-call | flops 10000000000 | bytes 1048576 | tf_op jit(solution)/shard_map/pick_columns/pallas_call | solution.py:156
  57.3 0.0 collective-permute-done.4.refs_2_
  57.3 0.0 collective-permute-done.5.refs_3_
  57.3 0.0 collective-permute-done.6.refs_5_
  57.3 0.0 collective-permute-done.7.refs_6_
  57.3 3.2 %collective-permute-done.8.refs_7_ = bf16[3,128,256]{2,1,0:T(8,128)(2,1)S(1)} collective-permute-done((bf16[3,128,256]{2,1,0:T(8,128)(2,1)S(1)}, bf16[3,128,256]{2,1,0:T(8,128)(2,1)S(1)}, u32[]{:S(2)}, u32[]{:S(2)}) %collective-permute-start.8) | collective-permute-done | bytes 196640 | tf_op jit(solution)/shard_map/ppermute | solution.py:409
  60.5 0.0 copy-start.1
  60.5 1.1 copy-done.1
  61.6 1.2 stack.21.near
  62.8 1.2 collective-permute-start.9
  64.0 0.0 all-to-all-done
  64.0 3.7 %own_part.1 = (bf16[512,1024]{1,0:T(8,128)(2,1)}, bf16[512,128]{1,0:T(8,128)(2,1)}) custom-call(bf16[512,1024]{1,0:T(8,128)(2,1)} %bitcast.6.got_ref, bf16[1024,384]{1,0:T(8,128)(2,1)} %pick_columns.1.w_ref.refs_8_), custom_call_target="tpu_custom_call" | custom-call | flops 999999995904 | bytes 4194304 | tf_op jit(solution)/shard_map/own_part/pallas_call | solution.py:261
  67.7 0.0 collective-permute-done.9.far
  67.7 9.2 %column_part.1 = bf16[64,4,8,256]{3,2,1,0:T(8,128)(2,1)} custom-call(s32[4]{0:T(128)} %pad_add_fusion.meta, bf16[512,1024]{1,0:T(8,128)(2,1)} %get-tuple-element.15.held, bf16[512,128]{1,0:T(8,128)(2,1)} %get-tuple-element.16.own, bf16[256,1024]{1,0:T(8,128)(2,1)} %own_ref.1, bf16[2,4,3,128,256]{4,3,2,1,0:T(8,128)(2,1)} %stack.21.near, ...), custom_call_target="tpu_custom_call" | custom-call | flops 3000000000 | bytes 6291456 | tf_op jit(solution)/shard_map/column_part/pallas_call | solution.py:318
  76.9 8.8 %all-to-all-start.1 = ((bf16[256,8,256]{2,1,0:T(8,128)(2,1)}), bf16[256,8,256]{2,1,0:T(8,128)(2,1)S(1)}, u32[]{:S(2)}, u32[]{:S(2)}) async-start(bf16[256,8,256]{2,1,0:T(8,128)(2,1)} %bitcast.16), calls=%async_computation.1 | async-start | bytes 2097152 | tf_op jit(solution)/shard_map/all_to_all | solution.py:446
  85.7 5.0 %all-gather.2.cloned.1.call-done = bf16[4,2048,128]{2,1,0:T(8,128)(2,1)} async-done(((bf16[1,2048,128]{2,1,0:T(8,128)(2,1)}), bf16[4,2048,128]{2,1,0:T(8,128)(2,1)}) %all-gather.2.cloned.1.call-update) | async-done | bytes 2097168 | tf_op jit(solution)/shard_map/all_gather | solution.py:428
  90.7 5.1 %mix.1.rows_ref = f32[4,4,128,256]{3,2,1,0:T(8,128)} custom-call(s32[4]{0:T(128)} %pad_add_fusion.meta, bf16[4,4,4,128,128]{4,3,2,1,0:T(8,128)(2,1)} %bitcast.18, bf16[256,1024]{1,0:T(8,128)(2,1)} %own_ref.1, bf16[384,256]{1,0:T(8,128)(2,1)} %copy-done.3), custom_call_target="tpu_custom_call" | custom-call | flops 2000000000 | bytes 5242880 | tf_op jit(solution)/shard_map/mix/pallas_call | solution.py:347
  95.8 24.1 %all-to-all-done.1 = bf16[256,8,256]{2,1,0:T(8,128)(2,1)S(1)} async-done(((bf16[256,8,256]{2,1,0:T(8,128)(2,1)}), bf16[256,8,256]{2,1,0:T(8,128)(2,1)S(1)}, u32[]{:S(2)}, u32[]{:S(2)}) %all-to-all-start.1) | async-done | bytes 1048608 | tf_op jit(solution)/shard_map/all_to_all | solution.py:446
  120.0 0.0 copy-start
  120.0 1.6 %copy-done = f32[4,4,128,256]{3,2,1,0:T(8,128)S(1)} copy-done((f32[4,4,128,256]{3,2,1,0:T(8,128)S(1)}, f32[4,4,128,256]{3,2,1,0:T(8,128)}, u32[]{:S(2)}) %copy-start) | copy-done | bytes 2097176
  121.6 2.3 %join.1 = bf16[4,4,128,256]{3,2,1,0:T(8,128)(2,1)} custom-call(bf16[64,4,8,256]{3,2,1,0:T(8,128)(2,1)S(1)} %bitcast.12, f32[4,4,128,256]{3,2,1,0:T(8,128)S(1)} %copy-done), custom_call_target="tpu_custom_call" | custom-call | flops 100000000 | bytes 4194304 | tf_op jit(solution)/shard_map/join/pallas_call | solution.py:385
  (1 shorter events, 0.0 us)
Async XLA Ops:
  9.8 32.3 %collective-permute-start = (bf16[128,768]{1,0:T(8,128)(2,1)}, bf16[128,768]{1,0:T(8,128)(2,1)S(1)}, u32[]{:S(2)}, u32[]{:S(2)}) collective-permute-start(bf16[128,768]{1,0:T(8,128)(2,1)} %get-tuple-element.17), channel_id=1, source_target_pairs={{0,2},{1,3},{2,0},{3,1},{4,6},{5,7},{6,4},{7,5},{8,10},{9,11},{10,... | collective-permute-start | bytes 589832 | tf_op jit(solution)/shard_map/ppermute | solution.py:399
  17.5 24.5 %collective-permute-start.1 = (bf16[128,768]{1,0:T(8,128)(2,1)}, bf16[128,768]{1,0:T(8,128)(2,1)S(1)}, u32[]{:S(2)}, u32[]{:S(2)}) collective-permute-start(bf16[128,768]{1,0:T(8,128)(2,1)} %get-tuple-element.18), channel_id=1, source_target_pairs={{0,1},{1,2},{2,3},{3,0},{4,5},{5,6},{6,7},{7,4},{8,9},{9,10},{10,1... | collective-permute-start | bytes 589832 | tf_op jit(solution)/shard_map/ppermute | solution.py:399
  18.7 23.3 %collective-permute-start.2 = (bf16[128,768]{1,0:T(8,128)(2,1)}, bf16[128,768]{1,0:T(8,128)(2,1)S(1)}, u32[]{:S(2)}, u32[]{:S(2)}) collective-permute-start(bf16[128,768]{1,0:T(8,128)(2,1)} %get-tuple-element.19), channel_id=1, source_target_pairs={{0,3},{1,0},{2,1},{3,2},{4,7},{5,4},{6,5},{7,6},{8,11},{9,8},{10,9... | collective-permute-start | bytes 589832 | tf_op jit(solution)/shard_map/ppermute | solution.py:399
  24.2 39.8 %all-to-all-start = ((bf16[64,8,1024]{2,1,0:T(8,128)(2,1)}), bf16[64,8,1024]{2,1,0:T(8,128)(2,1)}, u32[]{:S(2)}, u32[]{:S(2)}) async-start(bf16[64,8,1024]{2,1,0:T(8,128)(2,1)} %bitcast.15), calls=%async_computation | async-start | bytes 2097152 | tf_op jit(solution)/shard_map/all_to_all | solution.py:427
  33.8 56.9 %all-gather.2.cloned.1.call-start = ((), (), s32[]{:S(2)}) async-start(), calls=%async_computation.2 | async-start | bytes 2621440 | tf_op jit(solution)/shard_map/all_gather | solution.py:428
  42.0 0.7 copy-start.2
  42.8 0.7 copy-start.3
  43.4 9.2 %collective-permute-start.3 = (bf16[3,128,256]{2,1,0:T(8,128)(2,1)S(1)}, bf16[3,128,256]{2,1,0:T(8,128)(2,1)S(1)}, u32[]{:S(2)}, u32[]{:S(2)}) collective-permute-start(bf16[3,128,256]{2,1,0:T(8,128)(2,1)S(1)} %get-tuple-element.21.refs_0_), channel_id=1, source_target_pairs={{0,8},{4,12},{8,16},{12,20},{16,24},{20,28},{24,0},{28,4},{32,40},... | collective-permute-start | bytes 589832 | tf_op jit(solution)/shard_map/ppermute | solution.py:403
  44.9 12.4 %collective-permute-start.4 = (bf16[3,128,256]{2,1,0:T(8,128)(2,1)S(1)}, bf16[3,128,256]{2,1,0:T(8,128)(2,1)S(1)}, u32[]{:S(2)}, u32[]{:S(2)}) collective-permute-start(bf16[3,128,256]{2,1,0:T(8,128)(2,1)S(1)} %get-tuple-element.21.refs_0_), channel_id=1, source_target_pairs={{0,24},{4,28},{8,0},{12,4},{16,8},{20,12},{24,16},{28,20},{32,56},... | collective-permute-start | bytes 589832 | tf_op jit(solution)/shard_map/ppermute | solution.py:403
  46.2 11.0 %collective-permute-start.5 = (bf16[3,128,256]{2,1,0:T(8,128)(2,1)S(1)}, bf16[3,128,256]{2,1,0:T(8,128)(2,1)S(1)}, u32[]{:S(2)}, u32[]{:S(2)}) collective-permute-start(bf16[3,128,256]{2,1,0:T(8,128)(2,1)S(1)} %get-tuple-element.21.refs_0_), channel_id=1, source_target_pairs={{0,16},{4,20},{8,24},{12,28},{16,0},{20,4},{24,8},{28,12},{32,48},... | collective-permute-start | bytes 589832 | tf_op jit(solution)/shard_map/ppermute | solution.py:403
  47.9 9.4 %collective-permute-start.6 = (bf16[3,128,256]{2,1,0:T(8,128)(2,1)S(1)}, bf16[3,128,256]{2,1,0:T(8,128)(2,1)S(1)}, u32[]{:S(2)}, u32[]{:S(2)}) collective-permute-start(bf16[3,128,256]{2,1,0:T(8,128)(2,1)S(1)} %get-tuple-element.22.refs_4_), channel_id=1, source_target_pairs={{0,32},{4,36},{8,40},{12,44},{16,48},{20,52},{24,56},{28,60},{32,6... | collective-permute-start | bytes 589832 | tf_op jit(solution)/shard_map/ppermute | solution.py:409
  49.1 8.2 %collective-permute-start.7 = (bf16[3,128,256]{2,1,0:T(8,128)(2,1)S(1)}, bf16[3,128,256]{2,1,0:T(8,128)(2,1)S(1)}, u32[]{:S(2)}, u32[]{:S(2)}) collective-permute-start(bf16[3,128,256]{2,1,0:T(8,128)(2,1)S(1)} %get-tuple-element.22.refs_4_), channel_id=1, source_target_pairs={{0,96},{4,100},{8,104},{12,108},{16,112},{20,116},{24,120},{28,124... | collective-permute-start | bytes 589832 | tf_op jit(solution)/shard_map/ppermute | solution.py:409
  52.6 7.8 %collective-permute-start.8 = (bf16[3,128,256]{2,1,0:T(8,128)(2,1)S(1)}, bf16[3,128,256]{2,1,0:T(8,128)(2,1)S(1)}, u32[]{:S(2)}, u32[]{:S(2)}) collective-permute-start(bf16[3,128,256]{2,1,0:T(8,128)(2,1)S(1)} %get-tuple-element.22.refs_4_), channel_id=1, source_target_pairs={{0,64},{4,68},{8,72},{12,76},{16,80},{20,84},{24,88},{28,92},{32,9... | collective-permute-start | bytes 589832 | tf_op jit(solution)/shard_map/ppermute | solution.py:409
  60.5 1.1 copy-start.1
  62.8 4.9 %collective-permute-start.9 = (bf16[2,4,3,128,256]{4,3,2,1,0:T(8,128)(2,1)}, bf16[2,4,3,128,256]{4,3,2,1,0:T(8,128)(2,1)}, u32[]{:S(2)}, u32[]{:S(2)}) collective-permute-start(bf16[2,4,3,128,256]{4,3,2,1,0:T(8,128)(2,1)} %stack.21.near), channel_id=1, source_target_pairs={{0,4},{4,0},{8,12},{12,8},{16,20},{20,16},{24,28},{28,24},{32,36},... | collective-permute-start | bytes 4718600 | tf_op jit(solution)/shard_map/ppermute | solution.py:415
  76.9 43.0 %all-to-all-start.1 = ((bf16[256,8,256]{2,1,0:T(8,128)(2,1)}), bf16[256,8,256]{2,1,0:T(8,128)(2,1)S(1)}, u32[]{:S(2)}, u32[]{:S(2)}) async-start(bf16[256,8,256]{2,1,0:T(8,128)(2,1)} %bitcast.16), calls=%async_computation.1 | async-start | bytes 2097152 | tf_op jit(solution)/shard_map/all_to_all | solution.py:446
  120.0 1.6 %copy-start = (f32[4,4,128,256]{3,2,1,0:T(8,128)S(1)}, f32[4,4,128,256]{3,2,1,0:T(8,128)}, u32[]{:S(2)}) copy-start(f32[4,4,128,256]{3,2,1,0:T(8,128)} %mix.1.rows_ref) | copy-start | bytes 6291460
Sparse Core Ops, SparseCore 0:
  45.0 45.6 all-gather.1

commit v6 on v3

v6 whole, which is shorter than its diff:
```python
import jax
import jax.numpy as jnp
from jax import lax
from jax.experimental import pallas as pl
from jax.experimental.pallas import tpu as pltpu
from jax.sharding import PartitionSpec as P

D = 1024
HEADS = 16
C = 512
GROUPS = 4
DIM = 64
HALF = 128
ROWS_LOCAL = 4
BLOCK = 128
BF = jnp.bfloat16
F32 = jnp.float32
VMEM = pltpu.VMEM
MIB = 1 << 20
ORDER = (3, 1, 2)
STEPS = (2, 3, 1)
WIDE = 5 * HALF
BOTH = ("rows", "heads")
SCALE = 0.125 * 1.4426950408889634


def whole():
    return pl.BlockSpec(memory_space=VMEM)


def anywhere():
    return pl.BlockSpec(memory_space=pl.ANY)


def smem():
    return pl.BlockSpec(memory_space=pltpu.SMEM)


def one_hot(source_of):
    out_at = lax.broadcasted_iota(jnp.int32, (BLOCK, BLOCK), 0)
    in_at = lax.broadcasted_iota(jnp.int32, (BLOCK, BLOCK), 1)
    return (in_at == source_of(out_at)).astype(F32).astype(BF)


def move(pick, data):
    return jnp.dot(pick, data, preferred_element_type=F32).astype(BF)


def causal():
    at_query = lax.broadcasted_iota(jnp.int32, (2 * BLOCK, BLOCK), 0) % BLOCK
    return lax.broadcasted_iota(jnp.int32, (2 * BLOCK, BLOCK), 1) <= at_query


def attend(qkv, allowed, store):
    length = qkv.shape[0]
    first = lax.broadcasted_iota(jnp.int32, (1, HALF), 1) < DIM
    query = qkv[:, :HALF]
    query_a = jnp.where(first, query, 0.0).astype(BF)
    query_b = jnp.where(first, 0.0, query).astype(BF)
    key = qkv[:, HALF : 2 * HALF].astype(BF)
    value = qkv[:, 2 * HALF :].astype(BF)
    value = jnp.concatenate([value, jnp.ones((length, HALF), BF)], axis=1)
    for block in range(length // BLOCK):
        lo = block * BLOCK
        hi = lo + BLOCK
        both = jnp.concatenate([query_a[lo:hi], query_b[lo:hi]], axis=0)
        scores = lax.dot_general(
            both, key[:hi], (((1,), (1,)), ((), ())), preferred_element_type=F32
        )
        pieces = [scores[:, n * BLOCK : (n + 1) * BLOCK] for n in range(block)]
        pieces.append(jnp.where(allowed, scores[:, lo:], F32(-1e30)))
        top = pieces[0]
        for piece in pieces[1:]:
            top = jnp.maximum(top, piece)
        top = jnp.max(top, axis=-1, keepdims=True)
        expo = [jnp.exp2((piece - top) * F32(SCALE)).astype(BF) for piece in pieces]
        out = jnp.dot(jnp.concatenate(expo, axis=1), value[:hi], preferred_element_type=F32)
        out = jnp.where(jnp.concatenate([first, first], axis=1), out[:BLOCK], out[BLOCK:])
        store(lo, (out[:, :HALF] / out[:, HALF:]).astype(BF))


def call(kernel, name, flops=0, moved=MIB, vmem=56 * MIB, **options):
    return pl.pallas_call(
        kernel,
        compiler_params=pltpu.CompilerParams(vmem_limit_bytes=vmem),
        cost_estimate=pl.CostEstimate(flops=flops, bytes_accessed=moved, transcendentals=0),
        name=name,
        **options,
    )


def like(*shape):
    return jax.ShapeDtypeStruct(shape, BF)


def cut_kernel(meta, query_ref, key_ref, value_ref, mix_ref, out_ref):
    out_ref[:, :HALF] = query_ref[...]
    out_ref[:, HALF : 2 * HALF] = key_ref[...]
    out_ref[:, 2 * HALF : 3 * HALF] = value_ref[...]
    out_ref[:, 3 * HALF : 4 * HALF] = mix_ref[HALF:, :]
    out_ref[:, 4 * HALF :] = mix_ref[:HALF, :]


def cut(meta, w_qkv, w_out):
    def part(n, axis):
        return pl.BlockSpec((BLOCK, HALF), lambda b, meta: (meta[axis] * 2 + meta[2], 2 * n + 1))

    return call(
        cut_kernel,
        "cut",
        grid_spec=pltpu.PrefetchScalarGridSpec(
            num_scalar_prefetch=1,
            grid=(1,),
            in_specs=[
                part(0, 1),
                part(1, 1),
                part(2, 3),
                pl.BlockSpec((256, BLOCK), lambda b, meta: (0, meta[3] * 2 + meta[2])),
            ],
            out_specs=pl.BlockSpec((BLOCK, WIDE), lambda b, meta: (0, 0)),
        ),
        out_shape=like(BLOCK, WIDE),
    )(meta, w_qkv, w_qkv, w_qkv, w_out)


def mid_kernel(in0, in1, in2, x_ref, y_ref):
    for n, ref in enumerate((in0, in1, in2)):
        x_ref[n] = ref[:, :256]
        y_ref[n] = ref[:, 256:]


def mid(parts):
    return call(
        mid_kernel,
        "mid",
        flops=10**12,
        vmem=16 * MIB,
        in_specs=[whole()] * 3,
        out_specs=[whole()] * 2,
        out_shape=[like(3, BLOCK, 256), like(3, BLOCK, WIDE - 256)],
    )(*parts)


def stack_kernel(*refs):
    out_ref = refs[-1]
    for d in range(4):
        for n in range(3):
            out_ref[n, d, :, :256] = refs[d][n]
            out_ref[n, d, :, 256:] = refs[4 + d][n]


def stack(parts, after):
    return call(
        stack_kernel,
        "stack",
        flops=10**9,
        vmem=16 * MIB,
        in_specs=[whole()] * 8 + [anywhere()] * len(after),
        out_specs=whole(),
        out_shape=like(3, 4, BLOCK, WIDE),
    )(*parts, *after)


def prep_kernel(meta, sig_ref, out_ref):
    pick = one_hot(lambda o: ((o // 2) % 4) * 32 + (o // 8) * 2 + o % 2)
    for b in range(2):
        part = sig_ref[:, b * 32 : (b + 1) * 32, :].reshape(BLOCK, D)
        out_ref[b * BLOCK : (b + 1) * BLOCK, :] = move(pick, part)


def prep(meta, sig):
    return call(
        prep_kernel,
        "prep",
        flops=2 * C * D * BLOCK,
        moved=2 * MIB,
        grid_spec=pltpu.PrefetchScalarGridSpec(
            num_scalar_prefetch=1,
            grid=(2,),
            in_specs=[pl.BlockSpec((4, 64, D), lambda b, meta: (0, meta[0] * 2 + b, 0))],
            out_specs=pl.BlockSpec((256, D), lambda b, meta: (b, 0)),
        ),
        out_shape=like(C, D),
    )(meta, sig)


def row_kernel(sig_ref, query_ref, key_ref, value_ref, after, out_ref, token_ref, held):
    r = pl.program_id(0)
    weight = jnp.concatenate([query_ref[...], key_ref[...], value_ref[...]], axis=1)
    qkv = jnp.dot(sig_ref[0], weight, preferred_element_type=F32)

    def store(lo, out):
        held[r, lo : lo + BLOCK, :] = out

    attend(qkv, causal(), store)

    @pl.when(r == ROWS_LOCAL - 1)
    def _():
        token_ref[...] = jnp.zeros_like(token_ref)
        pick = one_hot(lambda o: ((o // 2) % 4) * 32 + (o // 8) * 2 + o % 2)
        for j in range(GROUPS):
            for b in range(4):
                lo = j * BLOCK + b * 32
                part = held[:, lo : lo + 32, :].reshape(BLOCK, HALF)
                out_ref[b * 16 : (b + 1) * 16, j] = move(pick, part).reshape(16, 8, HALF)


def row_part(sig, w_qkv, after):
    def part(n):
        return pl.BlockSpec((D, HALF), lambda r: (0, 2 * n))

    return call(
        row_kernel,
        "row_part",
        flops=10**10,
        moved=1,
        grid=(ROWS_LOCAL,),
        in_specs=[
            pl.BlockSpec((1, C, D), lambda r: (r, 0, 0)),
            part(0),
            part(1),
            part(2),
            anywhere(),
        ],
        out_specs=[
            pl.BlockSpec((64, GROUPS, 8, HALF), lambda r: (0, 0, 0, 0)),
            pl.BlockSpec((16, HALF), lambda r: (0, 0)),
        ],
        out_shape=[like(64, GROUPS, 8, HALF), like(16, HALF)],
        scratch_shapes=[VMEM((ROWS_LOCAL, C, HALF), BF)],
    )(sig, w_qkv, w_qkv, w_qkv, after)


def columns_of(qkv, allowed, keep):
    for c in range(2):

        def store(lo, out):
            keep(c * 256 + lo, out)

        attend(qkv[c * 256 : (c + 1) * 256], allowed, store)


def own_kernel(meta, got_ref, w_qkv, by_x, by_y, out_ref, held, weight, sems):
    copies = [
        pltpu.make_async_copy(
            w_qkv.at[:, 256 * n + HALF : 256 * (n + 1)],
            weight.at[:, HALF * n : HALF * (n + 1)],
            sems.at[n],
        )
        for n in range(3)
    ]
    for copy in copies:
        copy.start()
    pick = one_hot(lambda o: (o % 64) * 2 + o // 64)
    for b in range(4):
        moved = move(pick, got_ref[b * BLOCK : (b + 1) * BLOCK, :])
        held[b * 64 : b * 64 + 64, :] = moved[:64]
        held[256 + b * 64 : 256 + b * 64 + 64, :] = moved[64:]
    core = meta[2]
    for n, d in enumerate((0,) + STEPS):
        for far, on in enumerate((core, 1 - core)):
            lo = (4 * far + n) * BLOCK
            for at, out in ((meta[1], by_x), (meta[3], by_y)):
                source = pl.multiple_of((lax.rem(at + 4 - d, 4) * 2 + on) * BLOCK, BLOCK)
                out[:, lo : lo + BLOCK] = held[:, pl.ds(source, BLOCK)]

    def keep(lo, out):
        out_ref[lo : lo + BLOCK, :] = out

    for copy in copies:
        copy.wait()
    qkv = jnp.dot(held[...], weight[...], preferred_element_type=F32)
    columns_of(qkv, causal(), keep)


def own_part(meta, got, w_qkv):
    return call(
        own_kernel,
        "own_part",
        flops=10**12,
        moved=4 * MIB,
        vmem=20 * MIB,
        in_specs=[smem(), whole(), anywhere()],
        out_specs=[whole()] * 3,
        out_shape=[like(C, D), like(C, D), like(C, HALF)],
        scratch_shapes=[
            VMEM((C, D), BF),
            VMEM((D, 3 * HALF), BF),
            pltpu.SemaphoreType.DMA((3,)),
        ],
    )(meta, got, w_qkv)


def column_kernel(by_x, by_y, own, near, far, out_ref, outs):
    allowed = causal()
    outs[:, :HALF] = own[...]
    half = 4 * BLOCK
    for n in range(3):

        def keep(lo, out):
            outs[lo : lo + BLOCK, (n + 1) * HALF : (n + 2) * HALF] = out

        def product(left, lanes):
            return jnp.dot(
                left[:, :half],
                near[n, :, :, lanes].reshape(half, -1),
                preferred_element_type=F32,
            ) + jnp.dot(
                left[:, half:],
                far[n, :, :, lanes].reshape(half, -1),
                preferred_element_type=F32,
            )

        qkv = jnp.concatenate(
            [product(by_x, slice(0, 256)), product(by_y, slice(256, 256 + HALF))], axis=1
        )
        columns_of(qkv, allowed, keep)
    back = one_hot(lambda o: (o % 2) * 64 + o // 2)
    for b in range(4):
        both = jnp.concatenate(
            [outs[b * 64 : b * 64 + 64, :], outs[256 + b * 64 : 256 + b * 64 + 64, :]], axis=0
        )
        out_ref[b * BLOCK : (b + 1) * BLOCK, :] = move(back, both)


def column_part(by_x, by_y, own, near, far):
    return call(
        column_kernel,
        "column_part",
        flops=3 * 10**9,
        moved=6 * MIB,
        vmem=20 * MIB,
        in_specs=[whole()] * 5,
        out_specs=whole(),
        out_shape=like(C, C),
        scratch_shapes=[VMEM((C, C), BF)],
    )(by_x, by_y, own, near, far)


def mix_kernel(meta, columns, rows, w_out, near, far, out_ref):
    core = meta[2]
    left = jnp.concatenate(
        [columns[...]]
        + [
            rows[:, lax.rem(meta[0] + GROUPS - k, GROUPS)].reshape(C, HALF)
            for k in (0,) + ORDER
        ],
        axis=1,
    )
    for n, d in enumerate((0,) + STEPS):
        j = lax.rem(meta[3] + 4 - d, 4)
        own = w_out[:, pl.ds(pl.multiple_of(j * 256, 256), 256)]
        parts = []
        for lo, mine in ((3 * HALF, own[HALF:]), (4 * HALF, own[:HALF])):
            here = near[:, n, :, lo : lo + HALF].reshape(3 * BLOCK, HALF)
            there = far[:, n, :, lo : lo + HALF].reshape(3 * BLOCK, HALF)
            low = jnp.where(core == 0, here, there)
            high = jnp.where(core == 0, there, here)
            parts += [mine, jnp.concatenate([low, high], axis=1)]
        mixed = jnp.dot(left, jnp.concatenate(parts, axis=0), preferred_element_type=F32)
        out_ref[:, j] = mixed.astype(BF).reshape(64, 8, 256)


def mix(meta, columns, rows, w_out, near, far):
    return call(
        mix_kernel,
        "mix",
        flops=10**9,
        moved=6 * MIB,
        vmem=20 * MIB,
        in_specs=[smem()] + [whole()] * 5,
        out_specs=whole(),
        out_shape=like(64, GROUPS, 8, 256),
    )(meta, columns, rows, w_out, near, far)


def join_kernel(got_ref, out_ref):
    pick = one_hot(lambda o: ((o // 2) % 16) * 8 + (o // 32) * 2 + o % 2)
    for b in range(4):
        moved = move(pick, got_ref[b * 16 : (b + 1) * 16, 0].reshape(BLOCK, 256))
        for r in range(ROWS_LOCAL):
            out_ref[r, 0, b * 32 : (b + 1) * 32] = moved[r * 32 : (r + 1) * 32]


def join(got):
    return call(
        join_kernel,
        "join",
        flops=10**8,
        moved=4 * MIB,
        vmem=16 * MIB,
        grid=(GROUPS,),
        in_specs=[pl.BlockSpec((64, 1, 8, 256), lambda j: (0, j, 0, 0))],
        out_specs=pl.BlockSpec((ROWS_LOCAL, 1, BLOCK, 256), lambda j: (0, j, 0, 0)),
        out_shape=like(ROWS_LOCAL, GROUPS, BLOCK, 256),
    )(got)


def to_group(data, k):
    return lax.ppermute(data, "heads", [(j, (j + k) % GROUPS) for j in range(GROUPS)])


def along_x(data, d):
    return lax.ppermute(
        data, "rows", [(i, i // 8 * 8 + (i // 2 % 4 + d) % 4 * 2 + i % 2) for i in range(64)]
    )


def along_y(data, d):
    return lax.ppermute(
        data, "rows", [(i, i // 32 * 32 + (i // 8 % 4 + d) % 4 * 8 + i % 8) for i in range(64)]
    )


def other_core(data):
    return lax.ppermute(data, "rows", [(i, i ^ 1) for i in range(64)])


def local(signal, w_qkv, w_out):
    i = lax.axis_index("rows")
    g = lax.axis_index("heads")
    meta = jnp.stack([g, i // 2 % 4, i % 2, i // 8 % 4]).astype(jnp.int32)
    sig = signal.reshape(ROWS_LOCAL, C, D)

    send = prep(meta, sig)
    own_rows, rows_done = row_part(sig, w_qkv, send)
    got = lax.all_to_all(
        send.reshape(64, 8, D), "rows", split_axis=0, concat_axis=0, tiled=True
    ).reshape(C, D)
    rows = lax.all_to_all(
        own_rows.reshape(64 * GROUPS, 8, HALF), BOTH, split_axis=0, concat_axis=0, tiled=True
    ).reshape(64, GROUPS, 8, HALF)

    mine = cut(meta, w_qkv, w_out)
    others_x, others_y = mid([to_group(mine, k) for k in ORDER])
    near = stack(
        [others_x]
        + [along_x(others_x, d) for d in STEPS]
        + [others_y]
        + [along_y(others_y, d) for d in STEPS],
        [rows_done, got],
    )
    far = other_core(near)

    by_x, by_y, own = own_part(meta, got, w_qkv)
    columns = column_part(by_x, by_y, own, near, far)
    mixed = mix(meta, columns, rows, w_out, near, far).reshape(64 * GROUPS, 8, 256)
    back = lax.all_to_all(mixed, BOTH, split_axis=0, concat_axis=0, tiled=True)
    return join(back.reshape(64, GROUPS, 8, 256)).reshape(ROWS_LOCAL * C, 256)


def solution(mesh):
    return jax.shard_map(
        local,
        mesh=mesh,
        in_specs=(P("rows", None), P(None, "heads"), P("heads", None)),
        out_specs=P("rows", "heads"),
        check_vma=False,
    )
```

time: 150 us -> 130 us (0.87)
  blocking collectives: 0 us -> 37.8 us
  waiting for transfers between devices: 46.2 us -> 16.4 us
  between operations: 13.6 us -> 0.13 us
  starting transfers between devices: 49 us -> 42.9 us
  Pallas kernels: 36.6 us -> 30.9 us
  local copies, waits for them, and re-layouts: 3.86 us -> 0.68 us
    ppermute x6 -> x3, waiting for transfers between devices: 39.2 us -> 0.01 us  [to_group(): lax.ppermute(data, 'heads', [(j, (j + k) % GROUPS) for j in range(GROUPS)])]
    all_to_all x0 -> x1, blocking collectives: none -> 37.8 us  [local(): back = lax.all_to_all(mixed, BOTH, split_axis=0, concat_axis=0, tiled=True)]
    ppermute x6 -> x3, starting transfers between devices: 21.3 us -> 11.3 us  [to_group(): lax.ppermute(data, 'heads', [(j, (j + k) % GROUPS) for j in range(GROUPS)])]
    pallas_call x6 -> x7, Pallas kernels: 31 us -> 25.5 us  [the longest x1 8.56 us: row_part(): call(row_kernel, 'row_part', flops=10 ** 10, moved=1, grid=(ROWS_LOCAL,),...]
    all_to_all x2, waiting for transfers between devices: 0.01 us -> 4.79 us  [the longest x1 4.79 us: local(): lax.all_to_all(own_rows.reshape(64 * GROUPS, 8, HALF), BOTH, split_axis=0...]
    all_to_all x2, starting transfers between devices: 15 us -> 19.7 us  [the longest x1 10.1 us: local(): lax.all_to_all(own_rows.reshape(64 * GROUPS, 8, HALF), BOTH, split_axis=0...]
    ppermute x3, waiting for transfers between devices: 6.9 us -> 11.4 us  [along_x(): lax.ppermute(data, 'rows', [(i, i // 8 * 8 + (i // 2 % 4 + d) % 4 * 2 + i...]
    unnamed x32 -> x8, local copies, waits for them, and re-layouts: 3.86 us -> 0.68 us
  transfers between devices with their start and end apart: 16 -> 12, of which waited for: 2 -> 3; matrix products, arithmetic and copies ran while one was open for 0% -> 0% of each run, Pallas kernels for 19% -> 18%
where the time goes in v6:
time: 130 us; the launch traced here: 129 us
  starting transfers between devices  42.9 us (33%)
  blocking collectives  37.8 us (29%)
  Pallas kernels  30.9 us (24%)
  waiting for transfers between devices  16.4 us (13%)
    all_to_all x1, blocking collectives, local(): back = lax.all_to_all(mixed, BOTH, split_axis=0, concat_axis=0, tiled=True)  37.8 us
    ppermute x3, waiting for transfers between devices, along_x(): lax.ppermute(data, 'rows', [(i, i // 8 * 8 + (i // 2 % 4 + d) % 4 * 2 + i...  11.4 us
    ppermute x3, starting transfers between devices, to_group(): lax.ppermute(data, 'heads', [(j, (j + k) % GROUPS) for j in range(GROUPS)])  11.3 us
    all_to_all x1, starting transfers between devices, local(): lax.all_to_all(own_rows.reshape(64 * GROUPS, 8, HALF), BOTH, split_axis=0...  10.1 us
    all_to_all x1, starting transfers between devices, local(): lax.all_to_all(send.reshape(64, 8, D), 'rows', split_axis=0, concat_axis=...  9.66 us
    pallas_call x1, Pallas kernels, row_part(): call(row_kernel, 'row_part', flops=10 ** 10, moved=1, grid=(ROWS_LOCAL,),...  8.56 us
    pallas_call x1, Pallas kernels, column_part(): call(column_kernel, 'column_part', flops=3 * 10 ** 9, moved=6 * MIB, vmem...  5.94 us
    ppermute x3, starting transfers between devices, along_y(): lax.ppermute(data, 'rows', [(i, i // 32 * 32 + (i // 8 % 4 + d) % 4 * 8 +...  5.25 us
  transfers between devices with their start and end apart: 12, of which 3 were waited for; matrix products, arithmetic and copies ran while one was open for 0% of the time, Pallas kernels for 18%

profile of v6, /device:TPU:1, one launch (start us, length us, event | category | flops | bytes accessed | tf_op | source)
XLA Modules:
  0.0 129.5 jit_solution(2222206138950143034)
XLA Ops:
  0.0 0.7 pad_add_fusion.meta
  0.7 2.3 %cut.1 = bf16[128,640]{1,0:T(8,128)(2,1)} custom-call(s32[4]{0:T(128)} %pad_add_fusion.meta, bf16[1024,768]{1,0:T(8,128)(2,1)} %value_ref.3, bf16[1024,768]{1,0:T(8,128)(2,1)} %value_ref.3, bf16[1024,768]{1,0:T(8,128)(2,1)} %value_ref.3, bf16[256,1024]{1,0:T(8,128)(2,1)} %w_out.1), custom_call_target="tpu_custom_call" | custom-call | bytes 1048576 | tf_op jit(solution)/shard_map/cut/pallas_call | solution.py:108
  2.9 7.7 %collective-permute-start.2 = (bf16[128,640]{1,0:T(8,128)(2,1)}, bf16[128,640]{1,0:T(8,128)(2,1)S(1)}, u32[]{:S(2)}, u32[]{:S(2)}) collective-permute-start(bf16[128,640]{1,0:T(8,128)(2,1)} %cut.1), channel_id=1, source_target_pairs={{0,2},{1,3},{2,0},{3,1},{4,6},{5,7},{6,4},{7,5},{8,10},{9,11},{10,... | collective-permute-start | bytes 491528 | tf_op jit(solution)/shard_map/ppermute | solution.py:400
  10.7 1.2 collective-permute-start.1
  11.9 2.4 %collective-permute-start = (bf16[128,640]{1,0:T(8,128)(2,1)}, bf16[128,640]{1,0:T(8,128)(2,1)S(1)}, u32[]{:S(2)}, u32[]{:S(2)}) collective-permute-start(bf16[128,640]{1,0:T(8,128)(2,1)} %cut.1), channel_id=1, source_target_pairs={{0,3},{1,0},{2,1},{3,2},{4,7},{5,4},{6,5},{7,6},{8,11},{9,8},{10,9... | collective-permute-start | bytes 491528 | tf_op jit(solution)/shard_map/ppermute | solution.py:400
  14.2 3.1 %prep.1.after = bf16[512,1024]{1,0:T(8,128)(2,1)} custom-call(s32[4]{0:T(128)} %pad_add_fusion.meta, bf16[4,512,1024]{2,1,0:T(8,128)(2,1)} %bitcast.14), custom_call_target="tpu_custom_call" | custom-call | flops 134217728 | bytes 2097152 | tf_op jit(solution)/shard_map/prep/pallas_call | solution.py:172
  17.3 9.7 %all-to-all-start = ((bf16[64,8,1024]{2,1,0:T(8,128)(2,1)}), bf16[64,8,1024]{2,1,0:T(8,128)(2,1)}, u32[]{:S(2)}, u32[]{:S(2)}) async-start(bf16[64,8,1024]{2,1,0:T(8,128)(2,1)} %bitcast.16), calls=%async_computation | async-start | bytes 2097152 | tf_op jit(solution)/shard_map/all_to_all | solution.py:427
  27.0 0.0 collective-permute-done.2.in2
  27.0 0.0 collective-permute-done.1.in1
  27.0 0.0 collective-permute-done.in0
  27.1 1.5 %collective-permute-start.5 = (bf16[3,128,256]{2,1,0:T(8,128)(2,1)S(1)}, bf16[3,128,256]{2,1,0:T(8,128)(2,1)S(1)}, u32[]{:S(2)}, u32[]{:S(2)}) collective-permute-start(bf16[3,128,256]{2,1,0:T(8,128)(2,1)S(1)} %get-tuple-element.15.refs_0_), channel_id=1, source_target_pairs={{0,8},{4,12},{8,16},{12,20},{16,24},{20,28},{24,0},{28,4},{32,40},... | collective-permute-start | bytes 589832 | tf_op jit(solution)/shard_map/ppermute | solution.py:404
  28.6 1.3 %collective-permute-start.4 = (bf16[3,128,256]{2,1,0:T(8,128)(2,1)S(1)}, bf16[3,128,256]{2,1,0:T(8,128)(2,1)S(1)}, u32[]{:S(2)}, u32[]{:S(2)}) collective-permute-start(bf16[3,128,256]{2,1,0:T(8,128)(2,1)S(1)} %get-tuple-element.15.refs_0_), channel_id=1, source_target_pairs={{0,24},{4,28},{8,0},{12,4},{16,8},{20,12},{24,16},{28,20},{32,56},... | collective-permute-start | bytes 589832 | tf_op jit(solution)/shard_map/ppermute | solution.py:404
  29.9 1.7 %collective-permute-start.3 = (bf16[3,128,256]{2,1,0:T(8,128)(2,1)S(1)}, bf16[3,128,256]{2,1,0:T(8,128)(2,1)S(1)}, u32[]{:S(2)}, u32[]{:S(2)}) collective-permute-start(bf16[3,128,256]{2,1,0:T(8,128)(2,1)S(1)} %get-tuple-element.15.refs_0_), channel_id=1, source_target_pairs={{0,16},{4,20},{8,24},{12,28},{16,0},{20,4},{24,8},{28,12},{32,48},... | collective-permute-start | bytes 589832 | tf_op jit(solution)/shard_map/ppermute | solution.py:404
  31.5 1.2 collective-permute-start.8
  32.7 1.5 %collective-permute-start.7 = (bf16[3,128,384]{2,1,0:T(8,128)(2,1)S(1)}, bf16[3,128,384]{2,1,0:T(8,128)(2,1)S(1)}, u32[]{:S(2)}, u32[]{:S(2)}) collective-permute-start(bf16[3,128,384]{2,1,0:T(8,128)(2,1)S(1)} %get-tuple-element.16.refs_4_), channel_id=1, source_target_pairs={{0,96},{4,100},{8,104},{12,108},{16,112},{20,116},{24,120},{28,124... | collective-permute-start | bytes 884744 | tf_op jit(solution)/shard_map/ppermute | solution.py:410
  34.2 11.4 %collective-permute-done.5.refs_3_ = bf16[3,128,256]{2,1,0:T(8,128)(2,1)S(1)} collective-permute-done((bf16[3,128,256]{2,1,0:T(8,128)(2,1)S(1)}, bf16[3,128,256]{2,1,0:T(8,128)(2,1)S(1)}, u32[]{:S(2)}, u32[]{:S(2)}) %collective-permute-start.5) | collective-permute-done | bytes 196640 | tf_op jit(solution)/shard_map/ppermute | solution.py:404
  45.6 2.6 %collective-permute-start.6 = (bf16[3,128,384]{2,1,0:T(8,128)(2,1)S(1)}, bf16[3,128,384]{2,1,0:T(8,128)(2,1)S(1)}, u32[]{:S(2)}, u32[]{:S(2)}) collective-permute-start(bf16[3,128,384]{2,1,0:T(8,128)(2,1)S(1)} %get-tuple-element.16.refs_4_), channel_id=1, source_target_pairs={{0,64},{4,68},{8,72},{12,76},{16,80},{20,84},{24,88},{28,92},{32,9... | collective-permute-start | bytes 884744 | tf_op jit(solution)/shard_map/ppermute | solution.py:410
  48.2 8.6 %row_part.1 = (bf16[64,4,8,128]{3,2,1,0:T(8,128)(2,1)}, bf16[16,128]{1,0:T(8,128)(2,1)}) custom-call(bf16[4,512,1024]{2,1,0:T(8,128)(2,1)} %bitcast.15, bf16[1024,768]{1,0:T(8,128)(2,1)} %value_ref.3, bf16[1024,768]{1,0:T(8,128)(2,1)} %value_ref.3, bf16[1024,768]{1,0:T(8,128)(2,1)} %value_ref.3, bf16[512,1024]{1,0:T(8,128)(2,1)} %prep.1.after), custom_call_target="tpu_custom_call" | custom-call | flops 10000000000 | bytes 1 | tf_op jit(solution)/shard_map/row_part/pallas_call | solution.py:212
  56.8 0.0 all-to-all-done
  56.8 10.1 %all-to-all-start.1 = ((bf16[256,8,128]{2,1,0:T(8,128)(2,1)}), bf16[256,8,128]{2,1,0:T(8,128)(2,1)}, u32[]{:S(2)}, u32[]{:S(2)}) async-start(bf16[256,8,128]{2,1,0:T(8,128)(2,1)} %bitcast.17), calls=%async_computation.1 | async-start | bytes 1048576 | tf_op jit(solution)/shard_map/all_to_all | solution.py:430
  66.8 0.0 collective-permute-done.4.refs_2_
  66.9 0.0 collective-permute-done.3.refs_1_
  66.9 0.0 collective-permute-done.8.refs_7_
  66.9 0.0 collective-permute-done.7.refs_6_
  66.9 0.0 collective-permute-done.6.refs_5_
  66.9 0.0 copy-start.3
  66.9 0.7 copy-done.3
  67.6 0.0 copy-start
  67.6 0.0 copy-start.2
  67.6 1.4 %stack.21.near = bf16[3,4,128,640]{3,2,1,0:T(8,128)(2,1)} custom-call(bf16[3,128,256]{2,1,0:T(8,128)(2,1)S(1)} %get-tuple-element.15.refs_0_, bf16[3,128,256]{2,1,0:T(8,128)(2,1)S(1)} %collective-permute-done.3.refs_1_, bf16[3,128,256]{2,1,0:T(8,128)(2,1)S(1)} %collective-permute-done.4.refs_2_, bf16[3,128,256]{2,1,0:T(8,128)(2,1)S(1)} %collective-permute-done.5.refs_3_, ...), custom_call_target="tpu_custom_call" | custom-call | flops 1000000000 | bytes 1048576 | tf_op jit(solution)/shard_map/stack/pallas_call | solution.py:153
  69.0 2.2 %collective-permute-start.9 = (bf16[3,4,128,640]{3,2,1,0:T(8,128)(2,1)}, bf16[3,4,128,640]{3,2,1,0:T(8,128)(2,1)}, u32[]{:S(2)}, u32[]{:S(2)}) collective-permute-start(bf16[3,4,128,640]{3,2,1,0:T(8,128)(2,1)} %stack.21.near), channel_id=1, source_target_pairs={{0,4},{4,0},{8,12},{12,8},{16,20},{20,16},{24,28},{28,24},{32,36},... | collective-permute-start | bytes 5898248 | tf_op jit(solution)/shard_map/ppermute | solution.py:416
  71.2 0.0 copy-done
  71.2 0.0 copy-done.2
  71.3 3.7 %own_part.1 = (bf16[512,1024]{1,0:T(8,128)(2,1)S(1)}, bf16[512,1024]{1,0:T(8,128)(2,1)S(1)}, bf16[512,128]{1,0:T(8,128)(2,1)S(1)}) custom-call(s32[4]{0:T(128)S(1)} %copy-done.2, bf16[512,1024]{1,0:T(8,128)(2,1)} %bitcast.6.got_ref.refs_9_, bf16[1024,768]{1,0:T(8,128)(2,1)S(1)} %copy-done), custom_call_target="tpu_custom_call" | custom-call | flops 999999995904 | bytes 4194304 | tf_op jit(solution)/shard_map/own_part/pallas_call | solution.py:277
  75.0 0.2 collective-permute-done.9.far
  75.2 0.0 copy-start.1
  75.2 5.9 %column_part.1.columns = bf16[512,512]{1,0:T(8,128)(2,1)S(1)} custom-call(bf16[512,1024]{1,0:T(8,128)(2,1)S(1)} %get-tuple-element.12.by_x, bf16[512,1024]{1,0:T(8,128)(2,1)S(1)} %get-tuple-element.13.by_y, bf16[512,128]{1,0:T(8,128)(2,1)S(1)} %get-tuple-element.14.own, bf16[3,4,128,640]{3,2,1,0:T(8,128)(2,1)} %stack.21.near, ...), custom_call_target="tpu_custom_call" | custom-call | flops 3000000000 | bytes 6291456 | tf_op jit(solution)/shard_map/column_part/pallas_call | solution.py:327
  81.1 4.8 %all-to-all-done.1 = bf16[256,8,128]{2,1,0:T(8,128)(2,1)} async-done(((bf16[256,8,128]{2,1,0:T(8,128)(2,1)}), bf16[256,8,128]{2,1,0:T(8,128)(2,1)}, u32[]{:S(2)}, u32[]{:S(2)}) %all-to-all-start.1) | async-done | bytes 524320 | tf_op jit(solution)/shard_map/all_to_all | solution.py:430
  85.9 0.0 copy-done.1
  85.9 3.6 %mix.1 = bf16[64,4,8,256]{3,2,1,0:T(8,128)(2,1)S(1)} custom-call(s32[4]{0:T(128)S(1)} %copy-done.2, bf16[512,512]{1,0:T(8,128)(2,1)S(1)} %column_part.1.columns, bf16[64,4,8,128]{3,2,1,0:T(8,128)(2,1)} %bitcast.8.rows, bf16[256,1024]{1,0:T(8,128)(2,1)S(1)} %copy-done.1, bf16[3,4,128,640]{3,2,1,0:T(8,128)(2,1)} %stack.21.near, ...), custom_call_target="tpu_custom_call" | custom-call | flops 1000000000 | bytes 6291456 | tf_op jit(solution)/shard_map/mix/pallas_call | solution.py:365
  89.5 37.8 %all_to_all.15 = bf16[256,8,256]{2,1,0:T(8,128)(2,1)S(1)} all-to-all(bf16[256,8,256]{2,1,0:T(8,128)(2,1)S(1)} %bitcast.13), channel_id=1, replica_groups=mesh['rows'=64,'heads'=4] {'rows','heads'}, dimensions={0} | all-to-all | bytes 2097152 | tf_op jit(solution)/shard_map/all_to_all | solution.py:448
  127.3 2.2 %join.1 = bf16[4,4,128,256]{3,2,1,0:T(8,128)(2,1)} custom-call(bf16[64,4,8,256]{3,2,1,0:T(8,128)(2,1)S(1)} %bitcast.12), custom_call_target="tpu_custom_call" | custom-call | flops 100000000 | bytes 4194304 | tf_op jit(solution)/shard_map/join/pallas_call | solution.py:386
  (1 shorter events, 0.0 us)
Async XLA Ops:
  2.9 24.1 %collective-permute-start.2 = (bf16[128,640]{1,0:T(8,128)(2,1)}, bf16[128,640]{1,0:T(8,128)(2,1)S(1)}, u32[]{:S(2)}, u32[]{:S(2)}) collective-permute-start(bf16[128,640]{1,0:T(8,128)(2,1)} %cut.1), channel_id=1, source_target_pairs={{0,2},{1,3},{2,0},{3,1},{4,6},{5,7},{6,4},{7,5},{8,10},{9,11},{10,... | collective-permute-start | bytes 491528 | tf_op jit(solution)/shard_map/ppermute | solution.py:400
  10.7 16.4 %collective-permute-start.1 = (bf16[128,640]{1,0:T(8,128)(2,1)}, bf16[128,640]{1,0:T(8,128)(2,1)S(1)}, u32[]{:S(2)}, u32[]{:S(2)}) collective-permute-start(bf16[128,640]{1,0:T(8,128)(2,1)} %cut.1), channel_id=1, source_target_pairs={{0,1},{1,2},{2,3},{3,0},{4,5},{5,6},{6,7},{7,4},{8,9},{9,10},{10,1... | collective-permute-start | bytes 491528 | tf_op jit(solution)/shard_map/ppermute | solution.py:400
  11.9 15.2 %collective-permute-start = (bf16[128,640]{1,0:T(8,128)(2,1)}, bf16[128,640]{1,0:T(8,128)(2,1)S(1)}, u32[]{:S(2)}, u32[]{:S(2)}) collective-permute-start(bf16[128,640]{1,0:T(8,128)(2,1)} %cut.1), channel_id=1, source_target_pairs={{0,3},{1,0},{2,1},{3,2},{4,7},{5,4},{6,5},{7,6},{8,11},{9,8},{10,9... | collective-permute-start | bytes 491528 | tf_op jit(solution)/shard_map/ppermute | solution.py:400
  17.3 39.4 %all-to-all-start = ((bf16[64,8,1024]{2,1,0:T(8,128)(2,1)}), bf16[64,8,1024]{2,1,0:T(8,128)(2,1)}, u32[]{:S(2)}, u32[]{:S(2)}) async-start(bf16[64,8,1024]{2,1,0:T(8,128)(2,1)} %bitcast.16), calls=%async_computation | async-start | bytes 2097152 | tf_op jit(solution)/shard_map/all_to_all | solution.py:427
  27.1 18.5 %collective-permute-start.5 = (bf16[3,128,256]{2,1,0:T(8,128)(2,1)S(1)}, bf16[3,128,256]{2,1,0:T(8,128)(2,1)S(1)}, u32[]{:S(2)}, u32[]{:S(2)}) collective-permute-start(bf16[3,128,256]{2,1,0:T(8,128)(2,1)S(1)} %get-tuple-element.15.refs_0_), channel_id=1, source_target_pairs={{0,8},{4,12},{8,16},{12,20},{16,24},{20,28},{24,0},{28,4},{32,40},... | collective-permute-start | bytes 589832 | tf_op jit(solution)/shard_map/ppermute | solution.py:404
  28.6 38.3 %collective-permute-start.4 = (bf16[3,128,256]{2,1,0:T(8,128)(2,1)S(1)}, bf16[3,128,256]{2,1,0:T(8,128)(2,1)S(1)}, u32[]{:S(2)}, u32[]{:S(2)}) collective-permute-start(bf16[3,128,256]{2,1,0:T(8,128)(2,1)S(1)} %get-tuple-element.15.refs_0_), channel_id=1, source_target_pairs={{0,24},{4,28},{8,0},{12,4},{16,8},{20,12},{24,16},{28,20},{32,56},... | collective-permute-start | bytes 589832 | tf_op jit(solution)/shard_map/ppermute | solution.py:404
  29.9 37.0 %collective-permute-start.3 = (bf16[3,128,256]{2,1,0:T(8,128)(2,1)S(1)}, bf16[3,128,256]{2,1,0:T(8,128)(2,1)S(1)}, u32[]{:S(2)}, u32[]{:S(2)}) collective-permute-start(bf16[3,128,256]{2,1,0:T(8,128)(2,1)S(1)} %get-tuple-element.15.refs_0_), channel_id=1, source_target_pairs={{0,16},{4,20},{8,24},{12,28},{16,0},{20,4},{24,8},{28,12},{32,48},... | collective-permute-start | bytes 589832 | tf_op jit(solution)/shard_map/ppermute | solution.py:404
  31.5 35.3 %collective-permute-start.8 = (bf16[3,128,384]{2,1,0:T(8,128)(2,1)S(1)}, bf16[3,128,384]{2,1,0:T(8,128)(2,1)S(1)}, u32[]{:S(2)}, u32[]{:S(2)}) collective-permute-start(bf16[3,128,384]{2,1,0:T(8,128)(2,1)S(1)} %get-tuple-element.16.refs_4_), channel_id=1, source_target_pairs={{0,32},{4,36},{8,40},{12,44},{16,48},{20,52},{24,56},{28,60},{32,6... | collective-permute-start | bytes 884744 | tf_op jit(solution)/shard_map/ppermute | solution.py:410
  32.7 34.2 %collective-permute-start.7 = (bf16[3,128,384]{2,1,0:T(8,128)(2,1)S(1)}, bf16[3,128,384]{2,1,0:T(8,128)(2,1)S(1)}, u32[]{:S(2)}, u32[]{:S(2)}) collective-permute-start(bf16[3,128,384]{2,1,0:T(8,128)(2,1)S(1)} %get-tuple-element.16.refs_4_), channel_id=1, source_target_pairs={{0,96},{4,100},{8,104},{12,108},{16,112},{20,116},{24,120},{28,124... | collective-permute-start | bytes 884744 | tf_op jit(solution)/shard_map/ppermute | solution.py:410
  45.6 21.3 %collective-permute-start.6 = (bf16[3,128,384]{2,1,0:T(8,128)(2,1)S(1)}, bf16[3,128,384]{2,1,0:T(8,128)(2,1)S(1)}, u32[]{:S(2)}, u32[]{:S(2)}) collective-permute-start(bf16[3,128,384]{2,1,0:T(8,128)(2,1)S(1)} %get-tuple-element.16.refs_4_), channel_id=1, source_target_pairs={{0,64},{4,68},{8,72},{12,76},{16,80},{20,84},{24,88},{28,92},{32,9... | collective-permute-start | bytes 884744 | tf_op jit(solution)/shard_map/ppermute | solution.py:410
  56.8 29.2 %all-to-all-start.1 = ((bf16[256,8,128]{2,1,0:T(8,128)(2,1)}), bf16[256,8,128]{2,1,0:T(8,128)(2,1)}, u32[]{:S(2)}, u32[]{:S(2)}) async-start(bf16[256,8,128]{2,1,0:T(8,128)(2,1)} %bitcast.17), calls=%async_computation.1 | async-start | bytes 1048576 | tf_op jit(solution)/shard_map/all_to_all | solution.py:430
  66.9 0.7 copy-start.3
  67.6 3.7 %copy-start = (bf16[1024,768]{1,0:T(8,128)(2,1)S(1)}, bf16[1024,768]{1,0:T(8,128)(2,1)}, u32[]{:S(2)}) copy-start(bf16[1024,768]{1,0:T(8,128)(2,1)} %value_ref.3) | copy-start | bytes 4718596
  67.6 3.7 %copy-start.2 = (s32[4]{0:T(128)S(1)}, s32[4]{0:T(128)}, u32[]{:S(2)}) copy-start(s32[4]{0:T(128)} %pad_add_fusion.meta) | copy-start | bytes 52
  69.0 6.2 %collective-permute-start.9 = (bf16[3,4,128,640]{3,2,1,0:T(8,128)(2,1)}, bf16[3,4,128,640]{3,2,1,0:T(8,128)(2,1)}, u32[]{:S(2)}, u32[]{:S(2)}) collective-permute-start(bf16[3,4,128,640]{3,2,1,0:T(8,128)(2,1)} %stack.21.near), channel_id=1, source_target_pairs={{0,4},{4,0},{8,12},{12,8},{16,20},{20,16},{24,28},{28,24},{32,36},... | collective-permute-start | bytes 5898248 | tf_op jit(solution)/shard_map/ppermute | solution.py:416
  75.2 10.7 %copy-start.1 = (bf16[256,1024]{1,0:T(8,128)(2,1)S(1)}, bf16[256,1024]{1,0:T(8,128)(2,1)}, u32[]{:S(2)}) copy-start(bf16[256,1024]{1,0:T(8,128)(2,1)} %w_out.1) | copy-start | bytes 1572868

commit v7 on v6

--- a/solution.py
+++ b/solution.py
@@ -97,13 +97,13 @@
     out_ref[:, :HALF] = query_ref[...]
     out_ref[:, HALF : 2 * HALF] = key_ref[...]
     out_ref[:, 2 * HALF : 3 * HALF] = value_ref[...]
-    out_ref[:, 3 * HALF : 4 * HALF] = mix_ref[HALF:, :]
-    out_ref[:, 4 * HALF :] = mix_ref[:HALF, :]
+    out_ref[:, 3 * HALF : 5 * HALF] = mix_ref[HALF:, :]
+    out_ref[:, 5 * HALF :] = mix_ref[:HALF, :]
 
 
 def cut(meta, w_qkv, w_out):
-    def part(n, axis):
-        return pl.BlockSpec((BLOCK, HALF), lambda b, meta: (meta[axis] * 2 + meta[2], 2 * n + 1))
+    def part(n):
+        return pl.BlockSpec((BLOCK, HALF), lambda b, meta: (meta[1] * 2 + meta[2], 2 * n + 1))
 
     return call(
         cut_kernel,
@@ -112,41 +112,42 @@
             num_scalar_prefetch=1,
             grid=(1,),
             in_specs=[
-                part(0, 1),
-                part(1, 1),
-                part(2, 3),
-                pl.BlockSpec((256, BLOCK), lambda b, meta: (0, meta[3] * 2 + meta[2])),
+                part(0),
+                part(1),
+                part(2),
+                pl.BlockSpec((256, 256), lambda b, meta: (0, meta[3] * 2 + meta[2])),
             ],
-            out_specs=pl.BlockSpec((BLOCK, WIDE), lambda b, meta: (0, 0)),
+            out_specs=pl.BlockSpec((BLOCK, 7 * HALF), lambda b, meta: (0, 0)),
         ),
-        out_shape=like(BLOCK, WIDE),
+        out_shape=like(BLOCK, 7 * HALF),
     )(meta, w_qkv, w_qkv, w_qkv, w_out)
 
 
-def mid_kernel(in0, in1, in2, x_ref, y_ref):
+def mid_kernel(in0, in1, in2, after, x_ref, y_ref):
     for n, ref in enumerate((in0, in1, in2)):
-        x_ref[n] = ref[:, :256]
-        y_ref[n] = ref[:, 256:]
-
-
-def mid(parts):
+        x_ref[n] = ref[:, : 3 * HALF]
+        y_ref[n] = ref[:, 3 * HALF :]
+
+
+def mid(parts, after):
     return call(
         mid_kernel,
         "mid",
         flops=10**12,
         vmem=16 * MIB,
-        in_specs=[whole()] * 3,
+        in_specs=[whole()] * 3 + [anywhere()],
         out_specs=[whole()] * 2,
-        out_shape=[like(3, BLOCK, 256), like(3, BLOCK, WIDE - 256)],
-    )(*parts)
-
-
-def stack_kernel(*refs):
-    out_ref = refs[-1]
-    for d in range(4):
-        for n in range(3):
-            out_ref[n, d, :, :256] = refs[d][n]
-            out_ref[n, d, :, 256:] = refs[4 + d][n]
+        out_shape=[like(3, BLOCK, 3 * HALF), like(3, BLOCK, 4 * HALF)],
+    )(*parts, after)
+
+
+def stack_kernel(in0, in1, in2, in3, y0, y1, after, out_ref):
+    for n in range(3):
+        for d, ref in enumerate((in0, in1, in2, in3)):
+            out_ref[n, d, :, : 3 * HALF] = ref[n]
+        for d, ref in enumerate((y0, y1)):
+            out_ref[n, 2 * d, :, 3 * HALF :] = ref[n, :, :256]
+            out_ref[n, 2 * d + 1, :, 3 * HALF :] = ref[n, :, 256:]
 
 
 def stack(parts, after):
@@ -155,10 +156,10 @@
         "stack",
         flops=10**9,
         vmem=16 * MIB,
-        in_specs=[whole()] * 8 + [anywhere()] * len(after),
+        in_specs=[whole()] * 6 + [anywhere()],
         out_specs=whole(),
         out_shape=like(3, 4, BLOCK, WIDE),
-    )(*parts, *after)
+    )(*parts, after)
 
 
 def prep_kernel(meta, sig_ref, out_ref):
@@ -212,7 +213,6 @@
     return call(
         row_kernel,
         "row_part",
-        flops=10**10,
         moved=1,
         grid=(ROWS_LOCAL,),
         in_specs=[
@@ -240,7 +240,7 @@
         attend(qkv[c * 256 : (c + 1) * 256], allowed, store)
 
 
-def own_kernel(meta, got_ref, w_qkv, by_x, by_y, out_ref, held, weight, sems):
+def own_kernel(meta, got_ref, w_qkv, by_x, out_ref, held, weight, sems):
     copies = [
         pltpu.make_async_copy(
             w_qkv.at[:, 256 * n + HALF : 256 * (n + 1)],
@@ -260,9 +260,8 @@
     for n, d in enumerate((0,) + STEPS):
         for far, on in enumerate((core, 1 - core)):
             lo = (4 * far + n) * BLOCK
-            for at, out in ((meta[1], by_x), (meta[3], by_y)):
-                source = pl.multiple_of((lax.rem(at + 4 - d, 4) * 2 + on) * BLOCK, BLOCK)
-                out[:, lo : lo + BLOCK] = held[:, pl.ds(source, BLOCK)]
+            source = pl.multiple_of((lax.rem(meta[1] + 4 - d, 4) * 2 + on) * BLOCK, BLOCK)
+            by_x[:, lo : lo + BLOCK] = held[:, pl.ds(source, BLOCK)]
 
     def keep(lo, out):
         out_ref[lo : lo + BLOCK, :] = out
@@ -281,8 +280,8 @@
         moved=4 * MIB,
         vmem=20 * MIB,
         in_specs=[smem(), whole(), anywhere()],
-        out_specs=[whole()] * 3,
-        out_shape=[like(C, D), like(C, D), like(C, HALF)],
+        out_specs=[whole()] * 2,
+        out_shape=[like(C, D), like(C, HALF)],
         scratch_shapes=[
             VMEM((C, D), BF),
             VMEM((D, 3 * HALF), BF),
@@ -291,7 +290,7 @@
     )(meta, got, w_qkv)
 
 
-def column_kernel(by_x, by_y, own, near, far, out_ref, outs):
+def column_kernel(by_x, own, near, far, out_ref, outs):
     allowed = causal()
     outs[:, :HALF] = own[...]
     half = 4 * BLOCK
@@ -300,19 +299,14 @@
         def keep(lo, out):
             outs[lo : lo + BLOCK, (n + 1) * HALF : (n + 2) * HALF] = out
 
-        def product(left, lanes):
-            return jnp.dot(
-                left[:, :half],
-                near[n, :, :, lanes].reshape(half, -1),
-                preferred_element_type=F32,
-            ) + jnp.dot(
-                left[:, half:],
-                far[n, :, :, lanes].reshape(half, -1),
-                preferred_element_type=F32,
-            )
-
-        qkv = jnp.concatenate(
-            [product(by_x, slice(0, 256)), product(by_y, slice(256, 256 + HALF))], axis=1
+        qkv = jnp.dot(
+            by_x[:, :half],
+            near[n, :, :, : 3 * HALF].reshape(half, 3 * HALF),
+            preferred_element_type=F32,
+        ) + jnp.dot(
+            by_x[:, half:],
+            far[n, :, :, : 3 * HALF].reshape(half, 3 * HALF),
+            preferred_element_type=F32,
         )
         columns_of(qkv, allowed, keep)
     back = one_hot(lambda o: (o % 2) * 64 + o // 2)
@@ -323,18 +317,18 @@
         out_ref[b * BLOCK : (b + 1) * BLOCK, :] = move(back, both)
 
 
-def column_part(by_x, by_y, own, near, far):
+def column_part(by_x, own, near, far):
     return call(
         column_kernel,
         "column_part",
         flops=3 * 10**9,
         moved=6 * MIB,
         vmem=20 * MIB,
-        in_specs=[whole()] * 5,
+        in_specs=[whole()] * 4,
         out_specs=whole(),
         out_shape=like(C, C),
         scratch_shapes=[VMEM((C, C), BF)],
-    )(by_x, by_y, own, near, far)
+    )(by_x, own, near, far)
 
 
 def mix_kernel(meta, columns, rows, w_out, near, far, out_ref):
@@ -347,18 +341,21 @@
         ],
         axis=1,
     )
-    for n, d in enumerate((0,) + STEPS):
-        j = lax.rem(meta[3] + 4 - d, 4)
-        own = w_out[:, pl.ds(pl.multiple_of(j * 256, 256), 256)]
-        parts = []
-        for lo, mine in ((3 * HALF, own[HALF:]), (4 * HALF, own[:HALF])):
-            here = near[:, n, :, lo : lo + HALF].reshape(3 * BLOCK, HALF)
-            there = far[:, n, :, lo : lo + HALF].reshape(3 * BLOCK, HALF)
-            low = jnp.where(core == 0, here, there)
-            high = jnp.where(core == 0, there, here)
-            parts += [mine, jnp.concatenate([low, high], axis=1)]
-        mixed = jnp.dot(left, jnp.concatenate(parts, axis=0), preferred_element_type=F32)
-        out_ref[:, j] = mixed.astype(BF).reshape(64, 8, 256)
+    for source, on in ((near, core), (far, 1 - core)):
+        for d, y in enumerate((meta[3], 1 - meta[3])):
+            j = y * 2 + on
+            own = w_out[:, pl.ds(pl.multiple_of(j * 256, 256), 256)]
+            weight = jnp.concatenate(
+                [
+                    own[HALF:],
+                    source[:, 2 * d, :, 3 * HALF :].reshape(3 * BLOCK, 256),
+                    own[:HALF],
+                    source[:, 2 * d + 1, :, 3 * HALF :].reshape(3 * BLOCK, 256),
+                ],
+                axis=0,
+            )
+            mixed = jnp.dot(left, weight, preferred_element_type=F32)
+            out_ref[:, j] = mixed.astype(BF).reshape(64, 8, 256)
 
 
 def mix(meta, columns, rows, w_out, near, far):
@@ -406,10 +403,8 @@
     )
 
 
-def along_y(data, d):
-    return lax.ppermute(
-        data, "rows", [(i, i // 32 * 32 + (i // 8 % 4 + d) % 4 * 8 + i % 8) for i in range(64)]
-    )
+def other_y(data):
+    return lax.ppermute(data, "rows", [(i, i ^ 8) for i in range(64)])
 
 
 def other_core(data):
@@ -419,7 +414,7 @@
 def local(signal, w_qkv, w_out):
     i = lax.axis_index("rows")
     g = lax.axis_index("heads")
-    meta = jnp.stack([g, i // 2 % 4, i % 2, i // 8 % 4]).astype(jnp.int32)
+    meta = jnp.stack([g, i // 2 % 4, i % 2, i // 8 % 2]).astype(jnp.int32)
     sig = signal.reshape(ROWS_LOCAL, C, D)
 
     send = prep(meta, sig)
@@ -432,18 +427,14 @@
     ).reshape(64, GROUPS, 8, HALF)
 
     mine = cut(meta, w_qkv, w_out)
-    others_x, others_y = mid([to_group(mine, k) for k in ORDER])
+    others, blocks = mid([to_group(mine, k) for k in ORDER], rows_done)
     near = stack(
-        [others_x]
-        + [along_x(others_x, d) for d in STEPS]
-        + [others_y]
-        + [along_y(others_y, d) for d in STEPS],
-        [rows_done, got],
+        [others] + [along_x(others, d) for d in STEPS] + [blocks, other_y(blocks)], got
     )
     far = other_core(near)
 
-    by_x, by_y, own = own_part(meta, got, w_qkv)
-    columns = column_part(by_x, by_y, own, near, far)
+    by_x, own = own_part(meta, got, w_qkv)
+    columns = column_part(by_x, own, near, far)
     mixed = mix(meta, columns, rows, w_out, near, far).reshape(64 * GROUPS, 8, 256)
     back = lax.all_to_all(mixed, BOTH, split_axis=0, concat_axis=0, tiled=True)
     return join(back.reshape(64, GROUPS, 8, 256)).reshape(ROWS_LOCAL * C, 256)

time: 130 us -> 117 us (0.900)
  starting transfers between devices: 42.9 us -> 35.6 us
  waiting for transfers between devices: 16.4 us -> 12.1 us
    ppermute x3, waiting for transfers between devices: 11.4 us -> 1.21 us  [along_x(): lax.ppermute(data, 'rows', [(i, i // 8 * 8 + (i // 2 % 4 + d) % 4 * 2 + i...]
    all_to_all x1, waiting for transfers between devices: 0.01 us -> 4.93 us  [local(): lax.all_to_all(send.reshape(64, 8, D), 'rows', split_axis=0, concat_axis=...]
    ppermute x3 -> x1, starting transfers between devices: 5.25 us -> 1.48 us  [other_y(): return lax.ppermute(data, 'rows', [(i, i ^ 8) for i in range(64)])]
    all_to_all x1, starting transfers between devices: 10.1 us -> 7.95 us  [local(): lax.all_to_all(own_rows.reshape(64 * GROUPS, 8, HALF), BOTH, split_axis=0...]
  transfers between devices with their start and end apart: 12 -> 10, of which waited for: 3 -> 4; matrix products, arithmetic and copies ran while one was open for 0% -> 0% of each run, Pallas kernels for 18% -> 19%
where the time goes in v7:
time: 117 us
  blocking collectives  37 us (32%)
  starting transfers between devices  35.6 us (30%)
  Pallas kernels  30.8 us (26%)
  waiting for transfers between devices  12.1 us (10%)
    all_to_all x1, blocking collectives, local(): back = lax.all_to_all(mixed, BOTH, split_axis=0, concat_axis=0, tiled=True)  37 us
    ppermute x3, starting transfers between devices, to_group(): lax.ppermute(data, 'heads', [(j, (j + k) % GROUPS) for j in range(GROUPS)])  11.3 us
    all_to_all x1, starting transfers between devices, local(): lax.all_to_all(send.reshape(64, 8, D), 'rows', split_axis=0, concat_axis=...  9.64 us
    pallas_call x1, Pallas kernels, row_part(): call(row_kernel, 'row_part', moved=1, grid=(ROWS_LOCAL,), in_specs=[pl.Bl...  8.61 us
    all_to_all x1, starting transfers between devices, local(): lax.all_to_all(own_rows.reshape(64 * GROUPS, 8, HALF), BOTH, split_axis=0...  7.95 us
    pallas_call x1, Pallas kernels, column_part(): call(column_kernel, 'column_part', flops=3 * 10 ** 9, moved=6 * MIB, vmem...  5.94 us
    all_to_all x1, waiting for transfers between devices, local(): lax.all_to_all(own_rows.reshape(64 * GROUPS, 8, HALF), BOTH, split_axis=0...  5.45 us
    all_to_all x1, waiting for transfers between devices, local(): lax.all_to_all(send.reshape(64, 8, D), 'rows', split_axis=0, concat_axis=...  4.93 us
  transfers between devices with their start and end apart: 10, of which 4 were waited for; matrix products, arithmetic and copies ran while one was open for 0% of the time, Pallas kernels for 19%

profile of v7, /device:TPU:1, one launch (start us, length us, event | category | flops | bytes accessed | tf_op | source)
XLA Modules:
  0.0 116.8 jit_solution(3273912341645691028)
XLA Ops:
  0.0 0.6 pad_add_fusion.meta
  0.6 2.3 %cut.1 = bf16[128,896]{1,0:T(8,128)(2,1)} custom-call(s32[4]{0:T(128)} %pad_add_fusion.meta, bf16[1024,768]{1,0:T(8,128)(2,1)} %value_ref.3, bf16[1024,768]{1,0:T(8,128)(2,1)} %value_ref.3, bf16[1024,768]{1,0:T(8,128)(2,1)} %value_ref.3, bf16[256,1024]{1,0:T(8,128)(2,1)} %w_out.1), custom_call_target="tpu_custom_call" | custom-call | bytes 1048576 | tf_op jit(solution)/shard_map/cut/pallas_call | solution.py:108
  3.0 7.7 %collective-permute-start.2 = (bf16[128,896]{1,0:T(8,128)(2,1)}, bf16[128,896]{1,0:T(8,128)(2,1)S(1)}, u32[]{:S(2)}, u32[]{:S(2)}) collective-permute-start(bf16[128,896]{1,0:T(8,128)(2,1)} %cut.1), channel_id=1, source_target_pairs={{0,2},{1,3},{2,0},{3,1},{4,6},{5,7},{6,4},{7,5},{8,10},{9,11},{10,... | collective-permute-start | bytes 688136 | tf_op jit(solution)/shard_map/ppermute | solution.py:397
  10.7 1.2 %collective-permute-start.1 = (bf16[128,896]{1,0:T(8,128)(2,1)}, bf16[128,896]{1,0:T(8,128)(2,1)S(1)}, u32[]{:S(2)}, u32[]{:S(2)}) collective-permute-start(bf16[128,896]{1,0:T(8,128)(2,1)} %cut.1), channel_id=1, source_target_pairs={{0,1},{1,2},{2,3},{3,0},{4,5},{5,6},{6,7},{7,4},{8,9},{9,10},{10,1... | collective-permute-start | bytes 688136 | tf_op jit(solution)/shard_map/ppermute | solution.py:397
  11.9 2.4 %collective-permute-start = (bf16[128,896]{1,0:T(8,128)(2,1)}, bf16[128,896]{1,0:T(8,128)(2,1)S(1)}, u32[]{:S(2)}, u32[]{:S(2)}) collective-permute-start(bf16[128,896]{1,0:T(8,128)(2,1)} %cut.1), channel_id=1, source_target_pairs={{0,3},{1,0},{2,1},{3,2},{4,7},{5,4},{6,5},{7,6},{8,11},{9,8},{10,9... | collective-permute-start | bytes 688136 | tf_op jit(solution)/shard_map/ppermute | solution.py:397
  14.3 3.1 %prep.1.after = bf16[512,1024]{1,0:T(8,128)(2,1)} custom-call(s32[4]{0:T(128)} %pad_add_fusion.meta, bf16[4,512,1024]{2,1,0:T(8,128)(2,1)} %bitcast.14), custom_call_target="tpu_custom_call" | custom-call | flops 134217728 | bytes 2097152 | tf_op jit(solution)/shard_map/prep/pallas_call | solution.py:173
  17.4 9.6 %all-to-all-start = ((bf16[64,8,1024]{2,1,0:T(8,128)(2,1)}), bf16[64,8,1024]{2,1,0:T(8,128)(2,1)}, u32[]{:S(2)}, u32[]{:S(2)}) async-start(bf16[64,8,1024]{2,1,0:T(8,128)(2,1)} %bitcast.16), calls=%async_computation | async-start | bytes 2097152 | tf_op jit(solution)/shard_map/all_to_all | solution.py:422
  27.0 8.6 %row_part.1 = (bf16[64,4,8,128]{3,2,1,0:T(8,128)(2,1)}, bf16[16,128]{1,0:T(8,128)(2,1)}) custom-call(bf16[4,512,1024]{2,1,0:T(8,128)(2,1)} %bitcast.15, bf16[1024,768]{1,0:T(8,128)(2,1)} %value_ref.3, bf16[1024,768]{1,0:T(8,128)(2,1)} %value_ref.3, bf16[1024,768]{1,0:T(8,128)(2,1)} %value_ref.3, bf16[512,1024]{1,0:T(8,128)(2,1)} %prep.1.after), custom_call_target="tpu_custom_call" | custom-call | bytes 1 | tf_op jit(solution)/shard_map/row_part/pallas_call | solution.py:213
  35.6 0.0 collective-permute-done.2.in2
  35.6 0.0 collective-permute-done.1.in1
  35.7 0.0 collective-permute-done.in0
  35.7 0.0 copy-start.3
  35.7 0.7 copy-done.3
  36.3 0.1 mid.1
  36.4 1.5 %collective-permute-start.6 = (bf16[3,128,512]{2,1,0:T(8,128)(2,1)S(1)}, bf16[3,128,512]{2,1,0:T(8,128)(2,1)S(1)}, u32[]{:S(2)}, u32[]{:S(2)}) collective-permute-start(bf16[3,128,512]{2,1,0:T(8,128)(2,1)S(1)} %get-tuple-element.15.y0), channel_id=1, source_target_pairs={{0,32},{4,36},{8,40},{12,44},{16,48},{20,52},{24,56},{28,60},{32,0... | collective-permute-start | bytes 1179656 | tf_op jit(solution)/shard_map/ppermute | solution.py:407
  37.9 1.2 %collective-permute-start.5 = (bf16[3,128,384]{2,1,0:T(8,128)(2,1)S(1)}, bf16[3,128,384]{2,1,0:T(8,128)(2,1)S(1)}, u32[]{:S(2)}, u32[]{:S(2)}) collective-permute-start(bf16[3,128,384]{2,1,0:T(8,128)(2,1)S(1)} %get-tuple-element.14.in0), channel_id=1, source_target_pairs={{0,8},{4,12},{8,16},{12,20},{16,24},{20,28},{24,0},{28,4},{32,40},... | collective-permute-start | bytes 884744 | tf_op jit(solution)/shard_map/ppermute | solution.py:401
  39.1 1.5 %collective-permute-start.4 = (bf16[3,128,384]{2,1,0:T(8,128)(2,1)S(1)}, bf16[3,128,384]{2,1,0:T(8,128)(2,1)S(1)}, u32[]{:S(2)}, u32[]{:S(2)}) collective-permute-start(bf16[3,128,384]{2,1,0:T(8,128)(2,1)S(1)} %get-tuple-element.14.in0), channel_id=1, source_target_pairs={{0,24},{4,28},{8,0},{12,4},{16,8},{20,12},{24,16},{28,20},{32,56},... | collective-permute-start | bytes 884744 | tf_op jit(solution)/shard_map/ppermute | solution.py:401
  40.6 1.5 %collective-permute-start.3 = (bf16[3,128,384]{2,1,0:T(8,128)(2,1)S(1)}, bf16[3,128,384]{2,1,0:T(8,128)(2,1)S(1)}, u32[]{:S(2)}, u32[]{:S(2)}) collective-permute-start(bf16[3,128,384]{2,1,0:T(8,128)(2,1)S(1)} %get-tuple-element.14.in0), channel_id=1, source_target_pairs={{0,16},{4,20},{8,24},{12,28},{16,0},{20,4},{24,8},{28,12},{32,48},... | collective-permute-start | bytes 884744 | tf_op jit(solution)/shard_map/ppermute | solution.py:401
  42.0 4.9 %all-to-all-done = bf16[64,8,1024]{2,1,0:T(8,128)(2,1)} async-done(((bf16[64,8,1024]{2,1,0:T(8,128)(2,1)}), bf16[64,8,1024]{2,1,0:T(8,128)(2,1)}, u32[]{:S(2)}, u32[]{:S(2)}) %all-to-all-start) | async-done | bytes 1048608 | tf_op jit(solution)/shard_map/all_to_all | solution.py:422
  47.0 7.9 %all-to-all-start.1 = ((bf16[256,8,128]{2,1,0:T(8,128)(2,1)}), bf16[256,8,128]{2,1,0:T(8,128)(2,1)}, u32[]{:S(2)}, u32[]{:S(2)}) async-start(bf16[256,8,128]{2,1,0:T(8,128)(2,1)} %bitcast.7), calls=%async_computation.1 | async-start | bytes 1048576 | tf_op jit(solution)/shard_map/all_to_all | solution.py:425
  54.9 0.0 collective-permute-done.5.in3
  54.9 0.0 collective-permute-done.4.in2
  54.9 1.2 %collective-permute-done.3.in1 = bf16[3,128,384]{2,1,0:T(8,128)(2,1)S(1)} collective-permute-done((bf16[3,128,384]{2,1,0:T(8,128)(2,1)S(1)}, bf16[3,128,384]{2,1,0:T(8,128)(2,1)S(1)}, u32[]{:S(2)}, u32[]{:S(2)}) %collective-permute-start.3) | collective-permute-done | bytes 294944 | tf_op jit(solution)/shard_map/ppermute | solution.py:401
  56.1 0.0 collective-permute-done.6.y1
  56.1 0.0 copy-start
  56.1 0.0 copy-start.2
  56.2 1.4 %stack.21.near = bf16[3,4,128,640]{3,2,1,0:T(8,128)(2,1)} custom-call(bf16[3,128,384]{2,1,0:T(8,128)(2,1)S(1)} %get-tuple-element.14.in0, bf16[3,128,384]{2,1,0:T(8,128)(2,1)S(1)} %collective-permute-done.3.in1, bf16[3,128,384]{2,1,0:T(8,128)(2,1)S(1)} %collective-permute-done.4.in2, bf16[3,128,384]{2,1,0:T(8,128)(2,1)S(1)} %collective-permute-done.5.in3, ...), custom_call_target="tpu_custom_call" | custom-call | flops 1000000000 | bytes 1048576 | tf_op jit(solution)/shard_map/stack/pallas_call | solution.py:154
  57.6 1.1 collective-permute-start.7
  58.7 0.0 copy-done
  58.7 0.0 copy-done.2
  58.7 3.5 %own_part.1 = (bf16[512,1024]{1,0:T(8,128)(2,1)S(1)}, bf16[512,128]{1,0:T(8,128)(2,1)S(1)}) custom-call(s32[4]{0:T(128)S(1)} %copy-done.2, bf16[512,1024]{1,0:T(8,128)(2,1)} %bitcast.6.got_ref.after, bf16[1024,768]{1,0:T(8,128)(2,1)S(1)} %copy-done), custom_call_target="tpu_custom_call" | custom-call | flops 999999995904 | bytes 4194304 | tf_op jit(solution)/shard_map/own_part/pallas_call | solution.py:276
  62.2 0.5 collective-permute-done.7.far
  62.6 0.0 copy-start.1
  62.6 5.9 %column_part.1.columns = bf16[512,512]{1,0:T(8,128)(2,1)S(1)} custom-call(bf16[512,1024]{1,0:T(8,128)(2,1)S(1)} %get-tuple-element.11.by_x, bf16[512,128]{1,0:T(8,128)(2,1)S(1)} %get-tuple-element.12.own, bf16[3,4,128,640]{3,2,1,0:T(8,128)(2,1)} %stack.21.near, bf16[3,4,128,640]{3,2,1,0:T(8,128)(2,1)} %collective-permute-done.7.far), custom_call_target="tpu_custom_call" | custom-call | flops 3000000000 | bytes 6291456 | tf_op jit(solution)/shard_map/column_part/pallas_call | solution.py:321
  68.6 5.4 %all-to-all-done.1 = bf16[256,8,128]{2,1,0:T(8,128)(2,1)} async-done(((bf16[256,8,128]{2,1,0:T(8,128)(2,1)}), bf16[256,8,128]{2,1,0:T(8,128)(2,1)}, u32[]{:S(2)}, u32[]{:S(2)}) %all-to-all-start.1) | async-done | bytes 524320 | tf_op jit(solution)/shard_map/all_to_all | solution.py:425
  74.0 0.0 copy-done.1
  74.0 3.6 %mix.1 = bf16[64,4,8,256]{3,2,1,0:T(8,128)(2,1)S(1)} custom-call(s32[4]{0:T(128)S(1)} %copy-done.2, bf16[512,512]{1,0:T(8,128)(2,1)S(1)} %column_part.1.columns, bf16[64,4,8,128]{3,2,1,0:T(8,128)(2,1)} %bitcast.8.rows, bf16[256,1024]{1,0:T(8,128)(2,1)S(1)} %copy-done.1, bf16[3,4,128,640]{3,2,1,0:T(8,128)(2,1)} %stack.21.near, ...), custom_call_target="tpu_custom_call" | custom-call | flops 1000000000 | bytes 6291456 | tf_op jit(solution)/shard_map/mix/pallas_call | solution.py:362
  77.7 37.0 %all_to_all.15 = bf16[256,8,256]{2,1,0:T(8,128)(2,1)S(1)} all-to-all(bf16[256,8,256]{2,1,0:T(8,128)(2,1)S(1)} %bitcast.13), channel_id=1, replica_groups=mesh['rows'=64,'heads'=4] {'rows','heads'}, dimensions={0} | all-to-all | bytes 2097152 | tf_op jit(solution)/shard_map/all_to_all | solution.py:439
  114.6 2.2 %join.1 = bf16[4,4,128,256]{3,2,1,0:T(8,128)(2,1)} custom-call(bf16[64,4,8,256]{3,2,1,0:T(8,128)(2,1)S(1)} %bitcast.12), custom_call_target="tpu_custom_call" | custom-call | flops 100000000 | bytes 4194304 | tf_op jit(solution)/shard_map/join/pallas_call | solution.py:383
Async XLA Ops:
  3.0 32.7 %collective-permute-start.2 = (bf16[128,896]{1,0:T(8,128)(2,1)}, bf16[128,896]{1,0:T(8,128)(2,1)S(1)}, u32[]{:S(2)}, u32[]{:S(2)}) collective-permute-start(bf16[128,896]{1,0:T(8,128)(2,1)} %cut.1), channel_id=1, source_target_pairs={{0,2},{1,3},{2,0},{3,1},{4,6},{5,7},{6,4},{7,5},{8,10},{9,11},{10,... | collective-permute-start | bytes 688136 | tf_op jit(solution)/shard_map/ppermute | solution.py:397
  10.7 24.9 %collective-permute-start.1 = (bf16[128,896]{1,0:T(8,128)(2,1)}, bf16[128,896]{1,0:T(8,128)(2,1)S(1)}, u32[]{:S(2)}, u32[]{:S(2)}) collective-permute-start(bf16[128,896]{1,0:T(8,128)(2,1)} %cut.1), channel_id=1, source_target_pairs={{0,1},{1,2},{2,3},{3,0},{4,5},{5,6},{6,7},{7,4},{8,9},{9,10},{10,1... | collective-permute-start | bytes 688136 | tf_op jit(solution)/shard_map/ppermute | solution.py:397
  11.9 23.8 %collective-permute-start = (bf16[128,896]{1,0:T(8,128)(2,1)}, bf16[128,896]{1,0:T(8,128)(2,1)S(1)}, u32[]{:S(2)}, u32[]{:S(2)}) collective-permute-start(bf16[128,896]{1,0:T(8,128)(2,1)} %cut.1), channel_id=1, source_target_pairs={{0,3},{1,0},{2,1},{3,2},{4,7},{5,4},{6,5},{7,6},{8,11},{9,8},{10,9... | collective-permute-start | bytes 688136 | tf_op jit(solution)/shard_map/ppermute | solution.py:397
  17.4 29.6 %all-to-all-start = ((bf16[64,8,1024]{2,1,0:T(8,128)(2,1)}), bf16[64,8,1024]{2,1,0:T(8,128)(2,1)}, u32[]{:S(2)}, u32[]{:S(2)}) async-start(bf16[64,8,1024]{2,1,0:T(8,128)(2,1)} %bitcast.16), calls=%async_computation | async-start | bytes 2097152 | tf_op jit(solution)/shard_map/all_to_all | solution.py:422
  35.7 0.7 copy-start.3
  36.4 19.8 %collective-permute-start.6 = (bf16[3,128,512]{2,1,0:T(8,128)(2,1)S(1)}, bf16[3,128,512]{2,1,0:T(8,128)(2,1)S(1)}, u32[]{:S(2)}, u32[]{:S(2)}) collective-permute-start(bf16[3,128,512]{2,1,0:T(8,128)(2,1)S(1)} %get-tuple-element.15.y0), channel_id=1, source_target_pairs={{0,32},{4,36},{8,40},{12,44},{16,48},{20,52},{24,56},{28,60},{32,0... | collective-permute-start | bytes 1179656 | tf_op jit(solution)/shard_map/ppermute | solution.py:407
  37.9 17.0 %collective-permute-start.5 = (bf16[3,128,384]{2,1,0:T(8,128)(2,1)S(1)}, bf16[3,128,384]{2,1,0:T(8,128)(2,1)S(1)}, u32[]{:S(2)}, u32[]{:S(2)}) collective-permute-start(bf16[3,128,384]{2,1,0:T(8,128)(2,1)S(1)} %get-tuple-element.14.in0), channel_id=1, source_target_pairs={{0,8},{4,12},{8,16},{12,20},{16,24},{20,28},{24,0},{28,4},{32,40},... | collective-permute-start | bytes 884744 | tf_op jit(solution)/shard_map/ppermute | solution.py:401
  39.1 15.9 %collective-permute-start.4 = (bf16[3,128,384]{2,1,0:T(8,128)(2,1)S(1)}, bf16[3,128,384]{2,1,0:T(8,128)(2,1)S(1)}, u32[]{:S(2)}, u32[]{:S(2)}) collective-permute-start(bf16[3,128,384]{2,1,0:T(8,128)(2,1)S(1)} %get-tuple-element.14.in0), channel_id=1, source_target_pairs={{0,24},{4,28},{8,0},{12,4},{16,8},{20,12},{24,16},{28,20},{32,56},... | collective-permute-start | bytes 884744 | tf_op jit(solution)/shard_map/ppermute | solution.py:401
  40.6 15.6 %collective-permute-start.3 = (bf16[3,128,384]{2,1,0:T(8,128)(2,1)S(1)}, bf16[3,128,384]{2,1,0:T(8,128)(2,1)S(1)}, u32[]{:S(2)}, u32[]{:S(2)}) collective-permute-start(bf16[3,128,384]{2,1,0:T(8,128)(2,1)S(1)} %get-tuple-element.14.in0), channel_id=1, source_target_pairs={{0,16},{4,20},{8,24},{12,28},{16,0},{20,4},{24,8},{28,12},{32,48},... | collective-permute-start | bytes 884744 | tf_op jit(solution)/shard_map/ppermute | solution.py:401
  47.0 27.0 %all-to-all-start.1 = ((bf16[256,8,128]{2,1,0:T(8,128)(2,1)}), bf16[256,8,128]{2,1,0:T(8,128)(2,1)}, u32[]{:S(2)}, u32[]{:S(2)}) async-start(bf16[256,8,128]{2,1,0:T(8,128)(2,1)} %bitcast.7), calls=%async_computation.1 | async-start | bytes 1048576 | tf_op jit(solution)/shard_map/all_to_all | solution.py:425
  56.1 2.5 %copy-start = (bf16[1024,768]{1,0:T(8,128)(2,1)S(1)}, bf16[1024,768]{1,0:T(8,128)(2,1)}, u32[]{:S(2)}) copy-start(bf16[1024,768]{1,0:T(8,128)(2,1)} %value_ref.3) | copy-start | bytes 4718596
  56.1 2.5 %copy-start.2 = (s32[4]{0:T(128)S(1)}, s32[4]{0:T(128)}, u32[]{:S(2)}) copy-start(s32[4]{0:T(128)} %pad_add_fusion.meta) | copy-start | bytes 52
  57.6 5.0 %collective-permute-start.7 = (bf16[3,4,128,640]{3,2,1,0:T(8,128)(2,1)}, bf16[3,4,128,640]{3,2,1,0:T(8,128)(2,1)}, u32[]{:S(2)}, u32[]{:S(2)}) collective-permute-start(bf16[3,4,128,640]{3,2,1,0:T(8,128)(2,1)} %stack.21.near), channel_id=1, source_target_pairs={{0,4},{4,0},{8,12},{12,8},{16,20},{20,16},{24,28},{28,24},{32,36},... | collective-permute-start | bytes 5898248 | tf_op jit(solution)/shard_map/ppermute | solution.py:411
  62.6 11.4 %copy-start.1 = (bf16[256,1024]{1,0:T(8,128)(2,1)S(1)}, bf16[256,1024]{1,0:T(8,128)(2,1)}, u32[]{:S(2)}) copy-start(bf16[256,1024]{1,0:T(8,128)(2,1)} %w_out.1) | copy-start | bytes 1572868

commit v8 on v7

--- a/solution.py
+++ b/solution.py
@@ -17,7 +17,7 @@
 F32 = jnp.float32
 VMEM = pltpu.VMEM
 MIB = 1 << 20
-ORDER = (3, 1, 2)
+ORDER = (2, 1, 3)
 STEPS = (2, 3, 1)
 WIDE = 5 * HALF
 BOTH = ("rows", "heads")
@@ -141,13 +141,12 @@
     )(*parts, after)
 
 
-def stack_kernel(in0, in1, in2, in3, y0, y1, after, out_ref):
-    for n in range(3):
-        for d, ref in enumerate((in0, in1, in2, in3)):
-            out_ref[n, d, :, : 3 * HALF] = ref[n]
-        for d, ref in enumerate((y0, y1)):
-            out_ref[n, 2 * d, :, 3 * HALF :] = ref[n, :, :256]
-            out_ref[n, 2 * d + 1, :, 3 * HALF :] = ref[n, :, 256:]
+def stack_kernel(in0, in1, in2, in3, block0, block1, after, out_ref, blocks_ref):
+    for d, ref in enumerate((in0, in1, in2, in3)):
+        for n in range(3):
+            out_ref[n, d] = ref[n]
+    blocks_ref[0] = block0[...]
+    blocks_ref[1] = block1[...]
 
 
 def stack(parts, after):
@@ -157,8 +156,8 @@
         flops=10**9,
         vmem=16 * MIB,
         in_specs=[whole()] * 6 + [anywhere()],
-        out_specs=whole(),
-        out_shape=like(3, 4, BLOCK, WIDE),
+        out_specs=[whole()] * 2,
+        out_shape=[like(3, 4, BLOCK, 3 * HALF), like(2, 3, BLOCK, 4 * HALF)],
     )(*parts, after)
 
 
@@ -290,7 +289,13 @@
     )(meta, got, w_qkv)
 
 
-def column_kernel(by_x, own, near, far, out_ref, outs):
+def column_kernel(by_x, own, near, far, out_ref, near_v, far_v, outs, sems):
+    copies = []
+    for n in range(3):
+        copies.append(pltpu.make_async_copy(near.at[n], near_v.at[n], sems.at[2 * n]))
+        copies.append(pltpu.make_async_copy(far.at[n], far_v.at[n], sems.at[2 * n + 1]))
+    for copy in copies:
+        copy.start()
     allowed = causal()
     outs[:, :HALF] = own[...]
     half = 4 * BLOCK
@@ -299,15 +304,11 @@
         def keep(lo, out):
             outs[lo : lo + BLOCK, (n + 1) * HALF : (n + 2) * HALF] = out
 
+        copies[2 * n].wait()
+        copies[2 * n + 1].wait()
         qkv = jnp.dot(
-            by_x[:, :half],
-            near[n, :, :, : 3 * HALF].reshape(half, 3 * HALF),
-            preferred_element_type=F32,
-        ) + jnp.dot(
-            by_x[:, half:],
-            far[n, :, :, : 3 * HALF].reshape(half, 3 * HALF),
-            preferred_element_type=F32,
-        )
+            by_x[:, :half], near_v[n].reshape(half, 3 * HALF), preferred_element_type=F32
+        ) + jnp.dot(by_x[:, half:], far_v[n].reshape(half, 3 * HALF), preferred_element_type=F32)
         columns_of(qkv, allowed, keep)
     back = one_hot(lambda o: (o % 2) * 64 + o // 2)
     for b in range(4):
@@ -324,15 +325,21 @@
         flops=3 * 10**9,
         moved=6 * MIB,
         vmem=20 * MIB,
-        in_specs=[whole()] * 4,
+        in_specs=[whole()] * 2 + [anywhere()] * 2,
         out_specs=whole(),
         out_shape=like(C, C),
-        scratch_shapes=[VMEM((C, C), BF)],
+        scratch_shapes=[
+            VMEM((3, 4, BLOCK, 3 * HALF), BF),
+            VMEM((3, 4, BLOCK, 3 * HALF), BF),
+            VMEM((C, C), BF),
+            pltpu.SemaphoreType.DMA((6,)),
+        ],
     )(by_x, own, near, far)
 
 
 def mix_kernel(meta, columns, rows, w_out, near, far, out_ref):
     core = meta[2]
+    y = meta[3]
     left = jnp.concatenate(
         [columns[...]]
         + [
@@ -341,21 +348,25 @@
         ],
         axis=1,
     )
-    for source, on in ((near, core), (far, 1 - core)):
-        for d, y in enumerate((meta[3], 1 - meta[3])):
-            j = y * 2 + on
-            own = w_out[:, pl.ds(pl.multiple_of(j * 256, 256), 256)]
-            weight = jnp.concatenate(
-                [
-                    own[HALF:],
-                    source[:, 2 * d, :, 3 * HALF :].reshape(3 * BLOCK, 256),
-                    own[:HALF],
-                    source[:, 2 * d + 1, :, 3 * HALF :].reshape(3 * BLOCK, 256),
-                ],
-                axis=0,
-            )
-            mixed = jnp.dot(left, weight, preferred_element_type=F32)
-            out_ref[:, j] = mixed.astype(BF).reshape(64, 8, 256)
+    blocks = (
+        (near, 0, y * 2 + core),
+        (near, 1, (1 - y) * 2 + core),
+        (far, 0, y * 2 + 1 - core),
+        (far, 1, (1 - y) * 2 + 1 - core),
+    )
+    for source, n, j in blocks:
+        own = w_out[:, pl.ds(pl.multiple_of(j * 256, 256), 256)]
+        weight = jnp.concatenate(
+            [
+                own[HALF:],
+                source[n, :, :, :256].reshape(3 * BLOCK, 256),
+                own[:HALF],
+                source[n, :, :, 256:].reshape(3 * BLOCK, 256),
+            ],
+            axis=0,
+        )
+        mixed = jnp.dot(left, weight, preferred_element_type=F32)
+        out_ref[:, j] = mixed.astype(BF).reshape(64, 8, 256)
 
 
 def mix(meta, columns, rows, w_out, near, far):
@@ -428,14 +439,15 @@
 
     mine = cut(meta, w_qkv, w_out)
     others, blocks = mid([to_group(mine, k) for k in ORDER], rows_done)
-    near = stack(
+    near, blocks = stack(
         [others] + [along_x(others, d) for d in STEPS] + [blocks, other_y(blocks)], got
     )
     far = other_core(near)
+    far_blocks = other_core(blocks)
 
     by_x, own = own_part(meta, got, w_qkv)
     columns = column_part(by_x, own, near, far)
-    mixed = mix(meta, columns, rows, w_out, near, far).reshape(64 * GROUPS, 8, 256)
+    mixed = mix(meta, columns, rows, w_out, blocks, far_blocks).reshape(64 * GROUPS, 8, 256)
     back = lax.all_to_all(mixed, BOTH, split_axis=0, concat_axis=0, tiled=True)
     return join(back.reshape(64, GROUPS, 8, 256)).reshape(ROWS_LOCAL * C, 256)
 

time: 117 us -> 117 us (level)
  Pallas kernels: 30.8 us -> 29.5 us
  transfers between devices with their start and end apart: 10 -> 11, of which waited for: 4 -> 4; matrix products, arithmetic and copies ran while one was open for 0% -> 0% of each run, Pallas kernels for 19% -> 19%
where the time goes in v8:
time: 117 us
  blocking collectives  37 us (32%)
  starting transfers between devices  36.4 us (31%)
  Pallas kernels  29.5 us (25%)
  waiting for transfers between devices  12.2 us (10%)
    all_to_all x1, blocking collectives, local(): back = lax.all_to_all(mixed, BOTH, split_axis=0, concat_axis=0, tiled=True)  37 us
    ppermute x3, starting transfers between devices, to_group(): lax.ppermute(data, 'heads', [(j, (j + k) % GROUPS) for j in range(GROUPS)])  11.3 us
    all_to_all x1, starting transfers between devices, local(): lax.all_to_all(send.reshape(64, 8, D), 'rows', split_axis=0, concat_axis=...  9.65 us
    pallas_call x1, Pallas kernels, row_part(): call(row_kernel, 'row_part', moved=1, grid=(ROWS_LOCAL,), in_specs=[pl.Bl...  8.58 us
    all_to_all x1, starting transfers between devices, local(): lax.all_to_all(own_rows.reshape(64 * GROUPS, 8, HALF), BOTH, split_axis=0...  8.09 us
    all_to_all x1, waiting for transfers between devices, local(): lax.all_to_all(own_rows.reshape(64 * GROUPS, 8, HALF), BOTH, split_axis=0...  6.37 us
    pallas_call x1, Pallas kernels, column_part(): call(column_kernel, 'column_part', flops=3 * 10 ** 9, moved=6 * MIB, vmem...  5.48 us
    all_to_all x1, waiting for transfers between devices, local(): lax.all_to_all(send.reshape(64, 8, D), 'rows', split_axis=0, concat_axis=...  5.23 us
  transfers between devices with their start and end apart: 11, of which 4 were waited for; matrix products, arithmetic and copies ran while one was open for 0% of the time, Pallas kernels for 19%

profile of v8, /device:TPU:1, one launch (start us, length us, event | category | flops | bytes accessed | tf_op | source)
XLA Modules:
  0.0 116.5 jit_solution(8703403145746863443)
XLA Ops:
  0.0 0.6 pad_add_fusion.meta
  0.6 2.4 %cut.1 = bf16[128,896]{1,0:T(8,128)(2,1)} custom-call(s32[4]{0:T(128)} %pad_add_fusion.meta, bf16[1024,768]{1,0:T(8,128)(2,1)} %value_ref.3, bf16[1024,768]{1,0:T(8,128)(2,1)} %value_ref.3, bf16[1024,768]{1,0:T(8,128)(2,1)} %value_ref.3, bf16[256,1024]{1,0:T(8,128)(2,1)} %w_out.1), custom_call_target="tpu_custom_call" | custom-call | bytes 1048576 | tf_op jit(solution)/shard_map/cut/pallas_call | solution.py:108
  2.9 7.7 %collective-permute-start = (bf16[128,896]{1,0:T(8,128)(2,1)}, bf16[128,896]{1,0:T(8,128)(2,1)S(1)}, u32[]{:S(2)}, u32[]{:S(2)}) collective-permute-start(bf16[128,896]{1,0:T(8,128)(2,1)} %cut.1), channel_id=1, source_target_pairs={{0,2},{1,3},{2,0},{3,1},{4,6},{5,7},{6,4},{7,5},{8,10},{9,11},{10,... | collective-permute-start | bytes 688136 | tf_op jit(solution)/shard_map/ppermute | solution.py:408
  10.7 1.2 %collective-permute-start.1 = (bf16[128,896]{1,0:T(8,128)(2,1)}, bf16[128,896]{1,0:T(8,128)(2,1)S(1)}, u32[]{:S(2)}, u32[]{:S(2)}) collective-permute-start(bf16[128,896]{1,0:T(8,128)(2,1)} %cut.1), channel_id=1, source_target_pairs={{0,1},{1,2},{2,3},{3,0},{4,5},{5,6},{6,7},{7,4},{8,9},{9,10},{10,1... | collective-permute-start | bytes 688136 | tf_op jit(solution)/shard_map/ppermute | solution.py:408
  11.9 2.4 %collective-permute-start.2 = (bf16[128,896]{1,0:T(8,128)(2,1)}, bf16[128,896]{1,0:T(8,128)(2,1)S(1)}, u32[]{:S(2)}, u32[]{:S(2)}) collective-permute-start(bf16[128,896]{1,0:T(8,128)(2,1)} %cut.1), channel_id=1, source_target_pairs={{0,3},{1,0},{2,1},{3,2},{4,7},{5,4},{6,5},{7,6},{8,11},{9,8},{10,9... | collective-permute-start | bytes 688136 | tf_op jit(solution)/shard_map/ppermute | solution.py:408
  14.3 3.1 %prep.1.after = bf16[512,1024]{1,0:T(8,128)(2,1)} custom-call(s32[4]{0:T(128)} %pad_add_fusion.meta, bf16[4,512,1024]{2,1,0:T(8,128)(2,1)} %bitcast.14), custom_call_target="tpu_custom_call" | custom-call | flops 134217728 | bytes 2097152 | tf_op jit(solution)/shard_map/prep/pallas_call | solution.py:172
  17.4 9.6 %all-to-all-start = ((bf16[64,8,1024]{2,1,0:T(8,128)(2,1)}), bf16[64,8,1024]{2,1,0:T(8,128)(2,1)}, u32[]{:S(2)}, u32[]{:S(2)}) async-start(bf16[64,8,1024]{2,1,0:T(8,128)(2,1)} %bitcast.16), calls=%async_computation | async-start | bytes 2097152 | tf_op jit(solution)/shard_map/all_to_all | solution.py:433
  27.0 8.6 %row_part.1 = (bf16[64,4,8,128]{3,2,1,0:T(8,128)(2,1)}, bf16[16,128]{1,0:T(8,128)(2,1)}) custom-call(bf16[4,512,1024]{2,1,0:T(8,128)(2,1)} %bitcast.15, bf16[1024,768]{1,0:T(8,128)(2,1)} %value_ref.3, bf16[1024,768]{1,0:T(8,128)(2,1)} %value_ref.3, bf16[1024,768]{1,0:T(8,128)(2,1)} %value_ref.3, bf16[512,1024]{1,0:T(8,128)(2,1)} %prep.1.after), custom_call_target="tpu_custom_call" | custom-call | bytes 1 | tf_op jit(solution)/shard_map/row_part/pallas_call | solution.py:212
  35.6 0.0 collective-permute-done.in0
  35.6 0.0 collective-permute-done.1.in1
  35.6 0.0 collective-permute-done.2.in2
  35.6 0.0 copy-start.3
  35.6 0.7 copy-done.3
  36.3 0.1 mid.1
  36.4 1.5 %collective-permute-start.6 = (bf16[3,128,512]{2,1,0:T(8,128)(2,1)S(1)}, bf16[3,128,512]{2,1,0:T(8,128)(2,1)S(1)}, u32[]{:S(2)}, u32[]{:S(2)}) collective-permute-start(bf16[3,128,512]{2,1,0:T(8,128)(2,1)S(1)} %get-tuple-element.17.block0), channel_id=1, source_target_pairs={{0,32},{4,36},{8,40},{12,44},{16,48},{20,52},{24,56},{28,60},{32,0... | collective-permute-start | bytes 1179656 | tf_op jit(solution)/shard_map/ppermute | solution.py:418
  37.8 2.7 %collective-permute-start.3 = (bf16[3,128,384]{2,1,0:T(8,128)(2,1)S(1)}, bf16[3,128,384]{2,1,0:T(8,128)(2,1)S(1)}, u32[]{:S(2)}, u32[]{:S(2)}) collective-permute-start(bf16[3,128,384]{2,1,0:T(8,128)(2,1)S(1)} %get-tuple-element.16.in0), channel_id=1, source_target_pairs={{0,16},{4,20},{8,24},{12,28},{16,0},{20,4},{24,8},{28,12},{32,48},... | collective-permute-start | bytes 884744 | tf_op jit(solution)/shard_map/ppermute | solution.py:412
  40.5 0.9 collective-permute-start.4
  41.4 0.6 collective-permute-start.5
  42.0 5.2 %all-to-all-done = bf16[64,8,1024]{2,1,0:T(8,128)(2,1)} async-done(((bf16[64,8,1024]{2,1,0:T(8,128)(2,1)}), bf16[64,8,1024]{2,1,0:T(8,128)(2,1)}, u32[]{:S(2)}, u32[]{:S(2)}) %all-to-all-start) | async-done | bytes 1048608 | tf_op jit(solution)/shard_map/all_to_all | solution.py:433
  47.2 8.1 %all-to-all-start.1 = ((bf16[256,8,128]{2,1,0:T(8,128)(2,1)}), bf16[256,8,128]{2,1,0:T(8,128)(2,1)}, u32[]{:S(2)}, u32[]{:S(2)}) async-start(bf16[256,8,128]{2,1,0:T(8,128)(2,1)} %bitcast.7), calls=%async_computation.1 | async-start | bytes 1048576 | tf_op jit(solution)/shard_map/all_to_all | solution.py:436
  55.3 0.0 collective-permute-done.3.in1
  55.3 0.1 collective-permute-done.4.in2
  55.4 0.5 collective-permute-done.5.in3
  55.9 0.0 collective-permute-done.6.block1
  55.9 0.0 copy-start
  55.9 0.0 copy-start.2
  55.9 1.4 %stack.21 = (bf16[3,4,128,384]{3,2,1,0:T(8,128)(2,1)}, bf16[2,3,128,512]{3,2,1,0:T(8,128)(2,1)}) custom-call(bf16[3,128,384]{2,1,0:T(8,128)(2,1)S(1)} %get-tuple-element.16.in0, bf16[3,128,384]{2,1,0:T(8,128)(2,1)S(1)} %collective-permute-done.3.in1, bf16[3,128,384]{2,1,0:T(8,128)(2,1)S(1)} %collective-permute-done.4.in2, ...), custom_call_target="tpu_custom_call" | custom-call | flops 1000000000 | bytes 1048576 | tf_op jit(solution)/shard_map/stack/pallas_call | solution.py:153
  57.3 1.7 %collective-permute-start.7 = (bf16[3,4,128,384]{3,2,1,0:T(8,128)(2,1)}, bf16[3,4,128,384]{3,2,1,0:T(8,128)(2,1)}, u32[]{:S(2)}, u32[]{:S(2)}) collective-permute-start(bf16[3,4,128,384]{3,2,1,0:T(8,128)(2,1)} %get-tuple-element.18.near), channel_id=1, source_target_pairs={{0,4},{4,0},{8,12},{12,8},{16,20},{20,16},{24,28},{28,24},{32,36},... | collective-permute-start | bytes 3538952 | tf_op jit(solution)/shard_map/ppermute | solution.py:422
  59.0 0.0 collective-permute-start.8
  59.0 0.0 copy-done
  59.0 0.0 copy-done.2
  59.0 3.5 %own_part.1 = (bf16[512,1024]{1,0:T(8,128)(2,1)S(1)}, bf16[512,128]{1,0:T(8,128)(2,1)S(1)}) custom-call(s32[4]{0:T(128)S(1)} %copy-done.2, bf16[512,1024]{1,0:T(8,128)(2,1)} %bitcast.6.got_ref.after, bf16[1024,768]{1,0:T(8,128)(2,1)S(1)} %copy-done), custom_call_target="tpu_custom_call" | custom-call | flops 999999995904 | bytes 4194304 | tf_op jit(solution)/shard_map/own_part/pallas_call | solution.py:275
  62.5 0.0 collective-permute-done.7.far
  62.5 0.0 copy-start.1
  62.5 5.5 %column_part.1.columns = bf16[512,512]{1,0:T(8,128)(2,1)S(1)} custom-call(bf16[512,1024]{1,0:T(8,128)(2,1)S(1)} %get-tuple-element.13.by_x, bf16[512,128]{1,0:T(8,128)(2,1)S(1)} %get-tuple-element.14.own, bf16[3,4,128,384]{3,2,1,0:T(8,128)(2,1)} %get-tuple-element.18.near, bf16[3,4,128,384]{3,2,1,0:T(8,128)(2,1)} %collective-permute-done.7.far), custom_call_target="tpu_custom_call" | custom-call | flops 3000000000 | bytes 6291456 | tf_op jit(solution)/shard_map/column_part/pallas_call | solution.py:322
  68.0 6.4 %all-to-all-done.1 = bf16[256,8,128]{2,1,0:T(8,128)(2,1)} async-done(((bf16[256,8,128]{2,1,0:T(8,128)(2,1)}), bf16[256,8,128]{2,1,0:T(8,128)(2,1)}, u32[]{:S(2)}, u32[]{:S(2)}) %all-to-all-start.1) | async-done | bytes 524320 | tf_op jit(solution)/shard_map/all_to_all | solution.py:436
  74.4 0.0 collective-permute-done.8.far
  74.4 0.0 copy-done.1
  74.4 2.9 %mix.1 = bf16[64,4,8,256]{3,2,1,0:T(8,128)(2,1)S(1)} custom-call(s32[4]{0:T(128)S(1)} %copy-done.2, bf16[512,512]{1,0:T(8,128)(2,1)S(1)} %column_part.1.columns, bf16[64,4,8,128]{3,2,1,0:T(8,128)(2,1)} %bitcast.8.rows, bf16[256,1024]{1,0:T(8,128)(2,1)S(1)} %copy-done.1, bf16[2,3,128,512]{3,2,1,0:T(8,128)(2,1)} %get-tuple-element.20.near, ...), custom_call_target="tpu_custom_call" | custom-call | flops 1000000000 | bytes 6291456 | tf_op jit(solution)/shard_map/mix/pallas_call | solution.py:373
  77.3 37.0 %all_to_all.15 = bf16[256,8,256]{2,1,0:T(8,128)(2,1)S(1)} all-to-all(bf16[256,8,256]{2,1,0:T(8,128)(2,1)S(1)} %bitcast.12), channel_id=1, replica_groups=mesh['rows'=64,'heads'=4] {'rows','heads'}, dimensions={0} | all-to-all | bytes 2097152 | tf_op jit(solution)/shard_map/all_to_all | solution.py:451
  114.3 2.2 %join.1 = bf16[4,4,128,256]{3,2,1,0:T(8,128)(2,1)} custom-call(bf16[64,4,8,256]{3,2,1,0:T(8,128)(2,1)S(1)} %bitcast.13), custom_call_target="tpu_custom_call" | custom-call | flops 100000000 | bytes 4194304 | tf_op jit(solution)/shard_map/join/pallas_call | solution.py:394
Async XLA Ops:
  2.9 32.7 %collective-permute-start = (bf16[128,896]{1,0:T(8,128)(2,1)}, bf16[128,896]{1,0:T(8,128)(2,1)S(1)}, u32[]{:S(2)}, u32[]{:S(2)}) collective-permute-start(bf16[128,896]{1,0:T(8,128)(2,1)} %cut.1), channel_id=1, source_target_pairs={{0,2},{1,3},{2,0},{3,1},{4,6},{5,7},{6,4},{7,5},{8,10},{9,11},{10,... | collective-permute-start | bytes 688136 | tf_op jit(solution)/shard_map/ppermute | solution.py:408
  10.7 24.9 %collective-permute-start.1 = (bf16[128,896]{1,0:T(8,128)(2,1)}, bf16[128,896]{1,0:T(8,128)(2,1)S(1)}, u32[]{:S(2)}, u32[]{:S(2)}) collective-permute-start(bf16[128,896]{1,0:T(8,128)(2,1)} %cut.1), channel_id=1, source_target_pairs={{0,1},{1,2},{2,3},{3,0},{4,5},{5,6},{6,7},{7,4},{8,9},{9,10},{10,1... | collective-permute-start | bytes 688136 | tf_op jit(solution)/shard_map/ppermute | solution.py:408
  11.9 23.7 %collective-permute-start.2 = (bf16[128,896]{1,0:T(8,128)(2,1)}, bf16[128,896]{1,0:T(8,128)(2,1)S(1)}, u32[]{:S(2)}, u32[]{:S(2)}) collective-permute-start(bf16[128,896]{1,0:T(8,128)(2,1)} %cut.1), channel_id=1, source_target_pairs={{0,3},{1,0},{2,1},{3,2},{4,7},{5,4},{6,5},{7,6},{8,11},{9,8},{10,9... | collective-permute-start | bytes 688136 | tf_op jit(solution)/shard_map/ppermute | solution.py:408
  17.4 29.9 %all-to-all-start = ((bf16[64,8,1024]{2,1,0:T(8,128)(2,1)}), bf16[64,8,1024]{2,1,0:T(8,128)(2,1)}, u32[]{:S(2)}, u32[]{:S(2)}) async-start(bf16[64,8,1024]{2,1,0:T(8,128)(2,1)} %bitcast.16), calls=%async_computation | async-start | bytes 2097152 | tf_op jit(solution)/shard_map/all_to_all | solution.py:433
  35.6 0.7 copy-start.3
  36.4 19.6 %collective-permute-start.6 = (bf16[3,128,512]{2,1,0:T(8,128)(2,1)S(1)}, bf16[3,128,512]{2,1,0:T(8,128)(2,1)S(1)}, u32[]{:S(2)}, u32[]{:S(2)}) collective-permute-start(bf16[3,128,512]{2,1,0:T(8,128)(2,1)S(1)} %get-tuple-element.17.block0), channel_id=1, source_target_pairs={{0,32},{4,36},{8,40},{12,44},{16,48},{20,52},{24,56},{28,60},{32,0... | collective-permute-start | bytes 1179656 | tf_op jit(solution)/shard_map/ppermute | solution.py:418
  37.8 17.5 %collective-permute-start.3 = (bf16[3,128,384]{2,1,0:T(8,128)(2,1)S(1)}, bf16[3,128,384]{2,1,0:T(8,128)(2,1)S(1)}, u32[]{:S(2)}, u32[]{:S(2)}) collective-permute-start(bf16[3,128,384]{2,1,0:T(8,128)(2,1)S(1)} %get-tuple-element.16.in0), channel_id=1, source_target_pairs={{0,16},{4,20},{8,24},{12,28},{16,0},{20,4},{24,8},{28,12},{32,48},... | collective-permute-start | bytes 884744 | tf_op jit(solution)/shard_map/ppermute | solution.py:412
  40.5 14.9 %collective-permute-start.4 = (bf16[3,128,384]{2,1,0:T(8,128)(2,1)S(1)}, bf16[3,128,384]{2,1,0:T(8,128)(2,1)S(1)}, u32[]{:S(2)}, u32[]{:S(2)}) collective-permute-start(bf16[3,128,384]{2,1,0:T(8,128)(2,1)S(1)} %get-tuple-element.16.in0), channel_id=1, source_target_pairs={{0,24},{4,28},{8,0},{12,4},{16,8},{20,12},{24,16},{28,20},{32,56},... | collective-permute-start | bytes 884744 | tf_op jit(solution)/shard_map/ppermute | solution.py:412
  41.4 14.5 %collective-permute-start.5 = (bf16[3,128,384]{2,1,0:T(8,128)(2,1)S(1)}, bf16[3,128,384]{2,1,0:T(8,128)(2,1)S(1)}, u32[]{:S(2)}, u32[]{:S(2)}) collective-permute-start(bf16[3,128,384]{2,1,0:T(8,128)(2,1)S(1)} %get-tuple-element.16.in0), channel_id=1, source_target_pairs={{0,8},{4,12},{8,16},{12,20},{16,24},{20,28},{24,0},{28,4},{32,40},... | collective-permute-start | bytes 884744 | tf_op jit(solution)/shard_map/ppermute | solution.py:412
  47.2 27.2 %all-to-all-start.1 = ((bf16[256,8,128]{2,1,0:T(8,128)(2,1)}), bf16[256,8,128]{2,1,0:T(8,128)(2,1)}, u32[]{:S(2)}, u32[]{:S(2)}) async-start(bf16[256,8,128]{2,1,0:T(8,128)(2,1)} %bitcast.7), calls=%async_computation.1 | async-start | bytes 1048576 | tf_op jit(solution)/shard_map/all_to_all | solution.py:436
  55.9 3.1 %copy-start = (bf16[1024,768]{1,0:T(8,128)(2,1)S(1)}, bf16[1024,768]{1,0:T(8,128)(2,1)}, u32[]{:S(2)}) copy-start(bf16[1024,768]{1,0:T(8,128)(2,1)} %value_ref.3) | copy-start | bytes 4718596
  55.9 3.1 %copy-start.2 = (s32[4]{0:T(128)S(1)}, s32[4]{0:T(128)}, u32[]{:S(2)}) copy-start(s32[4]{0:T(128)} %pad_add_fusion.meta) | copy-start | bytes 52
  57.3 5.2 %collective-permute-start.7 = (bf16[3,4,128,384]{3,2,1,0:T(8,128)(2,1)}, bf16[3,4,128,384]{3,2,1,0:T(8,128)(2,1)}, u32[]{:S(2)}, u32[]{:S(2)}) collective-permute-start(bf16[3,4,128,384]{3,2,1,0:T(8,128)(2,1)} %get-tuple-element.18.near), channel_id=1, source_target_pairs={{0,4},{4,0},{8,12},{12,8},{16,20},{20,16},{24,28},{28,24},{32,36},... | collective-permute-start | bytes 3538952 | tf_op jit(solution)/shard_map/ppermute | solution.py:422
  59.0 15.4 %collective-permute-start.8 = (bf16[2,3,128,512]{3,2,1,0:T(8,128)(2,1)}, bf16[2,3,128,512]{3,2,1,0:T(8,128)(2,1)}, u32[]{:S(2)}, u32[]{:S(2)}) collective-permute-start(bf16[2,3,128,512]{3,2,1,0:T(8,128)(2,1)} %get-tuple-element.20.near), channel_id=1, source_target_pairs={{0,4},{4,0},{8,12},{12,8},{16,20},{20,16},{24,28},{28,24},{32,36},... | collective-permute-start | bytes 2359304 | tf_op jit(solution)/shard_map/ppermute | solution.py:422
  62.5 11.9 %copy-start.1 = (bf16[256,1024]{1,0:T(8,128)(2,1)S(1)}, bf16[256,1024]{1,0:T(8,128)(2,1)}, u32[]{:S(2)}) copy-start(bf16[256,1024]{1,0:T(8,128)(2,1)} %w_out.1) | copy-start | bytes 1572868

commit v9 on v8

--- a/solution.py
+++ b/solution.py
@@ -34,6 +34,22 @@
 
 def smem():
     return pl.BlockSpec(memory_space=pltpu.SMEM)
+
+
+def group_of(meta):
+    return meta[0] & 3
+
+
+def x_of(meta):
+    return (meta[0] >> 3) & 3
+
+
+def core_of(meta):
+    return (meta[0] >> 2) & 1
+
+
+def y_of(meta):
+    return (meta[0] >> 5) & 1
 
 
 def one_hot(source_of):
@@ -103,7 +119,7 @@
 
 def cut(meta, w_qkv, w_out):
     def part(n):
-        return pl.BlockSpec((BLOCK, HALF), lambda b, meta: (meta[1] * 2 + meta[2], 2 * n + 1))
+        return pl.BlockSpec((BLOCK, HALF), lambda b, meta: (x_of(meta) * 2 + core_of(meta), 2 * n + 1))
 
     return call(
         cut_kernel,
@@ -115,7 +131,7 @@
                 part(0),
                 part(1),
                 part(2),
-                pl.BlockSpec((256, 256), lambda b, meta: (0, meta[3] * 2 + meta[2])),
+                pl.BlockSpec((256, 256), lambda b, meta: (0, y_of(meta) * 2 + core_of(meta))),
             ],
             out_specs=pl.BlockSpec((BLOCK, 7 * HALF), lambda b, meta: (0, 0)),
         ),
@@ -177,7 +193,7 @@
         grid_spec=pltpu.PrefetchScalarGridSpec(
             num_scalar_prefetch=1,
             grid=(2,),
-            in_specs=[pl.BlockSpec((4, 64, D), lambda b, meta: (0, meta[0] * 2 + b, 0))],
+            in_specs=[pl.BlockSpec((4, 64, D), lambda b, meta: (0, group_of(meta) * 2 + b, 0))],
             out_specs=pl.BlockSpec((256, D), lambda b, meta: (b, 0)),
         ),
         out_shape=like(C, D),
@@ -255,11 +271,11 @@
         moved = move(pick, got_ref[b * BLOCK : (b + 1) * BLOCK, :])
         held[b * 64 : b * 64 + 64, :] = moved[:64]
         held[256 + b * 64 : 256 + b * 64 + 64, :] = moved[64:]
-    core = meta[2]
+    core = core_of(meta)
     for n, d in enumerate((0,) + STEPS):
         for far, on in enumerate((core, 1 - core)):
             lo = (4 * far + n) * BLOCK
-            source = pl.multiple_of((lax.rem(meta[1] + 4 - d, 4) * 2 + on) * BLOCK, BLOCK)
+            source = pl.multiple_of((lax.rem(x_of(meta) + 4 - d, 4) * 2 + on) * BLOCK, BLOCK)
             by_x[:, lo : lo + BLOCK] = held[:, pl.ds(source, BLOCK)]
 
     def keep(lo, out):
@@ -338,12 +354,12 @@
 
 
 def mix_kernel(meta, columns, rows, w_out, near, far, out_ref):
-    core = meta[2]
-    y = meta[3]
+    core = core_of(meta)
+    y = y_of(meta)
     left = jnp.concatenate(
         [columns[...]]
         + [
-            rows[:, lax.rem(meta[0] + GROUPS - k, GROUPS)].reshape(C, HALF)
+            rows[:, lax.rem(group_of(meta) + GROUPS - k, GROUPS)].reshape(C, HALF)
             for k in (0,) + ORDER
         ],
         axis=1,
@@ -383,9 +399,10 @@
 
 
 def join_kernel(got_ref, out_ref):
+    j = pl.program_id(0)
     pick = one_hot(lambda o: ((o // 2) % 16) * 8 + (o // 32) * 2 + o % 2)
     for b in range(4):
-        moved = move(pick, got_ref[b * 16 : (b + 1) * 16, 0].reshape(BLOCK, 256))
+        moved = move(pick, got_ref[b * 16 : (b + 1) * 16, j].reshape(BLOCK, 256))
         for r in range(ROWS_LOCAL):
             out_ref[r, 0, b * 32 : (b + 1) * 32] = moved[r * 32 : (r + 1) * 32]
 
@@ -398,7 +415,7 @@
         moved=4 * MIB,
         vmem=16 * MIB,
         grid=(GROUPS,),
-        in_specs=[pl.BlockSpec((64, 1, 8, 256), lambda j: (0, j, 0, 0))],
+        in_specs=[whole()],
         out_specs=pl.BlockSpec((ROWS_LOCAL, 1, BLOCK, 256), lambda j: (0, j, 0, 0)),
         out_shape=like(ROWS_LOCAL, GROUPS, BLOCK, 256),
     )(got)
@@ -423,9 +440,7 @@
 
 
 def local(signal, w_qkv, w_out):
-    i = lax.axis_index("rows")
-    g = lax.axis_index("heads")
-    meta = jnp.stack([g, i // 2 % 4, i % 2, i // 8 % 2]).astype(jnp.int32)
+    meta = lax.axis_index(("rows", "heads")).astype(jnp.int32).reshape(1)
     sig = signal.reshape(ROWS_LOCAL, C, D)
 
     send = prep(meta, sig)

time: 117 us -> 115 us (0.983)
  Pallas kernels: 29.5 us -> 27.9 us
  transfers between devices with their start and end apart: 11 -> 11, of which waited for: 4 -> 3; matrix products, arithmetic and copies ran while one was open for 0% -> 0% of each run, Pallas kernels for 19% -> 19%
where the time goes in v9:
time: 115 us
  blocking collectives  37 us (32%)
  starting transfers between devices  35.7 us (31%)
  Pallas kernels  27.9 us (24%)
  waiting for transfers between devices  13.2 us (11%)
    all_to_all x1, blocking collectives, local(): back = lax.all_to_all(mixed, BOTH, split_axis=0, concat_axis=0, tiled=True)  37 us
    ppermute x3, starting transfers between devices, to_group(): lax.ppermute(data, 'heads', [(j, (j + k) % GROUPS) for j in range(GROUPS)])  11.3 us
    all_to_all x1, starting transfers between devices, local(): lax.all_to_all(send.reshape(64, 8, D), 'rows', split_axis=0, concat_axis=...  9.64 us
    pallas_call x1, Pallas kernels, row_part(): call(row_kernel, 'row_part', moved=1, grid=(ROWS_LOCAL,), in_specs=[pl.Bl...  8.57 us
    all_to_all x1, starting transfers between devices, local(): lax.all_to_all(own_rows.reshape(64 * GROUPS, 8, HALF), BOTH, split_axis=0...  7.72 us
    all_to_all x1, waiting for transfers between devices, local(): lax.all_to_all(own_rows.reshape(64 * GROUPS, 8, HALF), BOTH, split_axis=0...  6.41 us
    all_to_all x1, waiting for transfers between devices, local(): lax.all_to_all(send.reshape(64, 8, D), 'rows', split_axis=0, concat_axis=...  5.92 us
    pallas_call x1, Pallas kernels, column_part(): call(column_kernel, 'column_part', flops=3 * 10 ** 9, moved=6 * MIB, vmem...  5.47 us
  transfers between devices with their start and end apart: 11, of which 3 were waited for; matrix products, arithmetic and copies ran while one was open for 0% of the time, Pallas kernels for 19%

profile of v9, /device:TPU:1, one launch (start us, length us, event | category | flops | bytes accessed | tf_op | source)
XLA Modules:
  0.0 114.6 jit_solution(14183962262100688033)
XLA Ops:
  0.0 1.7 %cut.1 = bf16[128,896]{1,0:T(8,128)(2,1)} custom-call(s32[1]{0:T(128)} %bitcast.meta, bf16[1024,768]{1,0:T(8,128)(2,1)} %value_ref.3, bf16[1024,768]{1,0:T(8,128)(2,1)} %value_ref.3, bf16[1024,768]{1,0:T(8,128)(2,1)} %value_ref.3, bf16[256,1024]{1,0:T(8,128)(2,1)} %w_out.1), custom_call_target="tpu_custom_call" | custom-call | bytes 1048576 | tf_op jit(solution)/shard_map/cut/pallas_call | solution.py:124
  1.7 7.7 %collective-permute-start = (bf16[128,896]{1,0:T(8,128)(2,1)}, bf16[128,896]{1,0:T(8,128)(2,1)S(1)}, u32[]{:S(2)}, u32[]{:S(2)}) collective-permute-start(bf16[128,896]{1,0:T(8,128)(2,1)} %cut.1), channel_id=1, source_target_pairs={{0,2},{1,3},{2,0},{3,1},{4,6},{5,7},{6,4},{7,5},{8,10},{9,11},{10,... | collective-permute-start | bytes 688136 | tf_op jit(solution)/shard_map/ppermute | solution.py:425
  9.4 1.2 %collective-permute-start.1 = (bf16[128,896]{1,0:T(8,128)(2,1)}, bf16[128,896]{1,0:T(8,128)(2,1)S(1)}, u32[]{:S(2)}, u32[]{:S(2)}) collective-permute-start(bf16[128,896]{1,0:T(8,128)(2,1)} %cut.1), channel_id=1, source_target_pairs={{0,1},{1,2},{2,3},{3,0},{4,5},{5,6},{6,7},{7,4},{8,9},{9,10},{10,1... | collective-permute-start | bytes 688136 | tf_op jit(solution)/shard_map/ppermute | solution.py:425
  10.6 2.4 %collective-permute-start.2 = (bf16[128,896]{1,0:T(8,128)(2,1)}, bf16[128,896]{1,0:T(8,128)(2,1)S(1)}, u32[]{:S(2)}, u32[]{:S(2)}) collective-permute-start(bf16[128,896]{1,0:T(8,128)(2,1)} %cut.1), channel_id=1, source_target_pairs={{0,3},{1,0},{2,1},{3,2},{4,7},{5,4},{6,5},{7,6},{8,11},{9,8},{10,9... | collective-permute-start | bytes 688136 | tf_op jit(solution)/shard_map/ppermute | solution.py:425
  13.0 2.4 %prep.1.after = bf16[512,1024]{1,0:T(8,128)(2,1)} custom-call(s32[1]{0:T(128)} %bitcast.meta, bf16[4,512,1024]{2,1,0:T(8,128)(2,1)} %bitcast.11), custom_call_target="tpu_custom_call" | custom-call | flops 134217728 | bytes 2097152 | tf_op jit(solution)/shard_map/prep/pallas_call | solution.py:188
  15.4 9.6 %all-to-all-start = ((bf16[64,8,1024]{2,1,0:T(8,128)(2,1)}), bf16[64,8,1024]{2,1,0:T(8,128)(2,1)}, u32[]{:S(2)}, u32[]{:S(2)}) async-start(bf16[64,8,1024]{2,1,0:T(8,128)(2,1)} %bitcast.13), calls=%async_computation | async-start | bytes 2097152 | tf_op jit(solution)/shard_map/all_to_all | solution.py:448
  25.1 8.6 %row_part.1 = (bf16[64,4,8,128]{3,2,1,0:T(8,128)(2,1)}, bf16[16,128]{1,0:T(8,128)(2,1)}) custom-call(bf16[4,512,1024]{2,1,0:T(8,128)(2,1)} %bitcast.12, bf16[1024,768]{1,0:T(8,128)(2,1)} %value_ref.3, bf16[1024,768]{1,0:T(8,128)(2,1)} %value_ref.3, bf16[1024,768]{1,0:T(8,128)(2,1)} %value_ref.3, bf16[512,1024]{1,0:T(8,128)(2,1)} %prep.1.after), custom_call_target="tpu_custom_call" | custom-call | bytes 1 | tf_op jit(solution)/shard_map/row_part/pallas_call | solution.py:228
  33.6 0.0 collective-permute-done.in0
  33.6 0.0 collective-permute-done.1.in1
  33.7 0.0 collective-permute-done.2.in2
  33.7 0.0 copy-start.2
  33.7 0.7 copy-done.2
  34.3 0.1 mid.1
  34.4 1.5 %collective-permute-start.6 = (bf16[3,128,512]{2,1,0:T(8,128)(2,1)S(1)}, bf16[3,128,512]{2,1,0:T(8,128)(2,1)S(1)}, u32[]{:S(2)}, u32[]{:S(2)}) collective-permute-start(bf16[3,128,512]{2,1,0:T(8,128)(2,1)S(1)} %get-tuple-element.17.block0), channel_id=1, source_target_pairs={{0,32},{4,36},{8,40},{12,44},{16,48},{20,52},{24,56},{28,60},{32,0... | collective-permute-start | bytes 1179656 | tf_op jit(solution)/shard_map/ppermute | solution.py:435
  35.9 2.7 %collective-permute-start.3 = (bf16[3,128,384]{2,1,0:T(8,128)(2,1)S(1)}, bf16[3,128,384]{2,1,0:T(8,128)(2,1)S(1)}, u32[]{:S(2)}, u32[]{:S(2)}) collective-permute-start(bf16[3,128,384]{2,1,0:T(8,128)(2,1)S(1)} %get-tuple-element.16.in0), channel_id=1, source_target_pairs={{0,16},{4,20},{8,24},{12,28},{16,0},{20,4},{24,8},{28,12},{32,48},... | collective-permute-start | bytes 884744 | tf_op jit(solution)/shard_map/ppermute | solution.py:429
  38.6 0.9 collective-permute-start.4
  39.5 0.6 collective-permute-start.5
  40.0 5.9 %all-to-all-done = bf16[64,8,1024]{2,1,0:T(8,128)(2,1)} async-done(((bf16[64,8,1024]{2,1,0:T(8,128)(2,1)}), bf16[64,8,1024]{2,1,0:T(8,128)(2,1)}, u32[]{:S(2)}, u32[]{:S(2)}) %all-to-all-start) | async-done | bytes 1048608 | tf_op jit(solution)/shard_map/all_to_all | solution.py:448
  46.0 7.7 %all-to-all-start.1 = ((bf16[256,8,128]{2,1,0:T(8,128)(2,1)}), bf16[256,8,128]{2,1,0:T(8,128)(2,1)}, u32[]{:S(2)}, u32[]{:S(2)}) async-start(bf16[256,8,128]{2,1,0:T(8,128)(2,1)} %bitcast.4), calls=%async_computation.1 | async-start | bytes 1048576 | tf_op jit(solution)/shard_map/all_to_all | solution.py:451
  53.7 0.0 collective-permute-done.3.in1
  53.7 0.0 collective-permute-done.4.in2
  53.7 0.8 collective-permute-done.5.in3
  54.5 0.0 collective-permute-done.6.block1
  54.5 0.0 copy-start
  54.5 1.4 %stack.1 = (bf16[3,4,128,384]{3,2,1,0:T(8,128)(2,1)}, bf16[2,3,128,512]{3,2,1,0:T(8,128)(2,1)}) custom-call(bf16[3,128,384]{2,1,0:T(8,128)(2,1)S(1)} %get-tuple-element.16.in0, bf16[3,128,384]{2,1,0:T(8,128)(2,1)S(1)} %collective-permute-done.3.in1, bf16[3,128,384]{2,1,0:T(8,128)(2,1)S(1)} %collective-permute-done.4.in2, ...), custom_call_target="tpu_custom_call" | custom-call | flops 1000000000 | bytes 1048576 | tf_op jit(solution)/shard_map/stack/pallas_call | solution.py:169
  55.9 1.4 %collective-permute-start.7 = (bf16[3,4,128,384]{3,2,1,0:T(8,128)(2,1)}, bf16[3,4,128,384]{3,2,1,0:T(8,128)(2,1)}, u32[]{:S(2)}, u32[]{:S(2)}) collective-permute-start(bf16[3,4,128,384]{3,2,1,0:T(8,128)(2,1)} %get-tuple-element.18.near), channel_id=1, source_target_pairs={{0,4},{4,0},{8,12},{12,8},{16,20},{20,16},{24,28},{28,24},{32,36},... | collective-permute-start | bytes 3538952 | tf_op jit(solution)/shard_map/ppermute | solution.py:439
  57.4 0.0 collective-permute-start.8
  57.4 0.0 copy-done
  57.4 3.5 %own_part.1 = (bf16[512,1024]{1,0:T(8,128)(2,1)S(1)}, bf16[512,128]{1,0:T(8,128)(2,1)S(1)}) custom-call(s32[1]{0:T(128)} %bitcast.meta, bf16[512,1024]{1,0:T(8,128)(2,1)} %bitcast.3.got_ref.after, bf16[1024,768]{1,0:T(8,128)(2,1)S(1)} %copy-done), custom_call_target="tpu_custom_call" | custom-call | flops 999999995904 | bytes 4194304 | tf_op jit(solution)/shard_map/own_part/pallas_call | solution.py:291
  60.8 0.0 collective-permute-done.7.far
  60.9 0.0 copy-start.1
  60.9 5.5 %column_part.1.columns = bf16[512,512]{1,0:T(8,128)(2,1)S(1)} custom-call(bf16[512,1024]{1,0:T(8,128)(2,1)S(1)} %get-tuple-element.13.by_x, bf16[512,128]{1,0:T(8,128)(2,1)S(1)} %get-tuple-element.14.own, bf16[3,4,128,384]{3,2,1,0:T(8,128)(2,1)} %get-tuple-element.18.near, bf16[3,4,128,384]{3,2,1,0:T(8,128)(2,1)} %collective-permute-done.7.far), custom_call_target="tpu_custom_call" | custom-call | flops 3000000000 | bytes 6291456 | tf_op jit(solution)/shard_map/column_part/pallas_call | solution.py:338
  66.4 6.4 %all-to-all-done.1 = bf16[256,8,128]{2,1,0:T(8,128)(2,1)} async-done(((bf16[256,8,128]{2,1,0:T(8,128)(2,1)}), bf16[256,8,128]{2,1,0:T(8,128)(2,1)}, u32[]{:S(2)}, u32[]{:S(2)}) %all-to-all-start.1) | async-done | bytes 524320 | tf_op jit(solution)/shard_map/all_to_all | solution.py:451
  72.8 0.0 collective-permute-done.8.far
  72.8 0.0 copy-done.1
  72.8 2.8 %mix.1 = bf16[64,4,8,256]{3,2,1,0:T(8,128)(2,1)S(1)} custom-call(s32[1]{0:T(128)} %bitcast.meta, bf16[512,512]{1,0:T(8,128)(2,1)S(1)} %column_part.1.columns, bf16[64,4,8,128]{3,2,1,0:T(8,128)(2,1)} %bitcast.5.rows, bf16[256,1024]{1,0:T(8,128)(2,1)S(1)} %copy-done.1, bf16[2,3,128,512]{3,2,1,0:T(8,128)(2,1)} %get-tuple-element.20.near, ...), custom_call_target="tpu_custom_call" | custom-call | flops 1000000000 | bytes 6291456 | tf_op jit(solution)/shard_map/mix/pallas_call | solution.py:389
  75.6 37.0 %all_to_all.15 = bf16[256,8,256]{2,1,0:T(8,128)(2,1)S(1)} all-to-all(bf16[256,8,256]{2,1,0:T(8,128)(2,1)S(1)} %bitcast.9), channel_id=1, replica_groups=mesh['rows'=64,'heads'=4] {'rows','heads'}, dimensions={0} | all-to-all | bytes 2097152 | tf_op jit(solution)/shard_map/all_to_all | solution.py:466
  112.6 2.1 %join.1 = bf16[4,4,128,256]{3,2,1,0:T(8,128)(2,1)} custom-call(bf16[64,4,8,256]{3,2,1,0:T(8,128)(2,1)S(1)} %bitcast.10), custom_call_target="tpu_custom_call" | custom-call | flops 100000000 | bytes 4194304 | tf_op jit(solution)/shard_map/join/pallas_call | solution.py:411
Async XLA Ops:
  1.7 32.0 %collective-permute-start = (bf16[128,896]{1,0:T(8,128)(2,1)}, bf16[128,896]{1,0:T(8,128)(2,1)S(1)}, u32[]{:S(2)}, u32[]{:S(2)}) collective-permute-start(bf16[128,896]{1,0:T(8,128)(2,1)} %cut.1), channel_id=1, source_target_pairs={{0,2},{1,3},{2,0},{3,1},{4,6},{5,7},{6,4},{7,5},{8,10},{9,11},{10,... | collective-permute-start | bytes 688136 | tf_op jit(solution)/shard_map/ppermute | solution.py:425
  9.4 24.2 %collective-permute-start.1 = (bf16[128,896]{1,0:T(8,128)(2,1)}, bf16[128,896]{1,0:T(8,128)(2,1)S(1)}, u32[]{:S(2)}, u32[]{:S(2)}) collective-permute-start(bf16[128,896]{1,0:T(8,128)(2,1)} %cut.1), channel_id=1, source_target_pairs={{0,1},{1,2},{2,3},{3,0},{4,5},{5,6},{6,7},{7,4},{8,9},{9,10},{10,1... | collective-permute-start | bytes 688136 | tf_op jit(solution)/shard_map/ppermute | solution.py:425
  10.6 23.1 %collective-permute-start.2 = (bf16[128,896]{1,0:T(8,128)(2,1)}, bf16[128,896]{1,0:T(8,128)(2,1)S(1)}, u32[]{:S(2)}, u32[]{:S(2)}) collective-permute-start(bf16[128,896]{1,0:T(8,128)(2,1)} %cut.1), channel_id=1, source_target_pairs={{0,3},{1,0},{2,1},{3,2},{4,7},{5,4},{6,5},{7,6},{8,11},{9,8},{10,9... | collective-permute-start | bytes 688136 | tf_op jit(solution)/shard_map/ppermute | solution.py:425
  15.4 30.5 %all-to-all-start = ((bf16[64,8,1024]{2,1,0:T(8,128)(2,1)}), bf16[64,8,1024]{2,1,0:T(8,128)(2,1)}, u32[]{:S(2)}, u32[]{:S(2)}) async-start(bf16[64,8,1024]{2,1,0:T(8,128)(2,1)} %bitcast.13), calls=%async_computation | async-start | bytes 2097152 | tf_op jit(solution)/shard_map/all_to_all | solution.py:448
  33.7 0.7 copy-start.2
  34.4 20.1 %collective-permute-start.6 = (bf16[3,128,512]{2,1,0:T(8,128)(2,1)S(1)}, bf16[3,128,512]{2,1,0:T(8,128)(2,1)S(1)}, u32[]{:S(2)}, u32[]{:S(2)}) collective-permute-start(bf16[3,128,512]{2,1,0:T(8,128)(2,1)S(1)} %get-tuple-element.17.block0), channel_id=1, source_target_pairs={{0,32},{4,36},{8,40},{12,44},{16,48},{20,52},{24,56},{28,60},{32,0... | collective-permute-start | bytes 1179656 | tf_op jit(solution)/shard_map/ppermute | solution.py:435
  35.9 17.8 %collective-permute-start.3 = (bf16[3,128,384]{2,1,0:T(8,128)(2,1)S(1)}, bf16[3,128,384]{2,1,0:T(8,128)(2,1)S(1)}, u32[]{:S(2)}, u32[]{:S(2)}) collective-permute-start(bf16[3,128,384]{2,1,0:T(8,128)(2,1)S(1)} %get-tuple-element.16.in0), channel_id=1, source_target_pairs={{0,16},{4,20},{8,24},{12,28},{16,0},{20,4},{24,8},{28,12},{32,48},... | collective-permute-start | bytes 884744 | tf_op jit(solution)/shard_map/ppermute | solution.py:429
  38.6 15.1 %collective-permute-start.4 = (bf16[3,128,384]{2,1,0:T(8,128)(2,1)S(1)}, bf16[3,128,384]{2,1,0:T(8,128)(2,1)S(1)}, u32[]{:S(2)}, u32[]{:S(2)}) collective-permute-start(bf16[3,128,384]{2,1,0:T(8,128)(2,1)S(1)} %get-tuple-element.16.in0), channel_id=1, source_target_pairs={{0,24},{4,28},{8,0},{12,4},{16,8},{20,12},{24,16},{28,20},{32,56},... | collective-permute-start | bytes 884744 | tf_op jit(solution)/shard_map/ppermute | solution.py:429
  39.5 15.1 %collective-permute-start.5 = (bf16[3,128,384]{2,1,0:T(8,128)(2,1)S(1)}, bf16[3,128,384]{2,1,0:T(8,128)(2,1)S(1)}, u32[]{:S(2)}, u32[]{:S(2)}) collective-permute-start(bf16[3,128,384]{2,1,0:T(8,128)(2,1)S(1)} %get-tuple-element.16.in0), channel_id=1, source_target_pairs={{0,8},{4,12},{8,16},{12,20},{16,24},{20,28},{24,0},{28,4},{32,40},... | collective-permute-start | bytes 884744 | tf_op jit(solution)/shard_map/ppermute | solution.py:429
  46.0 26.8 %all-to-all-start.1 = ((bf16[256,8,128]{2,1,0:T(8,128)(2,1)}), bf16[256,8,128]{2,1,0:T(8,128)(2,1)}, u32[]{:S(2)}, u32[]{:S(2)}) async-start(bf16[256,8,128]{2,1,0:T(8,128)(2,1)} %bitcast.4), calls=%async_computation.1 | async-start | bytes 1048576 | tf_op jit(solution)/shard_map/all_to_all | solution.py:451
  54.5 2.8 %copy-start = (bf16[1024,768]{1,0:T(8,128)(2,1)S(1)}, bf16[1024,768]{1,0:T(8,128)(2,1)}, u32[]{:S(2)}) copy-start(bf16[1024,768]{1,0:T(8,128)(2,1)} %value_ref.3) | copy-start | bytes 4718596
  55.9 4.9 %collective-permute-start.7 = (bf16[3,4,128,384]{3,2,1,0:T(8,128)(2,1)}, bf16[3,4,128,384]{3,2,1,0:T(8,128)(2,1)}, u32[]{:S(2)}, u32[]{:S(2)}) collective-permute-start(bf16[3,4,128,384]{3,2,1,0:T(8,128)(2,1)} %get-tuple-element.18.near), channel_id=1, source_target_pairs={{0,4},{4,0},{8,12},{12,8},{16,20},{20,16},{24,28},{28,24},{32,36},... | collective-permute-start | bytes 3538952 | tf_op jit(solution)/shard_map/ppermute | solution.py:439
  57.4 15.4 %collective-permute-start.8 = (bf16[2,3,128,512]{3,2,1,0:T(8,128)(2,1)}, bf16[2,3,128,512]{3,2,1,0:T(8,128)(2,1)}, u32[]{:S(2)}, u32[]{:S(2)}) collective-permute-start(bf16[2,3,128,512]{3,2,1,0:T(8,128)(2,1)} %get-tuple-element.20.near), channel_id=1, source_target_pairs={{0,4},{4,0},{8,12},{12,8},{16,20},{20,16},{24,28},{28,24},{32,36},... | collective-permute-start | bytes 2359304 | tf_op jit(solution)/shard_map/ppermute | solution.py:439
  60.9 11.9 %copy-start.1 = (bf16[256,1024]{1,0:T(8,128)(2,1)S(1)}, bf16[256,1024]{1,0:T(8,128)(2,1)}, u32[]{:S(2)}) copy-start(bf16[256,1024]{1,0:T(8,128)(2,1)} %w_out.1) | copy-start | bytes 1572868

commit v10 on v9

--- a/solution.py
+++ b/solution.py
@@ -20,7 +20,7 @@
 ORDER = (2, 1, 3)
 STEPS = (2, 3, 1)
 WIDE = 5 * HALF
-BOTH = ("rows", "heads")
+BOTH = ("heads", "rows")
 SCALE = 0.125 * 1.4426950408889634
 
 
@@ -218,7 +218,7 @@
             for b in range(4):
                 lo = j * BLOCK + b * 32
                 part = held[:, lo : lo + 32, :].reshape(BLOCK, HALF)
-                out_ref[b * 16 : (b + 1) * 16, j] = move(pick, part).reshape(16, 8, HALF)
+                out_ref[j, b * 16 : (b + 1) * 16] = move(pick, part).reshape(16, 8, HALF)
 
 
 def row_part(sig, w_qkv, after):
@@ -238,10 +238,10 @@
             anywhere(),
         ],
         out_specs=[
-            pl.BlockSpec((64, GROUPS, 8, HALF), lambda r: (0, 0, 0, 0)),
+            pl.BlockSpec((GROUPS, 64, 8, HALF), lambda r: (0, 0, 0, 0)),
             pl.BlockSpec((16, HALF), lambda r: (0, 0)),
         ],
-        out_shape=[like(64, GROUPS, 8, HALF), like(16, HALF)],
+        out_shape=[like(GROUPS, 64, 8, HALF), like(16, HALF)],
         scratch_shapes=[VMEM((ROWS_LOCAL, C, HALF), BF)],
     )(sig, w_qkv, w_qkv, w_qkv, after)
 
@@ -359,7 +359,7 @@
     left = jnp.concatenate(
         [columns[...]]
         + [
-            rows[:, lax.rem(group_of(meta) + GROUPS - k, GROUPS)].reshape(C, HALF)
+            rows[lax.rem(group_of(meta) + GROUPS - k, GROUPS)].reshape(C, HALF)
             for k in (0,) + ORDER
         ],
         axis=1,
@@ -382,7 +382,7 @@
             axis=0,
         )
         mixed = jnp.dot(left, weight, preferred_element_type=F32)
-        out_ref[:, j] = mixed.astype(BF).reshape(64, 8, 256)
+        out_ref[j] = mixed.astype(BF).reshape(64, 8, 256)
 
 
 def mix(meta, columns, rows, w_out, near, far):
@@ -394,7 +394,7 @@
         vmem=20 * MIB,
         in_specs=[smem()] + [whole()] * 5,
         out_specs=whole(),
-        out_shape=like(64, GROUPS, 8, 256),
+        out_shape=like(GROUPS, 64, 8, 256),
     )(meta, columns, rows, w_out, near, far)
 
 
@@ -402,7 +402,7 @@
     j = pl.program_id(0)
     pick = one_hot(lambda o: ((o // 2) % 16) * 8 + (o // 32) * 2 + o % 2)
     for b in range(4):
-        moved = move(pick, got_ref[b * 16 : (b + 1) * 16, j].reshape(BLOCK, 256))
+        moved = move(pick, got_ref[j, b * 16 : (b + 1) * 16].reshape(BLOCK, 256))
         for r in range(ROWS_LOCAL):
             out_ref[r, 0, b * 32 : (b + 1) * 32] = moved[r * 32 : (r + 1) * 32]
 
@@ -450,7 +450,7 @@
     ).reshape(C, D)
     rows = lax.all_to_all(
         own_rows.reshape(64 * GROUPS, 8, HALF), BOTH, split_axis=0, concat_axis=0, tiled=True
-    ).reshape(64, GROUPS, 8, HALF)
+    ).reshape(GROUPS, 64, 8, HALF)
 
     mine = cut(meta, w_qkv, w_out)
     others, blocks = mid([to_group(mine, k) for k in ORDER], rows_done)
@@ -464,7 +464,7 @@
     columns = column_part(by_x, own, near, far)
     mixed = mix(meta, columns, rows, w_out, blocks, far_blocks).reshape(64 * GROUPS, 8, 256)
     back = lax.all_to_all(mixed, BOTH, split_axis=0, concat_axis=0, tiled=True)
-    return join(back.reshape(64, GROUPS, 8, 256)).reshape(ROWS_LOCAL * C, 256)
+    return join(back.reshape(GROUPS, 64, 8, 256)).reshape(ROWS_LOCAL * C, 256)
 
 
 def solution(mesh):

time: 115 us -> 115 us (level)
  no operation moved by 1% of the time
where the time goes in v10:
time: 115 us; the launch traced here: 114 us
  blocking collectives  36.5 us (32%)
  starting transfers between devices  35.7 us (31%)
  Pallas kernels  27.9 us (24%)
  waiting for transfers between devices  13.1 us (11%)
    all_to_all x1, blocking collectives, local(): back = lax.all_to_all(mixed, BOTH, split_axis=0, concat_axis=0, tiled=True)  36.5 us
    ppermute x3, starting transfers between devices, to_group(): lax.ppermute(data, 'heads', [(j, (j + k) % GROUPS) for j in range(GROUPS)])  11.3 us
    all_to_all x1, starting transfers between devices, local(): lax.all_to_all(send.reshape(64, 8, D), 'rows', split_axis=0, concat_axis=...  9.64 us
    pallas_call x1, Pallas kernels, row_part(): call(row_kernel, 'row_part', moved=1, grid=(ROWS_LOCAL,), in_specs=[pl.Bl...  8.57 us
    all_to_all x1, starting transfers between devices, local(): lax.all_to_all(own_rows.reshape(64 * GROUPS, 8, HALF), BOTH, split_axis=0...  7.72 us
    all_to_all x1, waiting for transfers between devices, local(): lax.all_to_all(own_rows.reshape(64 * GROUPS, 8, HALF), BOTH, split_axis=0...  6.31 us
    all_to_all x1, waiting for transfers between devices, local(): lax.all_to_all(send.reshape(64, 8, D), 'rows', split_axis=0, concat_axis=...  5.92 us
    pallas_call x1, Pallas kernels, column_part(): call(column_kernel, 'column_part', flops=3 * 10 ** 9, moved=6 * MIB, vmem...  5.47 us
  transfers between devices with their start and end apart: 11, of which 3 were waited for; matrix products, arithmetic and copies ran while one was open for 0% of the time, Pallas kernels for 19%

profile of v10, /device:TPU:1, one launch (start us, length us, event | category | flops | bytes accessed | tf_op | source)
XLA Modules:
  0.0 114.1 jit_solution(16206489740975026871)
XLA Ops:
  0.0 1.7 %cut.1 = bf16[128,896]{1,0:T(8,128)(2,1)} custom-call(s32[1]{0:T(128)} %bitcast.meta, bf16[1024,768]{1,0:T(8,128)(2,1)} %value_ref.3, bf16[1024,768]{1,0:T(8,128)(2,1)} %value_ref.3, bf16[1024,768]{1,0:T(8,128)(2,1)} %value_ref.3, bf16[256,1024]{1,0:T(8,128)(2,1)} %w_out.1), custom_call_target="tpu_custom_call" | custom-call | bytes 1048576 | tf_op jit(solution)/shard_map/cut/pallas_call | solution.py:124
  1.7 7.7 %collective-permute-start = (bf16[128,896]{1,0:T(8,128)(2,1)}, bf16[128,896]{1,0:T(8,128)(2,1)S(1)}, u32[]{:S(2)}, u32[]{:S(2)}) collective-permute-start(bf16[128,896]{1,0:T(8,128)(2,1)} %cut.1), channel_id=1, source_target_pairs={{0,2},{1,3},{2,0},{3,1},{4,6},{5,7},{6,4},{7,5},{8,10},{9,11},{10,... | collective-permute-start | bytes 688136 | tf_op jit(solution)/shard_map/ppermute | solution.py:425
  9.4 1.2 %collective-permute-start.1 = (bf16[128,896]{1,0:T(8,128)(2,1)}, bf16[128,896]{1,0:T(8,128)(2,1)S(1)}, u32[]{:S(2)}, u32[]{:S(2)}) collective-permute-start(bf16[128,896]{1,0:T(8,128)(2,1)} %cut.1), channel_id=1, source_target_pairs={{0,1},{1,2},{2,3},{3,0},{4,5},{5,6},{6,7},{7,4},{8,9},{9,10},{10,1... | collective-permute-start | bytes 688136 | tf_op jit(solution)/shard_map/ppermute | solution.py:425
  10.6 2.4 %collective-permute-start.2 = (bf16[128,896]{1,0:T(8,128)(2,1)}, bf16[128,896]{1,0:T(8,128)(2,1)S(1)}, u32[]{:S(2)}, u32[]{:S(2)}) collective-permute-start(bf16[128,896]{1,0:T(8,128)(2,1)} %cut.1), channel_id=1, source_target_pairs={{0,3},{1,0},{2,1},{3,2},{4,7},{5,4},{6,5},{7,6},{8,11},{9,8},{10,9... | collective-permute-start | bytes 688136 | tf_op jit(solution)/shard_map/ppermute | solution.py:425
  13.0 2.4 %prep.1.after = bf16[512,1024]{1,0:T(8,128)(2,1)} custom-call(s32[1]{0:T(128)} %bitcast.meta, bf16[4,512,1024]{2,1,0:T(8,128)(2,1)} %bitcast.11), custom_call_target="tpu_custom_call" | custom-call | flops 134217728 | bytes 2097152 | tf_op jit(solution)/shard_map/prep/pallas_call | solution.py:188
  15.4 9.6 %all-to-all-start = ((bf16[64,8,1024]{2,1,0:T(8,128)(2,1)}), bf16[64,8,1024]{2,1,0:T(8,128)(2,1)}, u32[]{:S(2)}, u32[]{:S(2)}) async-start(bf16[64,8,1024]{2,1,0:T(8,128)(2,1)} %bitcast.13), calls=%async_computation | async-start | bytes 2097152 | tf_op jit(solution)/shard_map/all_to_all | solution.py:448
  25.1 8.6 %row_part.1 = (bf16[4,64,8,128]{3,2,1,0:T(8,128)(2,1)}, bf16[16,128]{1,0:T(8,128)(2,1)}) custom-call(bf16[4,512,1024]{2,1,0:T(8,128)(2,1)} %bitcast.12, bf16[1024,768]{1,0:T(8,128)(2,1)} %value_ref.3, bf16[1024,768]{1,0:T(8,128)(2,1)} %value_ref.3, bf16[1024,768]{1,0:T(8,128)(2,1)} %value_ref.3, bf16[512,1024]{1,0:T(8,128)(2,1)} %prep.1.after), custom_call_target="tpu_custom_call" | custom-call | bytes 1 | tf_op jit(solution)/shard_map/row_part/pallas_call | solution.py:228
  33.6 0.0 collective-permute-done.in0
  33.6 0.0 collective-permute-done.1.in1
  33.7 0.0 collective-permute-done.2.in2
  33.7 0.0 copy-start.2
  33.7 0.7 copy-done.2
  34.3 0.1 mid.1
  34.4 1.5 %collective-permute-start.6 = (bf16[3,128,512]{2,1,0:T(8,128)(2,1)S(1)}, bf16[3,128,512]{2,1,0:T(8,128)(2,1)S(1)}, u32[]{:S(2)}, u32[]{:S(2)}) collective-permute-start(bf16[3,128,512]{2,1,0:T(8,128)(2,1)S(1)} %get-tuple-element.17.block0), channel_id=1, source_target_pairs={{0,32},{4,36},{8,40},{12,44},{16,48},{20,52},{24,56},{28,60},{32,0... | collective-permute-start | bytes 1179656 | tf_op jit(solution)/shard_map/ppermute | solution.py:435
  35.9 2.7 %collective-permute-start.3 = (bf16[3,128,384]{2,1,0:T(8,128)(2,1)S(1)}, bf16[3,128,384]{2,1,0:T(8,128)(2,1)S(1)}, u32[]{:S(2)}, u32[]{:S(2)}) collective-permute-start(bf16[3,128,384]{2,1,0:T(8,128)(2,1)S(1)} %get-tuple-element.16.in0), channel_id=1, source_target_pairs={{0,16},{4,20},{8,24},{12,28},{16,0},{20,4},{24,8},{28,12},{32,48},... | collective-permute-start | bytes 884744 | tf_op jit(solution)/shard_map/ppermute | solution.py:429
  38.6 0.9 collective-permute-start.4
  39.5 0.6 collective-permute-start.5
  40.0 5.9 %all-to-all-done = bf16[64,8,1024]{2,1,0:T(8,128)(2,1)} async-done(((bf16[64,8,1024]{2,1,0:T(8,128)(2,1)}), bf16[64,8,1024]{2,1,0:T(8,128)(2,1)}, u32[]{:S(2)}, u32[]{:S(2)}) %all-to-all-start) | async-done | bytes 1048608 | tf_op jit(solution)/shard_map/all_to_all | solution.py:448
  46.0 7.7 %all-to-all-start.1 = ((bf16[256,8,128]{2,1,0:T(8,128)(2,1)}), bf16[256,8,128]{2,1,0:T(8,128)(2,1)}, u32[]{:S(2)}, u32[]{:S(2)}) async-start(bf16[256,8,128]{2,1,0:T(8,128)(2,1)} %bitcast.4), calls=%async_computation.1 | async-start | bytes 1048576 | tf_op jit(solution)/shard_map/all_to_all | solution.py:451
  53.7 0.0 collective-permute-done.3.in1
  53.7 0.0 collective-permute-done.4.in2
  53.7 0.8 collective-permute-done.5.in3
  54.5 0.0 collective-permute-done.6.block1
  54.5 0.0 copy-start
  54.5 1.4 %stack.1 = (bf16[3,4,128,384]{3,2,1,0:T(8,128)(2,1)}, bf16[2,3,128,512]{3,2,1,0:T(8,128)(2,1)}) custom-call(bf16[3,128,384]{2,1,0:T(8,128)(2,1)S(1)} %get-tuple-element.16.in0, bf16[3,128,384]{2,1,0:T(8,128)(2,1)S(1)} %collective-permute-done.3.in1, bf16[3,128,384]{2,1,0:T(8,128)(2,1)S(1)} %collective-permute-done.4.in2, ...), custom_call_target="tpu_custom_call" | custom-call | flops 1000000000 | bytes 1048576 | tf_op jit(solution)/shard_map/stack/pallas_call | solution.py:169
  55.9 1.4 %collective-permute-start.7 = (bf16[3,4,128,384]{3,2,1,0:T(8,128)(2,1)}, bf16[3,4,128,384]{3,2,1,0:T(8,128)(2,1)}, u32[]{:S(2)}, u32[]{:S(2)}) collective-permute-start(bf16[3,4,128,384]{3,2,1,0:T(8,128)(2,1)} %get-tuple-element.18.near), channel_id=1, source_target_pairs={{0,4},{4,0},{8,12},{12,8},{16,20},{20,16},{24,28},{28,24},{32,36},... | collective-permute-start | bytes 3538952 | tf_op jit(solution)/shard_map/ppermute | solution.py:439
  57.4 0.0 collective-permute-start.8
  57.4 0.0 copy-done
  57.4 3.5 %own_part.1 = (bf16[512,1024]{1,0:T(8,128)(2,1)S(1)}, bf16[512,128]{1,0:T(8,128)(2,1)S(1)}) custom-call(s32[1]{0:T(128)} %bitcast.meta, bf16[512,1024]{1,0:T(8,128)(2,1)} %bitcast.3.got_ref.after, bf16[1024,768]{1,0:T(8,128)(2,1)S(1)} %copy-done), custom_call_target="tpu_custom_call" | custom-call | flops 999999995904 | bytes 4194304 | tf_op jit(solution)/shard_map/own_part/pallas_call | solution.py:291
  60.8 0.0 collective-permute-done.7.far
  60.9 0.0 copy-start.1
  60.9 5.5 %column_part.1.columns = bf16[512,512]{1,0:T(8,128)(2,1)S(1)} custom-call(bf16[512,1024]{1,0:T(8,128)(2,1)S(1)} %get-tuple-element.13.by_x, bf16[512,128]{1,0:T(8,128)(2,1)S(1)} %get-tuple-element.14.own, bf16[3,4,128,384]{3,2,1,0:T(8,128)(2,1)} %get-tuple-element.18.near, bf16[3,4,128,384]{3,2,1,0:T(8,128)(2,1)} %collective-permute-done.7.far), custom_call_target="tpu_custom_call" | custom-call | flops 3000000000 | bytes 6291456 | tf_op jit(solution)/shard_map/column_part/pallas_call | solution.py:338
  66.4 6.3 %all-to-all-done.1 = bf16[256,8,128]{2,1,0:T(8,128)(2,1)} async-done(((bf16[256,8,128]{2,1,0:T(8,128)(2,1)}), bf16[256,8,128]{2,1,0:T(8,128)(2,1)}, u32[]{:S(2)}, u32[]{:S(2)}) %all-to-all-start.1) | async-done | bytes 524320 | tf_op jit(solution)/shard_map/all_to_all | solution.py:451
  72.7 0.0 collective-permute-done.8.far
  72.7 0.0 copy-done.1
  72.7 2.8 %mix.1 = bf16[4,64,8,256]{3,2,1,0:T(8,128)(2,1)S(1)} custom-call(s32[1]{0:T(128)} %bitcast.meta, bf16[512,512]{1,0:T(8,128)(2,1)S(1)} %column_part.1.columns, bf16[4,64,8,128]{3,2,1,0:T(8,128)(2,1)} %bitcast.5.rows, bf16[256,1024]{1,0:T(8,128)(2,1)S(1)} %copy-done.1, bf16[2,3,128,512]{3,2,1,0:T(8,128)(2,1)} %get-tuple-element.20.near, ...), custom_call_target="tpu_custom_call" | custom-call | flops 1000000000 | bytes 6291456 | tf_op jit(solution)/shard_map/mix/pallas_call | solution.py:389
  75.5 36.5 %all_to_all.15 = bf16[256,8,256]{2,1,0:T(8,128)(2,1)S(1)} all-to-all(bf16[256,8,256]{2,1,0:T(8,128)(2,1)S(1)} %bitcast.9), channel_id=1, replica_groups=mesh['rows'=64,'heads'=4] {'heads','rows'}, dimensions={0} | all-to-all | bytes 2097152 | tf_op jit(solution)/shard_map/all_to_all | solution.py:466
  112.0 2.1 %join.1 = bf16[4,4,128,256]{3,2,1,0:T(8,128)(2,1)} custom-call(bf16[4,64,8,256]{3,2,1,0:T(8,128)(2,1)S(1)} %bitcast.10), custom_call_target="tpu_custom_call" | custom-call | flops 100000000 | bytes 4194304 | tf_op jit(solution)/shard_map/join/pallas_call | solution.py:411
Async XLA Ops:
  1.7 32.0 %collective-permute-start = (bf16[128,896]{1,0:T(8,128)(2,1)}, bf16[128,896]{1,0:T(8,128)(2,1)S(1)}, u32[]{:S(2)}, u32[]{:S(2)}) collective-permute-start(bf16[128,896]{1,0:T(8,128)(2,1)} %cut.1), channel_id=1, source_target_pairs={{0,2},{1,3},{2,0},{3,1},{4,6},{5,7},{6,4},{7,5},{8,10},{9,11},{10,... | collective-permute-start | bytes 688136 | tf_op jit(solution)/shard_map/ppermute | solution.py:425
  9.4 24.2 %collective-permute-start.1 = (bf16[128,896]{1,0:T(8,128)(2,1)}, bf16[128,896]{1,0:T(8,128)(2,1)S(1)}, u32[]{:S(2)}, u32[]{:S(2)}) collective-permute-start(bf16[128,896]{1,0:T(8,128)(2,1)} %cut.1), channel_id=1, source_target_pairs={{0,1},{1,2},{2,3},{3,0},{4,5},{5,6},{6,7},{7,4},{8,9},{9,10},{10,1... | collective-permute-start | bytes 688136 | tf_op jit(solution)/shard_map/ppermute | solution.py:425
  10.6 23.1 %collective-permute-start.2 = (bf16[128,896]{1,0:T(8,128)(2,1)}, bf16[128,896]{1,0:T(8,128)(2,1)S(1)}, u32[]{:S(2)}, u32[]{:S(2)}) collective-permute-start(bf16[128,896]{1,0:T(8,128)(2,1)} %cut.1), channel_id=1, source_target_pairs={{0,3},{1,0},{2,1},{3,2},{4,7},{5,4},{6,5},{7,6},{8,11},{9,8},{10,9... | collective-permute-start | bytes 688136 | tf_op jit(solution)/shard_map/ppermute | solution.py:425
  15.4 30.5 %all-to-all-start = ((bf16[64,8,1024]{2,1,0:T(8,128)(2,1)}), bf16[64,8,1024]{2,1,0:T(8,128)(2,1)}, u32[]{:S(2)}, u32[]{:S(2)}) async-start(bf16[64,8,1024]{2,1,0:T(8,128)(2,1)} %bitcast.13), calls=%async_computation | async-start | bytes 2097152 | tf_op jit(solution)/shard_map/all_to_all | solution.py:448
  33.7 0.7 copy-start.2
  34.4 20.1 %collective-permute-start.6 = (bf16[3,128,512]{2,1,0:T(8,128)(2,1)S(1)}, bf16[3,128,512]{2,1,0:T(8,128)(2,1)S(1)}, u32[]{:S(2)}, u32[]{:S(2)}) collective-permute-start(bf16[3,128,512]{2,1,0:T(8,128)(2,1)S(1)} %get-tuple-element.17.block0), channel_id=1, source_target_pairs={{0,32},{4,36},{8,40},{12,44},{16,48},{20,52},{24,56},{28,60},{32,0... | collective-permute-start | bytes 1179656 | tf_op jit(solution)/shard_map/ppermute | solution.py:435
  35.9 17.8 %collective-permute-start.3 = (bf16[3,128,384]{2,1,0:T(8,128)(2,1)S(1)}, bf16[3,128,384]{2,1,0:T(8,128)(2,1)S(1)}, u32[]{:S(2)}, u32[]{:S(2)}) collective-permute-start(bf16[3,128,384]{2,1,0:T(8,128)(2,1)S(1)} %get-tuple-element.16.in0), channel_id=1, source_target_pairs={{0,16},{4,20},{8,24},{12,28},{16,0},{20,4},{24,8},{28,12},{32,48},... | collective-permute-start | bytes 884744 | tf_op jit(solution)/shard_map/ppermute | solution.py:429
  38.6 15.1 %collective-permute-start.4 = (bf16[3,128,384]{2,1,0:T(8,128)(2,1)S(1)}, bf16[3,128,384]{2,1,0:T(8,128)(2,1)S(1)}, u32[]{:S(2)}, u32[]{:S(2)}) collective-permute-start(bf16[3,128,384]{2,1,0:T(8,128)(2,1)S(1)} %get-tuple-element.16.in0), channel_id=1, source_target_pairs={{0,24},{4,28},{8,0},{12,4},{16,8},{20,12},{24,16},{28,20},{32,56},... | collective-permute-start | bytes 884744 | tf_op jit(solution)/shard_map/ppermute | solution.py:429
  39.5 15.1 %collective-permute-start.5 = (bf16[3,128,384]{2,1,0:T(8,128)(2,1)S(1)}, bf16[3,128,384]{2,1,0:T(8,128)(2,1)S(1)}, u32[]{:S(2)}, u32[]{:S(2)}) collective-permute-start(bf16[3,128,384]{2,1,0:T(8,128)(2,1)S(1)} %get-tuple-element.16.in0), channel_id=1, source_target_pairs={{0,8},{4,12},{8,16},{12,20},{16,24},{20,28},{24,0},{28,4},{32,40},... | collective-permute-start | bytes 884744 | tf_op jit(solution)/shard_map/ppermute | solution.py:429
  46.0 26.7 %all-to-all-start.1 = ((bf16[256,8,128]{2,1,0:T(8,128)(2,1)}), bf16[256,8,128]{2,1,0:T(8,128)(2,1)}, u32[]{:S(2)}, u32[]{:S(2)}) async-start(bf16[256,8,128]{2,1,0:T(8,128)(2,1)} %bitcast.4), calls=%async_computation.1 | async-start | bytes 1048576 | tf_op jit(solution)/shard_map/all_to_all | solution.py:451
  54.5 2.8 %copy-start = (bf16[1024,768]{1,0:T(8,128)(2,1)S(1)}, bf16[1024,768]{1,0:T(8,128)(2,1)}, u32[]{:S(2)}) copy-start(bf16[1024,768]{1,0:T(8,128)(2,1)} %value_ref.3) | copy-start | bytes 4718596
  55.9 4.9 %collective-permute-start.7 = (bf16[3,4,128,384]{3,2,1,0:T(8,128)(2,1)}, bf16[3,4,128,384]{3,2,1,0:T(8,128)(2,1)}, u32[]{:S(2)}, u32[]{:S(2)}) collective-permute-start(bf16[3,4,128,384]{3,2,1,0:T(8,128)(2,1)} %get-tuple-element.18.near), channel_id=1, source_target_pairs={{0,4},{4,0},{8,12},{12,8},{16,20},{20,16},{24,28},{28,24},{32,36},... | collective-permute-start | bytes 3538952 | tf_op jit(solution)/shard_map/ppermute | solution.py:439
  57.4 15.3 %collective-permute-start.8 = (bf16[2,3,128,512]{3,2,1,0:T(8,128)(2,1)}, bf16[2,3,128,512]{3,2,1,0:T(8,128)(2,1)}, u32[]{:S(2)}, u32[]{:S(2)}) collective-permute-start(bf16[2,3,128,512]{3,2,1,0:T(8,128)(2,1)} %get-tuple-element.20.near), channel_id=1, source_target_pairs={{0,4},{4,0},{8,12},{12,8},{16,20},{20,16},{24,28},{28,24},{32,36},... | collective-permute-start | bytes 2359304 | tf_op jit(solution)/shard_map/ppermute | solution.py:439
  60.9 11.8 %copy-start.1 = (bf16[256,1024]{1,0:T(8,128)(2,1)S(1)}, bf16[256,1024]{1,0:T(8,128)(2,1)}, u32[]{:S(2)}) copy-start(bf16[256,1024]{1,0:T(8,128)(2,1)} %w_out.1) | copy-start | bytes 1572868

commit v11 on v10

--- a/solution.py
+++ b/solution.py
@@ -399,12 +399,13 @@
 
 
 def join_kernel(got_ref, out_ref):
-    j = pl.program_id(0)
     pick = one_hot(lambda o: ((o // 2) % 16) * 8 + (o // 32) * 2 + o % 2)
-    for b in range(4):
-        moved = move(pick, got_ref[j, b * 16 : (b + 1) * 16].reshape(BLOCK, 256))
-        for r in range(ROWS_LOCAL):
-            out_ref[r, 0, b * 32 : (b + 1) * 32] = moved[r * 32 : (r + 1) * 32]
+    for n in range(2):
+        j = pl.program_id(0) * 2 + n
+        for b in range(4):
+            moved = move(pick, got_ref[j, b * 16 : (b + 1) * 16].reshape(BLOCK, 256))
+            for r in range(ROWS_LOCAL):
+                out_ref[r, n, b * 32 : (b + 1) * 32] = moved[r * 32 : (r + 1) * 32]
 
 
 def join(got):
@@ -414,9 +415,9 @@
         flops=10**8,
         moved=4 * MIB,
         vmem=16 * MIB,
-        grid=(GROUPS,),
+        grid=(2,),
         in_specs=[whole()],
-        out_specs=pl.BlockSpec((ROWS_LOCAL, 1, BLOCK, 256), lambda j: (0, j, 0, 0)),
+        out_specs=pl.BlockSpec((ROWS_LOCAL, 2, BLOCK, 256), lambda j: (0, j, 0, 0)),
         out_shape=like(ROWS_LOCAL, GROUPS, BLOCK, 256),
     )(got)
 

time: 115 us -> 114 us (level)
  no operation moved by 1% of the time
where the time goes in v11:
time: 114 us; the launch traced here: 113 us
  blocking collectives  36.5 us (32%)
  starting transfers between devices  35.7 us (31%)
  Pallas kernels  27.2 us (24%)
  waiting for transfers between devices  13.1 us (11%)
    all_to_all x1, blocking collectives, local(): back = lax.all_to_all(mixed, BOTH, split_axis=0, concat_axis=0, tiled=True)  36.5 us
    ppermute x3, starting transfers between devices, to_group(): lax.ppermute(data, 'heads', [(j, (j + k) % GROUPS) for j in range(GROUPS)])  11.3 us
    all_to_all x1, starting transfers between devices, local(): lax.all_to_all(send.reshape(64, 8, D), 'rows', split_axis=0, concat_axis=...  9.64 us
    pallas_call x1, Pallas kernels, row_part(): call(row_kernel, 'row_part', moved=1, grid=(ROWS_LOCAL,), in_specs=[pl.Bl...  8.57 us
    all_to_all x1, starting transfers between devices, local(): lax.all_to_all(own_rows.reshape(64 * GROUPS, 8, HALF), BOTH, split_axis=0...  7.72 us
    all_to_all x1, waiting for transfers between devices, local(): lax.all_to_all(own_rows.reshape(64 * GROUPS, 8, HALF), BOTH, split_axis=0...  6.31 us
    all_to_all x1, waiting for transfers between devices, local(): lax.all_to_all(send.reshape(64, 8, D), 'rows', split_axis=0, concat_axis=...  5.92 us
    pallas_call x1, Pallas kernels, column_part(): call(column_kernel, 'column_part', flops=3 * 10 ** 9, moved=6 * MIB, vmem...  5.47 us
  transfers between devices with their start and end apart: 11, of which 3 were waited for; matrix products, arithmetic and copies ran while one was open for 0% of the time, Pallas kernels for 19%

profile of v11, /device:TPU:1, one launch (start us, length us, event | category | flops | bytes accessed | tf_op | source)
XLA Modules:
  0.0 113.4 jit_solution(17832033512500071589)
XLA Ops:
  0.0 1.7 %cut.1 = bf16[128,896]{1,0:T(8,128)(2,1)} custom-call(s32[1]{0:T(128)} %bitcast.meta, bf16[1024,768]{1,0:T(8,128)(2,1)} %value_ref.3, bf16[1024,768]{1,0:T(8,128)(2,1)} %value_ref.3, bf16[1024,768]{1,0:T(8,128)(2,1)} %value_ref.3, bf16[256,1024]{1,0:T(8,128)(2,1)} %w_out.1), custom_call_target="tpu_custom_call" | custom-call | bytes 1048576 | tf_op jit(solution)/shard_map/cut/pallas_call | solution.py:124
  1.7 7.7 %collective-permute-start = (bf16[128,896]{1,0:T(8,128)(2,1)}, bf16[128,896]{1,0:T(8,128)(2,1)S(1)}, u32[]{:S(2)}, u32[]{:S(2)}) collective-permute-start(bf16[128,896]{1,0:T(8,128)(2,1)} %cut.1), channel_id=1, source_target_pairs={{0,2},{1,3},{2,0},{3,1},{4,6},{5,7},{6,4},{7,5},{8,10},{9,11},{10,... | collective-permute-start | bytes 688136 | tf_op jit(solution)/shard_map/ppermute | solution.py:426
  9.4 1.2 %collective-permute-start.1 = (bf16[128,896]{1,0:T(8,128)(2,1)}, bf16[128,896]{1,0:T(8,128)(2,1)S(1)}, u32[]{:S(2)}, u32[]{:S(2)}) collective-permute-start(bf16[128,896]{1,0:T(8,128)(2,1)} %cut.1), channel_id=1, source_target_pairs={{0,1},{1,2},{2,3},{3,0},{4,5},{5,6},{6,7},{7,4},{8,9},{9,10},{10,1... | collective-permute-start | bytes 688136 | tf_op jit(solution)/shard_map/ppermute | solution.py:426
  10.6 2.4 %collective-permute-start.2 = (bf16[128,896]{1,0:T(8,128)(2,1)}, bf16[128,896]{1,0:T(8,128)(2,1)S(1)}, u32[]{:S(2)}, u32[]{:S(2)}) collective-permute-start(bf16[128,896]{1,0:T(8,128)(2,1)} %cut.1), channel_id=1, source_target_pairs={{0,3},{1,0},{2,1},{3,2},{4,7},{5,4},{6,5},{7,6},{8,11},{9,8},{10,9... | collective-permute-start | bytes 688136 | tf_op jit(solution)/shard_map/ppermute | solution.py:426
  13.0 2.4 %prep.1.after = bf16[512,1024]{1,0:T(8,128)(2,1)} custom-call(s32[1]{0:T(128)} %bitcast.meta, bf16[4,512,1024]{2,1,0:T(8,128)(2,1)} %bitcast.11), custom_call_target="tpu_custom_call" | custom-call | flops 134217728 | bytes 2097152 | tf_op jit(solution)/shard_map/prep/pallas_call | solution.py:188
  15.4 9.6 %all-to-all-start = ((bf16[64,8,1024]{2,1,0:T(8,128)(2,1)}), bf16[64,8,1024]{2,1,0:T(8,128)(2,1)}, u32[]{:S(2)}, u32[]{:S(2)}) async-start(bf16[64,8,1024]{2,1,0:T(8,128)(2,1)} %bitcast.13), calls=%async_computation | async-start | bytes 2097152 | tf_op jit(solution)/shard_map/all_to_all | solution.py:449
  25.1 8.6 %row_part.1 = (bf16[4,64,8,128]{3,2,1,0:T(8,128)(2,1)}, bf16[16,128]{1,0:T(8,128)(2,1)}) custom-call(bf16[4,512,1024]{2,1,0:T(8,128)(2,1)} %bitcast.12, bf16[1024,768]{1,0:T(8,128)(2,1)} %value_ref.3, bf16[1024,768]{1,0:T(8,128)(2,1)} %value_ref.3, bf16[1024,768]{1,0:T(8,128)(2,1)} %value_ref.3, bf16[512,1024]{1,0:T(8,128)(2,1)} %prep.1.after), custom_call_target="tpu_custom_call" | custom-call | bytes 1 | tf_op jit(solution)/shard_map/row_part/pallas_call | solution.py:228
  33.6 0.0 collective-permute-done.in0
  33.6 0.0 collective-permute-done.1.in1
  33.7 0.0 collective-permute-done.2.in2
  33.7 0.0 copy-start.2
  33.7 0.7 copy-done.2
  34.3 0.1 mid.1
  34.4 1.5 %collective-permute-start.6 = (bf16[3,128,512]{2,1,0:T(8,128)(2,1)S(1)}, bf16[3,128,512]{2,1,0:T(8,128)(2,1)S(1)}, u32[]{:S(2)}, u32[]{:S(2)}) collective-permute-start(bf16[3,128,512]{2,1,0:T(8,128)(2,1)S(1)} %get-tuple-element.17.block0), channel_id=1, source_target_pairs={{0,32},{4,36},{8,40},{12,44},{16,48},{20,52},{24,56},{28,60},{32,0... | collective-permute-start | bytes 1179656 | tf_op jit(solution)/shard_map/ppermute | solution.py:436
  35.9 2.7 %collective-permute-start.3 = (bf16[3,128,384]{2,1,0:T(8,128)(2,1)S(1)}, bf16[3,128,384]{2,1,0:T(8,128)(2,1)S(1)}, u32[]{:S(2)}, u32[]{:S(2)}) collective-permute-start(bf16[3,128,384]{2,1,0:T(8,128)(2,1)S(1)} %get-tuple-element.16.in0), channel_id=1, source_target_pairs={{0,16},{4,20},{8,24},{12,28},{16,0},{20,4},{24,8},{28,12},{32,48},... | collective-permute-start | bytes 884744 | tf_op jit(solution)/shard_map/ppermute | solution.py:430
  38.6 0.9 collective-permute-start.4
  39.5 0.6 collective-permute-start.5
  40.0 5.9 %all-to-all-done = bf16[64,8,1024]{2,1,0:T(8,128)(2,1)} async-done(((bf16[64,8,1024]{2,1,0:T(8,128)(2,1)}), bf16[64,8,1024]{2,1,0:T(8,128)(2,1)}, u32[]{:S(2)}, u32[]{:S(2)}) %all-to-all-start) | async-done | bytes 1048608 | tf_op jit(solution)/shard_map/all_to_all | solution.py:449
  46.0 7.7 %all-to-all-start.1 = ((bf16[256,8,128]{2,1,0:T(8,128)(2,1)}), bf16[256,8,128]{2,1,0:T(8,128)(2,1)}, u32[]{:S(2)}, u32[]{:S(2)}) async-start(bf16[256,8,128]{2,1,0:T(8,128)(2,1)} %bitcast.4), calls=%async_computation.1 | async-start | bytes 1048576 | tf_op jit(solution)/shard_map/all_to_all | solution.py:452
  53.7 0.0 collective-permute-done.3.in1
  53.7 0.0 collective-permute-done.4.in2
  53.7 0.8 collective-permute-done.5.in3
  54.5 0.0 collective-permute-done.6.block1
  54.5 0.0 copy-start
  54.5 1.4 %stack.1 = (bf16[3,4,128,384]{3,2,1,0:T(8,128)(2,1)}, bf16[2,3,128,512]{3,2,1,0:T(8,128)(2,1)}) custom-call(bf16[3,128,384]{2,1,0:T(8,128)(2,1)S(1)} %get-tuple-element.16.in0, bf16[3,128,384]{2,1,0:T(8,128)(2,1)S(1)} %collective-permute-done.3.in1, bf16[3,128,384]{2,1,0:T(8,128)(2,1)S(1)} %collective-permute-done.4.in2, ...), custom_call_target="tpu_custom_call" | custom-call | flops 1000000000 | bytes 1048576 | tf_op jit(solution)/shard_map/stack/pallas_call | solution.py:169
  55.9 1.4 %collective-permute-start.7 = (bf16[3,4,128,384]{3,2,1,0:T(8,128)(2,1)}, bf16[3,4,128,384]{3,2,1,0:T(8,128)(2,1)}, u32[]{:S(2)}, u32[]{:S(2)}) collective-permute-start(bf16[3,4,128,384]{3,2,1,0:T(8,128)(2,1)} %get-tuple-element.18.near), channel_id=1, source_target_pairs={{0,4},{4,0},{8,12},{12,8},{16,20},{20,16},{24,28},{28,24},{32,36},... | collective-permute-start | bytes 3538952 | tf_op jit(solution)/shard_map/ppermute | solution.py:440
  57.4 0.0 collective-permute-start.8
  57.4 0.0 copy-done
  57.4 3.5 %own_part.1 = (bf16[512,1024]{1,0:T(8,128)(2,1)S(1)}, bf16[512,128]{1,0:T(8,128)(2,1)S(1)}) custom-call(s32[1]{0:T(128)} %bitcast.meta, bf16[512,1024]{1,0:T(8,128)(2,1)} %bitcast.3.got_ref.after, bf16[1024,768]{1,0:T(8,128)(2,1)S(1)} %copy-done), custom_call_target="tpu_custom_call" | custom-call | flops 999999995904 | bytes 4194304 | tf_op jit(solution)/shard_map/own_part/pallas_call | solution.py:291
  60.8 0.0 collective-permute-done.7.far
  60.9 0.0 copy-start.1
  60.9 5.5 %column_part.1.columns = bf16[512,512]{1,0:T(8,128)(2,1)S(1)} custom-call(bf16[512,1024]{1,0:T(8,128)(2,1)S(1)} %get-tuple-element.13.by_x, bf16[512,128]{1,0:T(8,128)(2,1)S(1)} %get-tuple-element.14.own, bf16[3,4,128,384]{3,2,1,0:T(8,128)(2,1)} %get-tuple-element.18.near, bf16[3,4,128,384]{3,2,1,0:T(8,128)(2,1)} %collective-permute-done.7.far), custom_call_target="tpu_custom_call" | custom-call | flops 3000000000 | bytes 6291456 | tf_op jit(solution)/shard_map/column_part/pallas_call | solution.py:338
  66.4 6.3 %all-to-all-done.1 = bf16[256,8,128]{2,1,0:T(8,128)(2,1)} async-done(((bf16[256,8,128]{2,1,0:T(8,128)(2,1)}), bf16[256,8,128]{2,1,0:T(8,128)(2,1)}, u32[]{:S(2)}, u32[]{:S(2)}) %all-to-all-start.1) | async-done | bytes 524320 | tf_op jit(solution)/shard_map/all_to_all | solution.py:452
  72.7 0.0 collective-permute-done.8.far
  72.7 0.0 copy-done.1
  72.7 2.8 %mix.1 = bf16[4,64,8,256]{3,2,1,0:T(8,128)(2,1)S(1)} custom-call(s32[1]{0:T(128)} %bitcast.meta, bf16[512,512]{1,0:T(8,128)(2,1)S(1)} %column_part.1.columns, bf16[4,64,8,128]{3,2,1,0:T(8,128)(2,1)} %bitcast.5.rows, bf16[256,1024]{1,0:T(8,128)(2,1)S(1)} %copy-done.1, bf16[2,3,128,512]{3,2,1,0:T(8,128)(2,1)} %get-tuple-element.20.near, ...), custom_call_target="tpu_custom_call" | custom-call | flops 1000000000 | bytes 6291456 | tf_op jit(solution)/shard_map/mix/pallas_call | solution.py:389
  75.5 36.5 %all_to_all.15 = bf16[256,8,256]{2,1,0:T(8,128)(2,1)S(1)} all-to-all(bf16[256,8,256]{2,1,0:T(8,128)(2,1)S(1)} %bitcast.9), channel_id=1, replica_groups=mesh['rows'=64,'heads'=4] {'heads','rows'}, dimensions={0} | all-to-all | bytes 2097152 | tf_op jit(solution)/shard_map/all_to_all | solution.py:467
  112.0 1.4 %join.1 = bf16[4,4,128,256]{3,2,1,0:T(8,128)(2,1)} custom-call(bf16[4,64,8,256]{3,2,1,0:T(8,128)(2,1)S(1)} %bitcast.10), custom_call_target="tpu_custom_call" | custom-call | flops 100000000 | bytes 4194304 | tf_op jit(solution)/shard_map/join/pallas_call | solution.py:412
Async XLA Ops:
  1.7 32.0 %collective-permute-start = (bf16[128,896]{1,0:T(8,128)(2,1)}, bf16[128,896]{1,0:T(8,128)(2,1)S(1)}, u32[]{:S(2)}, u32[]{:S(2)}) collective-permute-start(bf16[128,896]{1,0:T(8,128)(2,1)} %cut.1), channel_id=1, source_target_pairs={{0,2},{1,3},{2,0},{3,1},{4,6},{5,7},{6,4},{7,5},{8,10},{9,11},{10,... | collective-permute-start | bytes 688136 | tf_op jit(solution)/shard_map/ppermute | solution.py:426
  9.4 24.2 %collective-permute-start.1 = (bf16[128,896]{1,0:T(8,128)(2,1)}, bf16[128,896]{1,0:T(8,128)(2,1)S(1)}, u32[]{:S(2)}, u32[]{:S(2)}) collective-permute-start(bf16[128,896]{1,0:T(8,128)(2,1)} %cut.1), channel_id=1, source_target_pairs={{0,1},{1,2},{2,3},{3,0},{4,5},{5,6},{6,7},{7,4},{8,9},{9,10},{10,1... | collective-permute-start | bytes 688136 | tf_op jit(solution)/shard_map/ppermute | solution.py:426
  10.6 23.1 %collective-permute-start.2 = (bf16[128,896]{1,0:T(8,128)(2,1)}, bf16[128,896]{1,0:T(8,128)(2,1)S(1)}, u32[]{:S(2)}, u32[]{:S(2)}) collective-permute-start(bf16[128,896]{1,0:T(8,128)(2,1)} %cut.1), channel_id=1, source_target_pairs={{0,3},{1,0},{2,1},{3,2},{4,7},{5,4},{6,5},{7,6},{8,11},{9,8},{10,9... | collective-permute-start | bytes 688136 | tf_op jit(solution)/shard_map/ppermute | solution.py:426
  15.4 30.5 %all-to-all-start = ((bf16[64,8,1024]{2,1,0:T(8,128)(2,1)}), bf16[64,8,1024]{2,1,0:T(8,128)(2,1)}, u32[]{:S(2)}, u32[]{:S(2)}) async-start(bf16[64,8,1024]{2,1,0:T(8,128)(2,1)} %bitcast.13), calls=%async_computation | async-start | bytes 2097152 | tf_op jit(solution)/shard_map/all_to_all | solution.py:449
  33.7 0.7 copy-start.2
  34.4 20.1 %collective-permute-start.6 = (bf16[3,128,512]{2,1,0:T(8,128)(2,1)S(1)}, bf16[3,128,512]{2,1,0:T(8,128)(2,1)S(1)}, u32[]{:S(2)}, u32[]{:S(2)}) collective-permute-start(bf16[3,128,512]{2,1,0:T(8,128)(2,1)S(1)} %get-tuple-element.17.block0), channel_id=1, source_target_pairs={{0,32},{4,36},{8,40},{12,44},{16,48},{20,52},{24,56},{28,60},{32,0... | collective-permute-start | bytes 1179656 | tf_op jit(solution)/shard_map/ppermute | solution.py:436
  35.9 17.8 %collective-permute-start.3 = (bf16[3,128,384]{2,1,0:T(8,128)(2,1)S(1)}, bf16[3,128,384]{2,1,0:T(8,128)(2,1)S(1)}, u32[]{:S(2)}, u32[]{:S(2)}) collective-permute-start(bf16[3,128,384]{2,1,0:T(8,128)(2,1)S(1)} %get-tuple-element.16.in0), channel_id=1, source_target_pairs={{0,16},{4,20},{8,24},{12,28},{16,0},{20,4},{24,8},{28,12},{32,48},... | collective-permute-start | bytes 884744 | tf_op jit(solution)/shard_map/ppermute | solution.py:430
  38.6 15.1 %collective-permute-start.4 = (bf16[3,128,384]{2,1,0:T(8,128)(2,1)S(1)}, bf16[3,128,384]{2,1,0:T(8,128)(2,1)S(1)}, u32[]{:S(2)}, u32[]{:S(2)}) collective-permute-start(bf16[3,128,384]{2,1,0:T(8,128)(2,1)S(1)} %get-tuple-element.16.in0), channel_id=1, source_target_pairs={{0,24},{4,28},{8,0},{12,4},{16,8},{20,12},{24,16},{28,20},{32,56},... | collective-permute-start | bytes 884744 | tf_op jit(solution)/shard_map/ppermute | solution.py:430
  39.5 15.1 %collective-permute-start.5 = (bf16[3,128,384]{2,1,0:T(8,128)(2,1)S(1)}, bf16[3,128,384]{2,1,0:T(8,128)(2,1)S(1)}, u32[]{:S(2)}, u32[]{:S(2)}) collective-permute-start(bf16[3,128,384]{2,1,0:T(8,128)(2,1)S(1)} %get-tuple-element.16.in0), channel_id=1, source_target_pairs={{0,8},{4,12},{8,16},{12,20},{16,24},{20,28},{24,0},{28,4},{32,40},... | collective-permute-start | bytes 884744 | tf_op jit(solution)/shard_map/ppermute | solution.py:430
  46.0 26.7 %all-to-all-start.1 = ((bf16[256,8,128]{2,1,0:T(8,128)(2,1)}), bf16[256,8,128]{2,1,0:T(8,128)(2,1)}, u32[]{:S(2)}, u32[]{:S(2)}) async-start(bf16[256,8,128]{2,1,0:T(8,128)(2,1)} %bitcast.4), calls=%async_computation.1 | async-start | bytes 1048576 | tf_op jit(solution)/shard_map/all_to_all | solution.py:452
  54.5 2.8 %copy-start = (bf16[1024,768]{1,0:T(8,128)(2,1)S(1)}, bf16[1024,768]{1,0:T(8,128)(2,1)}, u32[]{:S(2)}) copy-start(bf16[1024,768]{1,0:T(8,128)(2,1)} %value_ref.3) | copy-start | bytes 4718596
  55.9 4.9 %collective-permute-start.7 = (bf16[3,4,128,384]{3,2,1,0:T(8,128)(2,1)}, bf16[3,4,128,384]{3,2,1,0:T(8,128)(2,1)}, u32[]{:S(2)}, u32[]{:S(2)}) collective-permute-start(bf16[3,4,128,384]{3,2,1,0:T(8,128)(2,1)} %get-tuple-element.18.near), channel_id=1, source_target_pairs={{0,4},{4,0},{8,12},{12,8},{16,20},{20,16},{24,28},{28,24},{32,36},... | collective-permute-start | bytes 3538952 | tf_op jit(solution)/shard_map/ppermute | solution.py:440
  57.4 15.3 %collective-permute-start.8 = (bf16[2,3,128,512]{3,2,1,0:T(8,128)(2,1)}, bf16[2,3,128,512]{3,2,1,0:T(8,128)(2,1)}, u32[]{:S(2)}, u32[]{:S(2)}) collective-permute-start(bf16[2,3,128,512]{3,2,1,0:T(8,128)(2,1)} %get-tuple-element.20.near), channel_id=1, source_target_pairs={{0,4},{4,0},{8,12},{12,8},{16,20},{20,16},{24,28},{28,24},{32,36},... | collective-permute-start | bytes 2359304 | tf_op jit(solution)/shard_map/ppermute | solution.py:440
  60.9 11.8 %copy-start.1 = (bf16[256,1024]{1,0:T(8,128)(2,1)S(1)}, bf16[256,1024]{1,0:T(8,128)(2,1)}, u32[]{:S(2)}) copy-start(bf16[256,1024]{1,0:T(8,128)(2,1)} %w_out.1) | copy-start | bytes 1572868
